TPU v7x, 32 devices: a whole 2x2x4 slice. The times are simulated.
32 devices in a mesh: section: 2 (over x), seq: 16 (over z, y, core).
Axes of the slice: x: 2, y: 2, z: 4, core: 2. Of those that a mesh axis runs over, the one named last changes fastest.
Arguments:
- cotangent: bfloat16 [2048, 4096], P('seq'), may hold values from -6 to 6
- in_gate: bfloat16 [2, 2048, 4096], P('section', 'seq'), may hold values from -4 to 4
- mid_gate: bfloat16 [2, 2048, 4096], P('section', 'seq'), may hold values from -4 to 4
- layer_inputs: bfloat16 [2, 2048, 4096], P('section', 'seq'), may hold values from -6 to 6
- filters: bfloat16 [2, 128, 256], P('section'), may hold values from -0.5 to 0.5
- steer_second: float32 [2, 4096], P('section', 'seq'), may hold values from 2048 to 32768
- filter_second: float32 [2, 128, 256], P('section', None, 'seq'), may hold values from 8192 to 131072
Outputs:
- steer_step: float32 [2, 4096], P('section', 'seq')
- filter_step: float32 [2, 128, 256], P('section', None, 'seq')
All inputs are finite; a program needn't handle non-finite values.
Results may differ from a plain program's by a relative error of at most 0.0095.
Values may be sent and summed in bfloat16 or wider, within the bound.
No kernel may reach another device: no remote copies, remote signals or barrier semaphores. Data moves between devices by JAX's collectives and lax.ppermute only.
A program may use at most 192 MiB of HBM per device.

v0:
```python
import math

import jax
import jax.numpy as jnp
from jax import lax
from jax.sharding import PartitionSpec as P


def from_behind(block, axis, distance):
    devices = range(lax.axis_size(axis))
    route = [(i - distance, i) for i in devices if i - distance in devices]
    return lax.ppermute(block, axis, route)


def band_matrix(kernel, block_len):
    filt_len, group_count = kernel.shape
    span_len = block_len + filt_len
    padded = jnp.concatenate([kernel.T, jnp.zeros((group_count, block_len + 1), kernel.dtype)], 1)
    tiled_rows = jnp.tile(padded, (1, block_len))[:, : block_len * span_len]
    return tiled_rows.reshape(group_count, block_len, span_len)


def to_columns(matrix, group_count):
    row_count, channel_count = matrix.shape
    return matrix.T.reshape(group_count, channel_count // group_count, row_count)


def filter_rows(band_part, extended):
    pieces = [jnp.einsum("gcs,grs->gcr", extended, band_part, preferred_element_type=jnp.float32)]
    if len(pieces) == 1:
        return pieces[0]
    return jnp.concatenate(pieces, 2)


def filter_grad(extended, values, block_len, filt_len):
    group_count = values.shape[0]
    span_len = block_len + filt_len
    pairwise = jnp.einsum("gcr,gcs->grs", values, extended, preferred_element_type=jnp.float32)
    flat_rows = pairwise.reshape(group_count, block_len * span_len)
    flat_rows = jnp.concatenate([flat_rows, jnp.zeros((group_count, block_len), jnp.float32)], 1)
    skewed = flat_rows.reshape(group_count, block_len, span_len + 1)
    total = jnp.sum(skewed[:, :, :filt_len], 1)
    return total.T


def weigh(current, gate_part):
    return (gate_part.astype(jnp.float32) * current.astype(jnp.float32)).astype(jnp.bfloat16)


def finish(current, mid_part, band_part, extended):
    filtered = filter_rows(band_part, extended)
    return (current.astype(jnp.float32) + mid_part.astype(jnp.float32) * filtered).astype(
        jnp.bfloat16
    )


def adagrad(grad_part, second_part):
    return grad_part / jnp.sqrt(second_part + grad_part * grad_part)


def body(cotangent, in_gate, mid_gate, layer_inputs, filters, steer_second, filter_second):
    row_count, channel_count = (in_gate.shape[1], in_gate.shape[2])
    filt_len, group_count = (filters.shape[1], filters.shape[2])
    group_size = channel_count // group_count
    block_len = math.gcd(row_count, 128)
    sections = lax.axis_size("section")
    my_section = lax.axis_index("section")
    last_section = sections - 1
    band_full = band_matrix(filters[0], block_len)
    gate_cols = to_columns(in_gate[0], group_count)
    mid_cols = to_columns(mid_gate[0], group_count)
    input_cols = to_columns(layer_inputs[0], group_count)
    cot_cols = to_columns(cotangent, group_count)
    group_width = group_count // sections

    def one_turn(turn_index, state_now):
        incoming, kept_ext, kept_grad = state_now
        block_index = turn_index - (last_section - my_section)
        inside = jnp.logical_and(block_index >= 0, block_index < sections)
        clipped = jnp.clip(block_index, 0, sections - 1)
        first_group = clipped * group_width
        fresh_block = lax.dynamic_slice_in_dim(cot_cols, first_group, group_width, 0)
        current = jnp.where(my_section == last_section, fresh_block, incoming)
        gate_block = lax.dynamic_slice_in_dim(gate_cols, first_group, group_width, 0)
        mid_block = lax.dynamic_slice_in_dim(mid_cols, first_group, group_width, 0)
        band_block = lax.dynamic_slice_in_dim(band_full, first_group, group_width, 0)
        weighted = weigh(current, gate_block)
        next_rows = from_behind(weighted, "seq", -1)
        extended = jnp.concatenate([weighted, next_rows], 2)
        outgoing = finish(current, mid_block, band_block, extended)
        old_ext = lax.dynamic_slice_in_dim(kept_ext, first_group, group_width, 0)
        old_grad = lax.dynamic_slice_in_dim(kept_grad, first_group, group_width, 0)
        kept_ext = lax.dynamic_update_slice_in_dim(
            kept_ext, jnp.where(inside, extended, old_ext), first_group, 0
        )
        kept_grad = lax.dynamic_update_slice_in_dim(
            kept_grad, jnp.where(inside, outgoing, old_grad), first_group, 0
        )
        passed = from_behind(outgoing, "section", -1)
        return (passed, kept_ext, kept_grad)

    start_state = (
        jnp.zeros((group_width, group_size, row_count), jnp.bfloat16),
        jnp.zeros((group_count, group_size, row_count + filt_len), jnp.bfloat16),
        jnp.zeros((group_count, group_size, row_count), jnp.bfloat16),
    )
    final_state = lax.fori_loop(0, sections + sections - 1, one_turn, start_state)
    values = (mid_cols.astype(jnp.float32) * input_cols.astype(jnp.float32)).astype(jnp.bfloat16)
    local_filter = filter_grad(final_state[1], values, block_len, filt_len)
    local_steer = jnp.sum(final_state[2].astype(jnp.float32), 2).reshape(channel_count)
    steer_part, filter_part = (
        lax.psum_scatter(local_steer, "seq", scatter_dimension=0, tiled=True),
        lax.psum_scatter(local_filter, "seq", scatter_dimension=1, tiled=True),
    )
    return (
        adagrad(steer_part, steer_second[0])[None],
        adagrad(filter_part, filter_second[0])[None],
    )


def solution(mesh):
    in_specs = (
        P("seq", None),
        P("section", "seq", None),
        P("section", "seq", None),
        P("section", "seq", None),
        P("section", None, None),
        P("section", "seq"),
        P("section", None, "seq"),
    )
    out_specs = (P("section", "seq"), P("section", None, "seq"))
    return jax.shard_map(body, mesh=mesh, in_specs=in_specs, out_specs=out_specs, check_vma=False)
```

profile of v0, /device:TPU:0, one launch (start us, length us, event | category | flops | bytes accessed | tf_op | source)
XLA Modules:
  0.0 384.1 jit_solution(3884457715300163099)
XLA Ops:
  7.2 0.0 copy-start.2
  7.2 0.0 reduce-scatter.4.cloned.1.call-start
  7.2 1.7 copy.28
  8.9 0.0 copy-done.2
  8.9 0.0 copy-start.3
  8.9 1.3 copy.29
  10.3 2.3 copy.30
  12.5 0.0 copy-done.3
  12.6 6.3 %tile.4 = bf16[256,128,257]{0,2,1:T(8,128)(2,1)} broadcast(bf16[256,257]{0,1:T(8,128)(2,1)S(1)} %concatenate.15), dimensions={0,2} | broadcast | bytes 16974336 | tf_op jit(solution)/shard_map/tile | solution.py:19
  18.8 19.2 %tile.10 = bf16[256,32896]{0,1:T(8,128)(2,1)} reshape(bf16[256,128,257]{0,2,1:T(8,128)(2,1)} %tile.4) | data formatting | bytes 33685504 | tf_op jit(solution)/shard_map/tile | solution.py:19
  38.1 13.8 %slice.8 = bf16[256,32768]{0,1:T(8,128)(2,1)} slice(bf16[256,32896]{0,1:T(8,128)(2,1)} %tile.10), slice={[0:256], [0:32768]} | slice | bytes 33554432 | tf_op jit(solution)/shard_map/slice | solution.py:19
  51.9 0.0 copy-done.1
  51.9 1.6 convert_bitcast_fusion
  53.5 2.9 copy.32
  56.4 0.1 broadcast_in_dim.17
  56.5 1.5 broadcast_in_dim.18
  58.0 1.1 broadcast_in_dim.19
  59.1 138.6 %while.19 = (s32[]{:T(128)}, bf16[128,16,128]{2,1,0:T(8,128)(2,1)S(1)}, bf16[256,16,256]{2,1,0:T(8,128)(2,1)}, bf16[256,16,128]{2,1,0:T(8,128)(2,1)}, pred[]{:T(...) while((s32[]{:T(128)}, ...), condition=%wide.region_1.2_spmd, body=%wide.region_0.1_spmd.sunk | while | flops 142082064 | bytes 55575380 | solution.py:107
  59.1 1.2 fusion.13
  60.3 1.3 collective-permute-start
  61.6 7.7 %constant_dynamic-slice_fusion.2 = bf16[128,128,256]{0,2,1:T(8,128)(2,1)} fusion(bf16[256,128,256]{0,2,1:T(8,128)(2,1)} %get-tuple-element.382, s32[]{:T(128)S(6)} %select_n.101), kind=kLoop, calls=%fused_computation.9.clone.1 | loop fusion | bytes 16777220 | tf_op jit(solution)/shard_map/while/body/eval_jaxpr/dynamic_slice | solution.py:86
  69.4 12.7 %copy.41 = bf16[128,128,256]{2,1,0:T(8,128)(2,1)} copy(bf16[128,128,256]{0,2,1:T(8,128)(2,1)} %constant_dynamic-slice_fusion.2) | data formatting | bytes 16777216 | tf_op jit(solution)/shard_map/while/body/eval_jaxpr/dynamic_slice | solution.py:86
  82.0 0.0 collective-permute-done
  82.0 6.7 %select_dynamic-update-slice_fusion.4 = (bf16[256,16,128]{2,1,0:T(8,128)(2,1)}, bf16[128,16,128]{2,1,0:T(8,128)(2,1)S(1)}) fusion(bf16[256,16,128]{2,1,0:T(8,128)(2,1)} %get-tuple-element.361, s32[]{:T(128)S(6)} %select_n.101, pred[]{:T(512)S(6)} %and.11, bf16[128,128,256]{2,1,0:T(8,128)(2,1)} %copy.41, ...), kind=kOutput, calls=%fused_computation.7.clone.1 | convolution fusion | flops 138149888 | bytes 12583429 | tf_op jit(solution)/shard_map/while/body/eval_jaxpr/gcs,grs->gcr/dot_general | solution.py:29
  88.7 1.3 collective-permute-start.1
  90.0 2.5 select_dynamic-update-slice_fusion.5
  92.5 12.8 %collective-permute-done.1 = bf16[128,16,128]{2,1,0:T(8,128)(2,1)S(1)} collective-permute-done((bf16[128,16,128]{2,1,0:T(8,128)(2,1)S(1)}, bf16[128,16,128]{2,1,0:T(8,128)(2,1)S(1)}, u32[]{:S(2)}, u32[]{:S(2)}) %collective-permute-start.1) | collective-permute-done | bytes 524320 | tf_op jit(solution)/shard_map/while/body/eval_jaxpr/ppermute | solution.py:12
  105.3 1.2 fusion.13
  106.6 1.3 collective-permute-start
  107.9 7.7 %constant_dynamic-slice_fusion.2 = bf16[128,128,256]{0,2,1:T(8,128)(2,1)} fusion(bf16[256,128,256]{0,2,1:T(8,128)(2,1)} %get-tuple-element.382, s32[]{:T(128)S(6)} %select_n.101), kind=kLoop, calls=%fused_computation.9.clone.1 | loop fusion | bytes 16777220 | tf_op jit(solution)/shard_map/while/body/eval_jaxpr/dynamic_slice | solution.py:86
  115.6 12.7 %copy.41 = bf16[128,128,256]{2,1,0:T(8,128)(2,1)} copy(bf16[128,128,256]{0,2,1:T(8,128)(2,1)} %constant_dynamic-slice_fusion.2) | data formatting | bytes 16777216 | tf_op jit(solution)/shard_map/while/body/eval_jaxpr/dynamic_slice | solution.py:86
  128.3 0.0 collective-permute-done
  128.3 6.7 %select_dynamic-update-slice_fusion.4 = (bf16[256,16,128]{2,1,0:T(8,128)(2,1)}, bf16[128,16,128]{2,1,0:T(8,128)(2,1)S(1)}) fusion(bf16[256,16,128]{2,1,0:T(8,128)(2,1)} %get-tuple-element.361, s32[]{:T(128)S(6)} %select_n.101, pred[]{:T(512)S(6)} %and.11, bf16[128,128,256]{2,1,0:T(8,128)(2,1)} %copy.41, ...), kind=kOutput, calls=%fused_computation.7.clone.1 | convolution fusion | flops 138149888 | bytes 12583429 | tf_op jit(solution)/shard_map/while/body/eval_jaxpr/gcs,grs->gcr/dot_general | solution.py:29
  135.0 1.3 collective-permute-start.1
  136.3 2.5 select_dynamic-update-slice_fusion.5
  138.8 12.7 %collective-permute-done.1 = bf16[128,16,128]{2,1,0:T(8,128)(2,1)S(1)} collective-permute-done((bf16[128,16,128]{2,1,0:T(8,128)(2,1)S(1)}, bf16[128,16,128]{2,1,0:T(8,128)(2,1)S(1)}, u32[]{:S(2)}, u32[]{:S(2)}) %collective-permute-start.1) | collective-permute-done | bytes 524320 | tf_op jit(solution)/shard_map/while/body/eval_jaxpr/ppermute | solution.py:12
  151.5 1.2 fusion.13
  152.7 1.3 collective-permute-start
  154.1 7.7 %constant_dynamic-slice_fusion.2 = bf16[128,128,256]{0,2,1:T(8,128)(2,1)} fusion(bf16[256,128,256]{0,2,1:T(8,128)(2,1)} %get-tuple-element.382, s32[]{:T(128)S(6)} %select_n.101), kind=kLoop, calls=%fused_computation.9.clone.1 | loop fusion | bytes 16777220 | tf_op jit(solution)/shard_map/while/body/eval_jaxpr/dynamic_slice | solution.py:86
  161.8 12.7 %copy.41 = bf16[128,128,256]{2,1,0:T(8,128)(2,1)} copy(bf16[128,128,256]{0,2,1:T(8,128)(2,1)} %constant_dynamic-slice_fusion.2) | data formatting | bytes 16777216 | tf_op jit(solution)/shard_map/while/body/eval_jaxpr/dynamic_slice | solution.py:86
  174.4 0.0 collective-permute-done
  174.5 6.7 %select_dynamic-update-slice_fusion.4 = (bf16[256,16,128]{2,1,0:T(8,128)(2,1)}, bf16[128,16,128]{2,1,0:T(8,128)(2,1)S(1)}) fusion(bf16[256,16,128]{2,1,0:T(8,128)(2,1)} %get-tuple-element.361, s32[]{:T(128)S(6)} %select_n.101, pred[]{:T(512)S(6)} %and.11, bf16[128,128,256]{2,1,0:T(8,128)(2,1)} %copy.41, ...), kind=kOutput, calls=%fused_computation.7.clone.1 | convolution fusion | flops 138149888 | bytes 12583429 | tf_op jit(solution)/shard_map/while/body/eval_jaxpr/gcs,grs->gcr/dot_general | solution.py:29
  181.1 1.3 collective-permute-start.1
  182.4 2.5 select_dynamic-update-slice_fusion.5
  184.9 12.7 %collective-permute-done.1 = bf16[128,16,128]{2,1,0:T(8,128)(2,1)S(1)} collective-permute-done((bf16[128,16,128]{2,1,0:T(8,128)(2,1)S(1)}, bf16[128,16,128]{2,1,0:T(8,128)(2,1)S(1)}, u32[]{:S(2)}, u32[]{:S(2)}) %collective-permute-start.1) | collective-permute-done | bytes 524320 | tf_op jit(solution)/shard_map/while/body/eval_jaxpr/ppermute | solution.py:12
  197.7 18.2 %fusion.4 = f32[256,128,256]{2,1,0:T(8,128)} fusion(bf16[256,16,256]{2,1,0:T(8,128)(2,1)} %get-tuple-element.221, f32[256,16,128]{2,1,0:T(8,128)} %bitcast.50, bf16[256,16,128]{2,1,0:T(8,128)(2,1)} %get-tuple-element.392), kind=kOutput, calls=%fused_computation.15 | convolution fusion | flops 270008320 | bytes 38797312 | tf_op jit(solution)/shard_map/gcr,gcs->grs/dot_general | solution.py:38
  215.8 35.0 %copy.36 = f32[256,128,256]{0,2,1:T(8,128)} copy(f32[256,128,256]{2,1,0:T(8,128)} %fusion.4) | data formatting | bytes 67108864 | tf_op jit(solution)/shard_map/reshape | solution.py:39
  250.8 22.5 %concatenate.16 = f32[256,32896]{0,1:T(8,128)} pad(f32[256,32768]{0,1:T(8,128)} %bitcast.46, f32[]{:T(128)} %constant.64.clone.1), padding=0_0x0_128 | pad | bytes 67239936 | tf_op jit(solution)/shard_map/concatenate | solution.py:40
  273.2 28.3 %reshape.40 = f32[256,128,257]{0,2,1:T(8,128)} reshape(f32[256,32896]{0,1:T(8,128)} %concatenate.16) | data formatting | bytes 67371008 | tf_op jit(solution)/shard_map/reshape | solution.py:41
  301.6 6.9 %slice_reduce_fusion = f32[256,128]{0,1:T(8,128)S(1)} fusion(f32[256,128,257]{0,2,1:T(8,128)} %reshape.40), kind=kLoop, calls=%fused_computation.11 | loop fusion | flops 4161536 | bytes 16908288 | tf_op jit(solution)/shard_map/reduce_sum | solution.py:42
  308.5 0.7 copy.37
  309.2 0.0 reduce-scatter.4.cloned.1.call-update
  309.2 0.0 copy-done
  309.3 0.6 convert_reduce_fusion
  309.9 0.1 reshape.38
  310.0 63.8 %all-reduce.2 = f32[4096]{0:T(1024)S(1)} all-reduce(f32[4096]{0:T(1024)S(1)} %reshape.38), channel_id=2, replica_groups=mesh['section'=2,'seq'=16] {'seq'}, use_global_device_ids=true, to_apply=%region_3.4.clone | all-reduce | flops 4096 | bytes 32768
  373.8 0.0 copy-done.4
  373.8 0.1 copy.34
  373.9 0.0 copy-done.6
  373.9 0.6 dynamic-slice
  375.1 0.0 copy-done.5
  375.2 0.6 rsqrt_multiply_fusion
  375.8 0.8 copy.38
  376.6 0.7 copy.35
  (8 shorter events, 0.0 us)
Async XLA Ops:
  7.2 1.8 copy-start.2
  7.2 368.6 %reduce-scatter.4.cloned.1.call-start = ((), (), s32[]{:S(2)}) async-start(), calls=%async_computation.1 | async-start | bytes 139264
  8.9 3.6 copy-start.3
  38.1 13.9 %copy-start.1 = (bf16[1,128,4096]{2,1,0:T(8,128)(2,1)S(1)}, bf16[1,128,4096]{2,1,0:T(8,128)(2,1)}, u32[]{:S(2)}) copy-start(bf16[1,128,4096]{2,1,0:T(8,128)(2,1)} %param.12) | copy-start | bytes 3145732
  60.3 21.7 %collective-permute-start = (bf16[128,16,128]{2,1,0:T(8,128)(2,1)S(1)}, bf16[128,16,128]{2,1,0:T(8,128)(2,1)S(1)}, u32[]{:S(2)}, u32[]{:S(2)}) collective-permute-start(bf16[128,16,128]{2,1,0:T(8,128)(2,1)S(1)} %fusion.13), channel_id=1, source_target_pairs={{1,0},{2,1},{3,2},{4,3},{5,4},{6,5},{7,6},{8,7},{9,8},{10,9},{11,1... | collective-permute-start | bytes 1572872 | tf_op jit(solution)/shard_map/while/body/eval_jaxpr/ppermute | solution.py:12
  88.7 16.6 %collective-permute-start.1 = (bf16[128,16,128]{2,1,0:T(8,128)(2,1)S(1)}, bf16[128,16,128]{2,1,0:T(8,128)(2,1)S(1)}, u32[]{:S(2)}, u32[]{:S(2)}) collective-permute-start(bf16[128,16,128]{2,1,0:T(8,128)(2,1)S(1)} %get-tuple-element.341), channel_id=1, source_target_pairs={{16,0},{17,1},{18,2},{19,3},{20,4},{21,5},{22,6},{23,7},{24,8},{25... | collective-permute-start | bytes 1572872 | tf_op jit(solution)/shard_map/while/body/eval_jaxpr/ppermute | solution.py:12
  106.6 21.7 %collective-permute-start = (bf16[128,16,128]{2,1,0:T(8,128)(2,1)S(1)}, bf16[128,16,128]{2,1,0:T(8,128)(2,1)S(1)}, u32[]{:S(2)}, u32[]{:S(2)}) collective-permute-start(bf16[128,16,128]{2,1,0:T(8,128)(2,1)S(1)} %fusion.13), channel_id=1, source_target_pairs={{1,0},{2,1},{3,2},{4,3},{5,4},{6,5},{7,6},{8,7},{9,8},{10,9},{11,1... | collective-permute-start | bytes 1572872 | tf_op jit(solution)/shard_map/while/body/eval_jaxpr/ppermute | solution.py:12
  135.0 16.5 %collective-permute-start.1 = (bf16[128,16,128]{2,1,0:T(8,128)(2,1)S(1)}, bf16[128,16,128]{2,1,0:T(8,128)(2,1)S(1)}, u32[]{:S(2)}, u32[]{:S(2)}) collective-permute-start(bf16[128,16,128]{2,1,0:T(8,128)(2,1)S(1)} %get-tuple-element.341), channel_id=1, source_target_pairs={{16,0},{17,1},{18,2},{19,3},{20,4},{21,5},{22,6},{23,7},{24,8},{25... | collective-permute-start | bytes 1572872 | tf_op jit(solution)/shard_map/while/body/eval_jaxpr/ppermute | solution.py:12
  152.7 21.7 %collective-permute-start = (bf16[128,16,128]{2,1,0:T(8,128)(2,1)S(1)}, bf16[128,16,128]{2,1,0:T(8,128)(2,1)S(1)}, u32[]{:S(2)}, u32[]{:S(2)}) collective-permute-start(bf16[128,16,128]{2,1,0:T(8,128)(2,1)S(1)} %fusion.13), channel_id=1, source_target_pairs={{1,0},{2,1},{3,2},{4,3},{5,4},{6,5},{7,6},{8,7},{9,8},{10,9},{11,1... | collective-permute-start | bytes 1572872 | tf_op jit(solution)/shard_map/while/body/eval_jaxpr/ppermute | solution.py:12
  181.1 16.5 %collective-permute-start.1 = (bf16[128,16,128]{2,1,0:T(8,128)(2,1)S(1)}, bf16[128,16,128]{2,1,0:T(8,128)(2,1)S(1)}, u32[]{:S(2)}, u32[]{:S(2)}) collective-permute-start(bf16[128,16,128]{2,1,0:T(8,128)(2,1)S(1)} %get-tuple-element.341), channel_id=1, source_target_pairs={{16,0},{17,1},{18,2},{19,3},{20,4},{21,5},{22,6},{23,7},{24,8},{25... | collective-permute-start | bytes 1572872 | tf_op jit(solution)/shard_map/while/body/eval_jaxpr/ppermute | solution.py:12
  301.5 7.7 %copy-start = (bf16[256,16,128]{2,1,0:T(8,128)(2,1)S(1)}, bf16[256,16,128]{2,1,0:T(8,128)(2,1)}, u32[]{:S(2)}) copy-start(bf16[256,16,128]{2,1,0:T(8,128)(2,1)} %get-tuple-element.220) | copy-start | bytes 3145732
  301.6 72.2 %copy-start.4 = (f32[1,128,16]{1,2,0:T(8,128)S(1)}, f32[1,128,16]{1,2,0:T(8,128)}, u32[]{:S(2)}) copy-start(f32[1,128,16]{1,2,0:T(8,128)} %param.15) | copy-start | bytes 24580
  301.6 72.4 %copy-start.6 = (u32[32]{0:T(128)S(1)}, u32[32]{0:T(128)}, u32[]{:S(2)}) copy-start(u32[32]{0:T(128)} %constant.77) | copy-start | bytes 388
  301.6 73.6 %copy-start.5 = (f32[1,256]{1,0:T(1,128)S(1)}, f32[1,256]{1,0:T(1,128)}, u32[]{:S(2)}) copy-start(f32[1,256]{1,0:T(1,128)} %param.14) | copy-start | bytes 3076
Sparse Core Ops, SparseCore 0:
  309.4 57.7 reduce-scatter.3
where the time goes:
time: 387 us; the launch traced here: 384 us
  local copies, waits for them, and re-layouts  200 us (52%)
  blocking collectives  63.8 us (16%)
  waiting for transfers between devices  38.3 us (10%)
  matrix products  38.2 us (10%)
  other arithmetic  21 us (5%)
  between operations  14.8 us (4%)
  starting transfers between devices  7.75 us (2%)
    unnamed x1, blocking collectives  63.8 us
    dynamic_slice x6, local copies, waits for them, and re-layouts, one_turn(): lax.dynamic_slice_in_dim(band_full, first_group, group_width, 0)  61.2 us
    ppermute x6, waiting for transfers between devices, from_behind(): return lax.ppermute(block, axis, route)  38.3 us
    reshape x1, local copies, waits for them, and re-layouts, filter_grad(): flat_rows = pairwise.reshape(group_count, block_len * span_len)  35 us
    reshape x1, local copies, waits for them, and re-layouts, filter_grad(): skewed = flat_rows.reshape(group_count, block_len, span_len + 1)  28.3 us
    another operation x2, local copies, waits for them, and re-layouts, band_matrix(): tiled_rows = jnp.tile(padded, (1, block_len))[:, :block_len * span_len]  25.5 us
    concatenate x1, local copies, waits for them, and re-layouts, filter_grad(): jnp.concatenate([flat_rows, jnp.zeros((group_count, block_len), jnp.float...  22.5 us
    dot_general x3, matrix products, filter_rows(): jnp.einsum('gcs,grs->gcr', extended, band_part, preferred_element_type=jn...  20 us
  transfers between devices with their start and end apart: 7, of which 3 were waited for; matrix products, arithmetic and copies ran while one was open for 18% of the time, Pallas kernels for 0%

commit v1 on v0

v1 whole, which is shorter than its diff:
```python
import functools

import jax
import jax.numpy as jnp
from jax import lax
from jax.experimental import pallas as pl
from jax.experimental.pallas import tpu as pltpu
from jax.sharding import PartitionSpec as P

F32 = jnp.float32
BF16 = jnp.bfloat16
LANES = 128
SUB = 32
FLOPS_A_CYCLE = 4 * 2 * 256 * 256


def lane_of(shape):
    return lax.broadcasted_iota(jnp.int32, shape, 1)


def row_of(shape):
    return lax.broadcasted_iota(jnp.int32, shape, 0)


def times(a, b):
    return (a.astype(F32) * b.astype(F32)).astype(BF16)


def turned(x):
    return pltpu.roll(x, LANES // 2, 1)


def spread(x, x_turned, parity, count):
    low = lane_of((count, LANES)) < LANES // 2
    natural, other = (x, x_turned) if parity == 0 else (x_turned, x)
    tiles = []
    for first in (0, 2 * SUB):
        tiles.append(jnp.where(low, natural[first : first + count], other[first + SUB : first + SUB + count]))
    return jnp.concatenate(tiles, 1)


def gathered(even, odd):
    low = lane_of((SUB, LANES)) < LANES // 2
    out = []
    for tile in range(2):
        a = even[:, tile * LANES : (tile + 1) * LANES]
        b = odd[:, tile * LANES : (tile + 1) * LANES]
        out.append(jnp.where(low, a, turned(b)))
        out.append(jnp.where(low, turned(a), b))
    return jnp.concatenate(out, 0)


def in_order(reverse, own, halo):
    return jnp.concatenate([jnp.where(reverse, halo, own), jnp.where(reverse, own, halo)], 0)


def diagonal_sums(circ):
    total = circ[:8]
    for first in range(8, circ.shape[0], 8):
        total = total + pltpu.roll(circ[first : first + 8], LANES - first, 1)
    for fold in (4, 2, 1):
        total = total + pltpu.roll(pltpu.roll(total, LANES - fold, 1), 8 - fold, 0)
    return total[:1]


def near(reverse_int, shape):
    return lane_of(shape) - row_of(shape) >= reverse_int


def tap_matrix(reverse, taps_by_group):
    taps = taps_by_group.shape[0]
    source = row_of((taps, taps))
    target = lane_of((taps, taps))
    mirrored = jnp.where(source == 0, 0, taps - source)
    pick = jnp.where(target == jnp.where(reverse, mirrored, source), 1.0, 0.0)
    return pick, taps


def weigh_kernel(role, gate, incoming, mid, out):
    reverse = role[0] > 0

    @pl.when(reverse)
    def _():
        out[...] = mid[...]

    @pl.when(jnp.logical_not(reverse))
    def _():
        out[...] = times(gate[...], incoming[...])


def values_kernel(role, mid, inputs, values):
    values[...] = times(mid[...], inputs[...])


def taps_kernel(role, filters, taps_out):
    pick, _ = tap_matrix(role[0] > 0, filters[...])
    taps_out[...] = lax.dot_general(
        filters[...], pick.astype(BF16), (((0,), (0,)), ((), ())), preferred_element_type=F32
    )


def conv_kernel(group_size, role, own, halo, taps, mid, incoming, outgoing, filtered):
    reverse = role[0] > 0
    width = own.shape[1]
    half = LANES // 2
    per_half = half // group_size
    mask = near(role[0], (SUB, LANES))
    zero = jnp.zeros((SUB, LANES), F32)
    lane_group = (lane_of((SUB, 2 * LANES)) % half) // group_size
    for pair in range(width // LANES):
        cols = pl.ds(pair * LANES, LANES)
        ext = in_order(reverse, own[:, cols], halo[:, cols])
        ext_turned = turned(ext)
        results = []
        for parity in range(2):
            window = spread(ext, ext_turned, parity, own.shape[0] + SUB)
            bands = []
            for g in range(per_half):
                row = taps[pl.ds((2 * pair + parity) * per_half + g, 1), :]
                circ = pltpu.roll(jnp.broadcast_to(row, (SUB, LANES)), 0, 1, stride=1, stride_axis=0)
                band = jnp.concatenate(
                    [jnp.where(mask, circ, zero), jnp.where(mask, zero, circ)[:, :SUB]], 1
                )
                bands.append(band.astype(BF16))
            product = jnp.dot(jnp.concatenate(bands, 0), window, preferred_element_type=F32)
            total = product[:SUB]
            for g in range(1, per_half):
                total = jnp.where(lane_group == g, product[g * SUB : (g + 1) * SUB], total)
            results.append(total)
        conv = gathered(*results)
        filtered[:, cols] = conv
        outgoing[:, cols] = (
            incoming[:, cols].astype(F32) + mid[:, cols].astype(F32) * conv
        ).astype(BF16)


def grad_kernel(
    group_size, role, gate, mid, inputs, values_halo, own, halo, outgoing, received, filtered,
    tap_grad, steer_grad, left, right_own, right_halo,
):
    reverse = role[0] > 0
    width = own.shape[1]
    half = LANES // 2
    per_half = half // group_size

    @pl.when(reverse)
    def _():
        grad = received[...]
        weighted = times(gate[...], grad)
        left[...] = weighted
        right_own[...] = times(mid[...], inputs[...])
        right_halo[...] = values_halo[...]
        grad_in = grad.astype(F32) + weighted.astype(F32) * filtered[...]
        steer_grad[...] = jnp.sum(grad_in, 0, keepdims=True)

    @pl.when(jnp.logical_not(reverse))
    def _():
        left[...] = times(mid[...], inputs[...])
        right_own[...] = own[...]
        right_halo[...] = halo[...]
        steer_grad[...] = jnp.sum(outgoing[...].astype(F32), 0, keepdims=True)

    mask = near(role[0], (SUB, LANES))
    lane_group = (lane_of((SUB, 2 * LANES)) % half) // group_size
    nothing = jnp.zeros((SUB, 2 * LANES), BF16)
    for pair in range(width // LANES):
        cols = pl.ds(pair * LANES, LANES)
        ext = in_order(reverse, right_own[:, cols], right_halo[:, cols])
        ext_turned = turned(ext)
        rows = left[:, cols]
        rows_turned = turned(rows)
        for parity in range(2):
            window = spread(ext, ext_turned, parity, own.shape[0] + SUB)
            short = spread(rows, rows_turned, parity, SUB)
            lhs = jnp.concatenate(
                [jnp.where(lane_group == g, short, nothing) for g in range(per_half)], 0
            )
            product = lax.dot_general(lhs, window, (((1,), (1,)), ((), ())), preferred_element_type=F32)
            for g in range(per_half):
                block = product[g * SUB : (g + 1) * SUB]
                late = jnp.concatenate([block[:, LANES:], jnp.zeros((SUB, LANES - SUB), F32)], 1)
                circ = jnp.where(mask, block[:, :LANES], late)
                tap_grad[pl.ds((2 * pair + parity) * per_half + g, 1), :] = diagonal_sums(circ)


def step_kernel(role, parts, steer_second, filter_second, steer_out, filter_out):
    total = jnp.sum(parts[...], 0)
    groups = filter_second.shape[0]
    pick, _ = tap_matrix(role[0] > 0, filter_second[...].T)
    tap_grad = jnp.dot(total[:groups], pick, preferred_element_type=F32, precision=lax.Precision.HIGHEST)
    filter_out[...] = tap_grad / jnp.sqrt(filter_second[...] + tap_grad * tap_grad)
    channels = steer_out.shape[1]
    for row in range(pl.cdiv(channels, LANES)):
        cols = min(LANES, channels - row * LANES)
        at = pl.ds(row * LANES, cols)
        grad = total[groups + row : groups + row + 1, :cols]
        steer_out[:, at] = grad / jnp.sqrt(steer_second[:, at] + grad * grad)


def spec(rows, width, first=0):
    return pl.BlockSpec((rows, width), lambda i: (0, i + first))


SMEM = pl.BlockSpec(memory_space=pltpu.SMEM)
ANY = pl.BlockSpec(memory_space=pl.ANY)


def call(kernel, grid, in_specs, out_specs, out_shape, scratch=(), name=None, cycles=100, after=()):
    count = len(in_specs)

    def with_after(*refs):
        kernel(*refs[:count], *refs[count + len(after) :])

    return pl.pallas_call(
        with_after,
        grid=grid,
        in_specs=list(in_specs) + [ANY] * len(after),
        out_specs=out_specs,
        out_shape=out_shape,
        scratch_shapes=list(scratch),
        compiler_params=pltpu.CompilerParams(vmem_limit_bytes=32 * 1024 * 1024),
        cost_estimate=pl.CostEstimate(flops=cycles * FLOPS_A_CYCLE, bytes_accessed=0, transcendentals=0),
        name=name,
    )


def body(cotangent, in_gate, mid_gate, layer_inputs, filters, steer_second, filter_second):
    in_gate, mid_gate, layer_inputs = in_gate[0], mid_gate[0], layer_inputs[0]
    rows, channels = in_gate.shape
    filt_len, groups = filters.shape[1:]
    group_size = channels // groups
    sections, seqs = lax.axis_size("section"), lax.axis_size("seq")
    my_section = lax.axis_index("section")
    role = (my_section == 0).astype(jnp.int32).reshape(1)

    chunks = 4
    width = channels // chunks
    block = min(width, 512)
    steps = width // block
    block_groups = block // group_size
    both = [(seqs * s + i, seqs * s + i - 1) for s in range(1, sections) for i in range(1, seqs)]
    ahead = [(i, i + 1) for i in range(seqs - 1)]
    down = [(s, s - 1) for s in range(1, sections)]

    def bf16(width_of):
        return jax.ShapeDtypeStruct((rows, width_of), BF16)

    def weigh(incoming, first, last, offset, after=()):
        return call(
            weigh_kernel,
            ((last - first) // block,),
            [SMEM, spec(rows, block, first // block), spec(rows, block, (first - offset) // block),
             spec(rows, block, first // block)],
            spec(rows, block),
            bf16(last - first),
            name="weigh",
            after=after,
        )(role, in_gate, incoming, mid_gate, *after)

    def gradients(k):
        own, halo, at = sources[k]
        here = spec(rows, block, k * steps)
        values_at = spec(rows, block, k * width % half // block)
        after = tuple(outgoing[-1:])
        return call(
            functools.partial(grad_kernel, group_size),
            (steps,),
            [SMEM, here, here, here, values_at, spec(rows, block, at), spec(rows, block, at)]
            + [spec(rows, block)] * 3,
            [pl.BlockSpec((block_groups, filt_len), lambda i: (i, 0)), pl.BlockSpec((1, block), lambda i: (0, i))],
            [jax.ShapeDtypeStruct((width // group_size, filt_len), F32), jax.ShapeDtypeStruct((1, width), F32)],
            scratch=[pltpu.VMEM((rows, block), BF16)] * 3,
            name="grads",
            cycles=2000,
            after=after,
        )(role, in_gate, mid_gate, layer_inputs, values_halos[k * width // half], own, halo, outgoing[k],
          received[k], filtered[k], *after)

    taps = call(
        taps_kernel,
        (1,),
        [SMEM, pl.BlockSpec((filt_len, groups), lambda i: (0, 0))],
        pl.BlockSpec((groups, filt_len), lambda i: (0, 0)),
        jax.ShapeDtypeStruct((groups, filt_len), F32),
        name="taps",
    )(role, filters[0])

    def values_of(first, last, after):
        here = spec(rows, block, first // block)
        values = call(
            values_kernel, ((last - first) // block,), [SMEM, here, here], spec(rows, block), bf16(last - first),
            name="values", after=after,
        )(role, mid_gate, layer_inputs, *after)
        return lax.ppermute(values, ("section", "seq"), ahead)

    half = channels // 2
    incoming = [(cotangent, 0)] * chunks
    for hop in range(sections - 1):
        final = hop == sections - 2
        starts = [0, width, half] if hop == 0 else [k * width for k in range(chunks)]
        ends = starts[1:] + [channels]
        owns, halos, sources, outgoing, filtered, received = [], [], [], [], [], []

        def segment(after):
            first, last = starts[len(owns)], ends[len(owns)]
            array, offset = incoming[first // width]
            owns.append(weigh(array, first, last, offset, after))
            halos.append(lax.ppermute(owns[-1], ("section", "seq"), both + ahead))

        for k in range(chunks):
            if k == 0:
                segment(())
                segment(tuple(owns))
            if starts[len(owns) - 1] <= k * width and len(owns) < len(starts):
                segment(tuple(outgoing[-1:]))
            part = max(i for i, first in enumerate(starts) if first <= k * width)
            at = (k * width - starts[part]) // block
            array, offset = incoming[k]
            before = tuple(outgoing[-1:]) + tuple(received[-2:-1])
            out, conv = call(
                functools.partial(conv_kernel, group_size),
                (steps,),
                [SMEM, spec(rows, block, at), spec(rows, block, at),
                 pl.BlockSpec((block_groups, filt_len), lambda i, k=k: (i + k * steps, 0)),
                 spec(rows, block, k * steps), spec(rows, block, (k * width - offset) // block)],
                [spec(rows, block), spec(rows, block)],
                [bf16(width), jax.ShapeDtypeStruct((rows, width), F32)],
                name="filter",
                cycles=1000,
                after=before,
            )(role, owns[part], halos[part], taps, mid_gate, array, *before)
            sources.append((owns[part], halos[part], at))
            outgoing.append(out)
            filtered.append(conv)
            received.append(lax.ppermute(out, "section", down))
            if final and k == 1:
                values_halos = [values_of(0, half, (out,)), values_of(half, channels, (out,))]
        last = my_section == sections - 1
        incoming = [
            (jnp.where(last, cotangent[:, k * width : (k + 1) * width], received[k]), k * width)
            for k in range(chunks)
        ]
    grads = [gradients(k) for k in range(chunks)]
    tap_grads, steer_grads = zip(*grads)

    tap_all = jnp.concatenate(tap_grads, 0).reshape(seqs, groups // seqs, filt_len)
    own_channels = channels // seqs
    steer_rows = pl.cdiv(own_channels, LANES)
    steer_all = jnp.concatenate(steer_grads, 1).reshape(seqs, own_channels)
    steer_all = jnp.pad(steer_all, ((0, 0), (0, steer_rows * LANES - own_channels)))
    packed = jnp.concatenate([tap_all, steer_all.reshape(seqs, steer_rows, LANES)], 1)
    parts = lax.all_to_all(packed, "seq", 0, 0)
    steer_step, filter_step = pl.pallas_call(
        step_kernel,
        in_specs=[SMEM] + [pl.BlockSpec(memory_space=pltpu.VMEM)] * 3,
        out_shape=[
            jax.ShapeDtypeStruct((1, own_channels), F32),
            jax.ShapeDtypeStruct((groups // seqs, filt_len), F32),
        ],
        name="step",
    )(role, parts, steer_second, filter_second[0].T)
    return steer_step, filter_step.T[None]


def solution(mesh):
    in_specs = (
        P("seq", None),
        P("section", "seq", None),
        P("section", "seq", None),
        P("section", "seq", None),
        P("section", None, None),
        P("section", "seq"),
        P("section", None, "seq"),
    )
    out_specs = (P("section", "seq"), P("section", None, "seq"))
    return jax.shard_map(body, mesh=mesh, in_specs=in_specs, out_specs=out_specs, check_vma=False)
```

time: 387 us -> 73.2 us (0.19)
  local copies, waits for them, and re-layouts: 200 us -> 3.79 us
  blocking collectives: 63.8 us -> 14.8 us
  matrix products: 38.2 us -> 0 us
  waiting for transfers between devices: 38.3 us -> 16.2 us
  other arithmetic: 21 us -> 0.05 us
  Pallas kernels: 0 us -> 15.4 us
  between operations: 14.8 us -> 0.94 us
  starting transfers between devices: 7.75 us -> 21.6 us
    unnamed x1 -> x0, blocking collectives: 63.8 us -> none
    reshape x3 -> x0, local copies, waits for them, and re-layouts: 63.4 us -> none  [the longest x1 35 us: filter_grad(): flat_rows = pairwise.reshape(group_count, block_len * span_len)]
    dynamic_slice x6 -> x0, local copies, waits for them, and re-layouts: 61.2 us -> none  [one_turn(): lax.dynamic_slice_in_dim(band_full, first_group, group_width, 0)]
    dot_general x4 -> x0, matrix products: 38.2 us -> none  [the longest x3 20 us: filter_rows(): jnp.einsum('gcs,grs->gcr', extended, band_part, preferred_element_type=jn...]
    another operation x2 -> x0, local copies, waits for them, and re-layouts: 25.5 us -> none  [band_matrix(): tiled_rows = jnp.tile(padded, (1, block_len))[:, :block_len * span_len]]
    concatenate x2 -> x0, local copies, waits for them, and re-layouts: 22.5 us -> none  [the longest x1 22.5 us: filter_grad(): jnp.concatenate([flat_rows, jnp.zeros((group_count, block_len), jnp.float...]
    ppermute x6 -> x9, waiting for transfers between devices: 38.3 us -> 16.2 us  [the longest x4 16.2 us: body(): received.append(lax.ppermute(out, 'section', down))]
    pallas_call x0 -> x15, Pallas kernels: none -> 15.4 us  [the longest x4 7.68 us: gradients(): call(functools.partial(grad_kernel, group_size), (steps,), [SMEM, here, h...]
  transfers between devices with their start and end apart: 7 -> 9, of which waited for: 3 -> 4; matrix products, arithmetic and copies ran while one was open for 18% -> 0% of each run, Pallas kernels for 0% -> 16%
where the time goes in v1:
time: 73.2 us; the launch traced here: 72.7 us
  starting transfers between devices  21.6 us (30%)
  waiting for transfers between devices  16.2 us (22%)
  Pallas kernels  15.4 us (21%)
  blocking collectives  14.8 us (20%)
  local copies, waits for them, and re-layouts  3.79 us (5%)
  between operations  0.94 us (1%)
    ppermute x4, waiting for transfers between devices, body(): received.append(lax.ppermute(out, 'section', down))  16.2 us
    all_to_all x1, blocking collectives, body(): parts = lax.all_to_all(packed, 'seq', 0, 0)  14.8 us
    ppermute x3, starting transfers between devices, segment(): halos.append(lax.ppermute(owns[-1], ('section', 'seq'), both + ahead))  9.97 us
    pallas_call x4, Pallas kernels, gradients(): call(functools.partial(grad_kernel, group_size), (steps,), [SMEM, here, h...  7.68 us
    ppermute x2, starting transfers between devices, values_of(): return lax.ppermute(values, ('section', 'seq'), ahead)  6.44 us
    ppermute x4, starting transfers between devices, body(): received.append(lax.ppermute(out, 'section', down))  5.17 us
    pallas_call x4, Pallas kernels, body(): call(functools.partial(conv_kernel, group_size), (steps,), [SMEM, spec(ro...  4.44 us
    unnamed x16, local copies, waits for them, and re-layouts  3.79 us
  transfers between devices with their start and end apart: 9, of which 4 were waited for; matrix products, arithmetic and copies ran while one was open for 0% of the time, Pallas kernels for 16%

profile of v1, /device:TPU:0, one launch (start us, length us, event | category | flops | bytes accessed | tf_op | source)
XLA Modules:
  0.0 72.7 jit_solution(3380010451121262946)
XLA Ops:
  0.6 0.0 copy-start
  0.6 1.2 %copy-done = bf16[1,128,4096]{2,1,0:T(8,128)(2,1)S(1)} copy-done((bf16[1,128,4096]{2,1,0:T(8,128)(2,1)S(1)}, bf16[1,128,4096]{2,1,0:T(8,128)(2,1)}, u32[]{:S(2)}) %copy-start) | copy-done | bytes 1048600
  1.9 0.0 copy-start.2
  1.9 1.2 %copy-done.2 = bf16[128,4096]{1,0:T(8,128)(2,1)S(1)} copy-done((bf16[128,4096]{1,0:T(8,128)(2,1)S(1)}, bf16[128,4096]{1,0:T(8,128)(2,1)}, u32[]{:S(2)}) %copy-start.2) | copy-done | bytes 1048600
  3.1 0.0 copy-start.4
  3.1 1.2 %copy-done.4 = bf16[1,128,4096]{2,1,0:T(8,128)(2,1)S(1)} copy-done((bf16[1,128,4096]{2,1,0:T(8,128)(2,1)S(1)}, bf16[1,128,4096]{2,1,0:T(8,128)(2,1)}, u32[]{:S(2)}) %copy-start.4) | copy-done | bytes 1048600
  4.3 0.2 weigh.3.refs_4_.refs_1_.refs_5_
  4.5 0.0 copy-start.7
  4.5 0.0 copy-start.1
  4.5 2.5 %collective-permute-start.1 = (bf16[128,1024]{1,0:T(8,128)(2,1)S(1)}, bf16[128,1024]{1,0:T(8,128)(2,1)S(1)}, u32[]{:S(2)}, u32[]{:S(2)}) collective-permute-start(bf16[128,1024]{1,0:T(8,128)(2,1)S(1)} %weigh.3.refs_4_.refs_1_.refs_5_), channel_id=1, source_target_pairs={{17,16},{18,17},{19,18},{20,19},{21,20},{22,21},{23,22},{24,23},{2... | collective-permute-start | bytes 786440 | tf_op jit(solution)/shard_map/ppermute | solution.py:308
  7.0 0.2 weigh.4.refs_1_.refs_5_
  7.2 4.5 %collective-permute-start = (bf16[128,1024]{1,0:T(8,128)(2,1)S(1)}, bf16[128,1024]{1,0:T(8,128)(2,1)S(1)}, u32[]{:S(2)}, u32[]{:S(2)}) collective-permute-start(bf16[128,1024]{1,0:T(8,128)(2,1)S(1)} %weigh.4.refs_1_.refs_5_), channel_id=1, source_target_pairs={{17,16},{18,17},{19,18},{20,19},{21,20},{22,21},{23,22},{24,23},{2... | collective-permute-start | bytes 786440 | tf_op jit(solution)/shard_map/ppermute | solution.py:308
  11.8 0.0 copy-done.7
  11.8 0.2 taps.1.refs_3_
  12.0 0.0 copy-start.5
  12.0 0.0 collective-permute-done.1.refs_2_.refs_6_
  12.0 0.0 copy-done.1
  12.0 1.1 %filter.4 = (bf16[128,1024]{1,0:T(8,128)(2,1)S(1)}, f32[128,1024]{1,0:T(8,128)S(1)}) custom-call(s32[1]{0:T(128)} %bitcast.refs_0_.role, bf16[128,1024]{1,0:T(8,128)(2,1)S(1)} %weigh.3.refs_4_.refs_1_.refs_5_, bf16[128,1024]{1,0:T(8,128)(2,1)S(1)} %collective-permute-done.1.refs_2_.refs_6_, f32[256,128]{1,0:T(8,128)S(1)} %taps.1.refs_3_, ...), custom_call_target="tpu_custom_call" | custom-call | flops 524288000 | tf_op jit(solution)/shard_map/filter/pallas_call | solution.py:320
  13.1 0.1 copy-done.5
  13.2 0.3 weigh.5.refs_1_.refs_5_
  13.5 0.0 copy-start.6
  13.6 2.9 %collective-permute-start.4 = (bf16[128,2048]{1,0:T(8,128)(2,1)S(1)}, bf16[128,2048]{1,0:T(8,128)(2,1)S(1)}, u32[]{:S(2)}, u32[]{:S(2)}) collective-permute-start(bf16[128,2048]{1,0:T(8,128)(2,1)S(1)} %weigh.5.refs_1_.refs_5_), channel_id=1, source_target_pairs={{17,16},{18,17},{19,18},{20,19},{21,20},{22,21},{23,22},{24,23},{2... | collective-permute-start | bytes 1572872 | tf_op jit(solution)/shard_map/ppermute | solution.py:308
  16.5 0.0 collective-permute-done.refs_2_.refs_6_
  16.5 1.1 %filter.5 = (bf16[128,1024]{1,0:T(8,128)(2,1)S(1)}, f32[128,1024]{1,0:T(8,128)S(1)}) custom-call(s32[1]{0:T(128)} %bitcast.refs_0_.role, bf16[128,1024]{1,0:T(8,128)(2,1)S(1)} %weigh.4.refs_1_.refs_5_, bf16[128,1024]{1,0:T(8,128)(2,1)S(1)} %collective-permute-done.refs_2_.refs_6_, f32[256,128]{1,0:T(8,128)S(1)} %taps.1.refs_3_, ...), custom_call_target="tpu_custom_call" | custom-call | flops 524288000 | tf_op jit(solution)/shard_map/filter/pallas_call | solution.py:320
  17.6 0.0 copy-done.6
  17.6 0.3 values.2
  18.0 0.0 copy-start.3
  18.0 4.5 %collective-permute-start.2 = (bf16[128,2048]{1,0:T(8,128)(2,1)S(1)}, bf16[128,2048]{1,0:T(8,128)(2,1)S(1)}, u32[]{:S(2)}, u32[]{:S(2)}) collective-permute-start(bf16[128,2048]{1,0:T(8,128)(2,1)S(1)} %values.2), channel_id=1, source_target_pairs={{0,1},{1,2},{2,3},{3,4},{4,5},{5,6},{6,7},{7,8},{8,9},{9,10},{10,1... | collective-permute-start | bytes 1572872 | tf_op jit(solution)/shard_map/ppermute | solution.py:294
  22.5 1.3 %collective-permute-start.3 = (bf16[128,1024]{1,0:T(8,128)(2,1)S(1)}, bf16[128,1024]{1,0:T(8,128)(2,1)S(1)}, u32[]{:S(2)}, u32[]{:S(2)}) collective-permute-start(bf16[128,1024]{1,0:T(8,128)(2,1)S(1)} %get-tuple-element.20.refs_6_.refs_4_.refs_7_), channel_id=1, source_target_pairs={{16,0},{17,1},{18,2},{19,3},{20,4},{21,5},{22,6},{23,7},{24,8},{25... | collective-permute-start | bytes 786440 | tf_op jit(solution)/shard_map/ppermute | solution.py:335
  23.8 1.3 %collective-permute-start.5 = (bf16[128,1024]{1,0:T(8,128)(2,1)S(1)}, bf16[128,1024]{1,0:T(8,128)(2,1)S(1)}, u32[]{:S(2)}, u32[]{:S(2)}) collective-permute-start(bf16[128,1024]{1,0:T(8,128)(2,1)S(1)} %get-tuple-element.21.refs_3_.refs_6_.refs_7_), channel_id=1, source_target_pairs={{16,0},{17,1},{18,2},{19,3},{20,4},{21,5},{22,6},{23,7},{24,8},{25... | collective-permute-start | bytes 786440 | tf_op jit(solution)/shard_map/ppermute | solution.py:335
  25.1 0.3 values.3
  25.5 1.9 %collective-permute-start.6 = (bf16[128,2048]{1,0:T(8,128)(2,1)S(1)}, bf16[128,2048]{1,0:T(8,128)(2,1)S(1)}, u32[]{:S(2)}, u32[]{:S(2)}) collective-permute-start(bf16[128,2048]{1,0:T(8,128)(2,1)S(1)} %values.3), channel_id=1, source_target_pairs={{0,1},{1,2},{2,3},{3,4},{4,5},{5,6},{6,7},{7,8},{8,9},{9,10},{10,1... | collective-permute-start | bytes 1572872 | tf_op jit(solution)/shard_map/ppermute | solution.py:294
  27.4 6.2 %collective-permute-done.3.refs_7_.refs_8_ = bf16[128,1024]{1,0:T(8,128)(2,1)S(1)} collective-permute-done((bf16[128,1024]{1,0:T(8,128)(2,1)S(1)}, bf16[128,1024]{1,0:T(8,128)(2,1)S(1)}, u32[]{:S(2)}, u32[]{:S(2)}) %collective-permute-start.3) | collective-permute-done | bytes 262176 | tf_op jit(solution)/shard_map/ppermute | solution.py:335
  33.6 0.0 collective-permute-done.4.refs_2_.refs_6_
  33.6 0.0 copy-done.3
  33.6 1.1 %filter.6 = (bf16[128,1024]{1,0:T(8,128)(2,1)S(1)}, f32[128,1024]{1,0:T(8,128)S(1)}) custom-call(s32[1]{0:T(128)} %bitcast.refs_0_.role, bf16[128,2048]{1,0:T(8,128)(2,1)S(1)} %weigh.5.refs_1_.refs_5_, bf16[128,2048]{1,0:T(8,128)(2,1)S(1)} %collective-permute-done.4.refs_2_.refs_6_, f32[256,128]{1,0:T(8,128)S(1)} %taps.1.refs_3_, ...), custom_call_target="tpu_custom_call" | custom-call | flops 524288000 | tf_op jit(solution)/shard_map/filter/pallas_call | solution.py:320
  34.7 3.5 %collective-permute-done.5.refs_7_.refs_8_ = bf16[128,1024]{1,0:T(8,128)(2,1)S(1)} collective-permute-done((bf16[128,1024]{1,0:T(8,128)(2,1)S(1)}, bf16[128,1024]{1,0:T(8,128)(2,1)S(1)}, u32[]{:S(2)}, u32[]{:S(2)}) %collective-permute-start.5) | collective-permute-done | bytes 262176 | tf_op jit(solution)/shard_map/ppermute | solution.py:335
  38.2 1.1 %filter.7 = (bf16[128,1024]{1,0:T(8,128)(2,1)S(1)}, f32[128,1024]{1,0:T(8,128)S(1)}) custom-call(s32[1]{0:T(128)} %bitcast.refs_0_.role, bf16[128,2048]{1,0:T(8,128)(2,1)S(1)} %weigh.5.refs_1_.refs_5_, bf16[128,2048]{1,0:T(8,128)(2,1)S(1)} %collective-permute-done.4.refs_2_.refs_6_, f32[256,128]{1,0:T(8,128)S(1)} %taps.1.refs_3_, ...), custom_call_target="tpu_custom_call" | custom-call | flops 524288000 | tf_op jit(solution)/shard_map/filter/pallas_call | solution.py:320
  39.3 1.3 %collective-permute-start.8 = (bf16[128,1024]{1,0:T(8,128)(2,1)S(1)}, bf16[128,1024]{1,0:T(8,128)(2,1)S(1)}, u32[]{:S(2)}, u32[]{:S(2)}) collective-permute-start(bf16[128,1024]{1,0:T(8,128)(2,1)S(1)} %get-tuple-element.24.refs_10_.refs_7_), channel_id=1, source_target_pairs={{16,0},{17,1},{18,2},{19,3},{20,4},{21,5},{22,6},{23,7},{24,8},{25... | collective-permute-start | bytes 786440 | tf_op jit(solution)/shard_map/ppermute | solution.py:335
  40.6 1.3 %collective-permute-start.7 = (bf16[128,1024]{1,0:T(8,128)(2,1)S(1)}, bf16[128,1024]{1,0:T(8,128)(2,1)S(1)}, u32[]{:S(2)}, u32[]{:S(2)}) collective-permute-start(bf16[128,1024]{1,0:T(8,128)(2,1)S(1)} %get-tuple-element.23.refs_6_.refs_7_), channel_id=1, source_target_pairs={{16,0},{17,1},{18,2},{19,3},{20,4},{21,5},{22,6},{23,7},{24,8},{25... | collective-permute-start | bytes 786440 | tf_op jit(solution)/shard_map/ppermute | solution.py:335
  41.9 0.0 collective-permute-done.2.refs_4_
  41.9 1.9 %grads.5 = (f32[64,128]{1,0:T(8,128)S(1)}, f32[1,1024]{1,0:T(1,128)S(1)}) custom-call(s32[1]{0:T(128)} %bitcast.refs_0_.role, bf16[128,4096]{1,0:T(8,128)(2,1)S(1)} %bitcast.29, bf16[128,4096]{1,0:T(8,128)(2,1)S(1)} %bitcast.22, bf16[128,4096]{1,0:T(8,128)(2,1)S(1)} %bitcast.35, bf16[128,2048]{1,0:T(8,128)(2,1)S(1)} %collective-permute-done.2.refs_4_, ...), custom_call_target="tpu_custom_call" | custom-call | flops 1048576000 | tf_op jit(solution)/shard_map/grads/pallas_call | solution.py:265
  43.9 1.9 %grads.4 = (f32[64,128]{1,0:T(8,128)S(1)}, f32[1,1024]{1,0:T(1,128)S(1)}) custom-call(s32[1]{0:T(128)} %bitcast.refs_0_.role, bf16[128,4096]{1,0:T(8,128)(2,1)S(1)} %bitcast.30, bf16[128,4096]{1,0:T(8,128)(2,1)S(1)} %bitcast.23, bf16[128,4096]{1,0:T(8,128)(2,1)S(1)} %bitcast.36, bf16[128,2048]{1,0:T(8,128)(2,1)S(1)} %collective-permute-done.2.refs_4_, ...), custom_call_target="tpu_custom_call" | custom-call | flops 1048576000 | tf_op jit(solution)/shard_map/grads/pallas_call | solution.py:265
  45.8 0.0 collective-permute-done.6.refs_4_
  45.8 4.7 %collective-permute-done.8.refs_8_ = bf16[128,1024]{1,0:T(8,128)(2,1)S(1)} collective-permute-done((bf16[128,1024]{1,0:T(8,128)(2,1)S(1)}, bf16[128,1024]{1,0:T(8,128)(2,1)S(1)}, u32[]{:S(2)}, u32[]{:S(2)}) %collective-permute-start.8) | collective-permute-done | bytes 262176 | tf_op jit(solution)/shard_map/ppermute | solution.py:335
  50.5 1.9 %grads.7 = (f32[64,128]{1,0:T(8,128)S(1)}, f32[1,1024]{1,0:T(1,128)S(1)}) custom-call(s32[1]{0:T(128)} %bitcast.refs_0_.role, bf16[128,4096]{1,0:T(8,128)(2,1)S(1)} %bitcast.31, bf16[128,4096]{1,0:T(8,128)(2,1)S(1)} %bitcast.24, bf16[128,4096]{1,0:T(8,128)(2,1)S(1)} %bitcast.37, bf16[128,2048]{1,0:T(8,128)(2,1)S(1)} %collective-permute-done.6.refs_4_, ...), custom_call_target="tpu_custom_call" | custom-call | flops 1048576000 | tf_op jit(solution)/shard_map/grads/pallas_call | solution.py:265
  52.4 1.8 %collective-permute-done.7.refs_8_ = bf16[128,1024]{1,0:T(8,128)(2,1)S(1)} collective-permute-done((bf16[128,1024]{1,0:T(8,128)(2,1)S(1)}, bf16[128,1024]{1,0:T(8,128)(2,1)S(1)}, u32[]{:S(2)}, u32[]{:S(2)}) %collective-permute-start.7) | collective-permute-done | bytes 262176 | tf_op jit(solution)/shard_map/ppermute | solution.py:335
  54.2 1.9 %grads.6 = (f32[64,128]{1,0:T(8,128)S(1)}, f32[1,1024]{1,0:T(1,128)S(1)}) custom-call(s32[1]{0:T(128)} %bitcast.refs_0_.role, bf16[128,4096]{1,0:T(8,128)(2,1)S(1)} %bitcast.32, bf16[128,4096]{1,0:T(8,128)(2,1)S(1)} %bitcast.25, bf16[128,4096]{1,0:T(8,128)(2,1)S(1)} %bitcast.38, bf16[128,2048]{1,0:T(8,128)(2,1)S(1)} %collective-permute-done.6.refs_4_, ...), custom_call_target="tpu_custom_call" | custom-call | flops 1048576000 | tf_op jit(solution)/shard_map/grads/pallas_call | solution.py:265
  56.2 14.8 %all_to_all.5.parts = f32[16,18,128]{2,1,0:T(8,128)} all-to-all(f32[16,18,128]{2,1,0:T(8,128)S(1)} %pad_maximum_fusion), channel_id=1, replica_groups=mesh['section'=2,'seq'=16] {'seq'}, dimensions={0} | all-to-all | bytes 294912 | tf_op jit(solution)/shard_map/all_to_all | solution.py:352
  70.9 1.7 %step.1 = (f32[1,256]{1,0:T(1,128)}, f32[16,128]{1,0:T(8,128)}) custom-call(s32[1]{0:T(128)} %bitcast.refs_0_.role, f32[16,18,128]{2,1,0:T(8,128)} %all_to_all.5.parts, f32[1,256]{1,0:T(1,128)} %steer_second.1, f32[16,128]{1,0:T(8,128)} %bitcast.42), custom_call_target="tpu_custom_call" | custom-call | tf_op jit(solution)/shard_map/step/pallas_call | solution.py:353
  (3 shorter events, 0.0 us)
Async XLA Ops:
  0.6 1.2 %copy-start = (bf16[1,128,4096]{2,1,0:T(8,128)(2,1)S(1)}, bf16[1,128,4096]{2,1,0:T(8,128)(2,1)}, u32[]{:S(2)}) copy-start(bf16[1,128,4096]{2,1,0:T(8,128)(2,1)} %param.9) | copy-start | bytes 3145732
  1.9 1.2 %copy-start.2 = (bf16[128,4096]{1,0:T(8,128)(2,1)S(1)}, bf16[128,4096]{1,0:T(8,128)(2,1)}, u32[]{:S(2)}) copy-start(bf16[128,4096]{1,0:T(8,128)(2,1)} %refs_5_.7) | copy-start | bytes 3145732
  3.1 1.2 %copy-start.4 = (bf16[1,128,4096]{2,1,0:T(8,128)(2,1)S(1)}, bf16[1,128,4096]{2,1,0:T(8,128)(2,1)}, u32[]{:S(2)}) copy-start(bf16[1,128,4096]{2,1,0:T(8,128)(2,1)} %param.8) | copy-start | bytes 3145732
  4.5 7.3 %copy-start.7 = (bf16[1,128,256]{2,1,0:T(8,128)(2,1)S(1)}, bf16[1,128,256]{2,1,0:T(8,128)(2,1)}, u32[]{:S(2)}) copy-start(bf16[1,128,256]{2,1,0:T(8,128)(2,1)} %param.11) | copy-start | bytes 196612
  4.5 7.5 %copy-start.1 = (bf16[1,128,4096]{2,1,0:T(8,128)(2,1)S(1)}, bf16[1,128,4096]{2,1,0:T(8,128)(2,1)}, u32[]{:S(2)}) copy-start(bf16[1,128,4096]{2,1,0:T(8,128)(2,1)} %param.9) | copy-start | bytes 3145732
  4.5 7.5 %collective-permute-start.1 = (bf16[128,1024]{1,0:T(8,128)(2,1)S(1)}, bf16[128,1024]{1,0:T(8,128)(2,1)S(1)}, u32[]{:S(2)}, u32[]{:S(2)}) collective-permute-start(bf16[128,1024]{1,0:T(8,128)(2,1)S(1)} %weigh.3.refs_4_.refs_1_.refs_5_), channel_id=1, source_target_pairs={{17,16},{18,17},{19,18},{20,19},{21,20},{22,21},{23,22},{24,23},{2... | collective-permute-start | bytes 786440 | tf_op jit(solution)/shard_map/ppermute | solution.py:308
  7.2 9.3 %collective-permute-start = (bf16[128,1024]{1,0:T(8,128)(2,1)S(1)}, bf16[128,1024]{1,0:T(8,128)(2,1)S(1)}, u32[]{:S(2)}, u32[]{:S(2)}) collective-permute-start(bf16[128,1024]{1,0:T(8,128)(2,1)S(1)} %weigh.4.refs_1_.refs_5_), channel_id=1, source_target_pairs={{17,16},{18,17},{19,18},{20,19},{21,20},{22,21},{23,22},{24,23},{2... | collective-permute-start | bytes 786440 | tf_op jit(solution)/shard_map/ppermute | solution.py:308
  12.0 1.2 %copy-start.5 = (bf16[1,128,4096]{2,1,0:T(8,128)(2,1)S(1)}, bf16[1,128,4096]{2,1,0:T(8,128)(2,1)}, u32[]{:S(2)}) copy-start(bf16[1,128,4096]{2,1,0:T(8,128)(2,1)} %param.8) | copy-start | bytes 3145732
  13.5 4.1 %copy-start.6 = (bf16[1,128,4096]{2,1,0:T(8,128)(2,1)S(1)}, bf16[1,128,4096]{2,1,0:T(8,128)(2,1)}, u32[]{:S(2)}) copy-start(bf16[1,128,4096]{2,1,0:T(8,128)(2,1)} %param.10) | copy-start | bytes 3145732
  13.6 20.0 %collective-permute-start.4 = (bf16[128,2048]{1,0:T(8,128)(2,1)S(1)}, bf16[128,2048]{1,0:T(8,128)(2,1)S(1)}, u32[]{:S(2)}, u32[]{:S(2)}) collective-permute-start(bf16[128,2048]{1,0:T(8,128)(2,1)S(1)} %weigh.5.refs_1_.refs_5_), channel_id=1, source_target_pairs={{17,16},{18,17},{19,18},{20,19},{21,20},{22,21},{23,22},{24,23},{2... | collective-permute-start | bytes 1572872 | tf_op jit(solution)/shard_map/ppermute | solution.py:308
  18.0 15.6 %copy-start.3 = (bf16[128,4096]{1,0:T(8,128)(2,1)S(1)}, bf16[128,4096]{1,0:T(8,128)(2,1)}, u32[]{:S(2)}) copy-start(bf16[128,4096]{1,0:T(8,128)(2,1)} %refs_5_.7) | copy-start | bytes 3145732
  18.0 24.0 %collective-permute-start.2 = (bf16[128,2048]{1,0:T(8,128)(2,1)S(1)}, bf16[128,2048]{1,0:T(8,128)(2,1)S(1)}, u32[]{:S(2)}, u32[]{:S(2)}) collective-permute-start(bf16[128,2048]{1,0:T(8,128)(2,1)S(1)} %values.2), channel_id=1, source_target_pairs={{0,1},{1,2},{2,3},{3,4},{4,5},{5,6},{6,7},{7,8},{8,9},{9,10},{10,1... | collective-permute-start | bytes 1572872 | tf_op jit(solution)/shard_map/ppermute | solution.py:294
  22.5 11.1 %collective-permute-start.3 = (bf16[128,1024]{1,0:T(8,128)(2,1)S(1)}, bf16[128,1024]{1,0:T(8,128)(2,1)S(1)}, u32[]{:S(2)}, u32[]{:S(2)}) collective-permute-start(bf16[128,1024]{1,0:T(8,128)(2,1)S(1)} %get-tuple-element.20.refs_6_.refs_4_.refs_7_), channel_id=1, source_target_pairs={{16,0},{17,1},{18,2},{19,3},{20,4},{21,5},{22,6},{23,7},{24,8},{25... | collective-permute-start | bytes 786440 | tf_op jit(solution)/shard_map/ppermute | solution.py:335
  23.8 14.4 %collective-permute-start.5 = (bf16[128,1024]{1,0:T(8,128)(2,1)S(1)}, bf16[128,1024]{1,0:T(8,128)(2,1)S(1)}, u32[]{:S(2)}, u32[]{:S(2)}) collective-permute-start(bf16[128,1024]{1,0:T(8,128)(2,1)S(1)} %get-tuple-element.21.refs_3_.refs_6_.refs_7_), channel_id=1, source_target_pairs={{16,0},{17,1},{18,2},{19,3},{20,4},{21,5},{22,6},{23,7},{24,8},{25... | collective-permute-start | bytes 786440 | tf_op jit(solution)/shard_map/ppermute | solution.py:335
  25.5 20.3 %collective-permute-start.6 = (bf16[128,2048]{1,0:T(8,128)(2,1)S(1)}, bf16[128,2048]{1,0:T(8,128)(2,1)S(1)}, u32[]{:S(2)}, u32[]{:S(2)}) collective-permute-start(bf16[128,2048]{1,0:T(8,128)(2,1)S(1)} %values.3), channel_id=1, source_target_pairs={{0,1},{1,2},{2,3},{3,4},{4,5},{5,6},{6,7},{7,8},{8,9},{9,10},{10,1... | collective-permute-start | bytes 1572872 | tf_op jit(solution)/shard_map/ppermute | solution.py:294
  39.3 11.1 %collective-permute-start.8 = (bf16[128,1024]{1,0:T(8,128)(2,1)S(1)}, bf16[128,1024]{1,0:T(8,128)(2,1)S(1)}, u32[]{:S(2)}, u32[]{:S(2)}) collective-permute-start(bf16[128,1024]{1,0:T(8,128)(2,1)S(1)} %get-tuple-element.24.refs_10_.refs_7_), channel_id=1, source_target_pairs={{16,0},{17,1},{18,2},{19,3},{20,4},{21,5},{22,6},{23,7},{24,8},{25... | collective-permute-start | bytes 786440 | tf_op jit(solution)/shard_map/ppermute | solution.py:335
  40.6 13.6 %collective-permute-start.7 = (bf16[128,1024]{1,0:T(8,128)(2,1)S(1)}, bf16[128,1024]{1,0:T(8,128)(2,1)S(1)}, u32[]{:S(2)}, u32[]{:S(2)}) collective-permute-start(bf16[128,1024]{1,0:T(8,128)(2,1)S(1)} %get-tuple-element.23.refs_6_.refs_7_), channel_id=1, source_target_pairs={{16,0},{17,1},{18,2},{19,3},{20,4},{21,5},{22,6},{23,7},{24,8},{25... | collective-permute-start | bytes 786440 | tf_op jit(solution)/shard_map/ppermute | solution.py:335

commit v2 on v1

v2 whole, which is shorter than its diff:
```python
import functools

import jax
import jax.numpy as jnp
from jax import lax
from jax.experimental import pallas as pl
from jax.experimental.pallas import tpu as pltpu
from jax.sharding import PartitionSpec as P

F32 = jnp.float32
BF16 = jnp.bfloat16
LANES = 128
SUB = 32
CHUNK_EDGES = (0, 2, 4, 6, 8)
HALO_EDGES = (0, 4, 8)
FIRST_VMEM = 61 * 1024 * 1024


def lane_of(shape):
    return lax.broadcasted_iota(jnp.int32, shape, 1)


def row_of(shape):
    return lax.broadcasted_iota(jnp.int32, shape, 0)


def times(a, b):
    return (a.astype(F32) * b.astype(F32)).astype(BF16)


def turned(x):
    return pltpu.roll(x, LANES // 2, 1)


def spread(x, x_turned, parity, count):
    low = lane_of((count, LANES)) < LANES // 2
    natural, other = (x, x_turned) if parity == 0 else (x_turned, x)
    tiles = []
    for first in (0, 2 * SUB):
        tiles.append(jnp.where(low, natural[first : first + count], other[first + SUB : first + SUB + count]))
    return jnp.concatenate(tiles, 1)


def gathered(even, odd):
    low = lane_of((SUB, LANES)) < LANES // 2
    out = []
    for tile in range(2):
        a = even[:, tile * LANES : (tile + 1) * LANES]
        b = odd[:, tile * LANES : (tile + 1) * LANES]
        out.append(jnp.where(low, a, turned(b)))
        out.append(jnp.where(low, turned(a), b))
    return jnp.concatenate(out, 0)


def in_order(reverse, own, halo):
    return jnp.concatenate([jnp.where(reverse, halo, own), jnp.where(reverse, own, halo)], 0)


def diagonal_sums(circ):
    total = circ[:8]
    for first in range(8, circ.shape[0], 8):
        total = total + pltpu.roll(circ[first : first + 8], LANES - first, 1)
    for fold in (4, 2, 1):
        total = total + pltpu.roll(pltpu.roll(total, LANES - fold, 1), 8 - fold, 0)
    return total[:1]


def near(reverse_int, shape):
    return lane_of(shape) - row_of(shape) >= reverse_int


def tap_matrix(reverse, taps_by_group):
    taps = taps_by_group.shape[0]
    source = row_of((taps, taps))
    target = lane_of((taps, taps))
    mirrored = jnp.where(source == 0, 0, taps - source)
    pick = jnp.where(target == jnp.where(reverse, mirrored, source), 1.0, 0.0)
    return pick, taps


def weigh_kernel(role, gate, incoming, out):
    @pl.when(role[0] == 0)
    def _():
        out[...] = times(gate[...], incoming[...])


def first_weigh_kernel(pieces, role, gate, incoming, *refs):
    outs, (gate_part, incoming_part, sems) = refs[:-3], refs[-3:]

    @pl.when(role[0] == 0)
    def _():
        copies = []
        for i, (first, last, _, _) in enumerate(pieces):
            cols = pl.ds(first, last - first)
            for which, (source, part) in enumerate(((gate, gate_part), (incoming, incoming_part))):
                copy = pltpu.make_async_copy(source.at[:, cols], part.at[:, cols], sems.at[which, i])
                copies.append(copy)
                copy.start()
        for i, (first, last, out, at) in enumerate(pieces):
            copies[2 * i].wait()
            copies[2 * i + 1].wait()
            cols = pl.ds(first, last - first)
            outs[out][:, pl.ds(at, last - first)] = times(gate_part[:, cols], incoming_part[:, cols])


def taps_kernel(role, filters, taps_out):
    pick, _ = tap_matrix(role[0] > 0, filters[...])
    taps_out[...] = lax.dot_general(
        filters[...], pick.astype(BF16), (((0,), (0,)), ((), ())), preferred_element_type=F32
    )


def convolved(reverse, group_size, own, halo, taps, first_group):
    half = LANES // 2
    per_half = half // group_size
    mask = near(int(reverse), (SUB, LANES))
    zero = jnp.zeros((SUB, LANES), F32)
    lane_group = (lane_of((SUB, 2 * LANES)) % half) // group_size
    ext = jnp.concatenate([halo, own] if reverse else [own, halo], 0)
    ext_turned = turned(ext)
    results = []
    for parity in range(2):
        window = spread(ext, ext_turned, parity, own.shape[0] + SUB)
        bands = []
        for g in range(per_half):
            row = taps[pl.ds(first_group + parity * per_half + g, 1), :]
            circ = pltpu.roll(jnp.broadcast_to(row, (SUB, LANES)), 0, 1, stride=1, stride_axis=0)
            band = jnp.concatenate([jnp.where(mask, circ, zero), jnp.where(mask, zero, circ)[:, :SUB]], 1)
            bands.append(band.astype(BF16))
        product = jnp.dot(jnp.concatenate(bands, 0), window, preferred_element_type=F32)
        total = product[:SUB]
        for g in range(1, per_half):
            total = jnp.where(lane_group == g, product[g * SUB : (g + 1) * SUB], total)
        results.append(total)
    return gathered(*results)


def filter_kernel(group_size, role, own, halo, taps, mid, incoming, outgoing):
    @pl.when(role[0] == 0)
    def _():
        for first in range(0, own.shape[1], LANES):
            cols = pl.ds(first, LANES)
            conv = convolved(False, group_size, own[:, cols], halo[:, cols], taps, first // group_size)
            outgoing[:, cols] = (
                incoming[:, cols].astype(F32) + mid[:, cols].astype(F32) * conv
            ).astype(BF16)


def turned_filter_kernel(group_size, role, mid, mid_halo, taps, filtered):
    @pl.when(role[0] > 0)
    def _():
        for first in range(0, mid.shape[1], LANES):
            cols = pl.ds(first, LANES)
            filtered[:, cols] = convolved(True, group_size, mid[:, cols], mid_halo[:, cols], taps, first // group_size)


def grad_kernel(
    group_size, role, gate, mid, inputs, mid_halo, inputs_halo, own, halo, outgoing, received, filtered,
    tap_grad, steer_grad, left, right_own, right_halo,
):
    reverse = role[0] > 0
    width = own.shape[1]
    half = LANES // 2
    per_half = half // group_size

    @pl.when(reverse)
    def _():
        grad = received[...]
        weighted = times(gate[...], grad)
        left[...] = weighted
        right_own[...] = times(mid[...], inputs[...])
        right_halo[...] = times(mid_halo[...], inputs_halo[...])
        grad_in = grad.astype(F32) + weighted.astype(F32) * filtered[...]
        steer_grad[...] = jnp.sum(grad_in, 0, keepdims=True)

    @pl.when(jnp.logical_not(reverse))
    def _():
        left[...] = times(mid[...], inputs[...])
        right_own[...] = own[...]
        right_halo[...] = halo[...]
        steer_grad[...] = jnp.sum(outgoing[...].astype(F32), 0, keepdims=True)

    mask = near(role[0], (SUB, LANES))
    lane_group = (lane_of((SUB, 2 * LANES)) % half) // group_size
    nothing = jnp.zeros((SUB, 2 * LANES), BF16)
    for pair in range(width // LANES):
        cols = pl.ds(pair * LANES, LANES)
        ext = in_order(reverse, right_own[:, cols], right_halo[:, cols])
        ext_turned = turned(ext)
        rows = left[:, cols]
        rows_turned = turned(rows)
        for parity in range(2):
            window = spread(ext, ext_turned, parity, own.shape[0] + SUB)
            short = spread(rows, rows_turned, parity, SUB)
            lhs = jnp.concatenate(
                [jnp.where(lane_group == g, short, nothing) for g in range(per_half)], 0
            )
            product = lax.dot_general(lhs, window, (((1,), (1,)), ((), ())), preferred_element_type=F32)
            for g in range(per_half):
                block = product[g * SUB : (g + 1) * SUB]
                late = jnp.concatenate([block[:, LANES:], jnp.zeros((SUB, LANES - SUB), F32)], 1)
                circ = jnp.where(mask, block[:, :LANES], late)
                tap_grad[pl.ds((2 * pair + parity) * per_half + g, 1), :] = diagonal_sums(circ)


def step_kernel(role, parts, steer_second, filter_second, steer_out, filter_out):
    total = jnp.sum(parts[...], 0)
    groups = filter_second.shape[0]
    tap_grad = total[:groups]
    lane = lane_of(tap_grad.shape)
    mirrored = jnp.where(lane == 0, 0, tap_grad.shape[1] - lane)
    tap_grad = jnp.take_along_axis(tap_grad, jnp.where(role[0] > 0, mirrored, lane), axis=1)
    filter_out[...] = tap_grad / jnp.sqrt(filter_second[...] + tap_grad * tap_grad)
    channels = steer_out.shape[1]
    for row in range(pl.cdiv(channels, LANES)):
        cols = min(LANES, channels - row * LANES)
        at = pl.ds(row * LANES, cols)
        grad = total[groups + row : groups + row + 1, :cols]
        steer_out[:, at] = grad / jnp.sqrt(steer_second[:, at] + grad * grad)


def spec(rows, width, first=0):
    return pl.BlockSpec((rows, width), lambda i: (0, i + first))


SMEM = pl.BlockSpec(memory_space=pltpu.SMEM)
ANY = pl.BlockSpec(memory_space=pl.ANY)


def call(kernel, grid, in_specs, out_specs, out_shape, scratch=(), name=None, cycles=100, after=()):
    count = len(in_specs)

    def with_after(*refs):
        kernel(*refs[:count], *refs[count + len(after) :])

    return pl.pallas_call(
        with_after,
        grid=grid,
        in_specs=list(in_specs) + [ANY] * len(after),
        out_specs=out_specs,
        out_shape=out_shape,
        scratch_shapes=list(scratch),
        compiler_params=pltpu.CompilerParams(vmem_limit_bytes=32 * 1024 * 1024),
        cost_estimate=pl.CostEstimate(flops=cycles, bytes_accessed=0, transcendentals=0),
        name=name,
    )


def body(cotangent, in_gate, mid_gate, layer_inputs, filters, steer_second, filter_second):
    in_gate, mid_gate, layer_inputs = in_gate[0], mid_gate[0], layer_inputs[0]
    rows, channels = in_gate.shape
    filt_len, groups = filters.shape[1:]
    group_size = channels // groups
    sections, seqs = lax.axis_size("section"), lax.axis_size("seq")
    my_section = lax.axis_index("section")
    role = (my_section == 0).astype(jnp.int32).reshape(1)

    edges = [channels * eighths // 8 for eighths in CHUNK_EDGES]
    bounds = list(zip(edges[:-1], edges[1:]))
    block = channels // 8
    block_groups = block // group_size
    behind = [(seqs * s + i, seqs * s + i - 1) for s in range(1, sections) for i in range(1, seqs)]
    ahead = [(i, i + 1) for i in range(seqs - 1)]
    down = [(s, s - 1) for s in range(1, sections)]

    def bf16(width_of):
        return jax.ShapeDtypeStruct((rows, width_of), BF16)

    def weigh(incoming, first, last):
        return call(
            weigh_kernel, ((last - first) // block,), [SMEM, spec(rows, block, first // block), spec(rows, block)],
            spec(rows, block), bf16(last - first), name="weigh",
        )(role, in_gate, incoming)

    def first_weigh(starts, ends):
        pieces = [
            (at, at + block, part, at - first)
            for part, (first, last) in enumerate(zip(starts, ends))
            for at in range(first, last, block)
        ]
        whole = pltpu.VMEM((rows, channels), BF16)
        return pl.pallas_call(
            functools.partial(first_weigh_kernel, pieces),
            in_specs=[SMEM] + [pl.BlockSpec(memory_space=pltpu.HBM)] * 2,
            out_specs=[pl.BlockSpec(memory_space=pltpu.VMEM)] * len(starts),
            out_shape=[bf16(last - first) for first, last in zip(starts, ends)],
            scratch_shapes=[whole, whole, pltpu.SemaphoreType.DMA((2, len(pieces)))],
            compiler_params=pltpu.CompilerParams(vmem_limit_bytes=FIRST_VMEM),
            name="first_weigh",
        )(role, in_gate, cotangent)

    mid_halo = lax.ppermute(mid_gate, ("section", "seq"), ahead)
    inputs_halo = lax.ppermute(layer_inputs, ("section", "seq"), ahead)
    taps = call(
        taps_kernel,
        (1,),
        [SMEM, pl.BlockSpec((filt_len, groups), lambda i: (0, 0))],
        pl.BlockSpec((groups, filt_len), lambda i: (0, 0)),
        jax.ShapeDtypeStruct((groups, filt_len), F32),
        name="taps",
    )(role, filters[0])
    group_spec = lambda first: pl.BlockSpec((block_groups, filt_len), lambda i: (i + first, 0))

    incoming = [(cotangent, 0)] * len(bounds)
    for hop in range(sections - 1):
        split = [channels * eighths // 8 for eighths in HALO_EDGES] if hop == 0 else edges
        starts, ends = split[:-1], split[1:]
        if hop == 0:
            owns = first_weigh(starts, ends)
        else:
            owns = [weigh(array, first, last) for (array, _), first, last in zip(incoming, starts, ends)]
        halos = [lax.ppermute(own, ("section", "seq"), behind) for own in owns]
        sources, outgoing, received = [], [], []
        for k, (first, last) in enumerate(bounds):
            part = max(i for i, start in enumerate(starts) if start <= first)
            at = (first - starts[part]) // block
            array, offset = incoming[k]
            before = tuple(outgoing[-1:])
            out = call(
                functools.partial(filter_kernel, group_size),
                ((last - first) // block,),
                [SMEM, spec(rows, block, at), spec(rows, block, at), group_spec(first // block),
                 spec(rows, block, first // block), spec(rows, block, (first - offset) // block)],
                spec(rows, block),
                bf16(last - first),
                name="filter",
                cycles=1000,
                after=before,
            )(role, owns[part], halos[part], taps, mid_gate, array, *before)
            sources.append((owns[part], halos[part], at))
            outgoing.append(out)
            received.append(lax.ppermute(out, "section", down))
        top = my_section == sections - 1
        incoming = [
            (jnp.where(top, cotangent[:, first:last], arrived), first)
            for (first, last), arrived in zip(bounds, received)
        ]

    filtered = call(
        functools.partial(turned_filter_kernel, group_size),
        (channels // block,),
        [SMEM, spec(rows, block), spec(rows, block), group_spec(0)],
        spec(rows, block),
        jax.ShapeDtypeStruct((rows, channels), F32),
        name="turned_filter",
        cycles=4000,
        after=tuple(outgoing[-1:]),
    )(role, mid_gate, mid_halo, taps, *outgoing[-1:])

    grads = []
    for k, (first, last) in enumerate(bounds):
        own, halo, at = sources[k]
        width = last - first
        here = spec(rows, block, first // block)
        after = tuple(grads[-1][:1] if grads else ())
        grads.append(call(
            functools.partial(grad_kernel, group_size),
            (width // block,),
            [SMEM, here, here, here, here, here, spec(rows, block, at), spec(rows, block, at)]
            + [spec(rows, block)] * 2 + [here],
            [group_spec(0), pl.BlockSpec((1, block), lambda i: (0, i))],
            [jax.ShapeDtypeStruct((width // group_size, filt_len), F32), jax.ShapeDtypeStruct((1, width), F32)],
            scratch=[pltpu.VMEM((rows, block), BF16)] * 3,
            name="grads",
            cycles=2000,
            after=after,
        )(role, in_gate, mid_gate, layer_inputs, mid_halo, inputs_halo, own, halo, outgoing[k],
          received[k], filtered, *after))
    tap_grads, steer_grads = zip(*grads)

    inner = max(d for d in range(1, seqs + 1) if seqs % d == 0 and d * d <= seqs)
    outer = seqs // inner
    own_channels = channels // seqs
    steer_rows = pl.cdiv(own_channels, LANES)
    tap_all = jnp.concatenate(tap_grads, 0).reshape(seqs, groups // seqs, filt_len)
    steer_all = jnp.concatenate(steer_grads, 1).reshape(seqs, own_channels)
    steer_all = jnp.pad(steer_all, ((0, 0), (0, steer_rows * LANES - own_channels)))
    packed = jnp.concatenate([tap_all, steer_all.reshape(seqs, steer_rows, LANES)], 1)
    packed = packed.reshape((outer, inner) + packed.shape[1:]).swapaxes(0, 1)
    near_by = [[o * inner + i for i in range(inner)] for o in range(outer)]
    far_off = [[o * inner + i for o in range(outer)] for i in range(inner)]
    parts = jnp.sum(lax.all_to_all(packed, "seq", 0, 0, axis_index_groups=near_by), 0)
    parts = lax.all_to_all(parts, "seq", 0, 0, axis_index_groups=far_off)
    steer_step, filter_step = pl.pallas_call(
        step_kernel,
        in_specs=[SMEM] + [pl.BlockSpec(memory_space=pltpu.VMEM)] * 3,
        out_shape=[
            jax.ShapeDtypeStruct((1, own_channels), F32),
            jax.ShapeDtypeStruct((groups // seqs, filt_len), F32),
        ],
        name="step",
    )(role, parts, steer_second, filter_second[0].T)
    return steer_step, filter_step.T[None]


def solution(mesh):
    in_specs = (
        P("seq", None),
        P("section", "seq", None),
        P("section", "seq", None),
        P("section", "seq", None),
        P("section", None, None),
        P("section", "seq"),
        P("section", None, "seq"),
    )
    out_specs = (P("section", "seq"), P("section", None, "seq"))
    return jax.shard_map(body, mesh=mesh, in_specs=in_specs, out_specs=out_specs, check_vma=False)
```

time: 73.2 us -> 69.9 us (0.955)
  blocking collectives: 14.8 us -> 28.6 us
  waiting for transfers between devices: 16.2 us -> 3.93 us
  starting transfers between devices: 21.6 us -> 14.8 us
  Pallas kernels: 15.4 us -> 18.5 us
  local copies, waits for them, and re-layouts: 3.79 us -> 2.39 us
    all_to_all x1 -> x2, blocking collectives: 14.8 us -> 28.6 us  [the longest x1 17.1 us: body(): lax.all_to_all(packed, 'seq', 0, 0, axis_index_groups=near_by)]
    ppermute x4, waiting for transfers between devices: 16.2 us -> 3.92 us  [body(): received.append(lax.ppermute(out, 'section', down))]
    ppermute x5 -> x4, starting transfers between devices: 16.4 us -> 9.4 us  [the longest x1 5.46 us: body(): inputs_halo = lax.ppermute(layer_inputs, ('section', 'seq'), ahead)]
    pallas_call x13 -> x10, Pallas kernels: 13.5 us -> 16.8 us  [the longest x4 10.8 us: body(): call(functools.partial(grad_kernel, group_size), (width // block,), [SMEM...]
    unnamed x16, local copies, waits for them, and re-layouts: 3.79 us -> 2.29 us
  transfers between devices with their start and end apart: 9 -> 8, of which waited for: 4 -> 2; matrix products, arithmetic and copies ran while one was open for 0% -> 0% of each run, Pallas kernels for 16% -> 21%
where the time goes in v2:
time: 69.9 us; the launch traced here: 69.3 us
  blocking collectives  28.6 us (41%)
  Pallas kernels  18.5 us (26%)
  starting transfers between devices  14.8 us (21%)
  waiting for transfers between devices  3.93 us (6%)
  local copies, waits for them, and re-layouts  2.39 us (3%)
  between operations  0.96 us (1%)
    all_to_all x1, blocking collectives, body(): lax.all_to_all(packed, 'seq', 0, 0, axis_index_groups=near_by)  17.1 us
    all_to_all x1, blocking collectives, body(): parts = lax.all_to_all(parts, 'seq', 0, 0, axis_index_groups=far_off)  11.5 us
    pallas_call x4, Pallas kernels, body(): call(functools.partial(grad_kernel, group_size), (width // block,), [SMEM...  10.8 us
    ppermute x1, starting transfers between devices, body(): inputs_halo = lax.ppermute(layer_inputs, ('section', 'seq'), ahead)  5.46 us
    ppermute x4, starting transfers between devices, body(): received.append(lax.ppermute(out, 'section', down))  5.43 us
    pallas_call x1, Pallas kernels, body(): call(functools.partial(turned_filter_kernel, group_size), (channels // bl...  4.09 us
    ppermute x4, waiting for transfers between devices, body(): received.append(lax.ppermute(out, 'section', down))  3.92 us
    ppermute x1, starting transfers between devices, body(): mid_halo = lax.ppermute(mid_gate, ('section', 'seq'), ahead)  2.55 us
  transfers between devices with their start and end apart: 8, of which 2 were waited for; matrix products, arithmetic and copies ran while one was open for 0% of the time, Pallas kernels for 21%

profile of v2, /device:TPU:0, one launch (start us, length us, event | category | flops | bytes accessed | tf_op | source)
XLA Modules:
  0.0 69.3 jit_solution(1446264617906244166)
XLA Ops:
  0.6 0.0 copy-start
  0.6 0.0 copy-start.7
  0.6 2.6 %collective-permute-start = (bf16[128,4096]{1,0:T(8,128)(2,1)}, bf16[128,4096]{1,0:T(8,128)(2,1)S(1)}, u32[]{:S(2)}, u32[]{:S(2)}) collective-permute-start(bf16[128,4096]{1,0:T(8,128)(2,1)} %bitcast.15), channel_id=1, source_target_pairs={{0,1},{1,2},{2,3},{3,4},{4,5},{5,6},{6,7},{7,8},{8,9},{9,10},{10,1... | collective-permute-start | bytes 3145736 | tf_op jit(solution)/shard_map/ppermute | solution.py:292
  3.2 5.5 %collective-permute-start.1 = (bf16[128,4096]{1,0:T(8,128)(2,1)}, bf16[128,4096]{1,0:T(8,128)(2,1)}, u32[]{:S(2)}, u32[]{:S(2)}) collective-permute-start(bf16[128,4096]{1,0:T(8,128)(2,1)} %bitcast.30), channel_id=1, source_target_pairs={{0,1},{1,2},{2,3},{3,4},{4,5},{5,6},{6,7},{7,8},{8,9},{9,10},{10,1... | collective-permute-start | bytes 3145736 | tf_op jit(solution)/shard_map/ppermute | solution.py:293
  8.7 1.1 %first_weigh.1 = (bf16[128,2048]{1,0:T(8,128)(2,1)}, bf16[128,2048]{1,0:T(8,128)(2,1)}) custom-call(s32[1]{0:T(128)} %bitcast.role.refs_0_, bf16[128,4096]{1,0:T(8,128)(2,1)} %bitcast.25, bf16[128,4096]{1,0:T(8,128)(2,1)} %refs_5_.7), custom_call_target="tpu_custom_call" | custom-call | tf_op jit(solution)/shard_map/first_weigh/pallas_call | solution.py:282
  9.8 0.7 %collective-permute-start.2 = (bf16[128,2048]{1,0:T(8,128)(2,1)}, bf16[128,2048]{1,0:T(8,128)(2,1)S(1)}, u32[]{:S(2)}, u32[]{:S(2)}) collective-permute-start(bf16[128,2048]{1,0:T(8,128)(2,1)} %get-tuple-element.14.refs_1_.refs_6_), channel_id=1, source_target_pairs={{17,16},{18,17},{19,18},{20,19},{21,20},{22,21},{23,22},{24,23},{2... | collective-permute-start | bytes 1572872 | tf_op jit(solution)/shard_map/ppermute | solution.py:312
  10.5 0.7 %collective-permute-start.4 = (bf16[128,2048]{1,0:T(8,128)(2,1)}, bf16[128,2048]{1,0:T(8,128)(2,1)S(1)}, u32[]{:S(2)}, u32[]{:S(2)}) collective-permute-start(bf16[128,2048]{1,0:T(8,128)(2,1)} %get-tuple-element.15.refs_1_.refs_6_), channel_id=1, source_target_pairs={{17,16},{18,17},{19,18},{20,19},{21,20},{22,21},{23,22},{24,23},{2... | collective-permute-start | bytes 1572872 | tf_op jit(solution)/shard_map/ppermute | solution.py:312
  11.2 0.0 copy-done.7
  11.2 0.2 taps.1.refs_3_
  11.4 0.0 collective-permute-done.2.refs_2_.refs_7_
  11.4 0.0 copy-done
  11.4 0.0 copy-start.2
  11.4 1.2 %copy-done.2 = bf16[128,4096]{1,0:T(8,128)(2,1)S(1)} copy-done((bf16[128,4096]{1,0:T(8,128)(2,1)S(1)}, bf16[128,4096]{1,0:T(8,128)(2,1)}, u32[]{:S(2)}) %copy-start.2) | copy-done | bytes 1048600
  12.7 0.0 copy-start.5
  12.7 1.0 %copy-done.5 = bf16[128,2048]{1,0:T(8,128)(2,1)S(1)} copy-done((bf16[128,2048]{1,0:T(8,128)(2,1)S(1)}, bf16[128,2048]{1,0:T(8,128)(2,1)}, u32[]{:S(2)}) %copy-start.5) | copy-done | bytes 524312
  13.7 0.2 filter.4.refs_6_.refs_8_
  13.9 0.0 copy-start.4
  13.9 1.4 %collective-permute-start.3 = (bf16[128,1024]{1,0:T(8,128)(2,1)S(1)}, bf16[128,1024]{1,0:T(8,128)(2,1)S(1)}, u32[]{:S(2)}, u32[]{:S(2)}) collective-permute-start(bf16[128,1024]{1,0:T(8,128)(2,1)S(1)} %filter.4.refs_6_.refs_8_), channel_id=1, source_target_pairs={{16,0},{17,1},{18,2},{19,3},{20,4},{21,5},{22,6},{23,7},{24,8},{25... | collective-permute-start | bytes 786440 | tf_op jit(solution)/shard_map/ppermute | solution.py:332
  15.3 0.2 filter.5.refs_6_.refs_8_
  15.5 1.3 %collective-permute-start.5 = (bf16[128,1024]{1,0:T(8,128)(2,1)S(1)}, bf16[128,1024]{1,0:T(8,128)(2,1)S(1)}, u32[]{:S(2)}, u32[]{:S(2)}) collective-permute-start(bf16[128,1024]{1,0:T(8,128)(2,1)S(1)} %filter.5.refs_6_.refs_8_), channel_id=1, source_target_pairs={{16,0},{17,1},{18,2},{19,3},{20,4},{21,5},{22,6},{23,7},{24,8},{25... | collective-permute-start | bytes 786440 | tf_op jit(solution)/shard_map/ppermute | solution.py:332
  16.8 0.0 collective-permute-done.4.refs_2_.refs_7_
  16.8 0.0 copy-done.4
  16.8 0.2 filter.6.refs_6_.refs_8_
  17.1 1.3 %collective-permute-start.6 = (bf16[128,1024]{1,0:T(8,128)(2,1)S(1)}, bf16[128,1024]{1,0:T(8,128)(2,1)S(1)}, u32[]{:S(2)}, u32[]{:S(2)}) collective-permute-start(bf16[128,1024]{1,0:T(8,128)(2,1)S(1)} %filter.6.refs_6_.refs_8_), channel_id=1, source_target_pairs={{16,0},{17,1},{18,2},{19,3},{20,4},{21,5},{22,6},{23,7},{24,8},{25... | collective-permute-start | bytes 786440 | tf_op jit(solution)/shard_map/ppermute | solution.py:332
  18.4 0.2 filter.7.refs_4_.refs_8_
  18.6 0.0 copy-start.1
  18.6 0.0 copy-start.3
  18.6 0.0 copy-start.6
  18.6 0.0 collective-permute-done.refs_2_.refs_4_
  18.6 1.4 %collective-permute-start.7 = (bf16[128,1024]{1,0:T(8,128)(2,1)S(1)}, bf16[128,1024]{1,0:T(8,128)(2,1)S(1)}, u32[]{:S(2)}, u32[]{:S(2)}) collective-permute-start(bf16[128,1024]{1,0:T(8,128)(2,1)S(1)} %filter.7.refs_4_.refs_8_), channel_id=1, source_target_pairs={{16,0},{17,1},{18,2},{19,3},{20,4},{21,5},{22,6},{23,7},{24,8},{25... | collective-permute-start | bytes 786440 | tf_op jit(solution)/shard_map/ppermute | solution.py:332
  20.1 4.1 %turned_filter.1.refs_10_ = f32[128,4096]{1,0:T(8,128)S(1)} custom-call(s32[1]{0:T(128)} %bitcast.role.refs_0_, bf16[128,4096]{1,0:T(8,128)(2,1)S(1)} %bitcast.20, bf16[128,4096]{1,0:T(8,128)(2,1)S(1)} %collective-permute-done.refs_2_.refs_4_, f32[256,128]{1,0:T(8,128)S(1)} %taps.1.refs_3_, bf16[128,1024]{1,0:T(8,128)(2,1)S(1)} %filter.7.refs_4_.refs_8_), custom_call_target="tpu_custom_call" | custom-call | flops 4000 | tf_op jit(solution)/shard_map/turned_filter/pallas_call | solution.py:339
  24.2 0.0 collective-permute-done.3.refs_9_
  24.2 0.0 collective-permute-done.1.refs_5_
  24.2 0.0 copy-done.1
  24.2 0.0 copy-done.3
  24.2 0.0 copy-done.6
  24.2 2.7 %grads.4 = (f32[64,128]{1,0:T(8,128)S(1)}, f32[1,1024]{1,0:T(1,128)S(1)}) custom-call(s32[1]{0:T(128)} %bitcast.role.refs_0_, bf16[128,4096]{1,0:T(8,128)(2,1)S(1)} %bitcast.26, bf16[128,4096]{1,0:T(8,128)(2,1)S(1)} %bitcast.21, bf16[128,4096]{1,0:T(8,128)(2,1)S(1)} %bitcast.31, bf16[128,4096]{1,0:T(8,128)(2,1)S(1)} %collective-permute-done.refs_2_.refs_4_, ...), custom_call_target="tpu_custom_call" | custom-call | flops 2000 | tf_op jit(solution)/shard_map/grads/pallas_call | solution.py:356
  26.9 0.0 collective-permute-done.5.refs_9_
  26.9 2.7 %grads.5 = (f32[64,128]{1,0:T(8,128)S(1)}, f32[1,1024]{1,0:T(1,128)S(1)}) custom-call(s32[1]{0:T(128)} %bitcast.role.refs_0_, bf16[128,4096]{1,0:T(8,128)(2,1)S(1)} %bitcast.27, bf16[128,4096]{1,0:T(8,128)(2,1)S(1)} %bitcast.22, bf16[128,4096]{1,0:T(8,128)(2,1)S(1)} %bitcast.32, bf16[128,4096]{1,0:T(8,128)(2,1)S(1)} %collective-permute-done.refs_2_.refs_4_, ...), custom_call_target="tpu_custom_call" | custom-call | flops 2000 | tf_op jit(solution)/shard_map/grads/pallas_call | solution.py:356
  29.7 1.0 %collective-permute-done.6.refs_9_ = bf16[128,1024]{1,0:T(8,128)(2,1)S(1)} collective-permute-done((bf16[128,1024]{1,0:T(8,128)(2,1)S(1)}, bf16[128,1024]{1,0:T(8,128)(2,1)S(1)}, u32[]{:S(2)}, u32[]{:S(2)}) %collective-permute-start.6) | collective-permute-done | bytes 262176 | tf_op jit(solution)/shard_map/ppermute | solution.py:332
  30.6 2.7 %grads.6 = (f32[64,128]{1,0:T(8,128)S(1)}, f32[1,1024]{1,0:T(1,128)S(1)}) custom-call(s32[1]{0:T(128)} %bitcast.role.refs_0_, bf16[128,4096]{1,0:T(8,128)(2,1)S(1)} %bitcast.28, bf16[128,4096]{1,0:T(8,128)(2,1)S(1)} %bitcast.23, bf16[128,4096]{1,0:T(8,128)(2,1)S(1)} %bitcast.33, bf16[128,4096]{1,0:T(8,128)(2,1)S(1)} %collective-permute-done.refs_2_.refs_4_, ...), custom_call_target="tpu_custom_call" | custom-call | flops 2000 | tf_op jit(solution)/shard_map/grads/pallas_call | solution.py:356
  33.3 2.9 %collective-permute-done.7.refs_9_ = bf16[128,1024]{1,0:T(8,128)(2,1)S(1)} collective-permute-done((bf16[128,1024]{1,0:T(8,128)(2,1)S(1)}, bf16[128,1024]{1,0:T(8,128)(2,1)S(1)}, u32[]{:S(2)}, u32[]{:S(2)}) %collective-permute-start.7) | collective-permute-done | bytes 262176 | tf_op jit(solution)/shard_map/ppermute | solution.py:332
  36.3 2.7 %grads.7 = (f32[64,128]{1,0:T(8,128)S(1)}, f32[1,1024]{1,0:T(1,128)S(1)}) custom-call(s32[1]{0:T(128)} %bitcast.role.refs_0_, bf16[128,4096]{1,0:T(8,128)(2,1)S(1)} %bitcast.29, bf16[128,4096]{1,0:T(8,128)(2,1)S(1)} %bitcast.24, bf16[128,4096]{1,0:T(8,128)(2,1)S(1)} %bitcast.34, bf16[128,4096]{1,0:T(8,128)(2,1)S(1)} %collective-permute-done.refs_2_.refs_4_, ...), custom_call_target="tpu_custom_call" | custom-call | flops 2000 | tf_op jit(solution)/shard_map/grads/pallas_call | solution.py:356
  39.0 0.1 copy.11
  39.2 17.1 %all_to_all.10 = f32[4,4,18,128]{3,1,2,0:T(4,128)S(1)} all-to-all(f32[4,4,18,128]{3,1,2,0:T(4,128)S(1)} %maximum_bitcast_fusion), channel_id=1, replica_groups={{0,1,2,3},{4,5,6,7},{8,9,10,11},{12,13,14,15},{16,17,18,19},{20,21,22,2..., dimensions={0} | all-to-all | bytes 294912 | tf_op jit(solution)/shard_map/all_to_all | solution.py:382
  56.3 11.5 %all_to_all.11.parts = f32[4,18,128]{2,1,0:T(8,128)} all-to-all(f32[4,18,128]{2,1,0:T(8,128)S(1)} %copy.13), channel_id=1, replica_groups={{0,4,8,12},{1,5,9,13},{2,6,10,14},{3,7,11,15},{16,20,24,28},{17,21,25,2..., dimensions={0} | all-to-all | bytes 73728 | tf_op jit(solution)/shard_map/all_to_all | solution.py:383
  67.8 1.5 %step.1 = (f32[1,256]{1,0:T(1,128)}, f32[16,128]{1,0:T(8,128)}) custom-call(s32[1]{0:T(128)} %bitcast.role.refs_0_, f32[4,18,128]{2,1,0:T(8,128)} %all_to_all.11.parts, f32[1,256]{1,0:T(1,128)} %steer_second.1, f32[16,128]{1,0:T(8,128)} %bitcast.38), custom_call_target="tpu_custom_call" | custom-call | tf_op jit(solution)/shard_map/step/pallas_call | solution.py:384
  (6 shorter events, 0.1 us)
Async XLA Ops:
  0.6 10.8 %copy-start = (bf16[1,128,4096]{2,1,0:T(8,128)(2,1)S(1)}, bf16[1,128,4096]{2,1,0:T(8,128)(2,1)}, u32[]{:S(2)}) copy-start(bf16[1,128,4096]{2,1,0:T(8,128)(2,1)} %param.9) | copy-start | bytes 3145732
  0.6 10.6 %copy-start.7 = (bf16[1,128,256]{2,1,0:T(8,128)(2,1)S(1)}, bf16[1,128,256]{2,1,0:T(8,128)(2,1)}, u32[]{:S(2)}) copy-start(bf16[1,128,256]{2,1,0:T(8,128)(2,1)} %param.11) | copy-start | bytes 196612
  0.6 18.0 %collective-permute-start = (bf16[128,4096]{1,0:T(8,128)(2,1)}, bf16[128,4096]{1,0:T(8,128)(2,1)S(1)}, u32[]{:S(2)}, u32[]{:S(2)}) collective-permute-start(bf16[128,4096]{1,0:T(8,128)(2,1)} %bitcast.15), channel_id=1, source_target_pairs={{0,1},{1,2},{2,3},{3,4},{4,5},{5,6},{6,7},{7,8},{8,9},{9,10},{10,1... | collective-permute-start | bytes 3145736 | tf_op jit(solution)/shard_map/ppermute | solution.py:292
  3.2 21.0 %collective-permute-start.1 = (bf16[128,4096]{1,0:T(8,128)(2,1)}, bf16[128,4096]{1,0:T(8,128)(2,1)}, u32[]{:S(2)}, u32[]{:S(2)}) collective-permute-start(bf16[128,4096]{1,0:T(8,128)(2,1)} %bitcast.30), channel_id=1, source_target_pairs={{0,1},{1,2},{2,3},{3,4},{4,5},{5,6},{6,7},{7,8},{8,9},{9,10},{10,1... | collective-permute-start | bytes 3145736 | tf_op jit(solution)/shard_map/ppermute | solution.py:293
  9.8 1.6 %collective-permute-start.2 = (bf16[128,2048]{1,0:T(8,128)(2,1)}, bf16[128,2048]{1,0:T(8,128)(2,1)S(1)}, u32[]{:S(2)}, u32[]{:S(2)}) collective-permute-start(bf16[128,2048]{1,0:T(8,128)(2,1)} %get-tuple-element.14.refs_1_.refs_6_), channel_id=1, source_target_pairs={{17,16},{18,17},{19,18},{20,19},{21,20},{22,21},{23,22},{24,23},{2... | collective-permute-start | bytes 1572872 | tf_op jit(solution)/shard_map/ppermute | solution.py:312
  10.5 6.3 %collective-permute-start.4 = (bf16[128,2048]{1,0:T(8,128)(2,1)}, bf16[128,2048]{1,0:T(8,128)(2,1)S(1)}, u32[]{:S(2)}, u32[]{:S(2)}) collective-permute-start(bf16[128,2048]{1,0:T(8,128)(2,1)} %get-tuple-element.15.refs_1_.refs_6_), channel_id=1, source_target_pairs={{17,16},{18,17},{19,18},{20,19},{21,20},{22,21},{23,22},{24,23},{2... | collective-permute-start | bytes 1572872 | tf_op jit(solution)/shard_map/ppermute | solution.py:312
  11.4 1.2 %copy-start.2 = (bf16[128,4096]{1,0:T(8,128)(2,1)S(1)}, bf16[128,4096]{1,0:T(8,128)(2,1)}, u32[]{:S(2)}) copy-start(bf16[128,4096]{1,0:T(8,128)(2,1)} %refs_5_.7) | copy-start | bytes 3145732
  12.7 1.0 %copy-start.5 = (bf16[128,2048]{1,0:T(8,128)(2,1)S(1)}, bf16[128,2048]{1,0:T(8,128)(2,1)}, u32[]{:S(2)}) copy-start(bf16[128,2048]{1,0:T(8,128)(2,1)} %get-tuple-element.14.refs_1_.refs_6_) | copy-start | bytes 1572868
  13.9 3.0 %copy-start.4 = (bf16[128,2048]{1,0:T(8,128)(2,1)S(1)}, bf16[128,2048]{1,0:T(8,128)(2,1)}, u32[]{:S(2)}) copy-start(bf16[128,2048]{1,0:T(8,128)(2,1)} %get-tuple-element.15.refs_1_.refs_6_) | copy-start | bytes 1572868
  13.9 10.3 %collective-permute-start.3 = (bf16[128,1024]{1,0:T(8,128)(2,1)S(1)}, bf16[128,1024]{1,0:T(8,128)(2,1)S(1)}, u32[]{:S(2)}, u32[]{:S(2)}) collective-permute-start(bf16[128,1024]{1,0:T(8,128)(2,1)S(1)} %filter.4.refs_6_.refs_8_), channel_id=1, source_target_pairs={{16,0},{17,1},{18,2},{19,3},{20,4},{21,5},{22,6},{23,7},{24,8},{25... | collective-permute-start | bytes 786440 | tf_op jit(solution)/shard_map/ppermute | solution.py:332
  15.5 11.4 %collective-permute-start.5 = (bf16[128,1024]{1,0:T(8,128)(2,1)S(1)}, bf16[128,1024]{1,0:T(8,128)(2,1)S(1)}, u32[]{:S(2)}, u32[]{:S(2)}) collective-permute-start(bf16[128,1024]{1,0:T(8,128)(2,1)S(1)} %filter.5.refs_6_.refs_8_), channel_id=1, source_target_pairs={{16,0},{17,1},{18,2},{19,3},{20,4},{21,5},{22,6},{23,7},{24,8},{25... | collective-permute-start | bytes 786440 | tf_op jit(solution)/shard_map/ppermute | solution.py:332
  17.1 13.6 %collective-permute-start.6 = (bf16[128,1024]{1,0:T(8,128)(2,1)S(1)}, bf16[128,1024]{1,0:T(8,128)(2,1)S(1)}, u32[]{:S(2)}, u32[]{:S(2)}) collective-permute-start(bf16[128,1024]{1,0:T(8,128)(2,1)S(1)} %filter.6.refs_6_.refs_8_), channel_id=1, source_target_pairs={{16,0},{17,1},{18,2},{19,3},{20,4},{21,5},{22,6},{23,7},{24,8},{25... | collective-permute-start | bytes 786440 | tf_op jit(solution)/shard_map/ppermute | solution.py:332
  18.6 5.6 %copy-start.1 = (bf16[1,128,4096]{2,1,0:T(8,128)(2,1)S(1)}, bf16[1,128,4096]{2,1,0:T(8,128)(2,1)}, u32[]{:S(2)}) copy-start(bf16[1,128,4096]{2,1,0:T(8,128)(2,1)} %param.8) | copy-start | bytes 3145732
  18.6 5.6 %copy-start.3 = (bf16[1,128,4096]{2,1,0:T(8,128)(2,1)S(1)}, bf16[1,128,4096]{2,1,0:T(8,128)(2,1)}, u32[]{:S(2)}) copy-start(bf16[1,128,4096]{2,1,0:T(8,128)(2,1)} %param.10) | copy-start | bytes 3145732
  18.6 5.6 %copy-start.6 = (bf16[128,2048]{1,0:T(8,128)(2,1)S(1)}, bf16[128,2048]{1,0:T(8,128)(2,1)}, u32[]{:S(2)}) copy-start(bf16[128,2048]{1,0:T(8,128)(2,1)} %get-tuple-element.14.refs_1_.refs_6_) | copy-start | bytes 1572868
  18.6 17.6 %collective-permute-start.7 = (bf16[128,1024]{1,0:T(8,128)(2,1)S(1)}, bf16[128,1024]{1,0:T(8,128)(2,1)S(1)}, u32[]{:S(2)}, u32[]{:S(2)}) collective-permute-start(bf16[128,1024]{1,0:T(8,128)(2,1)S(1)} %filter.7.refs_4_.refs_8_), channel_id=1, source_target_pairs={{16,0},{17,1},{18,2},{19,3},{20,4},{21,5},{22,6},{23,7},{24,8},{25... | collective-permute-start | bytes 786440 | tf_op jit(solution)/shard_map/ppermute | solution.py:332

commit v3 on v2

--- a/solution.py
+++ b/solution.py
@@ -11,9 +11,8 @@
 BF16 = jnp.bfloat16
 LANES = 128
 SUB = 32
-CHUNK_EDGES = (0, 2, 4, 6, 8)
-HALO_EDGES = (0, 4, 8)
-FIRST_VMEM = 61 * 1024 * 1024
+CHUNK_EDGES = (0, 3, 6, 7, 8)
+HALO_EDGES = (0, 3, 6, 8)
 
 
 def lane_of(shape):
@@ -56,13 +55,22 @@
     return jnp.concatenate([jnp.where(reverse, halo, own), jnp.where(reverse, own, halo)], 0)
 
 
-def diagonal_sums(circ):
-    total = circ[:8]
-    for first in range(8, circ.shape[0], 8):
-        total = total + pltpu.roll(circ[first : first + 8], LANES - first, 1)
+def diagonal_sums(blocks):
+    tiles = []
+    for block in blocks:
+        tile = block[:8]
+        for first in range(8, SUB, 8):
+            tile = tile + pltpu.roll(block[first : first + 8], LANES - first, 1)
+        tiles.append(tile)
+    row = row_of((8, LANES))
     for fold in (4, 2, 1):
-        total = total + pltpu.roll(pltpu.roll(total, LANES - fold, 1), 8 - fold, 0)
-    return total[:1]
+        upper = row % (2 * fold) < fold
+        tiles = [
+            jnp.where(upper, a, pltpu.roll(b, fold, 0))
+            + pltpu.roll(jnp.where(upper, pltpu.roll(a, 8 - fold, 0), b), LANES - fold, 1)
+            for a, b in zip(tiles[:fold], tiles[fold:])
+        ]
+    return tiles[0]
 
 
 def near(reverse_int, shape):
@@ -78,29 +86,12 @@
     return pick, taps
 
 
-def weigh_kernel(role, gate, incoming, out):
+def weigh_kernel(role, gate, incoming, mid, out, incoming_out, mid_out):
     @pl.when(role[0] == 0)
     def _():
         out[...] = times(gate[...], incoming[...])
-
-
-def first_weigh_kernel(pieces, role, gate, incoming, *refs):
-    outs, (gate_part, incoming_part, sems) = refs[:-3], refs[-3:]
-
-    @pl.when(role[0] == 0)
-    def _():
-        copies = []
-        for i, (first, last, _, _) in enumerate(pieces):
-            cols = pl.ds(first, last - first)
-            for which, (source, part) in enumerate(((gate, gate_part), (incoming, incoming_part))):
-                copy = pltpu.make_async_copy(source.at[:, cols], part.at[:, cols], sems.at[which, i])
-                copies.append(copy)
-                copy.start()
-        for i, (first, last, out, at) in enumerate(pieces):
-            copies[2 * i].wait()
-            copies[2 * i + 1].wait()
-            cols = pl.ds(first, last - first)
-            outs[out][:, pl.ds(at, last - first)] = times(gate_part[:, cols], incoming_part[:, cols])
+        incoming_out[...] = incoming[...]
+        mid_out[...] = mid[...]
 
 
 def taps_kernel(role, filters, taps_out):
@@ -189,6 +180,7 @@
         ext_turned = turned(ext)
         rows = left[:, cols]
         rows_turned = turned(rows)
+        blocks = []
         for parity in range(2):
             window = spread(ext, ext_turned, parity, own.shape[0] + SUB)
             short = spread(rows, rows_turned, parity, SUB)
@@ -199,12 +191,62 @@
             for g in range(per_half):
                 block = product[g * SUB : (g + 1) * SUB]
                 late = jnp.concatenate([block[:, LANES:], jnp.zeros((SUB, LANES - SUB), F32)], 1)
-                circ = jnp.where(mask, block[:, :LANES], late)
-                tap_grad[pl.ds((2 * pair + parity) * per_half + g, 1), :] = diagonal_sums(circ)
-
-
-def step_kernel(role, parts, steer_second, filter_second, steer_out, filter_out):
-    total = jnp.sum(parts[...], 0)
+                blocks.append(jnp.where(mask, block[:, :LANES], late))
+        tap_grad[pl.ds(8 * pair, 8), :] = diagonal_sums(blocks)
+
+
+def halves_of(bit, zero, one):
+    mine = bit > 0
+    return jnp.where(mine, zero, one), jnp.where(mine, one, zero)
+
+
+def pack_kernel(owners, bits, *refs):
+    count = (len(refs) - 2) // 2
+    taps, steers, (give, keep) = refs[:count], refs[count : 2 * count], refs[2 * count :]
+    groups = sum(ref.shape[0] for ref in taps) // owners
+    channels = sum(ref.shape[1] for ref in steers) // owners
+
+    def part(parts, axis, owner, size):
+        at = owner * size
+        for ref in parts:
+            if at < ref.shape[axis]:
+                return ref[at : at + size, :] if axis == 0 else ref[:, at : at + size]
+            at -= ref.shape[axis]
+
+    def packed(owner):
+        steer = part(steers, 1, owner, channels)
+        lines = [steer[:, at : at + LANES] for at in range(0, channels, LANES)]
+        short = LANES - lines[-1].shape[1]
+        if short > 0:
+            lines[-1] = jnp.concatenate([lines[-1], jnp.zeros((1, short), F32)], 1)
+        return [part(taps, 0, owner, groups)] + lines
+
+    order = reversed_bits(owners)
+    for i, (low, high) in enumerate(zip(order[: owners // 2], order[owners // 2 :])):
+        at = 0
+        for zero, one in zip(packed(low), packed(high)):
+            lines = zero.shape[0]
+            give[i, pl.ds(at, lines), :], keep[i, pl.ds(at, lines), :] = halves_of(bits[0], zero, one)
+            at += lines
+
+
+def reversed_bits(count):
+    order = [0]
+    while len(order) < count:
+        order = [2 * i for i in order] + [2 * i + 1 for i in order]
+    return order
+
+
+def fold_kernel(step, bits, kept, arrived, give, keep):
+    count = give.shape[0]
+    for i in range(count):
+        zero = kept[i] + arrived[i]
+        one = kept[count + i] + arrived[count + i]
+        give[i], keep[i] = halves_of(bits[step], zero, one)
+
+
+def step_kernel(role, kept, arrived, steer_second, filter_second, steer_out, filter_out):
+    total = kept[0] + arrived[0]
     groups = filter_second.shape[0]
     tap_grad = total[:groups]
     lane = lane_of(tap_grad.shape)
@@ -266,31 +308,19 @@
     def bf16(width_of):
         return jax.ShapeDtypeStruct((rows, width_of), BF16)
 
-    def weigh(incoming, first, last):
+    def weigh(incoming, first, last, offset, after):
         return call(
-            weigh_kernel, ((last - first) // block,), [SMEM, spec(rows, block, first // block), spec(rows, block)],
-            spec(rows, block), bf16(last - first), name="weigh",
-        )(role, in_gate, incoming)
-
-    def first_weigh(starts, ends):
-        pieces = [
-            (at, at + block, part, at - first)
-            for part, (first, last) in enumerate(zip(starts, ends))
-            for at in range(first, last, block)
-        ]
-        whole = pltpu.VMEM((rows, channels), BF16)
-        return pl.pallas_call(
-            functools.partial(first_weigh_kernel, pieces),
-            in_specs=[SMEM] + [pl.BlockSpec(memory_space=pltpu.HBM)] * 2,
-            out_specs=[pl.BlockSpec(memory_space=pltpu.VMEM)] * len(starts),
-            out_shape=[bf16(last - first) for first, last in zip(starts, ends)],
-            scratch_shapes=[whole, whole, pltpu.SemaphoreType.DMA((2, len(pieces)))],
-            compiler_params=pltpu.CompilerParams(vmem_limit_bytes=FIRST_VMEM),
-            name="first_weigh",
-        )(role, in_gate, cotangent)
-
-    mid_halo = lax.ppermute(mid_gate, ("section", "seq"), ahead)
-    inputs_halo = lax.ppermute(layer_inputs, ("section", "seq"), ahead)
+            weigh_kernel,
+            ((last - first) // block,),
+            [SMEM, spec(rows, block, first // block), spec(rows, block, (first - offset) // block),
+             spec(rows, block, first // block)],
+            [spec(rows, block)] * 3,
+            [bf16(last - first)] * 3,
+            name="weigh",
+            after=after,
+        )(role, *[pltpu.with_memory_space_constraint(array, pltpu.HBM) for array in (in_gate, incoming, mid_gate)],
+          *after)
+
     taps = call(
         taps_kernel,
         (1,),
@@ -305,28 +335,32 @@
     for hop in range(sections - 1):
         split = [channels * eighths // 8 for eighths in HALO_EDGES] if hop == 0 else edges
         starts, ends = split[:-1], split[1:]
+        weighed = []
+        for first, last in zip(starts, ends):
+            array, offset = next(entry for entry, edge in zip(incoming, edges) if edge == first)
+            weighed.append(weigh(array, first, last, offset, tuple(weighed[-1][:1] if weighed else ())))
+        owns, incomings, mids = zip(*weighed)
         if hop == 0:
-            owns = first_weigh(starts, ends)
-        else:
-            owns = [weigh(array, first, last) for (array, _), first, last in zip(incoming, starts, ends)]
+            mid_late, inputs_late, _ = lax.optimization_barrier((mid_gate, layer_inputs, owns[0]))
+            mid_halo = lax.ppermute(mid_late, ("section", "seq"), ahead)
+            inputs_halo = lax.ppermute(inputs_late, ("section", "seq"), ahead)
         halos = [lax.ppermute(own, ("section", "seq"), behind) for own in owns]
         sources, outgoing, received = [], [], []
         for k, (first, last) in enumerate(bounds):
             part = max(i for i, start in enumerate(starts) if start <= first)
             at = (first - starts[part]) // block
-            array, offset = incoming[k]
             before = tuple(outgoing[-1:])
             out = call(
                 functools.partial(filter_kernel, group_size),
                 ((last - first) // block,),
                 [SMEM, spec(rows, block, at), spec(rows, block, at), group_spec(first // block),
-                 spec(rows, block, first // block), spec(rows, block, (first - offset) // block)],
+                 spec(rows, block, at), spec(rows, block, at)],
                 spec(rows, block),
                 bf16(last - first),
                 name="filter",
                 cycles=1000,
                 after=before,
-            )(role, owns[part], halos[part], taps, mid_gate, array, *before)
+            )(role, owns[part], halos[part], taps, mids[part], incomings[part], *before)
             sources.append((owns[part], halos[part], at))
             outgoing.append(out)
             received.append(lax.ppermute(out, "section", down))
@@ -368,28 +402,43 @@
           received[k], filtered, *after))
     tap_grads, steer_grads = zip(*grads)
 
-    inner = max(d for d in range(1, seqs + 1) if seqs % d == 0 and d * d <= seqs)
-    outer = seqs // inner
     own_channels = channels // seqs
-    steer_rows = pl.cdiv(own_channels, LANES)
-    tap_all = jnp.concatenate(tap_grads, 0).reshape(seqs, groups // seqs, filt_len)
-    steer_all = jnp.concatenate(steer_grads, 1).reshape(seqs, own_channels)
-    steer_all = jnp.pad(steer_all, ((0, 0), (0, steer_rows * LANES - own_channels)))
-    packed = jnp.concatenate([tap_all, steer_all.reshape(seqs, steer_rows, LANES)], 1)
-    packed = packed.reshape((outer, inner) + packed.shape[1:]).swapaxes(0, 1)
-    near_by = [[o * inner + i for i in range(inner)] for o in range(outer)]
-    far_off = [[o * inner + i for o in range(outer)] for i in range(inner)]
-    parts = jnp.sum(lax.all_to_all(packed, "seq", 0, 0, axis_index_groups=near_by), 0)
-    parts = lax.all_to_all(parts, "seq", 0, 0, axis_index_groups=far_off)
+    lines = groups // seqs + pl.cdiv(own_channels, LANES)
+    place = lax.axis_index("seq")
+    steps = seqs.bit_length() - 1
+    bits = jnp.stack([(place >> step) & 1 for step in range(steps)]).astype(jnp.int32)
+
+    def halves(count):
+        return [jax.ShapeDtypeStruct((count, lines, LANES), F32)] * 2
+
+    vmem = pl.BlockSpec(memory_space=pltpu.VMEM)
+    give, keep = pl.pallas_call(
+        functools.partial(pack_kernel, seqs),
+        in_specs=[SMEM] + [vmem] * (2 * len(grads)),
+        out_specs=[vmem] * 2,
+        out_shape=halves(seqs // 2),
+        name="pack",
+    )(bits, *tap_grads, *steer_grads)
+    for step in range(steps):
+        route = [(i, i ^ (1 << step)) for i in range(seqs)]
+        arrived = lax.ppermute(give, "seq", route)
+        if step < steps - 1:
+            give, keep = pl.pallas_call(
+                functools.partial(fold_kernel, step + 1),
+                in_specs=[SMEM, vmem, vmem],
+                out_specs=[vmem] * 2,
+                out_shape=halves(keep.shape[0] // 2),
+                name="fold",
+            )(bits, keep, arrived)
     steer_step, filter_step = pl.pallas_call(
         step_kernel,
-        in_specs=[SMEM] + [pl.BlockSpec(memory_space=pltpu.VMEM)] * 3,
+        in_specs=[SMEM] + [vmem] * 4,
         out_shape=[
             jax.ShapeDtypeStruct((1, own_channels), F32),
             jax.ShapeDtypeStruct((groups // seqs, filt_len), F32),
         ],
         name="step",
-    )(role, parts, steer_second, filter_second[0].T)
+    )(role, keep, arrived, steer_second, filter_second[0].T)
     return steer_step, filter_step.T[None]
 
 

time: 69.9 us -> 75.7 us (1.083)
  blocking collectives: 28.6 us -> 0 us
  Pallas kernels: 18.5 us -> 35.6 us
  waiting for transfers between devices: 3.93 us -> 11 us
  starting transfers between devices: 14.8 us -> 21.8 us
  local copies, waits for them, and re-layouts: 2.39 us -> 4.9 us
    all_to_all x2 -> x0, blocking collectives: 28.6 us -> none  [the longest x1 17.1 us: body(): lax.all_to_all(packed, 'seq', 0, 0, axis_index_groups=near_by)]
    pallas_call x2 -> x8, Pallas kernels: 2.64 us -> 13.2 us  [the longest x3 5.76 us: weigh(): call(weigh_kernel, ((last - first) // block,), [SMEM, spec(rows, block, f...]
    ppermute x2 -> x6, waiting for transfers between devices: 0.01 us -> 7.94 us  [the longest x4 7.93 us: body(): arrived = lax.ppermute(give, 'seq', route)]
    ppermute x2 -> x6, starting transfers between devices: 8.02 us -> 14.5 us  [the longest x4 7.53 us: body(): arrived = lax.ppermute(give, 'seq', route)]
    pallas_call x4, Pallas kernels: 0.79 us -> 4.41 us  [body(): call(functools.partial(filter_kernel, group_size), ((last - first) // blo...]
    unnamed x16 -> x50, local copies, waits for them, and re-layouts: 2.29 us -> 4.9 us
    pallas_call x1, Pallas kernels: 4.09 us -> 6.18 us  [body(): call(functools.partial(turned_filter_kernel, group_size), (channels // bl...]
    ppermute x4, waiting for transfers between devices: 3.92 us -> 3.03 us  [body(): received.append(lax.ppermute(out, 'section', down))]
  transfers between devices with their start and end apart: 8 -> 13, of which waited for: 2 -> 5; matrix products, arithmetic and copies ran while one was open for 0% -> 1% of each run, Pallas kernels for 21% -> 32%
where the time goes in v3:
time: 75.7 us; the launch traced here: 74.8 us
  Pallas kernels  35.6 us (47%)
  starting transfers between devices  21.8 us (29%)
  waiting for transfers between devices  11 us (15%)
  local copies, waits for them, and re-layouts  4.9 us (6%)
  between operations  0.97 us (1%)
    pallas_call x4, Pallas kernels, body(): call(functools.partial(grad_kernel, group_size), (width // block,), [SMEM...  11.6 us
    ppermute x4, waiting for transfers between devices, body(): arrived = lax.ppermute(give, 'seq', route)  7.93 us
    ppermute x4, starting transfers between devices, body(): arrived = lax.ppermute(give, 'seq', route)  7.53 us
    pallas_call x1, Pallas kernels, body(): call(functools.partial(turned_filter_kernel, group_size), (channels // bl...  6.18 us
    pallas_call x3, Pallas kernels, weigh(): call(weigh_kernel, ((last - first) // block,), [SMEM, spec(rows, block, f...  5.76 us
    ppermute x4, starting transfers between devices, body(): received.append(lax.ppermute(out, 'section', down))  5.12 us
    unnamed x50, local copies, waits for them, and re-layouts  4.9 us
    ppermute x1, starting transfers between devices, body(): inputs_halo = lax.ppermute(inputs_late, ('section', 'seq'), ahead)  4.54 us
  transfers between devices with their start and end apart: 13, of which 5 were waited for; matrix products, arithmetic and copies ran while one was open for 1% of the time, Pallas kernels for 32%

profile of v3, /device:TPU:0, one launch (start us, length us, event | category | flops | bytes accessed | tf_op | source)
XLA Modules:
  0.0 74.8 jit_solution(3498066296147026133)
XLA Ops:
  0.6 0.0 copy-start.1
  0.6 2.3 %weigh.3 = (bf16[128,1536]{1,0:T(8,128)(2,1)S(1)}, bf16[128,1536]{1,0:T(8,128)(2,1)S(1)}, bf16[128,1536]{1,0:T(8,128)(2,1)S(1)}) custom-call(s32[1]{0:T(128)} %bitcast.refs_0_.role, bf16[128,4096]{1,0:T(8,128)(2,1)} %bitcast.15, bf16[128,4096]{1,0:T(8,128)(2,1)} %refs_2_.5, bf16[128,4096]{1,0:T(8,128)(2,1)} %bitcast.6.refs_3_.refs_1_.refs_2_), custom_call_target="tpu_custom_call" | custom-call | flops 100 | tf_op jit(solution)/shard_map/weigh/pallas_call | solution.py:312
  2.9 0.0 copy-start.4
  2.9 2.4 %collective-permute-start = (bf16[128,4096]{1,0:T(8,128)(2,1)}, bf16[128,4096]{1,0:T(8,128)(2,1)S(1)}, u32[]{:S(2)}, u32[]{:S(2)}) collective-permute-start(bf16[128,4096]{1,0:T(8,128)(2,1)} %bitcast.6.refs_3_.refs_1_.refs_2_), channel_id=1, source_target_pairs={{0,1},{1,2},{2,3},{3,4},{4,5},{5,6},{6,7},{7,8},{8,9},{9,10},{10,1... | collective-permute-start | bytes 3145736 | tf_op jit(solution)/shard_map/ppermute | solution.py:345
  5.4 0.0 copy-done.1
  5.4 4.5 %collective-permute-start.1 = (bf16[128,4096]{1,0:T(8,128)(2,1)S(1)}, bf16[128,4096]{1,0:T(8,128)(2,1)S(1)}, u32[]{:S(2)}, u32[]{:S(2)}) collective-permute-start(bf16[128,4096]{1,0:T(8,128)(2,1)S(1)} %bitcast.22), channel_id=1, source_target_pairs={{0,1},{1,2},{2,3},{3,4},{4,5},{5,6},{6,7},{7,8},{8,9},{9,10},{10,1... | collective-permute-start | bytes 3145736 | tf_op jit(solution)/shard_map/ppermute | solution.py:346
  9.9 0.7 collective-permute-start.2
  10.6 2.2 %weigh.4 = (bf16[128,1536]{1,0:T(8,128)(2,1)S(1)}, bf16[128,1536]{1,0:T(8,128)(2,1)S(1)}, bf16[128,1536]{1,0:T(8,128)(2,1)S(1)}) custom-call(s32[1]{0:T(128)} %bitcast.refs_0_.role, bf16[128,4096]{1,0:T(8,128)(2,1)} %bitcast.16, bf16[128,4096]{1,0:T(8,128)(2,1)} %refs_2_.5, bf16[128,4096]{1,0:T(8,128)(2,1)} %bitcast.6.refs_3_.refs_1_.refs_2_, ...), custom_call_target="tpu_custom_call" | custom-call | flops 100 | tf_op jit(solution)/shard_map/weigh/pallas_call | solution.py:312
  12.8 0.0 copy-start.6
  12.8 0.0 copy-start.15
  12.8 0.8 %collective-permute-start.5 = (bf16[128,1536]{1,0:T(8,128)(2,1)S(1)}, bf16[128,1536]{1,0:T(8,128)(2,1)S(1)}, u32[]{:S(2)}, u32[]{:S(2)}) collective-permute-start(bf16[128,1536]{1,0:T(8,128)(2,1)S(1)} %get-tuple-element.36.refs_4_.refs_1_.refs_6_), channel_id=1, source_target_pairs={{17,16},{18,17},{19,18},{20,19},{21,20},{22,21},{23,22},{24,23},{2... | collective-permute-start | bytes 1179656 | tf_op jit(solution)/shard_map/ppermute | solution.py:347
  13.7 1.3 %weigh.5 = (bf16[128,1024]{1,0:T(8,128)(2,1)S(1)}, bf16[128,1024]{1,0:T(8,128)(2,1)S(1)}, bf16[128,1024]{1,0:T(8,128)(2,1)S(1)}) custom-call(s32[1]{0:T(128)} %bitcast.refs_0_.role, bf16[128,4096]{1,0:T(8,128)(2,1)} %bitcast.17, bf16[128,4096]{1,0:T(8,128)(2,1)} %refs_2_.5, bf16[128,4096]{1,0:T(8,128)(2,1)} %bitcast.6.refs_3_.refs_1_.refs_2_, ...), custom_call_target="tpu_custom_call" | custom-call | flops 100 | tf_op jit(solution)/shard_map/weigh/pallas_call | solution.py:312
  15.0 0.7 collective-permute-start.4
  15.7 0.0 copy-done.15
  15.7 0.2 taps.1.refs_3_
  15.8 0.0 collective-permute-done.2.refs_2_.refs_7_
  15.9 1.5 %filter.4.refs_6_.refs_8_ = bf16[128,1536]{1,0:T(8,128)(2,1)} custom-call(s32[1]{0:T(128)} %bitcast.refs_0_.role, bf16[128,1536]{1,0:T(8,128)(2,1)S(1)} %get-tuple-element.31.refs_1_.refs_4_.refs_6_, bf16[128,1536]{1,0:T(8,128)(2,1)S(1)} %collective-permute-done.2.refs_2_.refs_7_, f32[256,128]{1,0:T(8,128)S(1)} %taps.1.refs_3_, ...), custom_call_target="tpu_custom_call" | custom-call | flops 1000 | tf_op jit(solution)/shard_map/filter/pallas_call | solution.py:353
  17.4 1.3 %collective-permute-start.3 = (bf16[128,1536]{1,0:T(8,128)(2,1)}, bf16[128,1536]{1,0:T(8,128)(2,1)}, u32[]{:S(2)}, u32[]{:S(2)}) collective-permute-start(bf16[128,1536]{1,0:T(8,128)(2,1)} %filter.4.refs_6_.refs_8_), channel_id=1, source_target_pairs={{16,0},{17,1},{18,2},{19,3},{20,4},{21,5},{22,6},{23,7},{24,8},{25... | collective-permute-start | bytes 1179656 | tf_op jit(solution)/shard_map/ppermute | solution.py:366
  18.7 0.0 collective-permute-done.5.refs_2_.refs_7_
  18.7 1.5 %filter.5.refs_6_.refs_8_ = bf16[128,1536]{1,0:T(8,128)(2,1)} custom-call(s32[1]{0:T(128)} %bitcast.refs_0_.role, bf16[128,1536]{1,0:T(8,128)(2,1)S(1)} %get-tuple-element.36.refs_4_.refs_1_.refs_6_, bf16[128,1536]{1,0:T(8,128)(2,1)S(1)} %collective-permute-done.5.refs_2_.refs_7_, f32[256,128]{1,0:T(8,128)S(1)} %taps.1.refs_3_, ...), custom_call_target="tpu_custom_call" | custom-call | flops 1000 | tf_op jit(solution)/shard_map/filter/pallas_call | solution.py:353
  20.2 0.0 copy-done.8
  20.2 1.3 %collective-permute-start.6 = (bf16[128,1536]{1,0:T(8,128)(2,1)}, bf16[128,1536]{1,0:T(8,128)(2,1)}, u32[]{:S(2)}, u32[]{:S(2)}) collective-permute-start(bf16[128,1536]{1,0:T(8,128)(2,1)} %filter.5.refs_6_.refs_8_), channel_id=1, source_target_pairs={{16,0},{17,1},{18,2},{19,3},{20,4},{21,5},{22,6},{23,7},{24,8},{25... | collective-permute-start | bytes 1179656 | tf_op jit(solution)/shard_map/ppermute | solution.py:366
  21.5 0.0 collective-permute-done.4.refs_2_.refs_7_
  21.5 0.0 copy-start.2
  21.5 0.7 filter.6.refs_6_.refs_8_
  22.2 1.3 %collective-permute-start.7 = (bf16[128,512]{1,0:T(8,128)(2,1)}, bf16[128,512]{1,0:T(8,128)(2,1)}, u32[]{:S(2)}, u32[]{:S(2)}) collective-permute-start(bf16[128,512]{1,0:T(8,128)(2,1)} %filter.6.refs_6_.refs_8_), channel_id=1, source_target_pairs={{16,0},{17,1},{18,2},{19,3},{20,4},{21,5},{22,6},{23,7},{24,8},{25... | collective-permute-start | bytes 393224 | tf_op jit(solution)/shard_map/ppermute | solution.py:366
  23.5 0.7 filter.7.refs_4_.refs_8_
  24.2 0.0 collective-permute-done.refs_2_.refs_4_
  24.2 0.0 copy-done.2
  24.2 1.3 %collective-permute-start.8 = (bf16[128,512]{1,0:T(8,128)(2,1)}, bf16[128,512]{1,0:T(8,128)(2,1)}, u32[]{:S(2)}, u32[]{:S(2)}) collective-permute-start(bf16[128,512]{1,0:T(8,128)(2,1)} %filter.7.refs_4_.refs_8_), channel_id=1, source_target_pairs={{16,0},{17,1},{18,2},{19,3},{20,4},{21,5},{22,6},{23,7},{24,8},{25... | collective-permute-start | bytes 393224 | tf_op jit(solution)/shard_map/ppermute | solution.py:366
  25.5 0.6 pad_add_fusion.bits
  26.1 6.2 %turned_filter.1.refs_10_ = f32[128,4096]{1,0:T(8,128)S(1)} custom-call(s32[1]{0:T(128)} %bitcast.refs_0_.role, bf16[128,4096]{1,0:T(8,128)(2,1)} %bitcast.6.refs_3_.refs_1_.refs_2_, bf16[128,4096]{1,0:T(8,128)(2,1)S(1)} %collective-permute-done.refs_2_.refs_4_, f32[256,128]{1,0:T(8,128)S(1)} %taps.1.refs_3_, bf16[128,512]{1,0:T(8,128)(2,1)} %filter.7.refs_4_.refs_8_), custom_call_target="tpu_custom_call" | custom-call | flops 4000 | tf_op jit(solution)/shard_map/turned_filter/pallas_call | solution.py:373
  32.3 0.0 collective-permute-done.3.refs_9_
  32.3 0.0 collective-permute-done.1.refs_5_
  32.4 3.9 %grads.4 = (f32[96,128]{1,0:T(8,128)S(1)}, f32[1,1536]{1,0:T(1,128)S(1)}) custom-call(s32[1]{0:T(128)} %bitcast.refs_0_.role, bf16[128,4096]{1,0:T(8,128)(2,1)S(1)} %bitcast.18, bf16[128,4096]{1,0:T(8,128)(2,1)} %bitcast.6.refs_3_.refs_1_.refs_2_, bf16[128,4096]{1,0:T(8,128)(2,1)S(1)} %bitcast.23, ...), custom_call_target="tpu_custom_call" | custom-call | flops 2000 | tf_op jit(solution)/shard_map/grads/pallas_call | solution.py:390
  36.3 0.6 copy-done.17
  36.9 3.0 %collective-permute-done.6.refs_9_ = bf16[128,1536]{1,0:T(8,128)(2,1)} collective-permute-done((bf16[128,1536]{1,0:T(8,128)(2,1)}, bf16[128,1536]{1,0:T(8,128)(2,1)}, u32[]{:S(2)}, u32[]{:S(2)}) %collective-permute-start.6) | collective-permute-done | bytes 393248 | tf_op jit(solution)/shard_map/ppermute | solution.py:366
  39.9 0.0 copy-done.11
  39.9 3.9 %grads.5 = (f32[96,128]{1,0:T(8,128)S(1)}, f32[1,1536]{1,0:T(1,128)S(1)}) custom-call(s32[1]{0:T(128)} %bitcast.refs_0_.role, bf16[128,4096]{1,0:T(8,128)(2,1)S(1)} %bitcast.19, bf16[128,4096]{1,0:T(8,128)(2,1)} %bitcast.6.refs_3_.refs_1_.refs_2_, bf16[128,4096]{1,0:T(8,128)(2,1)S(1)} %bitcast.24, ...), custom_call_target="tpu_custom_call" | custom-call | flops 2000 | tf_op jit(solution)/shard_map/grads/pallas_call | solution.py:390
  43.8 0.6 copy-done.18
  44.4 0.0 collective-permute-done.7.refs_9_
  44.4 1.9 %grads.6 = (f32[32,128]{1,0:T(8,128)S(1)}, f32[1,512]{1,0:T(1,128)S(1)}) custom-call(s32[1]{0:T(128)} %bitcast.refs_0_.role, bf16[128,4096]{1,0:T(8,128)(2,1)S(1)} %bitcast.20, bf16[128,4096]{1,0:T(8,128)(2,1)} %bitcast.6.refs_3_.refs_1_.refs_2_, bf16[128,4096]{1,0:T(8,128)(2,1)S(1)} %bitcast.25, bf16[128,4096]{1,0:T(8,128)(2,1)S(1)} %collective-permute-done.refs_2_.refs_4_, ...), custom_call_target="tpu_custom_call" | custom-call | flops 2000 | tf_op jit(solution)/shard_map/grads/pallas_call | solution.py:390
  46.3 0.0 copy-done.13
  46.3 0.0 collective-permute-done.8.refs_9_
  46.3 1.9 %grads.7 = (f32[32,128]{1,0:T(8,128)S(1)}, f32[1,512]{1,0:T(1,128)S(1)}) custom-call(s32[1]{0:T(128)} %bitcast.refs_0_.role, bf16[128,4096]{1,0:T(8,128)(2,1)S(1)} %bitcast.21, bf16[128,4096]{1,0:T(8,128)(2,1)} %bitcast.6.refs_3_.refs_1_.refs_2_, bf16[128,4096]{1,0:T(8,128)(2,1)S(1)} %bitcast.26, bf16[128,4096]{1,0:T(8,128)(2,1)S(1)} %collective-permute-done.refs_2_.refs_4_, ...), custom_call_target="tpu_custom_call" | custom-call | flops 2000 | tf_op jit(solution)/shard_map/grads/pallas_call | solution.py:390
  48.2 0.6 copy-done.16
  48.8 0.6 copy-done.20
  49.4 1.6 %pack.1 = (f32[8,18,128]{2,1,0:T(8,128)}, f32[8,18,128]{2,1,0:T(8,128)}) custom-call(s32[4]{0:T(128)} %pad_add_fusion.bits, f32[96,128]{1,0:T(8,128)} %copy-done.12, f32[96,128]{1,0:T(8,128)} %copy-done.13, f32[32,128]{1,0:T(8,128)} %copy-done.14, f32[32,128]{1,0:T(8,128)} %copy-done.16, f32[1,1536]{1,0:T(1,128)} %copy-done.17, f32[1,1536]{1,0:T(1,128)} %copy-done.18, ...), custom_call_target="tpu_custom_call" | custom-call | tf_op jit(solution)/shard_map/pack/pallas_call | solution.py:415
  51.0 0.0 collective-permute-start.9
  51.0 1.5 %collective-permute-done.9.arrived = f32[8,18,128]{2,1,0:T(8,128)S(1)} collective-permute-done((f32[8,18,128]{2,1,0:T(8,128)}, f32[8,18,128]{2,1,0:T(8,128)S(1)}, u32[]{:S(2)}, u32[]{:S(2)}) %collective-permute-start.9) | collective-permute-done | bytes 73760 | tf_op jit(solution)/shard_map/ppermute | solution.py:424
  52.5 0.6 copy-done.21
  53.2 1.6 %fold.3 = (f32[4,18,128]{2,1,0:T(8,128)}, f32[4,18,128]{2,1,0:T(8,128)}) custom-call(s32[4]{0:T(128)} %pad_add_fusion.bits, f32[8,18,128]{2,1,0:T(8,128)} %get-tuple-element.50.kept, f32[8,18,128]{2,1,0:T(8,128)} %copy-done.21), custom_call_target="tpu_custom_call" | custom-call | tf_op jit(solution)/shard_map/fold/pallas_call | solution.py:426
  54.8 1.8 %collective-permute-start.10 = (f32[4,18,128]{2,1,0:T(8,128)}, f32[4,18,128]{2,1,0:T(8,128)S(1)}, u32[]{:S(2)}, u32[]{:S(2)}) collective-permute-start(f32[4,18,128]{2,1,0:T(8,128)} %get-tuple-element.53), channel_id=1, source_target_pairs={{0,2},{1,3},{2,0},{3,1},{4,6},{5,7},{6,4},{7,5},{8,10},{9,11},{10,... | collective-permute-start | bytes 110600 | tf_op jit(solution)/shard_map/ppermute | solution.py:424
  56.5 2.5 %collective-permute-done.10.arrived = f32[4,18,128]{2,1,0:T(8,128)S(1)} collective-permute-done((f32[4,18,128]{2,1,0:T(8,128)}, f32[4,18,128]{2,1,0:T(8,128)S(1)}, u32[]{:S(2)}, u32[]{:S(2)}) %collective-permute-start.10) | collective-permute-done | bytes 36896 | tf_op jit(solution)/shard_map/ppermute | solution.py:424
  59.1 0.6 copy-done.22
  59.7 1.5 %fold.4 = (f32[2,18,128]{2,1,0:T(8,128)}, f32[2,18,128]{2,1,0:T(8,128)}) custom-call(s32[4]{0:T(128)} %pad_add_fusion.bits, f32[4,18,128]{2,1,0:T(8,128)} %get-tuple-element.52.kept, f32[4,18,128]{2,1,0:T(8,128)} %copy-done.22), custom_call_target="tpu_custom_call" | custom-call | tf_op jit(solution)/shard_map/fold/pallas_call | solution.py:426
  61.1 2.7 %collective-permute-start.11 = (f32[2,18,128]{2,1,0:T(8,128)}, f32[2,18,128]{2,1,0:T(8,128)S(1)}, u32[]{:S(2)}, u32[]{:S(2)}) collective-permute-start(f32[2,18,128]{2,1,0:T(8,128)} %get-tuple-element.55), channel_id=1, source_target_pairs={{0,4},{1,5},{2,6},{3,7},{4,0},{5,1},{6,2},{7,3},{8,12},{9,13},{10,... | collective-permute-start | bytes 55304 | tf_op jit(solution)/shard_map/ppermute | solution.py:424
  63.9 2.0 %collective-permute-done.11.arrived = f32[2,18,128]{2,1,0:T(8,128)S(1)} collective-permute-done((f32[2,18,128]{2,1,0:T(8,128)}, f32[2,18,128]{2,1,0:T(8,128)S(1)}, u32[]{:S(2)}, u32[]{:S(2)}) %collective-permute-start.11) | collective-permute-done | bytes 18464 | tf_op jit(solution)/shard_map/ppermute | solution.py:424
  65.9 0.6 copy-done.23
  66.5 1.4 %fold.5 = (f32[1,18,128]{2,1,0:T(8,128)}, f32[1,18,128]{2,1,0:T(8,128)}) custom-call(s32[4]{0:T(128)} %pad_add_fusion.bits, f32[2,18,128]{2,1,0:T(8,128)} %get-tuple-element.54.kept, f32[2,18,128]{2,1,0:T(8,128)} %copy-done.23), custom_call_target="tpu_custom_call" | custom-call | tf_op jit(solution)/shard_map/fold/pallas_call | solution.py:426
  67.8 3.0 %collective-permute-start.12 = (f32[1,18,128]{2,1,0:T(8,128)}, f32[1,18,128]{2,1,0:T(8,128)S(1)}, u32[]{:S(2)}, u32[]{:S(2)}) collective-permute-start(f32[1,18,128]{2,1,0:T(8,128)} %get-tuple-element.57), channel_id=1, source_target_pairs={{0,8},{1,9},{2,10},{3,11},{4,12},{5,13},{6,14},{7,15},{8,0},{9,1},... | collective-permute-start | bytes 27656 | tf_op jit(solution)/shard_map/ppermute | solution.py:424
  70.9 1.9 %collective-permute-done.12.arrived = f32[1,18,128]{2,1,0:T(8,128)S(1)} collective-permute-done((f32[1,18,128]{2,1,0:T(8,128)}, f32[1,18,128]{2,1,0:T(8,128)S(1)}, u32[]{:S(2)}, u32[]{:S(2)}) %collective-permute-start.12) | collective-permute-done | bytes 9248 | tf_op jit(solution)/shard_map/ppermute | solution.py:424
  72.8 0.6 copy-done.24
  73.4 1.4 %step.1 = (f32[1,256]{1,0:T(1,128)}, f32[16,128]{1,0:T(8,128)}) custom-call(s32[1]{0:T(128)} %bitcast.refs_0_.role, f32[1,18,128]{2,1,0:T(8,128)} %get-tuple-element.56.kept, f32[1,18,128]{2,1,0:T(8,128)} %copy-done.24, f32[1,256]{1,0:T(1,128)} %steer_second.1, f32[16,128]{1,0:T(8,128)} %bitcast.28), custom_call_target="tpu_custom_call" | custom-call | tf_op jit(solution)/shard_map/step/pallas_call | solution.py:433
  (31 shorter events, 0.1 us)
Async XLA Ops:
  0.6 4.7 %copy-start.1 = (bf16[1,128,4096]{2,1,0:T(8,128)(2,1)S(1)}, bf16[1,128,4096]{2,1,0:T(8,128)(2,1)}, u32[]{:S(2)}) copy-start(bf16[1,128,4096]{2,1,0:T(8,128)(2,1)} %param.10) | copy-start | bytes 3145732
  2.9 13.0 %copy-start.4 = (bf16[128,1536]{1,0:T(8,128)(2,1)}, bf16[128,1536]{1,0:T(8,128)(2,1)S(1)}, u32[]{:S(2)}) copy-start(bf16[128,1536]{1,0:T(8,128)(2,1)S(1)} %get-tuple-element.31.refs_1_.refs_4_.refs_6_) | copy-start | bytes 1179652
  2.9 21.3 %collective-permute-start = (bf16[128,4096]{1,0:T(8,128)(2,1)}, bf16[128,4096]{1,0:T(8,128)(2,1)S(1)}, u32[]{:S(2)}, u32[]{:S(2)}) collective-permute-start(bf16[128,4096]{1,0:T(8,128)(2,1)} %bitcast.6.refs_3_.refs_1_.refs_2_), channel_id=1, source_target_pairs={{0,1},{1,2},{2,3},{3,4},{4,5},{5,6},{6,7},{7,8},{8,9},{9,10},{10,1... | collective-permute-start | bytes 3145736 | tf_op jit(solution)/shard_map/ppermute | solution.py:345
  5.4 27.0 %collective-permute-start.1 = (bf16[128,4096]{1,0:T(8,128)(2,1)S(1)}, bf16[128,4096]{1,0:T(8,128)(2,1)S(1)}, u32[]{:S(2)}, u32[]{:S(2)}) collective-permute-start(bf16[128,4096]{1,0:T(8,128)(2,1)S(1)} %bitcast.22), channel_id=1, source_target_pairs={{0,1},{1,2},{2,3},{3,4},{4,5},{5,6},{6,7},{7,8},{8,9},{9,10},{10,1... | collective-permute-start | bytes 3145736 | tf_op jit(solution)/shard_map/ppermute | solution.py:346
  9.9 5.9 %collective-permute-start.2 = (bf16[128,1536]{1,0:T(8,128)(2,1)S(1)}, bf16[128,1536]{1,0:T(8,128)(2,1)S(1)}, u32[]{:S(2)}, u32[]{:S(2)}) collective-permute-start(bf16[128,1536]{1,0:T(8,128)(2,1)S(1)} %get-tuple-element.31.refs_1_.refs_4_.refs_6_), channel_id=1, source_target_pairs={{17,16},{18,17},{19,18},{20,19},{21,20},{22,21},{23,22},{24,23},{2... | collective-permute-start | bytes 1179656 | tf_op jit(solution)/shard_map/ppermute | solution.py:347
  12.8 5.9 %copy-start.6 = (bf16[128,1536]{1,0:T(8,128)(2,1)}, bf16[128,1536]{1,0:T(8,128)(2,1)S(1)}, u32[]{:S(2)}) copy-start(bf16[128,1536]{1,0:T(8,128)(2,1)S(1)} %get-tuple-element.36.refs_4_.refs_1_.refs_6_) | copy-start | bytes 1179652
  12.8 2.8 %copy-start.15 = (bf16[1,128,256]{2,1,0:T(8,128)(2,1)S(1)}, bf16[1,128,256]{2,1,0:T(8,128)(2,1)}, u32[]{:S(2)}) copy-start(bf16[1,128,256]{2,1,0:T(8,128)(2,1)} %param.11) | copy-start | bytes 196612
  12.8 5.8 %collective-permute-start.5 = (bf16[128,1536]{1,0:T(8,128)(2,1)S(1)}, bf16[128,1536]{1,0:T(8,128)(2,1)S(1)}, u32[]{:S(2)}, u32[]{:S(2)}) collective-permute-start(bf16[128,1536]{1,0:T(8,128)(2,1)S(1)} %get-tuple-element.36.refs_4_.refs_1_.refs_6_), channel_id=1, source_target_pairs={{17,16},{18,17},{19,18},{20,19},{21,20},{22,21},{23,22},{24,23},{2... | collective-permute-start | bytes 1179656 | tf_op jit(solution)/shard_map/ppermute | solution.py:347
  15.0 6.5 %collective-permute-start.4 = (bf16[128,1024]{1,0:T(8,128)(2,1)S(1)}, bf16[128,1024]{1,0:T(8,128)(2,1)S(1)}, u32[]{:S(2)}, u32[]{:S(2)}) collective-permute-start(bf16[128,1024]{1,0:T(8,128)(2,1)S(1)} %get-tuple-element.37.refs_1_.refs_6_), channel_id=1, source_target_pairs={{17,16},{18,17},{19,18},{20,19},{21,20},{22,21},{23,22},{24,23},{2... | collective-permute-start | bytes 786440 | tf_op jit(solution)/shard_map/ppermute | solution.py:347
  15.9 4.3 %copy-start.8 = (bf16[128,1536]{1,0:T(8,128)(2,1)}, bf16[128,1536]{1,0:T(8,128)(2,1)S(1)}, u32[]{:S(2)}) copy-start(bf16[128,1536]{1,0:T(8,128)(2,1)S(1)} %collective-permute-done.2.refs_2_.refs_7_) | copy-start | bytes 1179652
  17.4 14.9 %collective-permute-start.3 = (bf16[128,1536]{1,0:T(8,128)(2,1)}, bf16[128,1536]{1,0:T(8,128)(2,1)}, u32[]{:S(2)}, u32[]{:S(2)}) collective-permute-start(bf16[128,1536]{1,0:T(8,128)(2,1)} %filter.4.refs_6_.refs_8_), channel_id=1, source_target_pairs={{16,0},{17,1},{18,2},{19,3},{20,4},{21,5},{22,6},{23,7},{24,8},{25... | collective-permute-start | bytes 1179656 | tf_op jit(solution)/shard_map/ppermute | solution.py:366
  18.7 3.6 %copy-start.10 = (bf16[128,1536]{1,0:T(8,128)(2,1)}, bf16[128,1536]{1,0:T(8,128)(2,1)S(1)}, u32[]{:S(2)}) copy-start(bf16[128,1536]{1,0:T(8,128)(2,1)S(1)} %collective-permute-done.5.refs_2_.refs_7_) | copy-start | bytes 1179652
  20.2 19.7 %collective-permute-start.6 = (bf16[128,1536]{1,0:T(8,128)(2,1)}, bf16[128,1536]{1,0:T(8,128)(2,1)}, u32[]{:S(2)}, u32[]{:S(2)}) collective-permute-start(bf16[128,1536]{1,0:T(8,128)(2,1)} %filter.5.refs_6_.refs_8_), channel_id=1, source_target_pairs={{16,0},{17,1},{18,2},{19,3},{20,4},{21,5},{22,6},{23,7},{24,8},{25... | collective-permute-start | bytes 1179656 | tf_op jit(solution)/shard_map/ppermute | solution.py:366
  21.5 2.7 %copy-start.2 = (bf16[128,1024]{1,0:T(8,128)(2,1)}, bf16[128,1024]{1,0:T(8,128)(2,1)S(1)}, u32[]{:S(2)}) copy-start(bf16[128,1024]{1,0:T(8,128)(2,1)S(1)} %collective-permute-done.4.refs_2_.refs_7_) | copy-start | bytes 786436
  22.2 22.1 %collective-permute-start.7 = (bf16[128,512]{1,0:T(8,128)(2,1)}, bf16[128,512]{1,0:T(8,128)(2,1)}, u32[]{:S(2)}, u32[]{:S(2)}) collective-permute-start(bf16[128,512]{1,0:T(8,128)(2,1)} %filter.6.refs_6_.refs_8_), channel_id=1, source_target_pairs={{16,0},{17,1},{18,2},{19,3},{20,4},{21,5},{22,6},{23,7},{24,8},{25... | collective-permute-start | bytes 393224 | tf_op jit(solution)/shard_map/ppermute | solution.py:366
  24.2 22.1 %collective-permute-start.8 = (bf16[128,512]{1,0:T(8,128)(2,1)}, bf16[128,512]{1,0:T(8,128)(2,1)}, u32[]{:S(2)}, u32[]{:S(2)}) collective-permute-start(bf16[128,512]{1,0:T(8,128)(2,1)} %filter.7.refs_4_.refs_8_), channel_id=1, source_target_pairs={{16,0},{17,1},{18,2},{19,3},{20,4},{21,5},{22,6},{23,7},{24,8},{25... | collective-permute-start | bytes 393224 | tf_op jit(solution)/shard_map/ppermute | solution.py:366
  26.1 6.2 %copy-start = (bf16[1,128,4096]{2,1,0:T(8,128)(2,1)S(1)}, bf16[1,128,4096]{2,1,0:T(8,128)(2,1)}, u32[]{:S(2)}) copy-start(bf16[1,128,4096]{2,1,0:T(8,128)(2,1)} %param.8) | copy-start | bytes 3145732
  26.1 6.2 %copy-start.5 = (bf16[128,1536]{1,0:T(8,128)(2,1)S(1)}, bf16[128,1536]{1,0:T(8,128)(2,1)}, u32[]{:S(2)}) copy-start(bf16[128,1536]{1,0:T(8,128)(2,1)} %copy-done.4) | copy-start | bytes 1179652
  26.1 6.2 %copy-start.9 = (bf16[128,1536]{1,0:T(8,128)(2,1)S(1)}, bf16[128,1536]{1,0:T(8,128)(2,1)}, u32[]{:S(2)}) copy-start(bf16[128,1536]{1,0:T(8,128)(2,1)} %copy-done.8) | copy-start | bytes 1179652
  32.3 7.6 %copy-start.7 = (bf16[128,1536]{1,0:T(8,128)(2,1)S(1)}, bf16[128,1536]{1,0:T(8,128)(2,1)}, u32[]{:S(2)}) copy-start(bf16[128,1536]{1,0:T(8,128)(2,1)} %copy-done.6) | copy-start | bytes 1179652
  32.3 7.6 %copy-start.11 = (bf16[128,1536]{1,0:T(8,128)(2,1)S(1)}, bf16[128,1536]{1,0:T(8,128)(2,1)}, u32[]{:S(2)}) copy-start(bf16[128,1536]{1,0:T(8,128)(2,1)} %copy-done.10) | copy-start | bytes 1179652
  36.3 0.6 copy-start.17
  36.9 6.9 %copy-start.12 = (f32[96,128]{1,0:T(8,128)}, f32[96,128]{1,0:T(8,128)S(1)}, u32[]{:S(2)}) copy-start(f32[96,128]{1,0:T(8,128)S(1)} %get-tuple-element.42.refs_11_.refs_0_) | copy-start | bytes 147460
  39.9 4.5 %copy-start.3 = (bf16[128,1024]{1,0:T(8,128)(2,1)S(1)}, bf16[128,1024]{1,0:T(8,128)(2,1)}, u32[]{:S(2)}) copy-start(bf16[128,1024]{1,0:T(8,128)(2,1)} %copy-done.2) | copy-start | bytes 786436
  43.8 0.6 copy-start.18
  44.4 1.9 %copy-start.13 = (f32[96,128]{1,0:T(8,128)}, f32[96,128]{1,0:T(8,128)S(1)}, u32[]{:S(2)}) copy-start(f32[96,128]{1,0:T(8,128)S(1)} %get-tuple-element.43.refs_11_.refs_1_) | copy-start | bytes 147460
  46.3 1.9 %copy-start.14 = (f32[32,128]{1,0:T(8,128)}, f32[32,128]{1,0:T(8,128)S(1)}, u32[]{:S(2)}) copy-start(f32[32,128]{1,0:T(8,128)S(1)} %get-tuple-element.44.refs_11_.refs_2_) | copy-start | bytes 49156
  46.3 1.9 %copy-start.19 = (f32[1,512]{1,0:T(1,128)}, f32[1,512]{1,0:T(1,128)S(1)}, u32[]{:S(2)}) copy-start(f32[1,512]{1,0:T(1,128)S(1)} %get-tuple-element.48.refs_6_) | copy-start | bytes 6148
  48.2 0.6 copy-start.16
  48.8 0.6 copy-start.20
  51.0 1.5 %collective-permute-start.9 = (f32[8,18,128]{2,1,0:T(8,128)}, f32[8,18,128]{2,1,0:T(8,128)S(1)}, u32[]{:S(2)}, u32[]{:S(2)}) collective-permute-start(f32[8,18,128]{2,1,0:T(8,128)} %get-tuple-element.51), channel_id=1, source_target_pairs={{0,1},{1,0},{2,3},{3,2},{4,5},{5,4},{6,7},{7,6},{8,9},{9,8},{10,11... | collective-permute-start | bytes 221192 | tf_op jit(solution)/shard_map/ppermute | solution.py:424
  52.5 0.6 copy-start.21
  54.8 4.3 %collective-permute-start.10 = (f32[4,18,128]{2,1,0:T(8,128)}, f32[4,18,128]{2,1,0:T(8,128)S(1)}, u32[]{:S(2)}, u32[]{:S(2)}) collective-permute-start(f32[4,18,128]{2,1,0:T(8,128)} %get-tuple-element.53), channel_id=1, source_target_pairs={{0,2},{1,3},{2,0},{3,1},{4,6},{5,7},{6,4},{7,5},{8,10},{9,11},{10,... | collective-permute-start | bytes 110600 | tf_op jit(solution)/shard_map/ppermute | solution.py:424
  59.1 0.6 copy-start.22
  61.1 4.7 %collective-permute-start.11 = (f32[2,18,128]{2,1,0:T(8,128)}, f32[2,18,128]{2,1,0:T(8,128)S(1)}, u32[]{:S(2)}, u32[]{:S(2)}) collective-permute-start(f32[2,18,128]{2,1,0:T(8,128)} %get-tuple-element.55), channel_id=1, source_target_pairs={{0,4},{1,5},{2,6},{3,7},{4,0},{5,1},{6,2},{7,3},{8,12},{9,13},{10,... | collective-permute-start | bytes 55304 | tf_op jit(solution)/shard_map/ppermute | solution.py:424
  65.9 0.6 copy-start.23
  67.8 4.9 %collective-permute-start.12 = (f32[1,18,128]{2,1,0:T(8,128)}, f32[1,18,128]{2,1,0:T(8,128)S(1)}, u32[]{:S(2)}, u32[]{:S(2)}) collective-permute-start(f32[1,18,128]{2,1,0:T(8,128)} %get-tuple-element.57), channel_id=1, source_target_pairs={{0,8},{1,9},{2,10},{3,11},{4,12},{5,13},{6,14},{7,15},{8,0},{9,1},... | collective-permute-start | bytes 27656 | tf_op jit(solution)/shard_map/ppermute | solution.py:424
  72.8 0.6 copy-start.24

commit v4 on v3

--- a/solution.py
+++ b/solution.py
@@ -86,12 +86,30 @@
     return pick, taps
 
 
-def weigh_kernel(role, gate, incoming, mid, out, incoming_out, mid_out):
+def weigh_kernel(role, gate, incoming, out):
     @pl.when(role[0] == 0)
     def _():
         out[...] = times(gate[...], incoming[...])
-        incoming_out[...] = incoming[...]
-        mid_out[...] = mid[...]
+
+
+def first_weigh_kernel(block, role, gate, incoming, out, gate_part, incoming_part, sems):
+    @pl.when(role[0] == 0)
+    def _():
+        tiles = [pl.ds(at, block) for at in range(0, out.shape[1], block)]
+        copies = [
+            [
+                pltpu.make_async_copy(source.at[:, t], part.at[:, t], sems.at[which, i])
+                for which, (source, part) in enumerate(((gate, gate_part), (incoming, incoming_part)))
+            ]
+            for i, t in enumerate(tiles)
+        ]
+        for pair in copies:
+            for copy in pair:
+                copy.start()
+        for t, pair in zip(tiles, copies):
+            for copy in pair:
+                copy.wait()
+            out[:, t] = times(gate_part[:, t], incoming_part[:, t])
 
 
 def taps_kernel(role, filters, taps_out):
@@ -195,12 +213,12 @@
         tap_grad[pl.ds(8 * pair, 8), :] = diagonal_sums(blocks)
 
 
-def halves_of(bit, zero, one):
-    mine = bit > 0
+def halves_of(place, step, zero, one):
+    mine = (place[0] >> step) & 1 > 0
     return jnp.where(mine, zero, one), jnp.where(mine, one, zero)
 
 
-def pack_kernel(owners, bits, *refs):
+def pack_kernel(owners, place, *refs):
     count = (len(refs) - 2) // 2
     taps, steers, (give, keep) = refs[:count], refs[count : 2 * count], refs[2 * count :]
     groups = sum(ref.shape[0] for ref in taps) // owners
@@ -226,7 +244,7 @@
         at = 0
         for zero, one in zip(packed(low), packed(high)):
             lines = zero.shape[0]
-            give[i, pl.ds(at, lines), :], keep[i, pl.ds(at, lines), :] = halves_of(bits[0], zero, one)
+            give[i, pl.ds(at, lines), :], keep[i, pl.ds(at, lines), :] = halves_of(place, 0, zero, one)
             at += lines
 
 
@@ -237,12 +255,12 @@
     return order
 
 
-def fold_kernel(step, bits, kept, arrived, give, keep):
+def fold_kernel(step, place, kept, arrived, give, keep):
     count = give.shape[0]
     for i in range(count):
         zero = kept[i] + arrived[i]
         one = kept[count + i] + arrived[count + i]
-        give[i], keep[i] = halves_of(bits[step], zero, one)
+        give[i], keep[i] = halves_of(place, step, zero, one)
 
 
 def step_kernel(role, kept, arrived, steer_second, filter_second, steer_out, filter_out):
@@ -267,6 +285,7 @@
 
 SMEM = pl.BlockSpec(memory_space=pltpu.SMEM)
 ANY = pl.BlockSpec(memory_space=pl.ANY)
+SMALL = pltpu.CompilerParams(vmem_limit_bytes=4 * 1024 * 1024)
 
 
 def call(kernel, grid, in_specs, out_specs, out_shape, scratch=(), name=None, cycles=100, after=()):
@@ -282,7 +301,7 @@
         out_specs=out_specs,
         out_shape=out_shape,
         scratch_shapes=list(scratch),
-        compiler_params=pltpu.CompilerParams(vmem_limit_bytes=32 * 1024 * 1024),
+        compiler_params=pltpu.CompilerParams(vmem_limit_bytes=16 * 1024 * 1024),
         cost_estimate=pl.CostEstimate(flops=cycles, bytes_accessed=0, transcendentals=0),
         name=name,
     )
@@ -312,14 +331,24 @@
         return call(
             weigh_kernel,
             ((last - first) // block,),
-            [SMEM, spec(rows, block, first // block), spec(rows, block, (first - offset) // block),
-             spec(rows, block, first // block)],
-            [spec(rows, block)] * 3,
-            [bf16(last - first)] * 3,
+            [SMEM, spec(rows, block, first // block), spec(rows, block, (first - offset) // block)],
+            spec(rows, block),
+            bf16(last - first),
             name="weigh",
             after=after,
-        )(role, *[pltpu.with_memory_space_constraint(array, pltpu.HBM) for array in (in_gate, incoming, mid_gate)],
-          *after)
+        )(role, in_gate, incoming, *after)
+
+    def first_weigh(last):
+        part = pltpu.VMEM((rows, last), BF16)
+        return pl.pallas_call(
+            functools.partial(first_weigh_kernel, block),
+            in_specs=[SMEM] + [pl.BlockSpec(memory_space=pl.ANY)] * 2,
+            out_specs=pl.BlockSpec(memory_space=pltpu.VMEM),
+            out_shape=bf16(last),
+            scratch_shapes=[part, part, pltpu.SemaphoreType.DMA((2, last // block))],
+            compiler_params=SMALL,
+            name="first_weigh",
+        )(role, *[pltpu.with_memory_space_constraint(a, pltpu.HBM) for a in (in_gate, cotangent)])
 
     taps = call(
         taps_kernel,
@@ -335,32 +364,35 @@
     for hop in range(sections - 1):
         split = [channels * eighths // 8 for eighths in HALO_EDGES] if hop == 0 else edges
         starts, ends = split[:-1], split[1:]
-        weighed = []
+        owns = []
         for first, last in zip(starts, ends):
             array, offset = next(entry for entry, edge in zip(incoming, edges) if edge == first)
-            weighed.append(weigh(array, first, last, offset, tuple(weighed[-1][:1] if weighed else ())))
-        owns, incomings, mids = zip(*weighed)
+            if hop == 0 and first == 0:
+                owns.append(first_weigh(last))
+            else:
+                owns.append(weigh(array, first, last, offset, tuple(owns[-1:])))
         if hop == 0:
-            mid_late, inputs_late, _ = lax.optimization_barrier((mid_gate, layer_inputs, owns[0]))
-            mid_halo = lax.ppermute(mid_late, ("section", "seq"), ahead)
-            inputs_halo = lax.ppermute(inputs_late, ("section", "seq"), ahead)
+            mid_sent, inputs_sent, _ = lax.optimization_barrier((mid_gate, layer_inputs, owns[0]))
+            mid_halo = lax.ppermute(mid_sent, ("section", "seq"), ahead)
+            inputs_halo = lax.ppermute(inputs_sent, ("section", "seq"), ahead)
         halos = [lax.ppermute(own, ("section", "seq"), behind) for own in owns]
         sources, outgoing, received = [], [], []
         for k, (first, last) in enumerate(bounds):
             part = max(i for i, start in enumerate(starts) if start <= first)
             at = (first - starts[part]) // block
+            array, offset = incoming[k]
             before = tuple(outgoing[-1:])
             out = call(
                 functools.partial(filter_kernel, group_size),
                 ((last - first) // block,),
                 [SMEM, spec(rows, block, at), spec(rows, block, at), group_spec(first // block),
-                 spec(rows, block, at), spec(rows, block, at)],
+                 spec(rows, block, first // block), spec(rows, block, (first - offset) // block)],
                 spec(rows, block),
                 bf16(last - first),
                 name="filter",
                 cycles=1000,
                 after=before,
-            )(role, owns[part], halos[part], taps, mids[part], incomings[part], *before)
+            )(role, owns[part], halos[part], taps, mid_gate, array, *before)
             sources.append((owns[part], halos[part], at))
             outgoing.append(out)
             received.append(lax.ppermute(out, "section", down))
@@ -370,16 +402,19 @@
             for (first, last), arrived in zip(bounds, received)
         ]
 
-    filtered = call(
-        functools.partial(turned_filter_kernel, group_size),
-        (channels // block,),
-        [SMEM, spec(rows, block), spec(rows, block), group_spec(0)],
-        spec(rows, block),
-        jax.ShapeDtypeStruct((rows, channels), F32),
-        name="turned_filter",
-        cycles=4000,
-        after=tuple(outgoing[-1:]),
-    )(role, mid_gate, mid_halo, taps, *outgoing[-1:])
+    filtered = []
+    for first, last in bounds:
+        after = tuple(outgoing[-1:]) + tuple(filtered[-1:])
+        filtered.append(call(
+            functools.partial(turned_filter_kernel, group_size),
+            ((last - first) // block,),
+            [SMEM, spec(rows, block, first // block), spec(rows, block, first // block), group_spec(first // block)],
+            spec(rows, block),
+            jax.ShapeDtypeStruct((rows, last - first), F32),
+            name="turned_filter",
+            cycles=1000,
+            after=after,
+        )(role, mid_gate, mid_halo, taps, *after))
 
     grads = []
     for k, (first, last) in enumerate(bounds):
@@ -391,7 +426,7 @@
             functools.partial(grad_kernel, group_size),
             (width // block,),
             [SMEM, here, here, here, here, here, spec(rows, block, at), spec(rows, block, at)]
-            + [spec(rows, block)] * 2 + [here],
+            + [spec(rows, block)] * 3,
             [group_spec(0), pl.BlockSpec((1, block), lambda i: (0, i))],
             [jax.ShapeDtypeStruct((width // group_size, filt_len), F32), jax.ShapeDtypeStruct((1, width), F32)],
             scratch=[pltpu.VMEM((rows, block), BF16)] * 3,
@@ -399,14 +434,13 @@
             cycles=2000,
             after=after,
         )(role, in_gate, mid_gate, layer_inputs, mid_halo, inputs_halo, own, halo, outgoing[k],
-          received[k], filtered, *after))
+          received[k], filtered[k], *after))
     tap_grads, steer_grads = zip(*grads)
 
     own_channels = channels // seqs
     lines = groups // seqs + pl.cdiv(own_channels, LANES)
-    place = lax.axis_index("seq")
+    place = lax.axis_index("seq").reshape(1)
     steps = seqs.bit_length() - 1
-    bits = jnp.stack([(place >> step) & 1 for step in range(steps)]).astype(jnp.int32)
 
     def halves(count):
         return [jax.ShapeDtypeStruct((count, lines, LANES), F32)] * 2
@@ -417,8 +451,9 @@
         in_specs=[SMEM] + [vmem] * (2 * len(grads)),
         out_specs=[vmem] * 2,
         out_shape=halves(seqs // 2),
+        compiler_params=SMALL,
         name="pack",
-    )(bits, *tap_grads, *steer_grads)
+    )(place, *tap_grads, *steer_grads)
     for step in range(steps):
         route = [(i, i ^ (1 << step)) for i in range(seqs)]
         arrived = lax.ppermute(give, "seq", route)
@@ -428,8 +463,9 @@
                 in_specs=[SMEM, vmem, vmem],
                 out_specs=[vmem] * 2,
                 out_shape=halves(keep.shape[0] // 2),
+                compiler_params=SMALL,
                 name="fold",
-            )(bits, keep, arrived)
+            )(place, keep, arrived)
     steer_step, filter_step = pl.pallas_call(
         step_kernel,
         in_specs=[SMEM] + [vmem] * 4,
@@ -437,6 +473,7 @@
             jax.ShapeDtypeStruct((1, own_channels), F32),
             jax.ShapeDtypeStruct((groups // seqs, filt_len), F32),
         ],
+        compiler_params=SMALL,
         name="step",
     )(role, keep, arrived, steer_second, filter_second[0].T)
     return steer_step, filter_step.T[None]

time: 75.7 us -> 72.8 us (0.962)
  the two profiles are of different devices: /device:TPU:0 before, /device:TPU:14 now
where the time goes in v4:
time: 72.8 us; the launch traced here: 72.1 us
  starting transfers between devices  23 us (32%)
  Pallas kernels  21.3 us (29%)
  waiting for transfers between devices  16.5 us (23%)
  local copies, waits for them, and re-layouts  10.3 us (14%)
  between operations  0.95 us (1%)
    ppermute x4, waiting for transfers between devices, body(): arrived = lax.ppermute(give, 'seq', route)  12 us
    pallas_call x4, Pallas kernels, body(): call(functools.partial(grad_kernel, group_size), (width // block,), [SMEM...  11 us
    unnamed x52, local copies, waits for them, and re-layouts  10.3 us
    ppermute x4, starting transfers between devices, body(): received.append(lax.ppermute(out, 'section', down))  8.17 us
    ppermute x3, starting transfers between devices, body(): halos = [lax.ppermute(own, ('section', 'seq'), behind) for own in owns]  8.12 us
    pallas_call x4, Pallas kernels, body(): call(functools.partial(filter_kernel, group_size), ((last - first) // blo...  6.98 us
    ppermute x4, starting transfers between devices, body(): arrived = lax.ppermute(give, 'seq', route)  5.27 us
    ppermute x3, waiting for transfers between devices, body(): halos = [lax.ppermute(own, ('section', 'seq'), behind) for own in owns]  4.54 us
  transfers between devices with their start and end apart: 13, of which 6 were waited for; matrix products, arithmetic and copies ran while one was open for 0% of the time, Pallas kernels for 24%

profile of v4, /device:TPU:14, one launch (start us, length us, event | category | flops | bytes accessed | tf_op | source)
XLA Modules:
  0.0 72.1 jit_solution(2498550220480059597)
XLA Ops:
  0.6 0.0 copy-start
  0.6 0.0 copy-start.1
  0.7 1.4 %first_weigh.1.refs_1_.refs_3_.refs_6_ = bf16[128,1536]{1,0:T(8,128)(2,1)S(1)} custom-call(s32[1]{0:T(128)} %bitcast.role.refs_0_, bf16[128,4096]{1,0:T(8,128)(2,1)} %bitcast.25, bf16[128,4096]{1,0:T(8,128)(2,1)} %refs_5_.7), custom_call_target="tpu_custom_call" | custom-call | tf_op jit(solution)/shard_map/first_weigh/pallas_call | solution.py:343
  2.1 0.0 copy-start.12
  2.1 0.1 copy-done
  2.2 0.7 collective-permute-start
  2.9 0.7 %collective-permute-start.1 = (bf16[128,4096]{1,0:T(8,128)(2,1)}, bf16[128,4096]{1,0:T(8,128)(2,1)S(1)}, u32[]{:S(2)}, u32[]{:S(2)}) collective-permute-start(bf16[128,4096]{1,0:T(8,128)(2,1)} %bitcast.32), channel_id=1, source_target_pairs={{0,1},{1,2},{2,3},{3,4},{4,5},{5,6},{6,7},{7,8},{8,9},{9,10},{10,1... | collective-permute-start | bytes 3145736 | tf_op jit(solution)/shard_map/ppermute | solution.py:377
  3.7 1.9 %collective-permute-start.2 = (bf16[128,1536]{1,0:T(8,128)(2,1)S(1)}, bf16[128,1536]{1,0:T(8,128)(2,1)S(1)}, u32[]{:S(2)}, u32[]{:S(2)}) collective-permute-start(bf16[128,1536]{1,0:T(8,128)(2,1)S(1)} %first_weigh.1.refs_1_.refs_3_.refs_6_), channel_id=1, source_target_pairs={{17,16},{18,17},{19,18},{20,19},{21,20},{22,21},{23,22},{24,23},{2... | collective-permute-start | bytes 1179656 | tf_op jit(solution)/shard_map/ppermute | solution.py:378
  5.6 0.0 copy-start.2
  5.6 1.2 %copy-done.2 = bf16[1,128,4096]{2,1,0:T(8,128)(2,1)S(1)} copy-done((bf16[1,128,4096]{2,1,0:T(8,128)(2,1)S(1)}, bf16[1,128,4096]{2,1,0:T(8,128)(2,1)}, u32[]{:S(2)}) %copy-start.2) | copy-done | bytes 1048600
  6.8 0.3 weigh.2.refs_3_.refs_1_.refs_6_
  7.1 0.0 copy-start.23
  7.1 2.6 %collective-permute-start.5 = (bf16[128,1536]{1,0:T(8,128)(2,1)S(1)}, bf16[128,1536]{1,0:T(8,128)(2,1)S(1)}, u32[]{:S(2)}, u32[]{:S(2)}) collective-permute-start(bf16[128,1536]{1,0:T(8,128)(2,1)S(1)} %weigh.2.refs_3_.refs_1_.refs_6_), channel_id=1, source_target_pairs={{17,16},{18,17},{19,18},{20,19},{21,20},{22,21},{23,22},{24,23},{2... | collective-permute-start | bytes 1179656 | tf_op jit(solution)/shard_map/ppermute | solution.py:378
  9.8 0.2 weigh.3.refs_1_.refs_6_
  10.0 0.2 taps.1.refs_3_
  10.2 0.7 collective-permute-done.2.refs_2_.refs_7_
  10.9 2.4 %filter.4.refs_6_.refs_8_ = bf16[128,1536]{1,0:T(8,128)(2,1)} custom-call(s32[1]{0:T(128)} %bitcast.role.refs_0_, bf16[128,1536]{1,0:T(8,128)(2,1)S(1)} %first_weigh.1.refs_1_.refs_3_.refs_6_, bf16[128,1536]{1,0:T(8,128)(2,1)S(1)} %collective-permute-done.2.refs_2_.refs_7_, f32[256,128]{1,0:T(8,128)S(1)} %taps.1.refs_3_, bf16[128,4096]{1,0:T(8,128)(2,1)S(1)} %bitcast.13, ...), custom_call_target="tpu_custom_call" | custom-call | flops 1000 | tf_op jit(solution)/shard_map/filter/pallas_call | solution.py:385
  13.2 0.0 copy-done.21
  13.2 2.3 %collective-permute-start.3 = (bf16[128,1536]{1,0:T(8,128)(2,1)}, bf16[128,1536]{1,0:T(8,128)(2,1)}, u32[]{:S(2)}, u32[]{:S(2)}) collective-permute-start(bf16[128,1536]{1,0:T(8,128)(2,1)} %filter.4.refs_6_.refs_8_), channel_id=1, source_target_pairs={{16,0},{17,1},{18,2},{19,3},{20,4},{21,5},{22,6},{23,7},{24,8},{25... | collective-permute-start | bytes 1179656 | tf_op jit(solution)/shard_map/ppermute | solution.py:398
  15.5 0.0 collective-permute-done.5.refs_2_.refs_7_
  15.5 2.4 %filter.5.refs_6_.refs_8_ = bf16[128,1536]{1,0:T(8,128)(2,1)} custom-call(s32[1]{0:T(128)} %bitcast.role.refs_0_, bf16[128,1536]{1,0:T(8,128)(2,1)S(1)} %weigh.2.refs_3_.refs_1_.refs_6_, bf16[128,1536]{1,0:T(8,128)(2,1)S(1)} %collective-permute-done.5.refs_2_.refs_7_, f32[256,128]{1,0:T(8,128)S(1)} %taps.1.refs_3_, bf16[128,4096]{1,0:T(8,128)(2,1)S(1)} %bitcast.14, ...), custom_call_target="tpu_custom_call" | custom-call | flops 1000 | tf_op jit(solution)/shard_map/filter/pallas_call | solution.py:385
  17.9 2.0 %collective-permute-start.6 = (bf16[128,1536]{1,0:T(8,128)(2,1)}, bf16[128,1536]{1,0:T(8,128)(2,1)}, u32[]{:S(2)}, u32[]{:S(2)}) collective-permute-start(bf16[128,1536]{1,0:T(8,128)(2,1)} %filter.5.refs_6_.refs_8_), channel_id=1, source_target_pairs={{16,0},{17,1},{18,2},{19,3},{20,4},{21,5},{22,6},{23,7},{24,8},{25... | collective-permute-start | bytes 1179656 | tf_op jit(solution)/shard_map/ppermute | solution.py:398
  19.9 3.6 %collective-permute-start.4 = (bf16[128,1024]{1,0:T(8,128)(2,1)S(1)}, bf16[128,1024]{1,0:T(8,128)(2,1)S(1)}, u32[]{:S(2)}, u32[]{:S(2)}) collective-permute-start(bf16[128,1024]{1,0:T(8,128)(2,1)S(1)} %weigh.3.refs_1_.refs_6_), channel_id=1, source_target_pairs={{17,16},{18,17},{19,18},{20,19},{21,20},{22,21},{23,22},{24,23},{2... | collective-permute-start | bytes 786440 | tf_op jit(solution)/shard_map/ppermute | solution.py:378
  23.5 3.9 %collective-permute-done.4.refs_2_.refs_7_ = bf16[128,1024]{1,0:T(8,128)(2,1)S(1)} collective-permute-done((bf16[128,1024]{1,0:T(8,128)(2,1)S(1)}, bf16[128,1024]{1,0:T(8,128)(2,1)S(1)}, u32[]{:S(2)}, u32[]{:S(2)}) %collective-permute-start.4) | collective-permute-done | bytes 262176 | tf_op jit(solution)/shard_map/ppermute | solution.py:378
  27.3 1.1 %filter.6.refs_6_.refs_8_ = bf16[128,512]{1,0:T(8,128)(2,1)} custom-call(s32[1]{0:T(128)} %bitcast.role.refs_0_, bf16[128,1024]{1,0:T(8,128)(2,1)S(1)} %weigh.3.refs_1_.refs_6_, bf16[128,1024]{1,0:T(8,128)(2,1)S(1)} %collective-permute-done.4.refs_2_.refs_7_, f32[256,128]{1,0:T(8,128)S(1)} %taps.1.refs_3_, bf16[128,4096]{1,0:T(8,128)(2,1)S(1)} %bitcast.15, ...), custom_call_target="tpu_custom_call" | custom-call | flops 1000 | tf_op jit(solution)/shard_map/filter/pallas_call | solution.py:385
  28.5 1.9 %collective-permute-start.7 = (bf16[128,512]{1,0:T(8,128)(2,1)}, bf16[128,512]{1,0:T(8,128)(2,1)}, u32[]{:S(2)}, u32[]{:S(2)}) collective-permute-start(bf16[128,512]{1,0:T(8,128)(2,1)} %filter.6.refs_6_.refs_8_), channel_id=1, source_target_pairs={{16,0},{17,1},{18,2},{19,3},{20,4},{21,5},{22,6},{23,7},{24,8},{25... | collective-permute-start | bytes 393224 | tf_op jit(solution)/shard_map/ppermute | solution.py:398
  30.4 1.1 %filter.7.refs_4_.refs_8_ = bf16[128,512]{1,0:T(8,128)(2,1)} custom-call(s32[1]{0:T(128)} %bitcast.role.refs_0_, bf16[128,1024]{1,0:T(8,128)(2,1)S(1)} %weigh.3.refs_1_.refs_6_, bf16[128,1024]{1,0:T(8,128)(2,1)S(1)} %collective-permute-done.4.refs_2_.refs_7_, f32[256,128]{1,0:T(8,128)S(1)} %taps.1.refs_3_, bf16[128,4096]{1,0:T(8,128)(2,1)S(1)} %bitcast.16, ...), custom_call_target="tpu_custom_call" | custom-call | flops 1000 | tf_op jit(solution)/shard_map/filter/pallas_call | solution.py:385
  31.5 0.0 collective-permute-done.refs_2_.refs_4_
  31.5 1.9 %collective-permute-start.8 = (bf16[128,512]{1,0:T(8,128)(2,1)}, bf16[128,512]{1,0:T(8,128)(2,1)}, u32[]{:S(2)}, u32[]{:S(2)}) collective-permute-start(bf16[128,512]{1,0:T(8,128)(2,1)} %filter.7.refs_4_.refs_8_), channel_id=1, source_target_pairs={{16,0},{17,1},{18,2},{19,3},{20,4},{21,5},{22,6},{23,7},{24,8},{25... | collective-permute-start | bytes 393224 | tf_op jit(solution)/shard_map/ppermute | solution.py:398
  33.5 0.2 turned_filter.4.refs_10_.refs_5_
  33.7 0.2 turned_filter.5.refs_10_.refs_5_
  33.9 0.9 %copy-done.5 = f32[128,1536]{1,0:T(8,128)} copy-done((f32[128,1536]{1,0:T(8,128)}, f32[128,1536]{1,0:T(8,128)S(1)}, u32[]{:S(2)}) %copy-start.5) | copy-done | bytes 786456
  34.8 0.9 %copy-done.8 = f32[128,1536]{1,0:T(8,128)} copy-done((f32[128,1536]{1,0:T(8,128)}, f32[128,1536]{1,0:T(8,128)S(1)}, u32[]{:S(2)}) %copy-start.8) | copy-done | bytes 786456
  35.7 1.1 %copy-done.6 = f32[128,1536]{1,0:T(8,128)S(1)} copy-done((f32[128,1536]{1,0:T(8,128)S(1)}, f32[128,1536]{1,0:T(8,128)}, u32[]{:S(2)}) %copy-start.6) | copy-done | bytes 786456
  36.9 0.7 copy-done.16
  37.6 0.9 %copy-done.17 = f32[128,512]{1,0:T(8,128)S(1)} copy-done((f32[128,512]{1,0:T(8,128)S(1)}, f32[128,512]{1,0:T(8,128)}, u32[]{:S(2)}) %copy-start.17) | copy-done | bytes 262168
  38.6 0.0 collective-permute-done.3.refs_9_
  38.6 0.0 collective-permute-done.1.refs_5_
  38.6 1.2 %copy-done.3 = bf16[1,128,4096]{2,1,0:T(8,128)(2,1)S(1)} copy-done((bf16[1,128,4096]{2,1,0:T(8,128)(2,1)S(1)}, bf16[1,128,4096]{2,1,0:T(8,128)(2,1)}, u32[]{:S(2)}) %copy-start.3) | copy-done | bytes 1048600
  39.8 0.3 copy-done.4
  40.1 0.2 copy-done.9
  40.3 1.0 %copy-done.13 = bf16[128,1536]{1,0:T(8,128)(2,1)S(1)} copy-done((bf16[128,1536]{1,0:T(8,128)(2,1)S(1)}, bf16[128,1536]{1,0:T(8,128)(2,1)}, u32[]{:S(2)}) %copy-start.13) | copy-done | bytes 393240
  41.3 1.0 %copy-done.22 = bf16[128,1536]{1,0:T(8,128)(2,1)S(1)} copy-done((bf16[128,1536]{1,0:T(8,128)(2,1)S(1)}, bf16[128,1536]{1,0:T(8,128)(2,1)}, u32[]{:S(2)}) %copy-start.22) | copy-done | bytes 393240
  42.3 3.7 %grads.4 = (f32[96,128]{1,0:T(8,128)S(1)}, f32[1,1536]{1,0:T(1,128)S(1)}) custom-call(s32[1]{0:T(128)} %bitcast.role.refs_0_, bf16[128,4096]{1,0:T(8,128)(2,1)S(1)} %bitcast.28, bf16[128,4096]{1,0:T(8,128)(2,1)S(1)} %bitcast.21, bf16[128,4096]{1,0:T(8,128)(2,1)S(1)} %bitcast.33, bf16[128,4096]{1,0:T(8,128)(2,1)S(1)} %collective-permute-done.refs_2_.refs_4_, ...), custom_call_target="tpu_custom_call" | custom-call | flops 2000 | tf_op jit(solution)/shard_map/grads/pallas_call | solution.py:425
  46.0 0.0 collective-permute-done.6.refs_9_
  46.0 0.0 copy-done.11
  46.0 0.0 copy-done.20
  46.0 0.0 copy-start.15
  46.0 0.0 copy-start.18
  46.0 3.7 %grads.5 = (f32[96,128]{1,0:T(8,128)S(1)}, f32[1,1536]{1,0:T(1,128)S(1)}) custom-call(s32[1]{0:T(128)} %bitcast.role.refs_0_, bf16[128,4096]{1,0:T(8,128)(2,1)S(1)} %bitcast.29, bf16[128,4096]{1,0:T(8,128)(2,1)S(1)} %bitcast.22, bf16[128,4096]{1,0:T(8,128)(2,1)S(1)} %bitcast.34, bf16[128,4096]{1,0:T(8,128)(2,1)S(1)} %collective-permute-done.refs_2_.refs_4_, ...), custom_call_target="tpu_custom_call" | custom-call | flops 2000 | tf_op jit(solution)/shard_map/grads/pallas_call | solution.py:425
  49.8 0.0 collective-permute-done.7.refs_9_
  49.8 1.8 %grads.6 = (f32[32,128]{1,0:T(8,128)S(1)}, f32[1,512]{1,0:T(1,128)S(1)}) custom-call(s32[1]{0:T(128)} %bitcast.role.refs_0_, bf16[128,4096]{1,0:T(8,128)(2,1)S(1)} %bitcast.30, bf16[128,4096]{1,0:T(8,128)(2,1)S(1)} %bitcast.23, bf16[128,4096]{1,0:T(8,128)(2,1)S(1)} %bitcast.35, bf16[128,4096]{1,0:T(8,128)(2,1)S(1)} %collective-permute-done.refs_2_.refs_4_, ...), custom_call_target="tpu_custom_call" | custom-call | flops 2000 | tf_op jit(solution)/shard_map/grads/pallas_call | solution.py:425
  51.6 0.0 collective-permute-done.8.refs_9_
  51.6 1.8 %grads.7 = (f32[32,128]{1,0:T(8,128)S(1)}, f32[1,512]{1,0:T(1,128)S(1)}) custom-call(s32[1]{0:T(128)} %bitcast.role.refs_0_, bf16[128,4096]{1,0:T(8,128)(2,1)S(1)} %bitcast.31, bf16[128,4096]{1,0:T(8,128)(2,1)S(1)} %bitcast.24, bf16[128,4096]{1,0:T(8,128)(2,1)S(1)} %bitcast.36, bf16[128,4096]{1,0:T(8,128)(2,1)S(1)} %collective-permute-done.refs_2_.refs_4_, ...), custom_call_target="tpu_custom_call" | custom-call | flops 2000 | tf_op jit(solution)/shard_map/grads/pallas_call | solution.py:425
  53.4 3.6 %collective-permute-start.9 = (f32[8,18,128]{2,1,0:T(8,128)S(1)}, f32[8,18,128]{2,1,0:T(8,128)S(1)}, u32[]{:S(2)}, u32[]{:S(2)}) collective-permute-start(f32[8,18,128]{2,1,0:T(8,128)S(1)} %get-tuple-element.33), channel_id=1, source_target_pairs={{0,1},{1,0},{2,3},{3,2},{4,5},{5,4},{6,7},{7,6},{8,9},{9,8},{10,11... | collective-permute-start | bytes 221192 | tf_op jit(solution)/shard_map/ppermute | solution.py:459
  57.0 0.9 %collective-permute-done.9.arrived = f32[8,18,128]{2,1,0:T(8,128)S(1)} collective-permute-done((f32[8,18,128]{2,1,0:T(8,128)S(1)}, f32[8,18,128]{2,1,0:T(8,128)S(1)}, u32[]{:S(2)}, u32[]{:S(2)}) %collective-permute-start.9) | collective-permute-done | bytes 73760 | tf_op jit(solution)/shard_map/ppermute | solution.py:459
  58.0 0.1 collective-permute-start.10
  58.1 4.1 %collective-permute-done.10.arrived = f32[4,18,128]{2,1,0:T(8,128)S(1)} collective-permute-done((f32[4,18,128]{2,1,0:T(8,128)S(1)}, f32[4,18,128]{2,1,0:T(8,128)S(1)}, u32[]{:S(2)}, u32[]{:S(2)}) %collective-permute-start.10) | collective-permute-done | bytes 36896 | tf_op jit(solution)/shard_map/ppermute | solution.py:459
  62.2 0.5 collective-permute-start.11
  62.7 3.4 %collective-permute-done.11.arrived = f32[2,18,128]{2,1,0:T(8,128)S(1)} collective-permute-done((f32[2,18,128]{2,1,0:T(8,128)S(1)}, f32[2,18,128]{2,1,0:T(8,128)S(1)}, u32[]{:S(2)}, u32[]{:S(2)}) %collective-permute-start.11) | collective-permute-done | bytes 18464 | tf_op jit(solution)/shard_map/ppermute | solution.py:459
  66.1 1.1 %collective-permute-start.12 = (f32[1,18,128]{2,1,0:T(8,128)S(1)}, f32[1,18,128]{2,1,0:T(8,128)S(1)}, u32[]{:S(2)}, u32[]{:S(2)}) collective-permute-start(f32[1,18,128]{2,1,0:T(8,128)S(1)} %get-tuple-element.39), channel_id=1, source_target_pairs={{0,8},{1,9},{2,10},{3,11},{4,12},{5,13},{6,14},{7,15},{8,0},{9,1},... | collective-permute-start | bytes 27656 | tf_op jit(solution)/shard_map/ppermute | solution.py:459
  67.2 3.6 %collective-permute-done.12.arrived = f32[1,18,128]{2,1,0:T(8,128)S(1)} collective-permute-done((f32[1,18,128]{2,1,0:T(8,128)S(1)}, f32[1,18,128]{2,1,0:T(8,128)S(1)}, u32[]{:S(2)}, u32[]{:S(2)}) %collective-permute-start.12) | collective-permute-done | bytes 9248 | tf_op jit(solution)/shard_map/ppermute | solution.py:459
  70.8 0.7 copy-done.25
  71.4 0.7 step.1
  (35 shorter events, 0.1 us)
Async XLA Ops:
  0.6 1.6 %copy-start = (bf16[1,128,4096]{2,1,0:T(8,128)(2,1)S(1)}, bf16[1,128,4096]{2,1,0:T(8,128)(2,1)}, u32[]{:S(2)}) copy-start(bf16[1,128,4096]{2,1,0:T(8,128)(2,1)} %param.9) | copy-start | bytes 3145732
  0.6 4.9 %copy-start.1 = (bf16[128,4096]{1,0:T(8,128)(2,1)S(1)}, bf16[128,4096]{1,0:T(8,128)(2,1)}, u32[]{:S(2)}) copy-start(bf16[128,4096]{1,0:T(8,128)(2,1)} %refs_5_.7) | copy-start | bytes 3145732
  2.1 8.8 %copy-start.12 = (bf16[128,1536]{1,0:T(8,128)(2,1)}, bf16[128,1536]{1,0:T(8,128)(2,1)S(1)}, u32[]{:S(2)}) copy-start(bf16[128,1536]{1,0:T(8,128)(2,1)S(1)} %first_weigh.1.refs_1_.refs_3_.refs_6_) | copy-start | bytes 1179652
  2.2 29.3 %collective-permute-start = (bf16[128,4096]{1,0:T(8,128)(2,1)S(1)}, bf16[128,4096]{1,0:T(8,128)(2,1)S(1)}, u32[]{:S(2)}, u32[]{:S(2)}) collective-permute-start(bf16[128,4096]{1,0:T(8,128)(2,1)S(1)} %bitcast.12), channel_id=1, source_target_pairs={{0,1},{1,2},{2,3},{3,4},{4,5},{5,6},{6,7},{7,8},{8,9},{9,10},{10,1... | collective-permute-start | bytes 3145736 | tf_op jit(solution)/shard_map/ppermute | solution.py:376
  2.9 35.7 %collective-permute-start.1 = (bf16[128,4096]{1,0:T(8,128)(2,1)}, bf16[128,4096]{1,0:T(8,128)(2,1)S(1)}, u32[]{:S(2)}, u32[]{:S(2)}) collective-permute-start(bf16[128,4096]{1,0:T(8,128)(2,1)} %bitcast.32), channel_id=1, source_target_pairs={{0,1},{1,2},{2,3},{3,4},{4,5},{5,6},{6,7},{7,8},{8,9},{9,10},{10,1... | collective-permute-start | bytes 3145736 | tf_op jit(solution)/shard_map/ppermute | solution.py:377
  3.7 7.2 %collective-permute-start.2 = (bf16[128,1536]{1,0:T(8,128)(2,1)S(1)}, bf16[128,1536]{1,0:T(8,128)(2,1)S(1)}, u32[]{:S(2)}, u32[]{:S(2)}) collective-permute-start(bf16[128,1536]{1,0:T(8,128)(2,1)S(1)} %first_weigh.1.refs_1_.refs_3_.refs_6_), channel_id=1, source_target_pairs={{17,16},{18,17},{19,18},{20,19},{21,20},{22,21},{23,22},{24,23},{2... | collective-permute-start | bytes 1179656 | tf_op jit(solution)/shard_map/ppermute | solution.py:378
  5.6 1.2 %copy-start.2 = (bf16[1,128,4096]{2,1,0:T(8,128)(2,1)S(1)}, bf16[1,128,4096]{2,1,0:T(8,128)(2,1)}, u32[]{:S(2)}) copy-start(bf16[1,128,4096]{2,1,0:T(8,128)(2,1)} %param.8) | copy-start | bytes 3145732
  7.1 8.4 %copy-start.10 = (bf16[128,1536]{1,0:T(8,128)(2,1)}, bf16[128,1536]{1,0:T(8,128)(2,1)S(1)}, u32[]{:S(2)}) copy-start(bf16[128,1536]{1,0:T(8,128)(2,1)S(1)} %weigh.2.refs_3_.refs_1_.refs_6_) | copy-start | bytes 1179652
  7.1 2.9 %copy-start.23 = (bf16[1,128,256]{2,1,0:T(8,128)(2,1)S(1)}, bf16[1,128,256]{2,1,0:T(8,128)(2,1)}, u32[]{:S(2)}) copy-start(bf16[1,128,256]{2,1,0:T(8,128)(2,1)} %param.11) | copy-start | bytes 196612
  7.1 8.4 %collective-permute-start.5 = (bf16[128,1536]{1,0:T(8,128)(2,1)S(1)}, bf16[128,1536]{1,0:T(8,128)(2,1)S(1)}, u32[]{:S(2)}, u32[]{:S(2)}) collective-permute-start(bf16[128,1536]{1,0:T(8,128)(2,1)S(1)} %weigh.2.refs_3_.refs_1_.refs_6_), channel_id=1, source_target_pairs={{17,16},{18,17},{19,18},{20,19},{21,20},{22,21},{23,22},{24,23},{2... | collective-permute-start | bytes 1179656 | tf_op jit(solution)/shard_map/ppermute | solution.py:378
  10.9 2.4 %copy-start.21 = (bf16[128,1536]{1,0:T(8,128)(2,1)}, bf16[128,1536]{1,0:T(8,128)(2,1)S(1)}, u32[]{:S(2)}) copy-start(bf16[128,1536]{1,0:T(8,128)(2,1)S(1)} %collective-permute-done.2.refs_2_.refs_7_) | copy-start | bytes 1179652
  13.2 25.4 %collective-permute-start.3 = (bf16[128,1536]{1,0:T(8,128)(2,1)}, bf16[128,1536]{1,0:T(8,128)(2,1)}, u32[]{:S(2)}, u32[]{:S(2)}) collective-permute-start(bf16[128,1536]{1,0:T(8,128)(2,1)} %filter.4.refs_6_.refs_8_), channel_id=1, source_target_pairs={{16,0},{17,1},{18,2},{19,3},{20,4},{21,5},{22,6},{23,7},{24,8},{25... | collective-permute-start | bytes 1179656 | tf_op jit(solution)/shard_map/ppermute | solution.py:398
  15.5 2.4 %copy-start.19 = (bf16[128,1536]{1,0:T(8,128)(2,1)}, bf16[128,1536]{1,0:T(8,128)(2,1)S(1)}, u32[]{:S(2)}) copy-start(bf16[128,1536]{1,0:T(8,128)(2,1)S(1)} %collective-permute-done.5.refs_2_.refs_7_) | copy-start | bytes 1179652
  17.9 28.1 %collective-permute-start.6 = (bf16[128,1536]{1,0:T(8,128)(2,1)}, bf16[128,1536]{1,0:T(8,128)(2,1)}, u32[]{:S(2)}, u32[]{:S(2)}) collective-permute-start(bf16[128,1536]{1,0:T(8,128)(2,1)} %filter.5.refs_6_.refs_8_), channel_id=1, source_target_pairs={{16,0},{17,1},{18,2},{19,3},{20,4},{21,5},{22,6},{23,7},{24,8},{25... | collective-permute-start | bytes 1179656 | tf_op jit(solution)/shard_map/ppermute | solution.py:398
  19.9 7.4 %collective-permute-start.4 = (bf16[128,1024]{1,0:T(8,128)(2,1)S(1)}, bf16[128,1024]{1,0:T(8,128)(2,1)S(1)}, u32[]{:S(2)}, u32[]{:S(2)}) collective-permute-start(bf16[128,1024]{1,0:T(8,128)(2,1)S(1)} %weigh.3.refs_1_.refs_6_), channel_id=1, source_target_pairs={{17,16},{18,17},{19,18},{20,19},{21,20},{22,21},{23,22},{24,23},{2... | collective-permute-start | bytes 786440 | tf_op jit(solution)/shard_map/ppermute | solution.py:378
  27.3 3.1 %copy-start.14 = (bf16[128,1024]{1,0:T(8,128)(2,1)}, bf16[128,1024]{1,0:T(8,128)(2,1)S(1)}, u32[]{:S(2)}) copy-start(bf16[128,1024]{1,0:T(8,128)(2,1)S(1)} %collective-permute-done.4.refs_2_.refs_7_) | copy-start | bytes 786436
  28.5 21.3 %collective-permute-start.7 = (bf16[128,512]{1,0:T(8,128)(2,1)}, bf16[128,512]{1,0:T(8,128)(2,1)}, u32[]{:S(2)}, u32[]{:S(2)}) collective-permute-start(bf16[128,512]{1,0:T(8,128)(2,1)} %filter.6.refs_6_.refs_8_), channel_id=1, source_target_pairs={{16,0},{17,1},{18,2},{19,3},{20,4},{21,5},{22,6},{23,7},{24,8},{25... | collective-permute-start | bytes 393224 | tf_op jit(solution)/shard_map/ppermute | solution.py:398
  31.5 20.1 %collective-permute-start.8 = (bf16[128,512]{1,0:T(8,128)(2,1)}, bf16[128,512]{1,0:T(8,128)(2,1)}, u32[]{:S(2)}, u32[]{:S(2)}) collective-permute-start(bf16[128,512]{1,0:T(8,128)(2,1)} %filter.7.refs_4_.refs_8_), channel_id=1, source_target_pairs={{16,0},{17,1},{18,2},{19,3},{20,4},{21,5},{22,6},{23,7},{24,8},{25... | collective-permute-start | bytes 393224 | tf_op jit(solution)/shard_map/ppermute | solution.py:398
  33.9 0.9 %copy-start.5 = (f32[128,1536]{1,0:T(8,128)}, f32[128,1536]{1,0:T(8,128)S(1)}, u32[]{:S(2)}) copy-start(f32[128,1536]{1,0:T(8,128)S(1)} %turned_filter.5.refs_10_.refs_5_) | copy-start | bytes 2359300
  34.8 0.9 %copy-start.8 = (f32[128,1536]{1,0:T(8,128)}, f32[128,1536]{1,0:T(8,128)S(1)}, u32[]{:S(2)}) copy-start(f32[128,1536]{1,0:T(8,128)S(1)} %turned_filter.4.refs_10_.refs_5_) | copy-start | bytes 2359300
  35.7 1.1 %copy-start.6 = (f32[128,1536]{1,0:T(8,128)S(1)}, f32[128,1536]{1,0:T(8,128)}, u32[]{:S(2)}) copy-start(f32[128,1536]{1,0:T(8,128)} %copy-done.5) | copy-start | bytes 2359300
  36.9 0.7 copy-start.16
  37.6 0.9 %copy-start.17 = (f32[128,512]{1,0:T(8,128)S(1)}, f32[128,512]{1,0:T(8,128)}, u32[]{:S(2)}) copy-start(f32[128,512]{1,0:T(8,128)} %copy-done.16) | copy-start | bytes 786436
  38.5 1.2 %copy-start.3 = (bf16[1,128,4096]{2,1,0:T(8,128)(2,1)S(1)}, bf16[1,128,4096]{2,1,0:T(8,128)(2,1)}, u32[]{:S(2)}) copy-start(bf16[1,128,4096]{2,1,0:T(8,128)(2,1)} %param.8) | copy-start | bytes 3145732
  38.5 1.5 %copy-start.4 = (bf16[1,128,4096]{2,1,0:T(8,128)(2,1)S(1)}, bf16[1,128,4096]{2,1,0:T(8,128)(2,1)}, u32[]{:S(2)}) copy-start(bf16[1,128,4096]{2,1,0:T(8,128)(2,1)} %param.10) | copy-start | bytes 3145732
  38.6 1.8 %copy-start.9 = (f32[128,1536]{1,0:T(8,128)S(1)}, f32[128,1536]{1,0:T(8,128)}, u32[]{:S(2)}) copy-start(f32[128,1536]{1,0:T(8,128)} %copy-done.8) | copy-start | bytes 2359300
  38.6 7.4 %copy-start.7 = (f32[128,1536]{1,0:T(8,128)S(1)}, f32[128,1536]{1,0:T(8,128)}, u32[]{:S(2)}) copy-start(f32[128,1536]{1,0:T(8,128)} %copy-done.5) | copy-start | bytes 2359300
  38.6 7.4 %copy-start.11 = (bf16[128,1536]{1,0:T(8,128)(2,1)S(1)}, bf16[128,1536]{1,0:T(8,128)(2,1)}, u32[]{:S(2)}) copy-start(bf16[128,1536]{1,0:T(8,128)(2,1)} %copy-done.10) | copy-start | bytes 1179652
  40.3 1.0 %copy-start.13 = (bf16[128,1536]{1,0:T(8,128)(2,1)S(1)}, bf16[128,1536]{1,0:T(8,128)(2,1)}, u32[]{:S(2)}) copy-start(bf16[128,1536]{1,0:T(8,128)(2,1)} %copy-done.12) | copy-start | bytes 1179652
  41.3 1.0 %copy-start.22 = (bf16[128,1536]{1,0:T(8,128)(2,1)S(1)}, bf16[128,1536]{1,0:T(8,128)(2,1)}, u32[]{:S(2)}) copy-start(bf16[128,1536]{1,0:T(8,128)(2,1)} %copy-done.21) | copy-start | bytes 1179652
  42.3 3.7 %copy-start.20 = (bf16[128,1536]{1,0:T(8,128)(2,1)S(1)}, bf16[128,1536]{1,0:T(8,128)(2,1)}, u32[]{:S(2)}) copy-start(bf16[128,1536]{1,0:T(8,128)(2,1)} %copy-done.19) | copy-start | bytes 1179652
  46.0 3.7 %copy-start.15 = (bf16[128,1024]{1,0:T(8,128)(2,1)S(1)}, bf16[128,1024]{1,0:T(8,128)(2,1)}, u32[]{:S(2)}) copy-start(bf16[128,1024]{1,0:T(8,128)(2,1)} %copy-done.14) | copy-start | bytes 786436
  46.0 3.7 %copy-start.18 = (f32[128,512]{1,0:T(8,128)S(1)}, f32[128,512]{1,0:T(8,128)}, u32[]{:S(2)}) copy-start(f32[128,512]{1,0:T(8,128)} %copy-done.16) | copy-start | bytes 786436
  53.4 4.5 %collective-permute-start.9 = (f32[8,18,128]{2,1,0:T(8,128)S(1)}, f32[8,18,128]{2,1,0:T(8,128)S(1)}, u32[]{:S(2)}, u32[]{:S(2)}) collective-permute-start(f32[8,18,128]{2,1,0:T(8,128)S(1)} %get-tuple-element.33), channel_id=1, source_target_pairs={{0,1},{1,0},{2,3},{3,2},{4,5},{5,4},{6,7},{7,6},{8,9},{9,8},{10,11... | collective-permute-start | bytes 221192 | tf_op jit(solution)/shard_map/ppermute | solution.py:459
  58.0 4.2 %collective-permute-start.10 = (f32[4,18,128]{2,1,0:T(8,128)S(1)}, f32[4,18,128]{2,1,0:T(8,128)S(1)}, u32[]{:S(2)}, u32[]{:S(2)}) collective-permute-start(f32[4,18,128]{2,1,0:T(8,128)S(1)} %get-tuple-element.35), channel_id=1, source_target_pairs={{0,2},{1,3},{2,0},{3,1},{4,6},{5,7},{6,4},{7,5},{8,10},{9,11},{10,... | collective-permute-start | bytes 110600 | tf_op jit(solution)/shard_map/ppermute | solution.py:459
  62.2 3.9 %collective-permute-start.11 = (f32[2,18,128]{2,1,0:T(8,128)S(1)}, f32[2,18,128]{2,1,0:T(8,128)S(1)}, u32[]{:S(2)}, u32[]{:S(2)}) collective-permute-start(f32[2,18,128]{2,1,0:T(8,128)S(1)} %get-tuple-element.37), channel_id=1, source_target_pairs={{0,4},{1,5},{2,6},{3,7},{4,0},{5,1},{6,2},{7,3},{8,12},{9,13},{10,... | collective-permute-start | bytes 55304 | tf_op jit(solution)/shard_map/ppermute | solution.py:459
  66.1 4.7 %copy-start.24 = (f32[1,128,16]{1,2,0:T(8,128)S(1)}, f32[1,128,16]{1,2,0:T(8,128)}, u32[]{:S(2)}) copy-start(f32[1,128,16]{1,2,0:T(8,128)} %param.13) | copy-start | bytes 24580
  66.1 4.7 %collective-permute-start.12 = (f32[1,18,128]{2,1,0:T(8,128)S(1)}, f32[1,18,128]{2,1,0:T(8,128)S(1)}, u32[]{:S(2)}, u32[]{:S(2)}) collective-permute-start(f32[1,18,128]{2,1,0:T(8,128)S(1)} %get-tuple-element.39), channel_id=1, source_target_pairs={{0,8},{1,9},{2,10},{3,11},{4,12},{5,13},{6,14},{7,15},{8,0},{9,1},... | collective-permute-start | bytes 27656 | tf_op jit(solution)/shard_map/ppermute | solution.py:459
  70.7 0.7 copy-start.25

commit v5 on v4

--- a/solution.py
+++ b/solution.py
@@ -11,8 +11,8 @@
 BF16 = jnp.bfloat16
 LANES = 128
 SUB = 32
-CHUNK_EDGES = (0, 3, 6, 7, 8)
-HALO_EDGES = (0, 3, 6, 8)
+CHUNK_EDGES = (0, 2, 4, 6, 7, 8)
+HALO_EDGES = (0, 2, 4, 6, 8)
 
 
 def lane_of(shape):
@@ -21,6 +21,10 @@
 
 def row_of(shape):
     return lax.broadcasted_iota(jnp.int32, shape, 0)
+
+
+def first_section(role):
+    return (role[0] & 1) > 0
 
 
 def times(a, b):
@@ -87,13 +91,13 @@
 
 
 def weigh_kernel(role, gate, incoming, out):
-    @pl.when(role[0] == 0)
+    @pl.when(jnp.logical_not(first_section(role)))
     def _():
         out[...] = times(gate[...], incoming[...])
 
 
 def first_weigh_kernel(block, role, gate, incoming, out, gate_part, incoming_part, sems):
-    @pl.when(role[0] == 0)
+    @pl.when(jnp.logical_not(first_section(role)))
     def _():
         tiles = [pl.ds(at, block) for at in range(0, out.shape[1], block)]
         copies = [
@@ -113,7 +117,7 @@
 
 
 def taps_kernel(role, filters, taps_out):
-    pick, _ = tap_matrix(role[0] > 0, filters[...])
+    pick, _ = tap_matrix(first_section(role), filters[...])
     taps_out[...] = lax.dot_general(
         filters[...], pick.astype(BF16), (((0,), (0,)), ((), ())), preferred_element_type=F32
     )
@@ -145,7 +149,7 @@
 
 
 def filter_kernel(group_size, role, own, halo, taps, mid, incoming, outgoing):
-    @pl.when(role[0] == 0)
+    @pl.when(jnp.logical_not(first_section(role)))
     def _():
         for first in range(0, own.shape[1], LANES):
             cols = pl.ds(first, LANES)
@@ -156,7 +160,7 @@
 
 
 def turned_filter_kernel(group_size, role, mid, mid_halo, taps, filtered):
-    @pl.when(role[0] > 0)
+    @pl.when(first_section(role))
     def _():
         for first in range(0, mid.shape[1], LANES):
             cols = pl.ds(first, LANES)
@@ -167,7 +171,7 @@
     group_size, role, gate, mid, inputs, mid_halo, inputs_halo, own, halo, outgoing, received, filtered,
     tap_grad, steer_grad, left, right_own, right_halo,
 ):
-    reverse = role[0] > 0
+    reverse = first_section(role)
     width = own.shape[1]
     half = LANES // 2
     per_half = half // group_size
@@ -189,7 +193,7 @@
         right_halo[...] = halo[...]
         steer_grad[...] = jnp.sum(outgoing[...].astype(F32), 0, keepdims=True)
 
-    mask = near(role[0], (SUB, LANES))
+    mask = near(role[0] & 1, (SUB, LANES))
     lane_group = (lane_of((SUB, 2 * LANES)) % half) // group_size
     nothing = jnp.zeros((SUB, 2 * LANES), BF16)
     for pair in range(width // LANES):
@@ -213,12 +217,12 @@
         tap_grad[pl.ds(8 * pair, 8), :] = diagonal_sums(blocks)
 
 
-def halves_of(place, step, zero, one):
-    mine = (place[0] >> step) & 1 > 0
+def halves_of(role, step, zero, one):
+    mine = (role[0] >> (step + 1)) & 1 > 0
     return jnp.where(mine, zero, one), jnp.where(mine, one, zero)
 
 
-def pack_kernel(owners, place, *refs):
+def pack_kernel(owners, role, *refs):
     count = (len(refs) - 2) // 2
     taps, steers, (give, keep) = refs[:count], refs[count : 2 * count], refs[2 * count :]
     groups = sum(ref.shape[0] for ref in taps) // owners
@@ -244,7 +248,7 @@
         at = 0
         for zero, one in zip(packed(low), packed(high)):
             lines = zero.shape[0]
-            give[i, pl.ds(at, lines), :], keep[i, pl.ds(at, lines), :] = halves_of(place, 0, zero, one)
+            give[i, pl.ds(at, lines), :], keep[i, pl.ds(at, lines), :] = halves_of(role, 0, zero, one)
             at += lines
 
 
@@ -255,12 +259,12 @@
     return order
 
 
-def fold_kernel(step, place, kept, arrived, give, keep):
+def fold_kernel(step, role, kept, arrived, give, keep):
     count = give.shape[0]
     for i in range(count):
         zero = kept[i] + arrived[i]
         one = kept[count + i] + arrived[count + i]
-        give[i], keep[i] = halves_of(place, step, zero, one)
+        give[i], keep[i] = halves_of(role, step, zero, one)
 
 
 def step_kernel(role, kept, arrived, steer_second, filter_second, steer_out, filter_out):
@@ -269,7 +273,7 @@
     tap_grad = total[:groups]
     lane = lane_of(tap_grad.shape)
     mirrored = jnp.where(lane == 0, 0, tap_grad.shape[1] - lane)
-    tap_grad = jnp.take_along_axis(tap_grad, jnp.where(role[0] > 0, mirrored, lane), axis=1)
+    tap_grad = jnp.take_along_axis(tap_grad, jnp.where(first_section(role), mirrored, lane), axis=1)
     filter_out[...] = tap_grad / jnp.sqrt(filter_second[...] + tap_grad * tap_grad)
     channels = steer_out.shape[1]
     for row in range(pl.cdiv(channels, LANES)):
@@ -314,7 +318,7 @@
     group_size = channels // groups
     sections, seqs = lax.axis_size("section"), lax.axis_size("seq")
     my_section = lax.axis_index("section")
-    role = (my_section == 0).astype(jnp.int32).reshape(1)
+    role = (2 * lax.axis_index("seq") + (my_section == 0)).astype(jnp.int32).reshape(1)
 
     edges = [channels * eighths // 8 for eighths in CHUNK_EDGES]
     bounds = list(zip(edges[:-1], edges[1:]))
@@ -439,7 +443,6 @@
 
     own_channels = channels // seqs
     lines = groups // seqs + pl.cdiv(own_channels, LANES)
-    place = lax.axis_index("seq").reshape(1)
     steps = seqs.bit_length() - 1
 
     def halves(count):
@@ -453,7 +456,7 @@
         out_shape=halves(seqs // 2),
         compiler_params=SMALL,
         name="pack",
-    )(place, *tap_grads, *steer_grads)
+    )(role, *tap_grads, *steer_grads)
     for step in range(steps):
         route = [(i, i ^ (1 << step)) for i in range(seqs)]
         arrived = lax.ppermute(give, "seq", route)
@@ -465,7 +468,7 @@
                 out_shape=halves(keep.shape[0] // 2),
                 compiler_params=SMALL,
                 name="fold",
-            )(place, keep, arrived)
+            )(role, keep, arrived)
     steer_step, filter_step = pl.pallas_call(
         step_kernel,
         in_specs=[SMEM] + [vmem] * 4,

time: 72.8 us -> 60.7 us (0.83)
  the two profiles are of different devices: /device:TPU:14 before, /device:TPU:0 now
where the time goes in v5:
time: 60.7 us; the launch traced here: 60.2 us
  starting transfers between devices  26.7 us (44%)
  waiting for transfers between devices  14.5 us (24%)
  Pallas kernels  13.9 us (23%)
  local copies, waits for them, and re-layouts  4.11 us (7%)
  between operations  0.98 us (2%)
    ppermute x4, starting transfers between devices, body(): arrived = lax.ppermute(give, 'seq', route)  10.5 us
    ppermute x5, waiting for transfers between devices, body(): received.append(lax.ppermute(out, 'section', down))  8.02 us
    pallas_call x5, Pallas kernels, body(): call(functools.partial(grad_kernel, group_size), (width // block,), [SMEM...  7.68 us
    ppermute x4, waiting for transfers between devices, body(): arrived = lax.ppermute(give, 'seq', route)  6.49 us
    ppermute x5, starting transfers between devices, body(): received.append(lax.ppermute(out, 'section', down))  6.45 us
    ppermute x1, starting transfers between devices, body(): inputs_halo = lax.ppermute(inputs_sent, ('section', 'seq'), ahead)  4.54 us
    pallas_call x5, Pallas kernels, body(): call(functools.partial(turned_filter_kernel, group_size), ((last - first)...  4.13 us
    unnamed x16, local copies, waits for them, and re-layouts  4.11 us
  transfers between devices with their start and end apart: 15, of which 7 were waited for; matrix products, arithmetic and copies ran while one was open for 0% of the time, Pallas kernels for 20%

profile of v5, /device:TPU:0, one launch (start us, length us, event | category | flops | bytes accessed | tf_op | source)
XLA Modules:
  0.0 60.2 jit_solution(10685368380065988326)
XLA Ops:
  0.6 0.0 copy-start
  0.6 0.0 copy-start.1
  0.7 1.2 %copy-done = bf16[1,128,4096]{2,1,0:T(8,128)(2,1)S(1)} copy-done((bf16[1,128,4096]{2,1,0:T(8,128)(2,1)S(1)}, bf16[1,128,4096]{2,1,0:T(8,128)(2,1)}, u32[]{:S(2)}) %copy-start) | copy-done | bytes 1048600
  1.9 2.4 %collective-permute-start = (bf16[128,4096]{1,0:T(8,128)(2,1)S(1)}, bf16[128,4096]{1,0:T(8,128)(2,1)S(1)}, u32[]{:S(2)}, u32[]{:S(2)}) collective-permute-start(bf16[128,4096]{1,0:T(8,128)(2,1)S(1)} %bitcast.11), channel_id=1, source_target_pairs={{0,1},{1,2},{2,3},{3,4},{4,5},{5,6},{6,7},{7,8},{8,9},{9,10},{10,1... | collective-permute-start | bytes 3145736 | tf_op jit(solution)/shard_map/ppermute | solution.py:380
  4.3 4.5 %collective-permute-start.1 = (bf16[128,4096]{1,0:T(8,128)(2,1)}, bf16[128,4096]{1,0:T(8,128)(2,1)S(1)}, u32[]{:S(2)}, u32[]{:S(2)}) collective-permute-start(bf16[128,4096]{1,0:T(8,128)(2,1)} %bitcast.36), channel_id=1, source_target_pairs={{0,1},{1,2},{2,3},{3,4},{4,5},{5,6},{6,7},{7,8},{8,9},{9,10},{10,1... | collective-permute-start | bytes 3145736 | tf_op jit(solution)/shard_map/ppermute | solution.py:381
  8.8 0.7 %collective-permute-start.2 = (bf16[128,1024]{1,0:T(8,128)(2,1)S(1)}, bf16[128,1024]{1,0:T(8,128)(2,1)S(1)}, u32[]{:S(2)}, u32[]{:S(2)}) collective-permute-start(bf16[128,1024]{1,0:T(8,128)(2,1)S(1)} %first_weigh.1.refs_1_.refs_3_.refs_6_), channel_id=1, source_target_pairs={{17,16},{18,17},{19,18},{20,19},{21,20},{22,21},{23,22},{24,23},{2... | collective-permute-start | bytes 786440 | tf_op jit(solution)/shard_map/ppermute | solution.py:382
  9.5 0.0 copy-done.1
  9.5 0.0 copy-start.2
  9.5 1.2 %copy-done.2 = bf16[1,128,4096]{2,1,0:T(8,128)(2,1)S(1)} copy-done((bf16[1,128,4096]{2,1,0:T(8,128)(2,1)S(1)}, bf16[1,128,4096]{2,1,0:T(8,128)(2,1)}, u32[]{:S(2)}) %copy-start.2) | copy-done | bytes 1048600
  10.8 0.1 weigh.3.refs_3_.refs_1_.refs_6_
  10.9 0.7 %collective-permute-start.6 = (bf16[128,1024]{1,0:T(8,128)(2,1)S(1)}, bf16[128,1024]{1,0:T(8,128)(2,1)S(1)}, u32[]{:S(2)}, u32[]{:S(2)}) collective-permute-start(bf16[128,1024]{1,0:T(8,128)(2,1)S(1)} %weigh.3.refs_3_.refs_1_.refs_6_), channel_id=1, source_target_pairs={{17,16},{18,17},{19,18},{20,19},{21,20},{22,21},{23,22},{24,23},{2... | collective-permute-start | bytes 786440 | tf_op jit(solution)/shard_map/ppermute | solution.py:382
  11.6 0.2 weigh.4.refs_3_.refs_1_.refs_6_
  11.7 0.0 copy-start.5
  11.8 0.8 %collective-permute-start.5 = (bf16[128,1024]{1,0:T(8,128)(2,1)S(1)}, bf16[128,1024]{1,0:T(8,128)(2,1)S(1)}, u32[]{:S(2)}, u32[]{:S(2)}) collective-permute-start(bf16[128,1024]{1,0:T(8,128)(2,1)S(1)} %weigh.4.refs_3_.refs_1_.refs_6_), channel_id=1, source_target_pairs={{17,16},{18,17},{19,18},{20,19},{21,20},{22,21},{23,22},{24,23},{2... | collective-permute-start | bytes 786440 | tf_op jit(solution)/shard_map/ppermute | solution.py:382
  12.6 0.2 weigh.5.refs_1_.refs_6_
  12.7 0.0 collective-permute-done.2.refs_2_.refs_7_
  12.8 0.7 %collective-permute-start.4 = (bf16[128,1024]{1,0:T(8,128)(2,1)S(1)}, bf16[128,1024]{1,0:T(8,128)(2,1)S(1)}, u32[]{:S(2)}, u32[]{:S(2)}) collective-permute-start(bf16[128,1024]{1,0:T(8,128)(2,1)S(1)} %weigh.5.refs_1_.refs_6_), channel_id=1, source_target_pairs={{17,16},{18,17},{19,18},{20,19},{21,20},{22,21},{23,22},{24,23},{2... | collective-permute-start | bytes 786440 | tf_op jit(solution)/shard_map/ppermute | solution.py:382
  13.4 0.0 copy-done.5
  13.4 0.2 taps.1.refs_3_
  13.6 0.2 filter.5.refs_6_.refs_8_
  13.8 0.0 collective-permute-done.6.refs_2_.refs_7_
  13.8 1.3 %collective-permute-start.3 = (bf16[128,1024]{1,0:T(8,128)(2,1)S(1)}, bf16[128,1024]{1,0:T(8,128)(2,1)S(1)}, u32[]{:S(2)}, u32[]{:S(2)}) collective-permute-start(bf16[128,1024]{1,0:T(8,128)(2,1)S(1)} %filter.5.refs_6_.refs_8_), channel_id=1, source_target_pairs={{16,0},{17,1},{18,2},{19,3},{20,4},{21,5},{22,6},{23,7},{24,8},{25... | collective-permute-start | bytes 786440 | tf_op jit(solution)/shard_map/ppermute | solution.py:402
  15.1 0.2 filter.6.refs_6_.refs_8_
  15.3 0.0 collective-permute-done.5.refs_2_.refs_7_
  15.4 1.3 %collective-permute-start.7 = (bf16[128,1024]{1,0:T(8,128)(2,1)S(1)}, bf16[128,1024]{1,0:T(8,128)(2,1)S(1)}, u32[]{:S(2)}, u32[]{:S(2)}) collective-permute-start(bf16[128,1024]{1,0:T(8,128)(2,1)S(1)} %filter.6.refs_6_.refs_8_), channel_id=1, source_target_pairs={{16,0},{17,1},{18,2},{19,3},{20,4},{21,5},{22,6},{23,7},{24,8},{25... | collective-permute-start | bytes 786440 | tf_op jit(solution)/shard_map/ppermute | solution.py:402
  16.7 0.2 filter.7.refs_6_.refs_8_
  16.9 0.0 collective-permute-done.4.refs_2_.refs_7_
  16.9 1.3 %collective-permute-start.8 = (bf16[128,1024]{1,0:T(8,128)(2,1)S(1)}, bf16[128,1024]{1,0:T(8,128)(2,1)S(1)}, u32[]{:S(2)}, u32[]{:S(2)}) collective-permute-start(bf16[128,1024]{1,0:T(8,128)(2,1)S(1)} %filter.7.refs_6_.refs_8_), channel_id=1, source_target_pairs={{16,0},{17,1},{18,2},{19,3},{20,4},{21,5},{22,6},{23,7},{24,8},{25... | collective-permute-start | bytes 786440 | tf_op jit(solution)/shard_map/ppermute | solution.py:402
  18.2 5.8 %collective-permute-done.3.refs_9_ = bf16[128,1024]{1,0:T(8,128)(2,1)S(1)} collective-permute-done((bf16[128,1024]{1,0:T(8,128)(2,1)S(1)}, bf16[128,1024]{1,0:T(8,128)(2,1)S(1)}, u32[]{:S(2)}, u32[]{:S(2)}) %collective-permute-start.3) | collective-permute-done | bytes 262176 | tf_op jit(solution)/shard_map/ppermute | solution.py:402
  24.0 1.3 %collective-permute-start.9 = (bf16[128,512]{1,0:T(8,128)(2,1)S(1)}, bf16[128,512]{1,0:T(8,128)(2,1)S(1)}, u32[]{:S(2)}, u32[]{:S(2)}) collective-permute-start(bf16[128,512]{1,0:T(8,128)(2,1)S(1)} %filter.8.refs_6_.refs_8_), channel_id=1, source_target_pairs={{16,0},{17,1},{18,2},{19,3},{20,4},{21,5},{22,6},{23,7},{24,8},{25... | collective-permute-start | bytes 393224 | tf_op jit(solution)/shard_map/ppermute | solution.py:402
  25.4 0.0 collective-permute-done.refs_2_.refs_4_
  25.4 1.3 %collective-permute-start.10 = (bf16[128,512]{1,0:T(8,128)(2,1)S(1)}, bf16[128,512]{1,0:T(8,128)(2,1)S(1)}, u32[]{:S(2)}, u32[]{:S(2)}) collective-permute-start(bf16[128,512]{1,0:T(8,128)(2,1)S(1)} %filter.9.refs_4_.refs_8_), channel_id=1, source_target_pairs={{16,0},{17,1},{18,2},{19,3},{20,4},{21,5},{22,6},{23,7},{24,8},{25... | collective-permute-start | bytes 393224 | tf_op jit(solution)/shard_map/ppermute | solution.py:402
  26.7 1.1 %turned_filter.5.refs_10_.refs_5_ = f32[128,1024]{1,0:T(8,128)S(1)} custom-call(s32[1]{0:T(128)} %bitcast.role.refs_0_, bf16[128,4096]{1,0:T(8,128)(2,1)S(1)} %bitcast.17, bf16[128,4096]{1,0:T(8,128)(2,1)S(1)} %collective-permute-done.refs_2_.refs_4_, f32[256,128]{1,0:T(8,128)S(1)} %taps.1.refs_3_, bf16[128,512]{1,0:T(8,128)(2,1)S(1)} %filter.9.refs_4_.refs_8_), custom_call_target="tpu_custom_call" | custom-call | flops 1000 | tf_op jit(solution)/shard_map/turned_filter/pallas_call | solution.py:412
  27.7 1.1 %turned_filter.6.refs_10_.refs_5_ = f32[128,1024]{1,0:T(8,128)S(1)} custom-call(s32[1]{0:T(128)} %bitcast.role.refs_0_, bf16[128,4096]{1,0:T(8,128)(2,1)S(1)} %bitcast.18, bf16[128,4096]{1,0:T(8,128)(2,1)S(1)} %collective-permute-done.refs_2_.refs_4_, f32[256,128]{1,0:T(8,128)S(1)} %taps.1.refs_3_, bf16[128,512]{1,0:T(8,128)(2,1)S(1)} %filter.9.refs_4_.refs_8_, ...), custom_call_target="tpu_custom_call" | custom-call | flops 1000 | tf_op jit(solution)/shard_map/turned_filter/pallas_call | solution.py:412
  28.8 1.1 %turned_filter.7.refs_10_.refs_5_ = f32[128,1024]{1,0:T(8,128)S(1)} custom-call(s32[1]{0:T(128)} %bitcast.role.refs_0_, bf16[128,4096]{1,0:T(8,128)(2,1)S(1)} %bitcast.19, bf16[128,4096]{1,0:T(8,128)(2,1)S(1)} %collective-permute-done.refs_2_.refs_4_, f32[256,128]{1,0:T(8,128)S(1)} %taps.1.refs_3_, bf16[128,512]{1,0:T(8,128)(2,1)S(1)} %filter.9.refs_4_.refs_8_, ...), custom_call_target="tpu_custom_call" | custom-call | flops 1000 | tf_op jit(solution)/shard_map/turned_filter/pallas_call | solution.py:412
  29.9 0.5 turned_filter.8.refs_10_.refs_5_
  30.4 0.0 copy-start.3
  30.4 0.0 copy-start.4
  30.4 0.5 turned_filter.9.refs_10_
  30.9 0.0 collective-permute-done.1.refs_5_
  30.9 0.7 %copy-done.3 = bf16[1,128,4096]{2,1,0:T(8,128)(2,1)S(1)} copy-done((bf16[1,128,4096]{2,1,0:T(8,128)(2,1)S(1)}, bf16[1,128,4096]{2,1,0:T(8,128)(2,1)}, u32[]{:S(2)}) %copy-start.3) | copy-done | bytes 1048600
  31.6 0.3 copy-done.4
  31.9 1.9 %grads.5 = (f32[64,128]{1,0:T(8,128)S(1)}, f32[1,1024]{1,0:T(1,128)S(1)}) custom-call(s32[1]{0:T(128)} %bitcast.role.refs_0_, bf16[128,4096]{1,0:T(8,128)(2,1)S(1)} %bitcast.31, bf16[128,4096]{1,0:T(8,128)(2,1)S(1)} %bitcast.22, bf16[128,4096]{1,0:T(8,128)(2,1)S(1)} %bitcast.37, bf16[128,4096]{1,0:T(8,128)(2,1)S(1)} %collective-permute-done.refs_2_.refs_4_, ...), custom_call_target="tpu_custom_call" | custom-call | flops 2000 | tf_op jit(solution)/shard_map/grads/pallas_call | solution.py:429
  33.8 0.0 collective-permute-done.7.refs_9_
  33.8 2.0 %grads.6 = (f32[64,128]{1,0:T(8,128)S(1)}, f32[1,1024]{1,0:T(1,128)S(1)}) custom-call(s32[1]{0:T(128)} %bitcast.role.refs_0_, bf16[128,4096]{1,0:T(8,128)(2,1)S(1)} %bitcast.32, bf16[128,4096]{1,0:T(8,128)(2,1)S(1)} %bitcast.23, bf16[128,4096]{1,0:T(8,128)(2,1)S(1)} %bitcast.38, bf16[128,4096]{1,0:T(8,128)(2,1)S(1)} %collective-permute-done.refs_2_.refs_4_, ...), custom_call_target="tpu_custom_call" | custom-call | flops 2000 | tf_op jit(solution)/shard_map/grads/pallas_call | solution.py:429
  35.8 0.0 collective-permute-done.8.refs_9_
  35.8 2.0 %grads.7 = (f32[64,128]{1,0:T(8,128)S(1)}, f32[1,1024]{1,0:T(1,128)S(1)}) custom-call(s32[1]{0:T(128)} %bitcast.role.refs_0_, bf16[128,4096]{1,0:T(8,128)(2,1)S(1)} %bitcast.33, bf16[128,4096]{1,0:T(8,128)(2,1)S(1)} %bitcast.24, bf16[128,4096]{1,0:T(8,128)(2,1)S(1)} %bitcast.39, bf16[128,4096]{1,0:T(8,128)(2,1)S(1)} %collective-permute-done.refs_2_.refs_4_, ...), custom_call_target="tpu_custom_call" | custom-call | flops 2000 | tf_op jit(solution)/shard_map/grads/pallas_call | solution.py:429
  37.8 0.3 collective-permute-done.9.refs_9_
  38.1 0.9 %grads.8 = (f32[32,128]{1,0:T(8,128)S(1)}, f32[1,512]{1,0:T(1,128)S(1)}) custom-call(s32[1]{0:T(128)} %bitcast.role.refs_0_, bf16[128,4096]{1,0:T(8,128)(2,1)S(1)} %bitcast.34, bf16[128,4096]{1,0:T(8,128)(2,1)S(1)} %bitcast.25, bf16[128,4096]{1,0:T(8,128)(2,1)S(1)} %bitcast.40, bf16[128,4096]{1,0:T(8,128)(2,1)S(1)} %collective-permute-done.refs_2_.refs_4_, ...), custom_call_target="tpu_custom_call" | custom-call | flops 2000 | tf_op jit(solution)/shard_map/grads/pallas_call | solution.py:429
  39.0 1.9 %collective-permute-done.10.refs_9_ = bf16[128,512]{1,0:T(8,128)(2,1)S(1)} collective-permute-done((bf16[128,512]{1,0:T(8,128)(2,1)S(1)}, bf16[128,512]{1,0:T(8,128)(2,1)S(1)}, u32[]{:S(2)}, u32[]{:S(2)}) %collective-permute-start.10) | collective-permute-done | bytes 131104 | tf_op jit(solution)/shard_map/ppermute | solution.py:402
  40.9 0.9 %grads.9 = (f32[32,128]{1,0:T(8,128)S(1)}, f32[1,512]{1,0:T(1,128)S(1)}) custom-call(s32[1]{0:T(128)} %bitcast.role.refs_0_, bf16[128,4096]{1,0:T(8,128)(2,1)S(1)} %bitcast.35, bf16[128,4096]{1,0:T(8,128)(2,1)S(1)} %bitcast.26, bf16[128,4096]{1,0:T(8,128)(2,1)S(1)} %bitcast.41, bf16[128,4096]{1,0:T(8,128)(2,1)S(1)} %collective-permute-done.refs_2_.refs_4_, ...), custom_call_target="tpu_custom_call" | custom-call | flops 2000 | tf_op jit(solution)/shard_map/grads/pallas_call | solution.py:429
  41.8 0.8 %collective-permute-start.11 = (f32[8,18,128]{2,1,0:T(8,128)S(1)}, f32[8,18,128]{2,1,0:T(8,128)S(1)}, u32[]{:S(2)}, u32[]{:S(2)}) collective-permute-start(f32[8,18,128]{2,1,0:T(8,128)S(1)} %get-tuple-element.37), channel_id=1, source_target_pairs={{0,1},{1,0},{2,3},{3,2},{4,5},{5,4},{6,7},{7,6},{8,9},{9,8},{10,11... | collective-permute-start | bytes 221192 | tf_op jit(solution)/shard_map/ppermute | solution.py:462
  42.6 0.9 %collective-permute-done.11.arrived = f32[8,18,128]{2,1,0:T(8,128)S(1)} collective-permute-done((f32[8,18,128]{2,1,0:T(8,128)S(1)}, f32[8,18,128]{2,1,0:T(8,128)S(1)}, u32[]{:S(2)}, u32[]{:S(2)}) %collective-permute-start.11) | collective-permute-done | bytes 73760 | tf_op jit(solution)/shard_map/ppermute | solution.py:462
  43.6 3.7 %collective-permute-start.12 = (f32[4,18,128]{2,1,0:T(8,128)S(1)}, f32[4,18,128]{2,1,0:T(8,128)S(1)}, u32[]{:S(2)}, u32[]{:S(2)}) collective-permute-start(f32[4,18,128]{2,1,0:T(8,128)S(1)} %get-tuple-element.39), channel_id=1, source_target_pairs={{0,2},{1,3},{2,0},{3,1},{4,6},{5,7},{6,4},{7,5},{8,10},{9,11},{10,... | collective-permute-start | bytes 110600 | tf_op jit(solution)/shard_map/ppermute | solution.py:462
  47.2 2.1 %collective-permute-done.12.arrived = f32[4,18,128]{2,1,0:T(8,128)S(1)} collective-permute-done((f32[4,18,128]{2,1,0:T(8,128)S(1)}, f32[4,18,128]{2,1,0:T(8,128)S(1)}, u32[]{:S(2)}, u32[]{:S(2)}) %collective-permute-start.12) | collective-permute-done | bytes 36896 | tf_op jit(solution)/shard_map/ppermute | solution.py:462
  49.3 3.0 %collective-permute-start.13 = (f32[2,18,128]{2,1,0:T(8,128)S(1)}, f32[2,18,128]{2,1,0:T(8,128)S(1)}, u32[]{:S(2)}, u32[]{:S(2)}) collective-permute-start(f32[2,18,128]{2,1,0:T(8,128)S(1)} %get-tuple-element.41), channel_id=1, source_target_pairs={{0,4},{1,5},{2,6},{3,7},{4,0},{5,1},{6,2},{7,3},{8,12},{9,13},{10,... | collective-permute-start | bytes 55304 | tf_op jit(solution)/shard_map/ppermute | solution.py:462
  52.3 1.8 %collective-permute-done.13.arrived = f32[2,18,128]{2,1,0:T(8,128)S(1)} collective-permute-done((f32[2,18,128]{2,1,0:T(8,128)S(1)}, f32[2,18,128]{2,1,0:T(8,128)S(1)}, u32[]{:S(2)}, u32[]{:S(2)}) %collective-permute-start.13) | collective-permute-done | bytes 18464 | tf_op jit(solution)/shard_map/ppermute | solution.py:462
  54.1 0.0 copy-start.6
  54.1 3.1 %collective-permute-start.14 = (f32[1,18,128]{2,1,0:T(8,128)S(1)}, f32[1,18,128]{2,1,0:T(8,128)S(1)}, u32[]{:S(2)}, u32[]{:S(2)}) collective-permute-start(f32[1,18,128]{2,1,0:T(8,128)S(1)} %get-tuple-element.43), channel_id=1, source_target_pairs={{0,8},{1,9},{2,10},{3,11},{4,12},{5,13},{6,14},{7,15},{8,0},{9,1},... | collective-permute-start | bytes 27656 | tf_op jit(solution)/shard_map/ppermute | solution.py:462
  57.2 1.7 %collective-permute-done.14.arrived = f32[1,18,128]{2,1,0:T(8,128)S(1)} collective-permute-done((f32[1,18,128]{2,1,0:T(8,128)S(1)}, f32[1,18,128]{2,1,0:T(8,128)S(1)}, u32[]{:S(2)}, u32[]{:S(2)}) %collective-permute-start.14) | collective-permute-done | bytes 9248 | tf_op jit(solution)/shard_map/ppermute | solution.py:462
  58.9 0.0 copy-start.7
  58.9 0.0 copy-done.6
  58.9 0.7 %copy-done.7 = f32[1,256]{1,0:T(1,128)S(1)} copy-done((f32[1,256]{1,0:T(1,128)S(1)}, f32[1,256]{1,0:T(1,128)}, u32[]{:S(2)}) %copy-start.7) | copy-done | bytes 1048
  59.6 0.7 %step.1 = (f32[1,256]{1,0:T(1,128)}, f32[16,128]{1,0:T(8,128)}) custom-call(s32[1]{0:T(128)} %bitcast.role.refs_0_, f32[1,18,128]{2,1,0:T(8,128)S(1)} %get-tuple-element.42.kept, f32[1,18,128]{2,1,0:T(8,128)S(1)} %collective-permute-done.14.arrived, f32[1,256]{1,0:T(1,128)S(1)} %copy-done.7, f32[16,128]{1,0:T(8,128)S(1)} %bitcast.43), custom_call_target="tpu_custom_call" | custom-call | tf_op jit(solution)/shard_map/step/pallas_call | solution.py:472
  (7 shorter events, 0.2 us)
Async XLA Ops:
  0.6 1.2 %copy-start = (bf16[1,128,4096]{2,1,0:T(8,128)(2,1)S(1)}, bf16[1,128,4096]{2,1,0:T(8,128)(2,1)}, u32[]{:S(2)}) copy-start(bf16[1,128,4096]{2,1,0:T(8,128)(2,1)} %param.9) | copy-start | bytes 3145732
  0.6 8.9 %copy-start.1 = (bf16[128,4096]{1,0:T(8,128)(2,1)S(1)}, bf16[128,4096]{1,0:T(8,128)(2,1)}, u32[]{:S(2)}) copy-start(bf16[128,4096]{1,0:T(8,128)(2,1)} %refs_5_.9) | copy-start | bytes 3145732
  1.9 23.5 %collective-permute-start = (bf16[128,4096]{1,0:T(8,128)(2,1)S(1)}, bf16[128,4096]{1,0:T(8,128)(2,1)S(1)}, u32[]{:S(2)}, u32[]{:S(2)}) collective-permute-start(bf16[128,4096]{1,0:T(8,128)(2,1)S(1)} %bitcast.11), channel_id=1, source_target_pairs={{0,1},{1,2},{2,3},{3,4},{4,5},{5,6},{6,7},{7,8},{8,9},{9,10},{10,1... | collective-permute-start | bytes 3145736 | tf_op jit(solution)/shard_map/ppermute | solution.py:380
  4.3 26.6 %collective-permute-start.1 = (bf16[128,4096]{1,0:T(8,128)(2,1)}, bf16[128,4096]{1,0:T(8,128)(2,1)S(1)}, u32[]{:S(2)}, u32[]{:S(2)}) collective-permute-start(bf16[128,4096]{1,0:T(8,128)(2,1)} %bitcast.36), channel_id=1, source_target_pairs={{0,1},{1,2},{2,3},{3,4},{4,5},{5,6},{6,7},{7,8},{8,9},{9,10},{10,1... | collective-permute-start | bytes 3145736 | tf_op jit(solution)/shard_map/ppermute | solution.py:381
  8.8 3.9 %collective-permute-start.2 = (bf16[128,1024]{1,0:T(8,128)(2,1)S(1)}, bf16[128,1024]{1,0:T(8,128)(2,1)S(1)}, u32[]{:S(2)}, u32[]{:S(2)}) collective-permute-start(bf16[128,1024]{1,0:T(8,128)(2,1)S(1)} %first_weigh.1.refs_1_.refs_3_.refs_6_), channel_id=1, source_target_pairs={{17,16},{18,17},{19,18},{20,19},{21,20},{22,21},{23,22},{24,23},{2... | collective-permute-start | bytes 786440 | tf_op jit(solution)/shard_map/ppermute | solution.py:382
  9.5 1.2 %copy-start.2 = (bf16[1,128,4096]{2,1,0:T(8,128)(2,1)S(1)}, bf16[1,128,4096]{2,1,0:T(8,128)(2,1)}, u32[]{:S(2)}) copy-start(bf16[1,128,4096]{2,1,0:T(8,128)(2,1)} %param.8) | copy-start | bytes 3145732
  10.9 2.9 %collective-permute-start.6 = (bf16[128,1024]{1,0:T(8,128)(2,1)S(1)}, bf16[128,1024]{1,0:T(8,128)(2,1)S(1)}, u32[]{:S(2)}, u32[]{:S(2)}) collective-permute-start(bf16[128,1024]{1,0:T(8,128)(2,1)S(1)} %weigh.3.refs_3_.refs_1_.refs_6_), channel_id=1, source_target_pairs={{17,16},{18,17},{19,18},{20,19},{21,20},{22,21},{23,22},{24,23},{2... | collective-permute-start | bytes 786440 | tf_op jit(solution)/shard_map/ppermute | solution.py:382
  11.7 1.7 %copy-start.5 = (bf16[1,128,256]{2,1,0:T(8,128)(2,1)S(1)}, bf16[1,128,256]{2,1,0:T(8,128)(2,1)}, u32[]{:S(2)}) copy-start(bf16[1,128,256]{2,1,0:T(8,128)(2,1)} %param.11) | copy-start | bytes 196612
  11.8 3.6 %collective-permute-start.5 = (bf16[128,1024]{1,0:T(8,128)(2,1)S(1)}, bf16[128,1024]{1,0:T(8,128)(2,1)S(1)}, u32[]{:S(2)}, u32[]{:S(2)}) collective-permute-start(bf16[128,1024]{1,0:T(8,128)(2,1)S(1)} %weigh.4.refs_3_.refs_1_.refs_6_), channel_id=1, source_target_pairs={{17,16},{18,17},{19,18},{20,19},{21,20},{22,21},{23,22},{24,23},{2... | collective-permute-start | bytes 786440 | tf_op jit(solution)/shard_map/ppermute | solution.py:382
  12.8 4.1 %collective-permute-start.4 = (bf16[128,1024]{1,0:T(8,128)(2,1)S(1)}, bf16[128,1024]{1,0:T(8,128)(2,1)S(1)}, u32[]{:S(2)}, u32[]{:S(2)}) collective-permute-start(bf16[128,1024]{1,0:T(8,128)(2,1)S(1)} %weigh.5.refs_1_.refs_6_), channel_id=1, source_target_pairs={{17,16},{18,17},{19,18},{20,19},{21,20},{22,21},{23,22},{24,23},{2... | collective-permute-start | bytes 786440 | tf_op jit(solution)/shard_map/ppermute | solution.py:382
  13.8 10.2 %collective-permute-start.3 = (bf16[128,1024]{1,0:T(8,128)(2,1)S(1)}, bf16[128,1024]{1,0:T(8,128)(2,1)S(1)}, u32[]{:S(2)}, u32[]{:S(2)}) collective-permute-start(bf16[128,1024]{1,0:T(8,128)(2,1)S(1)} %filter.5.refs_6_.refs_8_), channel_id=1, source_target_pairs={{16,0},{17,1},{18,2},{19,3},{20,4},{21,5},{22,6},{23,7},{24,8},{25... | collective-permute-start | bytes 786440 | tf_op jit(solution)/shard_map/ppermute | solution.py:402
  15.4 18.5 %collective-permute-start.7 = (bf16[128,1024]{1,0:T(8,128)(2,1)S(1)}, bf16[128,1024]{1,0:T(8,128)(2,1)S(1)}, u32[]{:S(2)}, u32[]{:S(2)}) collective-permute-start(bf16[128,1024]{1,0:T(8,128)(2,1)S(1)} %filter.6.refs_6_.refs_8_), channel_id=1, source_target_pairs={{16,0},{17,1},{18,2},{19,3},{20,4},{21,5},{22,6},{23,7},{24,8},{25... | collective-permute-start | bytes 786440 | tf_op jit(solution)/shard_map/ppermute | solution.py:402
  16.9 18.9 %collective-permute-start.8 = (bf16[128,1024]{1,0:T(8,128)(2,1)S(1)}, bf16[128,1024]{1,0:T(8,128)(2,1)S(1)}, u32[]{:S(2)}, u32[]{:S(2)}) collective-permute-start(bf16[128,1024]{1,0:T(8,128)(2,1)S(1)} %filter.7.refs_6_.refs_8_), channel_id=1, source_target_pairs={{16,0},{17,1},{18,2},{19,3},{20,4},{21,5},{22,6},{23,7},{24,8},{25... | collective-permute-start | bytes 786440 | tf_op jit(solution)/shard_map/ppermute | solution.py:402
  24.0 14.0 %collective-permute-start.9 = (bf16[128,512]{1,0:T(8,128)(2,1)S(1)}, bf16[128,512]{1,0:T(8,128)(2,1)S(1)}, u32[]{:S(2)}, u32[]{:S(2)}) collective-permute-start(bf16[128,512]{1,0:T(8,128)(2,1)S(1)} %filter.8.refs_6_.refs_8_), channel_id=1, source_target_pairs={{16,0},{17,1},{18,2},{19,3},{20,4},{21,5},{22,6},{23,7},{24,8},{25... | collective-permute-start | bytes 393224 | tf_op jit(solution)/shard_map/ppermute | solution.py:402
  25.4 15.5 %collective-permute-start.10 = (bf16[128,512]{1,0:T(8,128)(2,1)S(1)}, bf16[128,512]{1,0:T(8,128)(2,1)S(1)}, u32[]{:S(2)}, u32[]{:S(2)}) collective-permute-start(bf16[128,512]{1,0:T(8,128)(2,1)S(1)} %filter.9.refs_4_.refs_8_), channel_id=1, source_target_pairs={{16,0},{17,1},{18,2},{19,3},{20,4},{21,5},{22,6},{23,7},{24,8},{25... | collective-permute-start | bytes 393224 | tf_op jit(solution)/shard_map/ppermute | solution.py:402
  30.4 1.2 %copy-start.3 = (bf16[1,128,4096]{2,1,0:T(8,128)(2,1)S(1)}, bf16[1,128,4096]{2,1,0:T(8,128)(2,1)}, u32[]{:S(2)}) copy-start(bf16[1,128,4096]{2,1,0:T(8,128)(2,1)} %param.8) | copy-start | bytes 3145732
  30.4 1.5 %copy-start.4 = (bf16[1,128,4096]{2,1,0:T(8,128)(2,1)S(1)}, bf16[1,128,4096]{2,1,0:T(8,128)(2,1)}, u32[]{:S(2)}) copy-start(bf16[1,128,4096]{2,1,0:T(8,128)(2,1)} %param.10) | copy-start | bytes 3145732
  41.8 1.7 %collective-permute-start.11 = (f32[8,18,128]{2,1,0:T(8,128)S(1)}, f32[8,18,128]{2,1,0:T(8,128)S(1)}, u32[]{:S(2)}, u32[]{:S(2)}) collective-permute-start(f32[8,18,128]{2,1,0:T(8,128)S(1)} %get-tuple-element.37), channel_id=1, source_target_pairs={{0,1},{1,0},{2,3},{3,2},{4,5},{5,4},{6,7},{7,6},{8,9},{9,8},{10,11... | collective-permute-start | bytes 221192 | tf_op jit(solution)/shard_map/ppermute | solution.py:462
  43.6 5.8 %collective-permute-start.12 = (f32[4,18,128]{2,1,0:T(8,128)S(1)}, f32[4,18,128]{2,1,0:T(8,128)S(1)}, u32[]{:S(2)}, u32[]{:S(2)}) collective-permute-start(f32[4,18,128]{2,1,0:T(8,128)S(1)} %get-tuple-element.39), channel_id=1, source_target_pairs={{0,2},{1,3},{2,0},{3,1},{4,6},{5,7},{6,4},{7,5},{8,10},{9,11},{10,... | collective-permute-start | bytes 110600 | tf_op jit(solution)/shard_map/ppermute | solution.py:462
  49.3 4.8 %collective-permute-start.13 = (f32[2,18,128]{2,1,0:T(8,128)S(1)}, f32[2,18,128]{2,1,0:T(8,128)S(1)}, u32[]{:S(2)}, u32[]{:S(2)}) collective-permute-start(f32[2,18,128]{2,1,0:T(8,128)S(1)} %get-tuple-element.41), channel_id=1, source_target_pairs={{0,4},{1,5},{2,6},{3,7},{4,0},{5,1},{6,2},{7,3},{8,12},{9,13},{10,... | collective-permute-start | bytes 55304 | tf_op jit(solution)/shard_map/ppermute | solution.py:462
  54.1 4.8 %copy-start.6 = (f32[1,128,16]{1,2,0:T(8,128)S(1)}, f32[1,128,16]{1,2,0:T(8,128)}, u32[]{:S(2)}) copy-start(f32[1,128,16]{1,2,0:T(8,128)} %param.13) | copy-start | bytes 24580
  54.1 4.8 %collective-permute-start.14 = (f32[1,18,128]{2,1,0:T(8,128)S(1)}, f32[1,18,128]{2,1,0:T(8,128)S(1)}, u32[]{:S(2)}, u32[]{:S(2)}) collective-permute-start(f32[1,18,128]{2,1,0:T(8,128)S(1)} %get-tuple-element.43), channel_id=1, source_target_pairs={{0,8},{1,9},{2,10},{3,11},{4,12},{5,13},{6,14},{7,15},{8,0},{9,1},... | collective-permute-start | bytes 27656 | tf_op jit(solution)/shard_map/ppermute | solution.py:462
  58.9 0.7 %copy-start.7 = (f32[1,256]{1,0:T(1,128)S(1)}, f32[1,256]{1,0:T(1,128)}, u32[]{:S(2)}) copy-start(f32[1,256]{1,0:T(1,128)} %steer_second.1) | copy-start | bytes 3076

commit v6 on v5

--- a/solution.py
+++ b/solution.py
@@ -11,8 +11,8 @@
 BF16 = jnp.bfloat16
 LANES = 128
 SUB = 32
-CHUNK_EDGES = (0, 2, 4, 6, 7, 8)
-HALO_EDGES = (0, 2, 4, 6, 8)
+CHUNK_EDGES = (0, 2, 4, 5, 6, 8)
+HALO_EDGES = (0, 4, 8)
 
 
 def lane_of(shape):
@@ -25,6 +25,10 @@
 
 def first_section(role):
     return (role[0] & 1) > 0
+
+
+def second_section(role):
+    return (role[0] & 2) > 0
 
 
 def times(a, b):
@@ -90,13 +94,27 @@
     return pick, taps
 
 
-def weigh_kernel(role, gate, incoming, out):
-    @pl.when(jnp.logical_not(first_section(role)))
+def weigh_kernel(own_blocks, role, gate, incoming, raw, out):
+    width = out.shape[1]
+    step = pl.program_id(0)
+    foreign = jnp.logical_and(second_section(role), step >= own_blocks)
+
+    @pl.when(foreign)
+    def _():
+        at = pl.multiple_of(jnp.maximum(step - own_blocks, 0) * width, width)
+        out[...] = times(raw[:, pl.ds(at, width)], incoming[...])
+
+    @pl.when(jnp.logical_not(jnp.logical_or(foreign, first_section(role))))
     def _():
         out[...] = times(gate[...], incoming[...])
 
 
-def first_weigh_kernel(block, role, gate, incoming, out, gate_part, incoming_part, sems):
+def first_weigh_kernel(block, first_raw, role, gate, incoming, mid, filters, out, raw, gate_part, incoming_part, sems):
+    channels = gate.shape[1]
+    foreign = channels - first_raw
+    tap_lanes = raw.shape[1] - 2 * foreign
+    groups = filters.shape[1]
+
     @pl.when(jnp.logical_not(first_section(role)))
     def _():
         tiles = [pl.ds(at, block) for at in range(0, out.shape[1], block)]
@@ -107,13 +125,23 @@
             ]
             for i, t in enumerate(tiles)
         ]
+        parts = (
+            (gate.at[:, pl.ds(first_raw, foreign)], raw.at[:, pl.ds(0, foreign)]),
+            (mid.at[:, pl.ds(first_raw, foreign)], raw.at[:, pl.ds(foreign, foreign)]),
+            (filters.at[:, pl.ds(groups - tap_lanes, tap_lanes)], raw.at[:, pl.ds(2 * foreign, tap_lanes)]),
+        )
+        raws = [pltpu.make_async_copy(source, part, sems.at[2, i]) for i, (source, part) in enumerate(parts)]
         for pair in copies:
             for copy in pair:
                 copy.start()
+        for copy in raws:
+            copy.start()
         for t, pair in zip(tiles, copies):
             for copy in pair:
                 copy.wait()
             out[:, t] = times(gate_part[:, t], incoming_part[:, t])
+        for copy in raws:
+            copy.wait()
 
 
 def taps_kernel(role, filters, taps_out):
@@ -159,6 +187,39 @@
             ).astype(BF16)
 
 
+def raw_filter_kernel(group_size, foreign, role, own, halo, taps, mid, incoming, raw, outgoing, raw_taps):
+    width = own.shape[1]
+    step = pl.program_id(0)
+    tap_lanes = raw.shape[1] - 2 * foreign
+
+    def run(own_taps, first_group, gate_of):
+        for first in range(0, width, LANES):
+            cols = pl.ds(first, LANES)
+            conv = convolved(
+                False, group_size, own[:, cols], halo[:, cols], own_taps, first_group + first // group_size
+            )
+            outgoing[:, cols] = (
+                incoming[:, cols].astype(F32) + gate_of(first).astype(F32) * conv
+            ).astype(BF16)
+
+    @pl.when(second_section(role))
+    def _():
+        pick = jnp.where(row_of((taps.shape[1],) * 2) == lane_of((taps.shape[1],) * 2), 1.0, 0.0).astype(BF16)
+        raw_taps[...] = lax.dot_general(
+            raw[:, pl.ds(2 * foreign, tap_lanes)], pick, (((0,), (0,)), ((), ())), preferred_element_type=F32
+        )
+        skipped = tap_lanes - foreign // group_size
+        run(
+            raw_taps,
+            skipped + step * (width // group_size),
+            lambda first: raw[:, pl.ds(pl.multiple_of(foreign + step * width + first, LANES), LANES)],
+        )
+
+    @pl.when(jnp.logical_not(jnp.logical_or(first_section(role), second_section(role))))
+    def _():
+        run(taps, 0, lambda first: mid[:, pl.ds(first, LANES)])
+
+
 def turned_filter_kernel(group_size, role, mid, mid_halo, taps, filtered):
     @pl.when(first_section(role))
     def _():
@@ -217,58 +278,30 @@
         tap_grad[pl.ds(8 * pair, 8), :] = diagonal_sums(blocks)
 
 
-def halves_of(role, step, zero, one):
-    mine = (role[0] >> (step + 1)) & 1 > 0
-    return jnp.where(mine, zero, one), jnp.where(mine, one, zero)
-
-
-def pack_kernel(owners, role, *refs):
-    count = (len(refs) - 2) // 2
-    taps, steers, (give, keep) = refs[:count], refs[count : 2 * count], refs[2 * count :]
+def pack_kernel(owners, *refs):
+    count = (len(refs) - 1) // 2
+    taps, steers, out = refs[:count], refs[count : 2 * count], refs[-1]
     groups = sum(ref.shape[0] for ref in taps) // owners
     channels = sum(ref.shape[1] for ref in steers) // owners
 
-    def part(parts, axis, owner, size):
-        at = owner * size
+    def part(parts, axis, at, size):
         for ref in parts:
             if at < ref.shape[axis]:
                 return ref[at : at + size, :] if axis == 0 else ref[:, at : at + size]
             at -= ref.shape[axis]
 
-    def packed(owner):
-        steer = part(steers, 1, owner, channels)
-        lines = [steer[:, at : at + LANES] for at in range(0, channels, LANES)]
-        short = LANES - lines[-1].shape[1]
-        if short > 0:
-            lines[-1] = jnp.concatenate([lines[-1], jnp.zeros((1, short), F32)], 1)
-        return [part(taps, 0, owner, groups)] + lines
-
-    order = reversed_bits(owners)
-    for i, (low, high) in enumerate(zip(order[: owners // 2], order[owners // 2 :])):
-        at = 0
-        for zero, one in zip(packed(low), packed(high)):
-            lines = zero.shape[0]
-            give[i, pl.ds(at, lines), :], keep[i, pl.ds(at, lines), :] = halves_of(role, 0, zero, one)
-            at += lines
-
-
-def reversed_bits(count):
-    order = [0]
-    while len(order) < count:
-        order = [2 * i for i in order] + [2 * i + 1 for i in order]
-    return order
-
-
-def fold_kernel(step, role, kept, arrived, give, keep):
-    count = give.shape[0]
-    for i in range(count):
-        zero = kept[i] + arrived[i]
-        one = kept[count + i] + arrived[count + i]
-        give[i], keep[i] = halves_of(role, step, zero, one)
-
-
-def step_kernel(role, kept, arrived, steer_second, filter_second, steer_out, filter_out):
-    total = kept[0] + arrived[0]
+    for owner in range(owners):
+        out[owner, pl.ds(0, groups), :] = part(taps, 0, owner * groups, groups)
+        for line, at in enumerate(range(0, channels, LANES)):
+            size = min(LANES, channels - at)
+            steer = part(steers, 1, owner * channels + at, size)
+            if size < LANES:
+                steer = jnp.concatenate([steer, jnp.zeros((1, LANES - size), F32)], 1)
+            out[owner, pl.ds(groups + line, 1), :] = steer
+
+
+def step_kernel(role, parts, steer_second, filter_second, steer_out, filter_out):
+    total = jnp.sum(parts[...], 0)
     groups = filter_second.shape[0]
     tap_grad = total[:groups]
     lane = lane_of(tap_grad.shape)
@@ -318,41 +351,43 @@
     group_size = channels // groups
     sections, seqs = lax.axis_size("section"), lax.axis_size("seq")
     my_section = lax.axis_index("section")
-    role = (2 * lax.axis_index("seq") + (my_section == 0)).astype(jnp.int32).reshape(1)
+    role = ((my_section == 0) + 2 * (my_section == sections - 2)).astype(jnp.int32).reshape(1)
 
     edges = [channels * eighths // 8 for eighths in CHUNK_EDGES]
     bounds = list(zip(edges[:-1], edges[1:]))
     block = channels // 8
     block_groups = block // group_size
     behind = [(seqs * s + i, seqs * s + i - 1) for s in range(1, sections) for i in range(1, seqs)]
+    below = [(i, i - 1) for i in range(1, seqs)] if sections == 2 else []
     ahead = [(i, i + 1) for i in range(seqs - 1)]
     down = [(s, s - 1) for s in range(1, sections)]
 
     def bf16(width_of):
         return jax.ShapeDtypeStruct((rows, width_of), BF16)
 
-    def weigh(incoming, first, last, offset, after):
+    def weigh(incoming, first, last, offset, raw, own_blocks, after):
         return call(
-            weigh_kernel,
+            functools.partial(weigh_kernel, own_blocks),
             ((last - first) // block,),
-            [SMEM, spec(rows, block, first // block), spec(rows, block, (first - offset) // block)],
+            [SMEM, spec(rows, block, first // block), spec(rows, block, (first - offset) // block),
+             pl.BlockSpec(raw.shape, lambda i: (0, 0))],
             spec(rows, block),
             bf16(last - first),
             name="weigh",
             after=after,
-        )(role, in_gate, incoming, *after)
+        )(role, in_gate, incoming, raw, *after)
 
     def first_weigh(last):
         part = pltpu.VMEM((rows, last), BF16)
         return pl.pallas_call(
-            functools.partial(first_weigh_kernel, block),
-            in_specs=[SMEM] + [pl.BlockSpec(memory_space=pl.ANY)] * 2,
-            out_specs=pl.BlockSpec(memory_space=pltpu.VMEM),
-            out_shape=bf16(last),
-            scratch_shapes=[part, part, pltpu.SemaphoreType.DMA((2, last // block))],
+            functools.partial(first_weigh_kernel, block, first_raw),
+            in_specs=[SMEM] + [pl.BlockSpec(memory_space=pl.ANY)] * 4,
+            out_specs=[pl.BlockSpec(memory_space=pltpu.VMEM)] * 2,
+            out_shape=[bf16(last), bf16(2 * foreign + min(groups, LANES))],
+            scratch_shapes=[part, part, pltpu.SemaphoreType.DMA((3, max(3, last // block)))],
             compiler_params=SMALL,
             name="first_weigh",
-        )(role, *[pltpu.with_memory_space_constraint(a, pltpu.HBM) for a in (in_gate, cotangent)])
+        )(role, *[pltpu.with_memory_space_constraint(a, pltpu.HBM) for a in (in_gate, cotangent, mid_gate, filters[0])])
 
     taps = call(
         taps_kernel,
@@ -362,44 +397,61 @@
         jax.ShapeDtypeStruct((groups, filt_len), F32),
         name="taps",
     )(role, filters[0])
+    first_raw = edges[-2]
+    foreign = channels - first_raw
     group_spec = lambda first: pl.BlockSpec((block_groups, filt_len), lambda i: (i + first, 0))
 
     incoming = [(cotangent, 0)] * len(bounds)
+    raws = []
     for hop in range(sections - 1):
         split = [channels * eighths // 8 for eighths in HALO_EDGES] if hop == 0 else edges
         starts, ends = split[:-1], split[1:]
-        owns = []
-        for first, last in zip(starts, ends):
+        owns, halos = [], []
+
+        def send_halo(after):
+            first, last = starts[len(owns)], ends[len(owns)]
             array, offset = next(entry for entry, edge in zip(incoming, edges) if edge == first)
             if hop == 0 and first == 0:
-                owns.append(first_weigh(last))
+                own, sent = first_weigh(last)
+                owns.append(own)
+                raws.append(lax.ppermute(sent, "section", [(sections - 1, sections - 2)]))
             else:
-                owns.append(weigh(array, first, last, offset, tuple(owns[-1:])))
+                own_blocks = (first_raw - first if hop == 0 else channels) // block
+                owns.append(weigh(array, first, last, offset, raws[0], own_blocks, after))
+            halos.append(lax.ppermute(owns[-1], ("section", "seq"), behind + (below if hop == 0 and last == channels else [])))
+
+        send_halo(())
         if hop == 0:
             mid_sent, inputs_sent, _ = lax.optimization_barrier((mid_gate, layer_inputs, owns[0]))
             mid_halo = lax.ppermute(mid_sent, ("section", "seq"), ahead)
             inputs_halo = lax.ppermute(inputs_sent, ("section", "seq"), ahead)
-        halos = [lax.ppermute(own, ("section", "seq"), behind) for own in owns]
+        send_halo((owns[0],))
         sources, outgoing, received = [], [], []
         for k, (first, last) in enumerate(bounds):
             part = max(i for i, start in enumerate(starts) if start <= first)
+            while part >= len(owns):
+                send_halo(tuple(outgoing[-1:]))
             at = (first - starts[part]) // block
             array, offset = incoming[k]
             before = tuple(outgoing[-1:])
+            shared = hop == 0 and first == first_raw
             out = call(
-                functools.partial(filter_kernel, group_size),
+                functools.partial(raw_filter_kernel, group_size, foreign) if shared
+                else functools.partial(filter_kernel, group_size),
                 ((last - first) // block,),
                 [SMEM, spec(rows, block, at), spec(rows, block, at), group_spec(first // block),
-                 spec(rows, block, first // block), spec(rows, block, (first - offset) // block)],
+                 spec(rows, block, first // block), spec(rows, block, (first - offset) // block)]
+                + [pl.BlockSpec(raw.shape, lambda i: (0, 0)) for raw in raws[:shared]],
                 spec(rows, block),
                 bf16(last - first),
+                scratch=[pltpu.VMEM((min(groups, LANES), filt_len), F32)] * shared,
                 name="filter",
                 cycles=1000,
                 after=before,
-            )(role, owns[part], halos[part], taps, mid_gate, array, *before)
+            )(role, owns[part], halos[part], taps, mid_gate, array, *raws[:shared], *before)
             sources.append((owns[part], halos[part], at))
             outgoing.append(out)
-            received.append(lax.ppermute(out, "section", down))
+            received.append(out if shared else lax.ppermute(out, "section", down))
         top = my_section == sections - 1
         incoming = [
             (jnp.where(top, cotangent[:, first:last], arrived), first)
@@ -420,13 +472,14 @@
             after=after,
         )(role, mid_gate, mid_halo, taps, *after))
 
-    grads = []
-    for k, (first, last) in enumerate(bounds):
+    grads, latest = {}, ()
+    for k in [0, len(bounds) - 1] + list(range(1, len(bounds) - 1)):
+        first, last = bounds[k]
         own, halo, at = sources[k]
         width = last - first
         here = spec(rows, block, first // block)
-        after = tuple(grads[-1][:1] if grads else ())
-        grads.append(call(
+        after = tuple(latest[:1])
+        latest = grads[k] = call(
             functools.partial(grad_kernel, group_size),
             (width // block,),
             [SMEM, here, here, here, here, here, spec(rows, block, at), spec(rows, block, at)]
@@ -438,47 +491,31 @@
             cycles=2000,
             after=after,
         )(role, in_gate, mid_gate, layer_inputs, mid_halo, inputs_halo, own, halo, outgoing[k],
-          received[k], filtered[k], *after))
-    tap_grads, steer_grads = zip(*grads)
+          received[k], filtered[k], *after)
+    tap_grads, steer_grads = zip(*(grads[k] for k in range(len(bounds))))
 
     own_channels = channels // seqs
     lines = groups // seqs + pl.cdiv(own_channels, LANES)
-    steps = seqs.bit_length() - 1
-
-    def halves(count):
-        return [jax.ShapeDtypeStruct((count, lines, LANES), F32)] * 2
-
     vmem = pl.BlockSpec(memory_space=pltpu.VMEM)
-    give, keep = pl.pallas_call(
+    packed = pl.pallas_call(
         functools.partial(pack_kernel, seqs),
-        in_specs=[SMEM] + [vmem] * (2 * len(grads)),
-        out_specs=[vmem] * 2,
-        out_shape=halves(seqs // 2),
+        in_specs=[vmem] * (2 * len(grads)),
+        out_specs=vmem,
+        out_shape=jax.ShapeDtypeStruct((seqs, lines, LANES), F32),
         compiler_params=SMALL,
         name="pack",
-    )(role, *tap_grads, *steer_grads)
-    for step in range(steps):
-        route = [(i, i ^ (1 << step)) for i in range(seqs)]
-        arrived = lax.ppermute(give, "seq", route)
-        if step < steps - 1:
-            give, keep = pl.pallas_call(
-                functools.partial(fold_kernel, step + 1),
-                in_specs=[SMEM, vmem, vmem],
-                out_specs=[vmem] * 2,
-                out_shape=halves(keep.shape[0] // 2),
-                compiler_params=SMALL,
-                name="fold",
-            )(role, keep, arrived)
+    )(*tap_grads, *steer_grads)
+    parts = lax.all_to_all(packed, "seq", 0, 0)
     steer_step, filter_step = pl.pallas_call(
         step_kernel,
-        in_specs=[SMEM] + [vmem] * 4,
+        in_specs=[SMEM] + [vmem] * 3,
         out_shape=[
             jax.ShapeDtypeStruct((1, own_channels), F32),
             jax.ShapeDtypeStruct((groups // seqs, filt_len), F32),
         ],
         compiler_params=SMALL,
         name="step",
-    )(role, keep, arrived, steer_second, filter_second[0].T)
+    )(role, parts, steer_second, filter_second[0].T)
     return steer_step, filter_step.T[None]
 
 

time: 60.7 us -> 69.2 us (1.14)
  blocking collectives: 0 us -> 23.1 us
  starting transfers between devices: 26.7 us -> 15.7 us
  local copies, waits for them, and re-layouts: 4.11 us -> 0.83 us
  waiting for transfers between devices: 14.5 us -> 13.2 us
  Pallas kernels: 13.9 us -> 15.1 us
    all_to_all x0 -> x1, blocking collectives: none -> 23.1 us  [body(): parts = lax.all_to_all(packed, 'seq', 0, 0)]
    ppermute x13 -> x7, starting transfers between devices: 19.8 us -> 8.71 us  [the longest x4 5.17 us: body(): received.append(out if shared else lax.ppermute(out, 'section', down))]
    unnamed x16 -> x14, local copies, waits for them, and re-layouts: 4.11 us -> 0.83 us
    ppermute x13 -> x7, waiting for transfers between devices: 14.5 us -> 13.2 us  [the longest x1 9.16 us: send_halo(): raws.append(lax.ppermute(sent, 'section', [(sections - 1, sections - 2)]))]
    pallas_call x14 -> x9, Pallas kernels: 1.9 us -> 3.1 us  [the longest x5 1.92 us: body(): call(functools.partial(raw_filter_kernel, group_size, foreign) if shared...]
  transfers between devices with their start and end apart: 15 -> 9, of which waited for: 7 -> 4; matrix products, arithmetic and copies ran while one was open for 0% -> 0% of each run, Pallas kernels for 20% -> 19%
where the time goes in v6:
time: 69.2 us; the launch traced here: 68.8 us
  blocking collectives  23.1 us (33%)
  starting transfers between devices  15.7 us (23%)
  Pallas kernels  15.1 us (22%)
  waiting for transfers between devices  13.2 us (19%)
  between operations  0.93 us (1%)
  local copies, waits for them, and re-layouts  0.83 us (1%)
    all_to_all x1, blocking collectives, body(): parts = lax.all_to_all(packed, 'seq', 0, 0)  23.1 us
    ppermute x1, waiting for transfers between devices, send_halo(): raws.append(lax.ppermute(sent, 'section', [(sections - 1, sections - 2)]))  9.16 us
    pallas_call x5, Pallas kernels, body(): call(functools.partial(grad_kernel, group_size), (width // block,), [SMEM...  7.69 us
    ppermute x4, starting transfers between devices, body(): received.append(out if shared else lax.ppermute(out, 'section', down))  5.17 us
    ppermute x1, starting transfers between devices, body(): inputs_halo = lax.ppermute(inputs_sent, ('section', 'seq'), ahead)  4.54 us
    pallas_call x5, Pallas kernels, body(): call(functools.partial(turned_filter_kernel, group_size), ((last - first)...  4.14 us
    ppermute x4, waiting for transfers between devices, body(): received.append(out if shared else lax.ppermute(out, 'section', down))  4.07 us
    ppermute x1, starting transfers between devices, body(): mid_halo = lax.ppermute(mid_sent, ('section', 'seq'), ahead)  2.42 us
  transfers between devices with their start and end apart: 9, of which 4 were waited for; matrix products, arithmetic and copies ran while one was open for 0% of the time, Pallas kernels for 19%

profile of v6, /device:TPU:0, one launch (start us, length us, event | category | flops | bytes accessed | tf_op | source)
XLA Modules:
  0.0 68.8 jit_solution(279553806454578946)
XLA Ops:
  0.6 0.0 copy-start
  0.6 0.0 copy-start.1
  0.7 0.0 copy-start.2
  0.7 0.1 first_weigh.1
  0.8 1.6 %collective-permute-start.4 = (bf16[128,2176]{1,0:T(8,128)(2,1)S(1)}, bf16[128,2176]{1,0:T(8,128)(2,1)S(1)}, u32[]{:S(2)}, u32[]{:S(2)}) collective-permute-start(bf16[128,2176]{1,0:T(8,128)(2,1)S(1)} %get-tuple-element.21), channel_id=1, source_target_pairs={{16,0},{17,1},{18,2},{19,3},{20,4},{21,5},{22,6},{23,7},{24,8},{25... | collective-permute-start | bytes 1671176 | tf_op jit(solution)/shard_map/ppermute | solution.py:417
  2.4 0.0 copy-done
  2.4 0.0 copy-start.4
  2.4 2.4 %collective-permute-start = (bf16[128,4096]{1,0:T(8,128)(2,1)S(1)}, bf16[128,4096]{1,0:T(8,128)(2,1)S(1)}, u32[]{:S(2)}, u32[]{:S(2)}) collective-permute-start(bf16[128,4096]{1,0:T(8,128)(2,1)S(1)} %bitcast.12), channel_id=1, source_target_pairs={{0,1},{1,2},{2,3},{3,4},{4,5},{5,6},{6,7},{7,8},{8,9},{9,10},{10,1... | collective-permute-start | bytes 3145736 | tf_op jit(solution)/shard_map/ppermute | solution.py:426
  4.8 4.5 %collective-permute-start.1 = (bf16[128,4096]{1,0:T(8,128)(2,1)}, bf16[128,4096]{1,0:T(8,128)(2,1)S(1)}, u32[]{:S(2)}, u32[]{:S(2)}) collective-permute-start(bf16[128,4096]{1,0:T(8,128)(2,1)} %bitcast.35), channel_id=1, source_target_pairs={{0,1},{1,2},{2,3},{3,4},{4,5},{5,6},{6,7},{7,8},{8,9},{9,10},{10,1... | collective-permute-start | bytes 3145736 | tf_op jit(solution)/shard_map/ppermute | solution.py:427
  9.4 0.7 %collective-permute-start.2 = (bf16[128,2048]{1,0:T(8,128)(2,1)S(1)}, bf16[128,2048]{1,0:T(8,128)(2,1)S(1)}, u32[]{:S(2)}, u32[]{:S(2)}) collective-permute-start(bf16[128,2048]{1,0:T(8,128)(2,1)S(1)} %get-tuple-element.18.refs_1_.refs_4_.refs_6_), channel_id=1, source_target_pairs={{17,16},{18,17},{19,18},{20,19},{21,20},{22,21},{23,22},{24,23},{2... | collective-permute-start | bytes 1572872 | tf_op jit(solution)/shard_map/ppermute | solution.py:421
  10.1 9.2 %collective-permute-done.4.refs_3_.refs_6_ = bf16[128,2176]{1,0:T(8,128)(2,1)S(1)} collective-permute-done((bf16[128,2176]{1,0:T(8,128)(2,1)S(1)}, bf16[128,2176]{1,0:T(8,128)(2,1)S(1)}, u32[]{:S(2)}, u32[]{:S(2)}) %collective-permute-start.4) | collective-permute-done | bytes 557088 | tf_op jit(solution)/shard_map/ppermute | solution.py:417
  19.2 0.0 copy-done.1
  19.2 0.0 copy-done.2
  19.2 0.3 weigh.1.refs_1_.refs_6_
  19.6 1.3 %collective-permute-start.5 = (bf16[128,2048]{1,0:T(8,128)(2,1)S(1)}, bf16[128,2048]{1,0:T(8,128)(2,1)S(1)}, u32[]{:S(2)}, u32[]{:S(2)}) collective-permute-start(bf16[128,2048]{1,0:T(8,128)(2,1)S(1)} %weigh.1.refs_1_.refs_6_), channel_id=1, source_target_pairs={{17,16},{18,17},{19,18},{20,19},{21,20},{22,21},{23,22},{24,23},{2... | collective-permute-start | bytes 1572872 | tf_op jit(solution)/shard_map/ppermute | solution.py:421
  20.9 0.0 copy-done.4
  20.9 0.2 taps.1.refs_3_
  21.1 0.0 collective-permute-done.2.refs_2_.refs_7_
  21.1 0.2 filter.5.refs_6_.refs_8_
  21.3 1.3 %collective-permute-start.3 = (bf16[128,1024]{1,0:T(8,128)(2,1)S(1)}, bf16[128,1024]{1,0:T(8,128)(2,1)S(1)}, u32[]{:S(2)}, u32[]{:S(2)}) collective-permute-start(bf16[128,1024]{1,0:T(8,128)(2,1)S(1)} %filter.5.refs_6_.refs_8_), channel_id=1, source_target_pairs={{16,0},{17,1},{18,2},{19,3},{20,4},{21,5},{22,6},{23,7},{24,8},{25... | collective-permute-start | bytes 786440 | tf_op jit(solution)/shard_map/ppermute | solution.py:454
  22.6 0.2 filter.6.refs_6_.refs_8_
  22.8 1.3 %collective-permute-start.6 = (bf16[128,1024]{1,0:T(8,128)(2,1)S(1)}, bf16[128,1024]{1,0:T(8,128)(2,1)S(1)}, u32[]{:S(2)}, u32[]{:S(2)}) collective-permute-start(bf16[128,1024]{1,0:T(8,128)(2,1)S(1)} %filter.6.refs_6_.refs_8_), channel_id=1, source_target_pairs={{16,0},{17,1},{18,2},{19,3},{20,4},{21,5},{22,6},{23,7},{24,8},{25... | collective-permute-start | bytes 786440 | tf_op jit(solution)/shard_map/ppermute | solution.py:454
  24.1 0.0 collective-permute-done.5.refs_2_.refs_7_
  24.2 1.3 %collective-permute-start.7 = (bf16[128,512]{1,0:T(8,128)(2,1)S(1)}, bf16[128,512]{1,0:T(8,128)(2,1)S(1)}, u32[]{:S(2)}, u32[]{:S(2)}) collective-permute-start(bf16[128,512]{1,0:T(8,128)(2,1)S(1)} %filter.7.refs_6_.refs_8_), channel_id=1, source_target_pairs={{16,0},{17,1},{18,2},{19,3},{20,4},{21,5},{22,6},{23,7},{24,8},{25... | collective-permute-start | bytes 393224 | tf_op jit(solution)/shard_map/ppermute | solution.py:454
  25.5 0.0 collective-permute-done.refs_2_.refs_4_
  25.5 1.3 %collective-permute-start.8 = (bf16[128,512]{1,0:T(8,128)(2,1)S(1)}, bf16[128,512]{1,0:T(8,128)(2,1)S(1)}, u32[]{:S(2)}, u32[]{:S(2)}) collective-permute-start(bf16[128,512]{1,0:T(8,128)(2,1)S(1)} %filter.8.refs_7_.refs_8_), channel_id=1, source_target_pairs={{16,0},{17,1},{18,2},{19,3},{20,4},{21,5},{22,6},{23,7},{24,8},{25... | collective-permute-start | bytes 393224 | tf_op jit(solution)/shard_map/ppermute | solution.py:454
  26.8 1.4 %filter.9.refs_4_.refs_8_.refs_9_ = bf16[128,1024]{1,0:T(8,128)(2,1)S(1)} custom-call(s32[1]{0:T(128)} %bitcast.role.refs_0_, bf16[128,2048]{1,0:T(8,128)(2,1)S(1)} %weigh.1.refs_1_.refs_6_, bf16[128,2048]{1,0:T(8,128)(2,1)S(1)} %collective-permute-done.5.refs_2_.refs_7_, f32[256,128]{1,0:T(8,128)S(1)} %taps.1.refs_3_, bf16[128,4096]{1,0:T(8,128)(2,1)S(1)} %bitcast.17, ...), custom_call_target="tpu_custom_call" | custom-call | flops 1000 | tf_op jit(solution)/shard_map/filter/pallas_call | solution.py:438
  28.3 1.1 %turned_filter.5.refs_10_.refs_5_ = f32[128,1024]{1,0:T(8,128)S(1)} custom-call(s32[1]{0:T(128)} %bitcast.role.refs_0_, bf16[128,4096]{1,0:T(8,128)(2,1)S(1)} %bitcast.18, bf16[128,4096]{1,0:T(8,128)(2,1)S(1)} %collective-permute-done.refs_2_.refs_4_, f32[256,128]{1,0:T(8,128)S(1)} %taps.1.refs_3_, bf16[128,1024]{1,0:T(8,128)(2,1)S(1)} %filter.9.refs_4_.refs_8_.refs_9_), custom_call_target="tpu_custom_call" | custom-call | flops 1000 | tf_op jit(solution)/shard_map/turned_filter/pallas_call | solution.py:464
  29.3 1.1 %turned_filter.6.refs_5_.refs_10_ = f32[128,1024]{1,0:T(8,128)S(1)} custom-call(s32[1]{0:T(128)} %bitcast.role.refs_0_, bf16[128,4096]{1,0:T(8,128)(2,1)S(1)} %bitcast.19, bf16[128,4096]{1,0:T(8,128)(2,1)S(1)} %collective-permute-done.refs_2_.refs_4_, f32[256,128]{1,0:T(8,128)S(1)} %taps.1.refs_3_, bf16[128,1024]{1,0:T(8,128)(2,1)S(1)} %filter.9.refs_4_.refs_8_.refs_9_, ...), custom_call_target="tpu_custom_call" | custom-call | flops 1000 | tf_op jit(solution)/shard_map/turned_filter/pallas_call | solution.py:464
  30.4 0.5 turned_filter.7.refs_5_.refs_10_
  30.9 0.5 turned_filter.8.refs_5_.refs_10_
  31.4 0.0 copy-start.3
  31.4 1.1 %turned_filter.9.refs_10_ = f32[128,1024]{1,0:T(8,128)S(1)} custom-call(s32[1]{0:T(128)} %bitcast.role.refs_0_, bf16[128,4096]{1,0:T(8,128)(2,1)S(1)} %bitcast.22, bf16[128,4096]{1,0:T(8,128)(2,1)S(1)} %collective-permute-done.refs_2_.refs_4_, f32[256,128]{1,0:T(8,128)S(1)} %taps.1.refs_3_, bf16[128,1024]{1,0:T(8,128)(2,1)S(1)} %filter.9.refs_4_.refs_8_.refs_9_, ...), custom_call_target="tpu_custom_call" | custom-call | flops 1000 | tf_op jit(solution)/shard_map/turned_filter/pallas_call | solution.py:464
  32.5 0.0 collective-permute-done.3.refs_9_
  32.5 0.0 collective-permute-done.1.refs_5_
  32.5 0.1 copy-done.3
  32.6 1.9 %grads.5 = (f32[64,128]{1,0:T(8,128)S(1)}, f32[1,1024]{1,0:T(1,128)S(1)}) custom-call(s32[1]{0:T(128)} %bitcast.role.refs_0_, bf16[128,4096]{1,0:T(8,128)(2,1)S(1)} %bitcast.30, bf16[128,4096]{1,0:T(8,128)(2,1)S(1)} %bitcast.23, bf16[128,4096]{1,0:T(8,128)(2,1)S(1)} %bitcast.36, bf16[128,4096]{1,0:T(8,128)(2,1)S(1)} %collective-permute-done.refs_2_.refs_4_, ...), custom_call_target="tpu_custom_call" | custom-call | flops 2000 | tf_op jit(solution)/shard_map/grads/pallas_call | solution.py:482
  34.5 2.0 %grads.6 = (f32[64,128]{1,0:T(8,128)S(1)}, f32[1,1024]{1,0:T(1,128)S(1)}) custom-call(s32[1]{0:T(128)} %bitcast.role.refs_0_, bf16[128,4096]{1,0:T(8,128)(2,1)S(1)} %bitcast.31, bf16[128,4096]{1,0:T(8,128)(2,1)S(1)} %bitcast.24, bf16[128,4096]{1,0:T(8,128)(2,1)S(1)} %bitcast.37, bf16[128,4096]{1,0:T(8,128)(2,1)S(1)} %collective-permute-done.refs_2_.refs_4_, ...), custom_call_target="tpu_custom_call" | custom-call | flops 2000 | tf_op jit(solution)/shard_map/grads/pallas_call | solution.py:482
  36.5 1.3 %collective-permute-done.6.refs_9_ = bf16[128,1024]{1,0:T(8,128)(2,1)S(1)} collective-permute-done((bf16[128,1024]{1,0:T(8,128)(2,1)S(1)}, bf16[128,1024]{1,0:T(8,128)(2,1)S(1)}, u32[]{:S(2)}, u32[]{:S(2)}) %collective-permute-start.6) | collective-permute-done | bytes 262176 | tf_op jit(solution)/shard_map/ppermute | solution.py:454
  37.8 2.0 %grads.7 = (f32[64,128]{1,0:T(8,128)S(1)}, f32[1,1024]{1,0:T(1,128)S(1)}) custom-call(s32[1]{0:T(128)} %bitcast.role.refs_0_, bf16[128,4096]{1,0:T(8,128)(2,1)S(1)} %bitcast.32, bf16[128,4096]{1,0:T(8,128)(2,1)S(1)} %bitcast.25, bf16[128,4096]{1,0:T(8,128)(2,1)S(1)} %bitcast.38, bf16[128,4096]{1,0:T(8,128)(2,1)S(1)} %collective-permute-done.refs_2_.refs_4_, ...), custom_call_target="tpu_custom_call" | custom-call | flops 2000 | tf_op jit(solution)/shard_map/grads/pallas_call | solution.py:482
  39.8 0.9 %collective-permute-done.7.refs_9_ = bf16[128,512]{1,0:T(8,128)(2,1)S(1)} collective-permute-done((bf16[128,512]{1,0:T(8,128)(2,1)S(1)}, bf16[128,512]{1,0:T(8,128)(2,1)S(1)}, u32[]{:S(2)}, u32[]{:S(2)}) %collective-permute-start.7) | collective-permute-done | bytes 131104 | tf_op jit(solution)/shard_map/ppermute | solution.py:454
  40.6 0.9 %grads.8 = (f32[32,128]{1,0:T(8,128)S(1)}, f32[1,512]{1,0:T(1,128)S(1)}) custom-call(s32[1]{0:T(128)} %bitcast.role.refs_0_, bf16[128,4096]{1,0:T(8,128)(2,1)S(1)} %bitcast.33, bf16[128,4096]{1,0:T(8,128)(2,1)S(1)} %bitcast.26, bf16[128,4096]{1,0:T(8,128)(2,1)S(1)} %bitcast.39, bf16[128,4096]{1,0:T(8,128)(2,1)S(1)} %collective-permute-done.refs_2_.refs_4_, ...), custom_call_target="tpu_custom_call" | custom-call | flops 2000 | tf_op jit(solution)/shard_map/grads/pallas_call | solution.py:482
  41.5 1.9 %collective-permute-done.8.refs_9_ = bf16[128,512]{1,0:T(8,128)(2,1)S(1)} collective-permute-done((bf16[128,512]{1,0:T(8,128)(2,1)S(1)}, bf16[128,512]{1,0:T(8,128)(2,1)S(1)}, u32[]{:S(2)}, u32[]{:S(2)}) %collective-permute-start.8) | collective-permute-done | bytes 131104 | tf_op jit(solution)/shard_map/ppermute | solution.py:454
  43.4 0.9 %grads.9 = (f32[32,128]{1,0:T(8,128)S(1)}, f32[1,512]{1,0:T(1,128)S(1)}) custom-call(s32[1]{0:T(128)} %bitcast.role.refs_0_, bf16[128,4096]{1,0:T(8,128)(2,1)S(1)} %bitcast.34, bf16[128,4096]{1,0:T(8,128)(2,1)S(1)} %bitcast.27, bf16[128,4096]{1,0:T(8,128)(2,1)S(1)} %bitcast.40, bf16[128,4096]{1,0:T(8,128)(2,1)S(1)} %collective-permute-done.refs_2_.refs_4_, ...), custom_call_target="tpu_custom_call" | custom-call | flops 2000 | tf_op jit(solution)/shard_map/grads/pallas_call | solution.py:482
  44.4 0.0 copy-start.5
  44.4 23.1 %all_to_all.5.parts = f32[16,18,128]{2,1,0:T(8,128)S(1)} all-to-all(f32[16,18,128]{2,1,0:T(8,128)S(1)} %pack.1), channel_id=1, replica_groups=mesh['section'=2,'seq'=16] {'seq'}, dimensions={0} | all-to-all | bytes 294912 | tf_op jit(solution)/shard_map/all_to_all | solution.py:508
  67.4 0.0 copy-start.6
  67.4 0.0 copy-done.5
  67.5 0.7 copy-done.6
  68.1 0.7 %step.1 = (f32[1,256]{1,0:T(1,128)}, f32[16,128]{1,0:T(8,128)}) custom-call(s32[1]{0:T(128)} %bitcast.role.refs_0_, f32[16,18,128]{2,1,0:T(8,128)S(1)} %all_to_all.5.parts, f32[1,256]{1,0:T(1,128)S(1)} %copy-done.6, f32[16,128]{1,0:T(8,128)S(1)} %bitcast.43), custom_call_target="tpu_custom_call" | custom-call | tf_op jit(solution)/shard_map/step/pallas_call | solution.py:509
  (3 shorter events, 0.1 us)
Async XLA Ops:
  0.6 1.7 %copy-start = (bf16[1,128,4096]{2,1,0:T(8,128)(2,1)S(1)}, bf16[1,128,4096]{2,1,0:T(8,128)(2,1)}, u32[]{:S(2)}) copy-start(bf16[1,128,4096]{2,1,0:T(8,128)(2,1)} %param.9) | copy-start | bytes 3145732
  0.6 18.6 %copy-start.1 = (bf16[128,4096]{1,0:T(8,128)(2,1)S(1)}, bf16[128,4096]{1,0:T(8,128)(2,1)}, u32[]{:S(2)}) copy-start(bf16[128,4096]{1,0:T(8,128)(2,1)} %refs_5_.9) | copy-start | bytes 3145732
  0.7 18.6 %copy-start.2 = (bf16[1,128,4096]{2,1,0:T(8,128)(2,1)S(1)}, bf16[1,128,4096]{2,1,0:T(8,128)(2,1)}, u32[]{:S(2)}) copy-start(bf16[1,128,4096]{2,1,0:T(8,128)(2,1)} %param.8) | copy-start | bytes 3145732
  0.8 18.4 %collective-permute-start.4 = (bf16[128,2176]{1,0:T(8,128)(2,1)S(1)}, bf16[128,2176]{1,0:T(8,128)(2,1)S(1)}, u32[]{:S(2)}, u32[]{:S(2)}) collective-permute-start(bf16[128,2176]{1,0:T(8,128)(2,1)S(1)} %get-tuple-element.21), channel_id=1, source_target_pairs={{16,0},{17,1},{18,2},{19,3},{20,4},{21,5},{22,6},{23,7},{24,8},{25... | collective-permute-start | bytes 1671176 | tf_op jit(solution)/shard_map/ppermute | solution.py:417
  2.4 18.5 %copy-start.4 = (bf16[1,128,256]{2,1,0:T(8,128)(2,1)S(1)}, bf16[1,128,256]{2,1,0:T(8,128)(2,1)}, u32[]{:S(2)}) copy-start(bf16[1,128,256]{2,1,0:T(8,128)(2,1)} %param.11) | copy-start | bytes 196612
  2.4 23.1 %collective-permute-start = (bf16[128,4096]{1,0:T(8,128)(2,1)S(1)}, bf16[128,4096]{1,0:T(8,128)(2,1)S(1)}, u32[]{:S(2)}, u32[]{:S(2)}) collective-permute-start(bf16[128,4096]{1,0:T(8,128)(2,1)S(1)} %bitcast.12), channel_id=1, source_target_pairs={{0,1},{1,2},{2,3},{3,4},{4,5},{5,6},{6,7},{7,8},{8,9},{9,10},{10,1... | collective-permute-start | bytes 3145736 | tf_op jit(solution)/shard_map/ppermute | solution.py:426
  4.8 27.7 %collective-permute-start.1 = (bf16[128,4096]{1,0:T(8,128)(2,1)}, bf16[128,4096]{1,0:T(8,128)(2,1)S(1)}, u32[]{:S(2)}, u32[]{:S(2)}) collective-permute-start(bf16[128,4096]{1,0:T(8,128)(2,1)} %bitcast.35), channel_id=1, source_target_pairs={{0,1},{1,2},{2,3},{3,4},{4,5},{5,6},{6,7},{7,8},{8,9},{9,10},{10,1... | collective-permute-start | bytes 3145736 | tf_op jit(solution)/shard_map/ppermute | solution.py:427
  9.4 11.7 %collective-permute-start.2 = (bf16[128,2048]{1,0:T(8,128)(2,1)S(1)}, bf16[128,2048]{1,0:T(8,128)(2,1)S(1)}, u32[]{:S(2)}, u32[]{:S(2)}) collective-permute-start(bf16[128,2048]{1,0:T(8,128)(2,1)S(1)} %get-tuple-element.18.refs_1_.refs_4_.refs_6_), channel_id=1, source_target_pairs={{17,16},{18,17},{19,18},{20,19},{21,20},{22,21},{23,22},{24,23},{2... | collective-permute-start | bytes 1572872 | tf_op jit(solution)/shard_map/ppermute | solution.py:421
  19.6 4.5 %collective-permute-start.5 = (bf16[128,2048]{1,0:T(8,128)(2,1)S(1)}, bf16[128,2048]{1,0:T(8,128)(2,1)S(1)}, u32[]{:S(2)}, u32[]{:S(2)}) collective-permute-start(bf16[128,2048]{1,0:T(8,128)(2,1)S(1)} %weigh.1.refs_1_.refs_6_), channel_id=1, source_target_pairs={{17,16},{18,17},{19,18},{20,19},{21,20},{22,21},{23,22},{24,23},{2... | collective-permute-start | bytes 1572872 | tf_op jit(solution)/shard_map/ppermute | solution.py:421
  21.3 11.2 %collective-permute-start.3 = (bf16[128,1024]{1,0:T(8,128)(2,1)S(1)}, bf16[128,1024]{1,0:T(8,128)(2,1)S(1)}, u32[]{:S(2)}, u32[]{:S(2)}) collective-permute-start(bf16[128,1024]{1,0:T(8,128)(2,1)S(1)} %filter.5.refs_6_.refs_8_), channel_id=1, source_target_pairs={{16,0},{17,1},{18,2},{19,3},{20,4},{21,5},{22,6},{23,7},{24,8},{25... | collective-permute-start | bytes 786440 | tf_op jit(solution)/shard_map/ppermute | solution.py:454
  22.8 15.0 %collective-permute-start.6 = (bf16[128,1024]{1,0:T(8,128)(2,1)S(1)}, bf16[128,1024]{1,0:T(8,128)(2,1)S(1)}, u32[]{:S(2)}, u32[]{:S(2)}) collective-permute-start(bf16[128,1024]{1,0:T(8,128)(2,1)S(1)} %filter.6.refs_6_.refs_8_), channel_id=1, source_target_pairs={{16,0},{17,1},{18,2},{19,3},{20,4},{21,5},{22,6},{23,7},{24,8},{25... | collective-permute-start | bytes 786440 | tf_op jit(solution)/shard_map/ppermute | solution.py:454
  24.2 16.5 %collective-permute-start.7 = (bf16[128,512]{1,0:T(8,128)(2,1)S(1)}, bf16[128,512]{1,0:T(8,128)(2,1)S(1)}, u32[]{:S(2)}, u32[]{:S(2)}) collective-permute-start(bf16[128,512]{1,0:T(8,128)(2,1)S(1)} %filter.7.refs_6_.refs_8_), channel_id=1, source_target_pairs={{16,0},{17,1},{18,2},{19,3},{20,4},{21,5},{22,6},{23,7},{24,8},{25... | collective-permute-start | bytes 393224 | tf_op jit(solution)/shard_map/ppermute | solution.py:454
  25.5 17.9 %collective-permute-start.8 = (bf16[128,512]{1,0:T(8,128)(2,1)S(1)}, bf16[128,512]{1,0:T(8,128)(2,1)S(1)}, u32[]{:S(2)}, u32[]{:S(2)}) collective-permute-start(bf16[128,512]{1,0:T(8,128)(2,1)S(1)} %filter.8.refs_7_.refs_8_), channel_id=1, source_target_pairs={{16,0},{17,1},{18,2},{19,3},{20,4},{21,5},{22,6},{23,7},{24,8},{25... | collective-permute-start | bytes 393224 | tf_op jit(solution)/shard_map/ppermute | solution.py:454
  31.4 1.2 %copy-start.3 = (bf16[1,128,4096]{2,1,0:T(8,128)(2,1)S(1)}, bf16[1,128,4096]{2,1,0:T(8,128)(2,1)}, u32[]{:S(2)}) copy-start(bf16[1,128,4096]{2,1,0:T(8,128)(2,1)} %param.10) | copy-start | bytes 3145732
  44.4 23.1 %copy-start.5 = (f32[1,128,16]{1,2,0:T(8,128)S(1)}, f32[1,128,16]{1,2,0:T(8,128)}, u32[]{:S(2)}) copy-start(f32[1,128,16]{1,2,0:T(8,128)} %param.13) | copy-start | bytes 24580
  67.4 0.7 copy-start.6

commit v7 on v5

--- a/solution.py
+++ b/solution.py
@@ -11,8 +11,8 @@
 BF16 = jnp.bfloat16
 LANES = 128
 SUB = 32
-CHUNK_EDGES = (0, 2, 4, 6, 7, 8)
-HALO_EDGES = (0, 2, 4, 6, 8)
+CHUNK_EDGES = (0, 3, 6, 7, 8)
+HALO_EDGES = (0, 3, 6, 8)
 
 
 def lane_of(shape):
@@ -217,58 +217,31 @@
         tap_grad[pl.ds(8 * pair, 8), :] = diagonal_sums(blocks)
 
 
-def halves_of(role, step, zero, one):
-    mine = (role[0] >> (step + 1)) & 1 > 0
-    return jnp.where(mine, zero, one), jnp.where(mine, one, zero)
-
-
-def pack_kernel(owners, role, *refs):
-    count = (len(refs) - 2) // 2
-    taps, steers, (give, keep) = refs[:count], refs[count : 2 * count], refs[2 * count :]
+def pack_kernel(owners, *refs):
+    count = (len(refs) - 1) // 2
+    taps, steers, out = refs[:count], refs[count : 2 * count], refs[-1]
     groups = sum(ref.shape[0] for ref in taps) // owners
     channels = sum(ref.shape[1] for ref in steers) // owners
 
-    def part(parts, axis, owner, size):
-        at = owner * size
+    def part(parts, axis, at, size):
         for ref in parts:
             if at < ref.shape[axis]:
                 return ref[at : at + size, :] if axis == 0 else ref[:, at : at + size]
             at -= ref.shape[axis]
 
-    def packed(owner):
-        steer = part(steers, 1, owner, channels)
-        lines = [steer[:, at : at + LANES] for at in range(0, channels, LANES)]
-        short = LANES - lines[-1].shape[1]
-        if short > 0:
-            lines[-1] = jnp.concatenate([lines[-1], jnp.zeros((1, short), F32)], 1)
-        return [part(taps, 0, owner, groups)] + lines
-
-    order = reversed_bits(owners)
-    for i, (low, high) in enumerate(zip(order[: owners // 2], order[owners // 2 :])):
-        at = 0
-        for zero, one in zip(packed(low), packed(high)):
-            lines = zero.shape[0]
-            give[i, pl.ds(at, lines), :], keep[i, pl.ds(at, lines), :] = halves_of(role, 0, zero, one)
-            at += lines
-
-
-def reversed_bits(count):
-    order = [0]
-    while len(order) < count:
-        order = [2 * i for i in order] + [2 * i + 1 for i in order]
-    return order
-
-
-def fold_kernel(step, role, kept, arrived, give, keep):
-    count = give.shape[0]
-    for i in range(count):
-        zero = kept[i] + arrived[i]
-        one = kept[count + i] + arrived[count + i]
-        give[i], keep[i] = halves_of(role, step, zero, one)
-
-
-def step_kernel(role, kept, arrived, steer_second, filter_second, steer_out, filter_out):
-    total = kept[0] + arrived[0]
+    for owner in range(owners):
+        lines = [part(taps, 0, owner * groups, groups)]
+        for at in range(0, channels, LANES):
+            size = min(LANES, channels - at)
+            steer = part(steers, 1, owner * channels + at, size)
+            if size < LANES:
+                steer = jnp.concatenate([steer, jnp.zeros((1, LANES - size), F32)], 1)
+            lines.append(steer)
+        out[owner] = jnp.concatenate(lines, 0).astype(BF16)
+
+
+def step_kernel(role, parts, steer_second, filter_second, steer_out, filter_out):
+    total = jnp.sum(parts[...].astype(F32), 0)
     groups = filter_second.shape[0]
     tap_grad = total[:groups]
     lane = lane_of(tap_grad.shape)
@@ -318,7 +291,7 @@
     group_size = channels // groups
     sections, seqs = lax.axis_size("section"), lax.axis_size("seq")
     my_section = lax.axis_index("section")
-    role = (2 * lax.axis_index("seq") + (my_section == 0)).astype(jnp.int32).reshape(1)
+    role = (my_section == 0).astype(jnp.int32).reshape(1)
 
     edges = [channels * eighths // 8 for eighths in CHUNK_EDGES]
     bounds = list(zip(edges[:-1], edges[1:]))
@@ -368,21 +341,28 @@
     for hop in range(sections - 1):
         split = [channels * eighths // 8 for eighths in HALO_EDGES] if hop == 0 else edges
         starts, ends = split[:-1], split[1:]
-        owns = []
-        for first, last in zip(starts, ends):
+        owns, halos = [], []
+
+        def send_halo(after):
+            first, last = starts[len(owns)], ends[len(owns)]
             array, offset = next(entry for entry, edge in zip(incoming, edges) if edge == first)
             if hop == 0 and first == 0:
                 owns.append(first_weigh(last))
             else:
-                owns.append(weigh(array, first, last, offset, tuple(owns[-1:])))
+                owns.append(weigh(array, first, last, offset, after))
+            halos.append(lax.ppermute(owns[-1], ("section", "seq"), behind))
+
+        send_halo(())
         if hop == 0:
             mid_sent, inputs_sent, _ = lax.optimization_barrier((mid_gate, layer_inputs, owns[0]))
             mid_halo = lax.ppermute(mid_sent, ("section", "seq"), ahead)
             inputs_halo = lax.ppermute(inputs_sent, ("section", "seq"), ahead)
-        halos = [lax.ppermute(own, ("section", "seq"), behind) for own in owns]
+        send_halo((owns[0],))
         sources, outgoing, received = [], [], []
         for k, (first, last) in enumerate(bounds):
             part = max(i for i, start in enumerate(starts) if start <= first)
+            while part >= len(owns):
+                send_halo(tuple(received[:1]))
             at = (first - starts[part]) // block
             array, offset = incoming[k]
             before = tuple(outgoing[-1:])
@@ -443,42 +423,26 @@
 
     own_channels = channels // seqs
     lines = groups // seqs + pl.cdiv(own_channels, LANES)
-    steps = seqs.bit_length() - 1
-
-    def halves(count):
-        return [jax.ShapeDtypeStruct((count, lines, LANES), F32)] * 2
-
     vmem = pl.BlockSpec(memory_space=pltpu.VMEM)
-    give, keep = pl.pallas_call(
+    packed = pl.pallas_call(
         functools.partial(pack_kernel, seqs),
-        in_specs=[SMEM] + [vmem] * (2 * len(grads)),
-        out_specs=[vmem] * 2,
-        out_shape=halves(seqs // 2),
+        in_specs=[vmem] * (2 * len(grads)),
+        out_specs=vmem,
+        out_shape=jax.ShapeDtypeStruct((seqs, lines, LANES), BF16),
         compiler_params=SMALL,
         name="pack",
-    )(role, *tap_grads, *steer_grads)
-    for step in range(steps):
-        route = [(i, i ^ (1 << step)) for i in range(seqs)]
-        arrived = lax.ppermute(give, "seq", route)
-        if step < steps - 1:
-            give, keep = pl.pallas_call(
-                functools.partial(fold_kernel, step + 1),
-                in_specs=[SMEM, vmem, vmem],
-                out_specs=[vmem] * 2,
-                out_shape=halves(keep.shape[0] // 2),
-                compiler_params=SMALL,
-                name="fold",
-            )(role, keep, arrived)
+    )(*tap_grads, *steer_grads)
+    parts = lax.all_to_all(packed, "seq", 0, 0)
     steer_step, filter_step = pl.pallas_call(
         step_kernel,
-        in_specs=[SMEM] + [vmem] * 4,
+        in_specs=[SMEM] + [vmem] * 3,
         out_shape=[
             jax.ShapeDtypeStruct((1, own_channels), F32),
             jax.ShapeDtypeStruct((groups // seqs, filt_len), F32),
         ],
         compiler_params=SMALL,
         name="step",
-    )(role, keep, arrived, steer_second, filter_second[0].T)
+    )(role, parts, steer_second, filter_second[0].T)
     return steer_step, filter_step.T[None]
 
 

time: 60.7 us -> 58.8 us (0.969)
  the two profiles are of different devices: /device:TPU:0 before, /device:TPU:2 now
where the time goes in v7:
time: 58.8 us; the launch traced here: 58.3 us
  blocking collectives  18.3 us (31%)
  Pallas kernels  14.5 us (25%)
  starting transfers between devices  12.3 us (21%)
  waiting for transfers between devices  9.11 us (15%)
  local copies, waits for them, and re-layouts  3.1 us (5%)
  between operations  0.91 us (2%)
    all_to_all x1, blocking collectives, body(): parts = lax.all_to_all(packed, 'seq', 0, 0)  18.3 us
    pallas_call x4, Pallas kernels, body(): call(functools.partial(grad_kernel, group_size), (width // block,), [SMEM...  7.07 us
    ppermute x4, starting transfers between devices, body(): received.append(lax.ppermute(out, 'section', down))  6.99 us
    ppermute x4, waiting for transfers between devices, body(): received.append(lax.ppermute(out, 'section', down))  5.71 us
    pallas_call x4, Pallas kernels, body(): call(functools.partial(filter_kernel, group_size), ((last - first) // blo...  4.16 us
    ppermute x3, starting transfers between devices, send_halo(): halos.append(lax.ppermute(owns[-1], ('section', 'seq'), behind))  3.88 us
    ppermute x3, waiting for transfers between devices, send_halo(): halos.append(lax.ppermute(owns[-1], ('section', 'seq'), behind))  3.39 us
    unnamed x16, local copies, waits for them, and re-layouts  3.1 us
  transfers between devices with their start and end apart: 9, of which 2 were waited for; matrix products, arithmetic and copies ran while one was open for 0% of the time, Pallas kernels for 20%

profile of v7, /device:TPU:2, one launch (start us, length us, event | category | flops | bytes accessed | tf_op | source)
XLA Modules:
  0.0 58.3 jit_solution(15938263726729033241)
XLA Ops:
  0.6 0.0 copy-start
  0.6 0.0 copy-start.1
  0.7 1.4 %first_weigh.1.refs_1_.refs_3_.refs_6_ = bf16[128,1536]{1,0:T(8,128)(2,1)S(1)} custom-call(s32[1]{0:T(128)} %bitcast.role.refs_0_, bf16[128,4096]{1,0:T(8,128)(2,1)} %bitcast.24, bf16[128,4096]{1,0:T(8,128)(2,1)} %refs_5_.7), custom_call_target="tpu_custom_call" | custom-call | tf_op jit(solution)/shard_map/first_weigh/pallas_call | solution.py:320
  2.1 1.3 %collective-permute-start.2 = (bf16[128,1536]{1,0:T(8,128)(2,1)S(1)}, bf16[128,1536]{1,0:T(8,128)(2,1)S(1)}, u32[]{:S(2)}, u32[]{:S(2)}) collective-permute-start(bf16[128,1536]{1,0:T(8,128)(2,1)S(1)} %first_weigh.1.refs_1_.refs_3_.refs_6_), channel_id=1, source_target_pairs={{17,16},{18,17},{19,18},{20,19},{21,20},{22,21},{23,22},{24,23},{2... | collective-permute-start | bytes 1179656 | tf_op jit(solution)/shard_map/ppermute | solution.py:353
  3.4 0.0 copy-done
  3.4 0.7 %collective-permute-start = (bf16[128,4096]{1,0:T(8,128)(2,1)S(1)}, bf16[128,4096]{1,0:T(8,128)(2,1)S(1)}, u32[]{:S(2)}, u32[]{:S(2)}) collective-permute-start(bf16[128,4096]{1,0:T(8,128)(2,1)S(1)} %bitcast.11), channel_id=1, source_target_pairs={{0,1},{1,2},{2,3},{3,4},{4,5},{5,6},{6,7},{7,8},{8,9},{9,10},{10,1... | collective-permute-start | bytes 3145736 | tf_op jit(solution)/shard_map/ppermute | solution.py:358
  4.1 0.7 %collective-permute-start.1 = (bf16[128,4096]{1,0:T(8,128)(2,1)}, bf16[128,4096]{1,0:T(8,128)(2,1)S(1)}, u32[]{:S(2)}, u32[]{:S(2)}) collective-permute-start(bf16[128,4096]{1,0:T(8,128)(2,1)} %bitcast.31), channel_id=1, source_target_pairs={{0,1},{1,2},{2,3},{3,4},{4,5},{5,6},{6,7},{7,8},{8,9},{9,10},{10,1... | collective-permute-start | bytes 3145736 | tf_op jit(solution)/shard_map/ppermute | solution.py:359
  4.9 0.0 copy-done.1
  4.9 0.0 copy-start.2
  4.9 1.2 %copy-done.2 = bf16[1,128,4096]{2,1,0:T(8,128)(2,1)S(1)} copy-done((bf16[1,128,4096]{2,1,0:T(8,128)(2,1)S(1)}, bf16[1,128,4096]{2,1,0:T(8,128)(2,1)}, u32[]{:S(2)}) %copy-start.2) | copy-done | bytes 1048600
  6.1 0.0 copy-start.5
  6.1 0.3 weigh.3.refs_1_.refs_6_
  6.4 1.3 %collective-permute-start.5 = (bf16[128,1536]{1,0:T(8,128)(2,1)S(1)}, bf16[128,1536]{1,0:T(8,128)(2,1)S(1)}, u32[]{:S(2)}, u32[]{:S(2)}) collective-permute-start(bf16[128,1536]{1,0:T(8,128)(2,1)S(1)} %weigh.3.refs_1_.refs_6_), channel_id=1, source_target_pairs={{17,16},{18,17},{19,18},{20,19},{21,20},{22,21},{23,22},{24,23},{2... | collective-permute-start | bytes 1179656 | tf_op jit(solution)/shard_map/ppermute | solution.py:353
  7.7 0.0 copy-done.5
  7.7 0.2 taps.1.refs_3_
  7.9 0.0 collective-permute-done.2.refs_2_.refs_7_
  7.9 1.6 %filter.4.refs_6_.refs_8_ = bf16[128,1536]{1,0:T(8,128)(2,1)S(1)} custom-call(s32[1]{0:T(128)} %bitcast.role.refs_0_, bf16[128,1536]{1,0:T(8,128)(2,1)S(1)} %first_weigh.1.refs_1_.refs_3_.refs_6_, bf16[128,1536]{1,0:T(8,128)(2,1)S(1)} %collective-permute-done.2.refs_2_.refs_7_, f32[256,128]{1,0:T(8,128)S(1)} %taps.1.refs_3_, bf16[128,4096]{1,0:T(8,128)(2,1)S(1)} %bitcast.12, ...), custom_call_target="tpu_custom_call" | custom-call | flops 1000 | tf_op jit(solution)/shard_map/filter/pallas_call | solution.py:369
  9.5 0.0 copy-start.3
  9.5 3.1 %collective-permute-start.3 = (bf16[128,1536]{1,0:T(8,128)(2,1)S(1)}, bf16[128,1536]{1,0:T(8,128)(2,1)S(1)}, u32[]{:S(2)}, u32[]{:S(2)}) collective-permute-start(bf16[128,1536]{1,0:T(8,128)(2,1)S(1)} %filter.4.refs_6_.refs_8_), channel_id=1, source_target_pairs={{16,0},{17,1},{18,2},{19,3},{20,4},{21,5},{22,6},{23,7},{24,8},{25... | collective-permute-start | bytes 1179656 | tf_op jit(solution)/shard_map/ppermute | solution.py:382
  12.6 0.0 collective-permute-done.5.refs_2_.refs_7_
  12.6 1.6 %filter.5.refs_6_.refs_8_ = bf16[128,1536]{1,0:T(8,128)(2,1)S(1)} custom-call(s32[1]{0:T(128)} %bitcast.role.refs_0_, bf16[128,1536]{1,0:T(8,128)(2,1)S(1)} %weigh.3.refs_1_.refs_6_, bf16[128,1536]{1,0:T(8,128)(2,1)S(1)} %collective-permute-done.5.refs_2_.refs_7_, f32[256,128]{1,0:T(8,128)S(1)} %taps.1.refs_3_, bf16[128,4096]{1,0:T(8,128)(2,1)S(1)} %bitcast.13, ...), custom_call_target="tpu_custom_call" | custom-call | flops 1000 | tf_op jit(solution)/shard_map/filter/pallas_call | solution.py:369
  14.2 1.3 %collective-permute-start.6 = (bf16[128,1536]{1,0:T(8,128)(2,1)S(1)}, bf16[128,1536]{1,0:T(8,128)(2,1)S(1)}, u32[]{:S(2)}, u32[]{:S(2)}) collective-permute-start(bf16[128,1536]{1,0:T(8,128)(2,1)S(1)} %filter.5.refs_6_.refs_8_), channel_id=1, source_target_pairs={{16,0},{17,1},{18,2},{19,3},{20,4},{21,5},{22,6},{23,7},{24,8},{25... | collective-permute-start | bytes 1179656 | tf_op jit(solution)/shard_map/ppermute | solution.py:382
  15.5 5.7 %collective-permute-done.3.refs_3_.refs_9_ = bf16[128,1536]{1,0:T(8,128)(2,1)S(1)} collective-permute-done((bf16[128,1536]{1,0:T(8,128)(2,1)S(1)}, bf16[128,1536]{1,0:T(8,128)(2,1)S(1)}, u32[]{:S(2)}, u32[]{:S(2)}) %collective-permute-start.3) | collective-permute-done | bytes 393248 | tf_op jit(solution)/shard_map/ppermute | solution.py:382
  21.2 0.0 copy-done.3
  21.3 0.2 weigh.2.refs_1_.refs_6_
  21.5 1.3 %collective-permute-start.4 = (bf16[128,1024]{1,0:T(8,128)(2,1)S(1)}, bf16[128,1024]{1,0:T(8,128)(2,1)S(1)}, u32[]{:S(2)}, u32[]{:S(2)}) collective-permute-start(bf16[128,1024]{1,0:T(8,128)(2,1)S(1)} %weigh.2.refs_1_.refs_6_), channel_id=1, source_target_pairs={{17,16},{18,17},{19,18},{20,19},{21,20},{22,21},{23,22},{24,23},{2... | collective-permute-start | bytes 786440 | tf_op jit(solution)/shard_map/ppermute | solution.py:353
  22.8 3.4 %collective-permute-done.4.refs_2_.refs_7_ = bf16[128,1024]{1,0:T(8,128)(2,1)S(1)} collective-permute-done((bf16[128,1024]{1,0:T(8,128)(2,1)S(1)}, bf16[128,1024]{1,0:T(8,128)(2,1)S(1)}, u32[]{:S(2)}, u32[]{:S(2)}) %collective-permute-start.4) | collective-permute-done | bytes 262176 | tf_op jit(solution)/shard_map/ppermute | solution.py:353
  26.1 0.5 filter.6.refs_6_.refs_8_
  26.6 1.3 %collective-permute-start.7 = (bf16[128,512]{1,0:T(8,128)(2,1)S(1)}, bf16[128,512]{1,0:T(8,128)(2,1)S(1)}, u32[]{:S(2)}, u32[]{:S(2)}) collective-permute-start(bf16[128,512]{1,0:T(8,128)(2,1)S(1)} %filter.6.refs_6_.refs_8_), channel_id=1, source_target_pairs={{16,0},{17,1},{18,2},{19,3},{20,4},{21,5},{22,6},{23,7},{24,8},{25... | collective-permute-start | bytes 393224 | tf_op jit(solution)/shard_map/ppermute | solution.py:382
  27.9 0.5 filter.7.refs_4_.refs_8_
  28.4 1.3 %collective-permute-start.8 = (bf16[128,512]{1,0:T(8,128)(2,1)S(1)}, bf16[128,512]{1,0:T(8,128)(2,1)S(1)}, u32[]{:S(2)}, u32[]{:S(2)}) collective-permute-start(bf16[128,512]{1,0:T(8,128)(2,1)S(1)} %filter.7.refs_4_.refs_8_), channel_id=1, source_target_pairs={{16,0},{17,1},{18,2},{19,3},{20,4},{21,5},{22,6},{23,7},{24,8},{25... | collective-permute-start | bytes 393224 | tf_op jit(solution)/shard_map/ppermute | solution.py:382
  29.7 0.0 collective-permute-done.refs_2_.refs_4_
  29.8 0.2 turned_filter.4.refs_10_.refs_5_
  30.0 0.2 turned_filter.5.refs_10_.refs_5_
  30.3 0.0 copy-start.4
  30.3 0.0 collective-permute-done.1.refs_5_
  30.3 1.2 %copy-done.4 = bf16[1,128,4096]{2,1,0:T(8,128)(2,1)S(1)} copy-done((bf16[1,128,4096]{2,1,0:T(8,128)(2,1)S(1)}, bf16[1,128,4096]{2,1,0:T(8,128)(2,1)}, u32[]{:S(2)}) %copy-start.4) | copy-done | bytes 1048600
  31.5 2.7 %grads.4 = (f32[96,128]{1,0:T(8,128)S(1)}, f32[1,1536]{1,0:T(1,128)S(1)}) custom-call(s32[1]{0:T(128)} %bitcast.role.refs_0_, bf16[128,4096]{1,0:T(8,128)(2,1)S(1)} %bitcast.27, bf16[128,4096]{1,0:T(8,128)(2,1)S(1)} %bitcast.20, bf16[128,4096]{1,0:T(8,128)(2,1)S(1)} %bitcast.32, bf16[128,4096]{1,0:T(8,128)(2,1)S(1)} %collective-permute-done.refs_2_.refs_4_, ...), custom_call_target="tpu_custom_call" | custom-call | flops 2000 | tf_op jit(solution)/shard_map/grads/pallas_call | solution.py:409
  34.2 0.0 collective-permute-done.6.refs_9_
  34.2 2.7 %grads.5 = (f32[96,128]{1,0:T(8,128)S(1)}, f32[1,1536]{1,0:T(1,128)S(1)}) custom-call(s32[1]{0:T(128)} %bitcast.role.refs_0_, bf16[128,4096]{1,0:T(8,128)(2,1)S(1)} %bitcast.28, bf16[128,4096]{1,0:T(8,128)(2,1)S(1)} %bitcast.21, bf16[128,4096]{1,0:T(8,128)(2,1)S(1)} %bitcast.33, bf16[128,4096]{1,0:T(8,128)(2,1)S(1)} %collective-permute-done.refs_2_.refs_4_, ...), custom_call_target="tpu_custom_call" | custom-call | flops 2000 | tf_op jit(solution)/shard_map/grads/pallas_call | solution.py:409
  36.9 0.0 collective-permute-done.7.refs_9_
  36.9 0.8 %grads.6 = (f32[32,128]{1,0:T(8,128)S(1)}, f32[1,512]{1,0:T(1,128)S(1)}) custom-call(s32[1]{0:T(128)} %bitcast.role.refs_0_, bf16[128,4096]{1,0:T(8,128)(2,1)S(1)} %bitcast.29, bf16[128,4096]{1,0:T(8,128)(2,1)S(1)} %bitcast.22, bf16[128,4096]{1,0:T(8,128)(2,1)S(1)} %bitcast.34, bf16[128,4096]{1,0:T(8,128)(2,1)S(1)} %collective-permute-done.refs_2_.refs_4_, ...), custom_call_target="tpu_custom_call" | custom-call | flops 2000 | tf_op jit(solution)/shard_map/grads/pallas_call | solution.py:409
  37.7 0.0 collective-permute-done.8.refs_9_
  37.7 0.8 %grads.7 = (f32[32,128]{1,0:T(8,128)S(1)}, f32[1,512]{1,0:T(1,128)S(1)}) custom-call(s32[1]{0:T(128)} %bitcast.role.refs_0_, bf16[128,4096]{1,0:T(8,128)(2,1)S(1)} %bitcast.30, bf16[128,4096]{1,0:T(8,128)(2,1)S(1)} %bitcast.23, bf16[128,4096]{1,0:T(8,128)(2,1)S(1)} %bitcast.35, bf16[128,4096]{1,0:T(8,128)(2,1)S(1)} %collective-permute-done.refs_2_.refs_4_, ...), custom_call_target="tpu_custom_call" | custom-call | flops 2000 | tf_op jit(solution)/shard_map/grads/pallas_call | solution.py:409
  38.6 0.0 copy-start.6
  38.6 18.3 %all_to_all.5.parts = bf16[16,18,128]{2,1,0:T(8,128)(2,1)S(1)} all-to-all(bf16[16,18,128]{2,1,0:T(8,128)(2,1)S(1)} %pack.1), channel_id=1, replica_groups=mesh['section'=2,'seq'=16] {'seq'}, dimensions={0} | all-to-all | bytes 147456 | tf_op jit(solution)/shard_map/all_to_all | solution.py:435
  56.9 0.0 copy-start.7
  56.9 0.0 copy-done.6
  56.9 0.7 %copy-done.7 = f32[1,256]{1,0:T(1,128)S(1)} copy-done((f32[1,256]{1,0:T(1,128)S(1)}, f32[1,256]{1,0:T(1,128)}, u32[]{:S(2)}) %copy-start.7) | copy-done | bytes 1048
  57.6 0.7 %step.1 = (f32[1,256]{1,0:T(1,128)}, f32[16,128]{1,0:T(8,128)}) custom-call(s32[1]{0:T(128)} %bitcast.role.refs_0_, bf16[16,18,128]{2,1,0:T(8,128)(2,1)S(1)} %all_to_all.5.parts, f32[1,256]{1,0:T(1,128)S(1)} %copy-done.7, f32[16,128]{1,0:T(8,128)S(1)} %bitcast.37), custom_call_target="tpu_custom_call" | custom-call | tf_op jit(solution)/shard_map/step/pallas_call | solution.py:436
  (3 shorter events, 0.1 us)
Async XLA Ops:
  0.6 2.8 %copy-start = (bf16[1,128,4096]{2,1,0:T(8,128)(2,1)S(1)}, bf16[1,128,4096]{2,1,0:T(8,128)(2,1)}, u32[]{:S(2)}) copy-start(bf16[1,128,4096]{2,1,0:T(8,128)(2,1)} %param.9) | copy-start | bytes 3145732
  0.6 4.2 %copy-start.1 = (bf16[128,4096]{1,0:T(8,128)(2,1)S(1)}, bf16[128,4096]{1,0:T(8,128)(2,1)}, u32[]{:S(2)}) copy-start(bf16[128,4096]{1,0:T(8,128)(2,1)} %refs_5_.7) | copy-start | bytes 3145732
  2.1 5.8 %collective-permute-start.2 = (bf16[128,1536]{1,0:T(8,128)(2,1)S(1)}, bf16[128,1536]{1,0:T(8,128)(2,1)S(1)}, u32[]{:S(2)}, u32[]{:S(2)}) collective-permute-start(bf16[128,1536]{1,0:T(8,128)(2,1)S(1)} %first_weigh.1.refs_1_.refs_3_.refs_6_), channel_id=1, source_target_pairs={{17,16},{18,17},{19,18},{20,19},{21,20},{22,21},{23,22},{24,23},{2... | collective-permute-start | bytes 1179656 | tf_op jit(solution)/shard_map/ppermute | solution.py:353
  3.4 26.3 %collective-permute-start = (bf16[128,4096]{1,0:T(8,128)(2,1)S(1)}, bf16[128,4096]{1,0:T(8,128)(2,1)S(1)}, u32[]{:S(2)}, u32[]{:S(2)}) collective-permute-start(bf16[128,4096]{1,0:T(8,128)(2,1)S(1)} %bitcast.11), channel_id=1, source_target_pairs={{0,1},{1,2},{2,3},{3,4},{4,5},{5,6},{6,7},{7,8},{8,9},{9,10},{10,1... | collective-permute-start | bytes 3145736 | tf_op jit(solution)/shard_map/ppermute | solution.py:358
  4.1 26.2 %collective-permute-start.1 = (bf16[128,4096]{1,0:T(8,128)(2,1)}, bf16[128,4096]{1,0:T(8,128)(2,1)S(1)}, u32[]{:S(2)}, u32[]{:S(2)}) collective-permute-start(bf16[128,4096]{1,0:T(8,128)(2,1)} %bitcast.31), channel_id=1, source_target_pairs={{0,1},{1,2},{2,3},{3,4},{4,5},{5,6},{6,7},{7,8},{8,9},{9,10},{10,1... | collective-permute-start | bytes 3145736 | tf_op jit(solution)/shard_map/ppermute | solution.py:359
  4.9 1.2 %copy-start.2 = (bf16[1,128,4096]{2,1,0:T(8,128)(2,1)S(1)}, bf16[1,128,4096]{2,1,0:T(8,128)(2,1)}, u32[]{:S(2)}) copy-start(bf16[1,128,4096]{2,1,0:T(8,128)(2,1)} %param.8) | copy-start | bytes 3145732
  6.1 1.6 %copy-start.5 = (bf16[1,128,256]{2,1,0:T(8,128)(2,1)S(1)}, bf16[1,128,256]{2,1,0:T(8,128)(2,1)}, u32[]{:S(2)}) copy-start(bf16[1,128,256]{2,1,0:T(8,128)(2,1)} %param.11) | copy-start | bytes 196612
  6.4 6.2 %collective-permute-start.5 = (bf16[128,1536]{1,0:T(8,128)(2,1)S(1)}, bf16[128,1536]{1,0:T(8,128)(2,1)S(1)}, u32[]{:S(2)}, u32[]{:S(2)}) collective-permute-start(bf16[128,1536]{1,0:T(8,128)(2,1)S(1)} %weigh.3.refs_1_.refs_6_), channel_id=1, source_target_pairs={{17,16},{18,17},{19,18},{20,19},{21,20},{22,21},{23,22},{24,23},{2... | collective-permute-start | bytes 1179656 | tf_op jit(solution)/shard_map/ppermute | solution.py:353
  9.5 11.7 %copy-start.3 = (bf16[1,128,4096]{2,1,0:T(8,128)(2,1)S(1)}, bf16[1,128,4096]{2,1,0:T(8,128)(2,1)}, u32[]{:S(2)}) copy-start(bf16[1,128,4096]{2,1,0:T(8,128)(2,1)} %param.8) | copy-start | bytes 3145732
  9.5 11.7 %collective-permute-start.3 = (bf16[128,1536]{1,0:T(8,128)(2,1)S(1)}, bf16[128,1536]{1,0:T(8,128)(2,1)S(1)}, u32[]{:S(2)}, u32[]{:S(2)}) collective-permute-start(bf16[128,1536]{1,0:T(8,128)(2,1)S(1)} %filter.4.refs_6_.refs_8_), channel_id=1, source_target_pairs={{16,0},{17,1},{18,2},{19,3},{20,4},{21,5},{22,6},{23,7},{24,8},{25... | collective-permute-start | bytes 1179656 | tf_op jit(solution)/shard_map/ppermute | solution.py:382
  14.2 20.0 %collective-permute-start.6 = (bf16[128,1536]{1,0:T(8,128)(2,1)S(1)}, bf16[128,1536]{1,0:T(8,128)(2,1)S(1)}, u32[]{:S(2)}, u32[]{:S(2)}) collective-permute-start(bf16[128,1536]{1,0:T(8,128)(2,1)S(1)} %filter.5.refs_6_.refs_8_), channel_id=1, source_target_pairs={{16,0},{17,1},{18,2},{19,3},{20,4},{21,5},{22,6},{23,7},{24,8},{25... | collective-permute-start | bytes 1179656 | tf_op jit(solution)/shard_map/ppermute | solution.py:382
  21.5 4.7 %collective-permute-start.4 = (bf16[128,1024]{1,0:T(8,128)(2,1)S(1)}, bf16[128,1024]{1,0:T(8,128)(2,1)S(1)}, u32[]{:S(2)}, u32[]{:S(2)}) collective-permute-start(bf16[128,1024]{1,0:T(8,128)(2,1)S(1)} %weigh.2.refs_1_.refs_6_), channel_id=1, source_target_pairs={{17,16},{18,17},{19,18},{20,19},{21,20},{22,21},{23,22},{24,23},{2... | collective-permute-start | bytes 786440 | tf_op jit(solution)/shard_map/ppermute | solution.py:353
  26.6 10.3 %collective-permute-start.7 = (bf16[128,512]{1,0:T(8,128)(2,1)S(1)}, bf16[128,512]{1,0:T(8,128)(2,1)S(1)}, u32[]{:S(2)}, u32[]{:S(2)}) collective-permute-start(bf16[128,512]{1,0:T(8,128)(2,1)S(1)} %filter.6.refs_6_.refs_8_), channel_id=1, source_target_pairs={{16,0},{17,1},{18,2},{19,3},{20,4},{21,5},{22,6},{23,7},{24,8},{25... | collective-permute-start | bytes 393224 | tf_op jit(solution)/shard_map/ppermute | solution.py:382
  28.4 9.3 %collective-permute-start.8 = (bf16[128,512]{1,0:T(8,128)(2,1)S(1)}, bf16[128,512]{1,0:T(8,128)(2,1)S(1)}, u32[]{:S(2)}, u32[]{:S(2)}) collective-permute-start(bf16[128,512]{1,0:T(8,128)(2,1)S(1)} %filter.7.refs_4_.refs_8_), channel_id=1, source_target_pairs={{16,0},{17,1},{18,2},{19,3},{20,4},{21,5},{22,6},{23,7},{24,8},{25... | collective-permute-start | bytes 393224 | tf_op jit(solution)/shard_map/ppermute | solution.py:382
  30.3 1.2 %copy-start.4 = (bf16[1,128,4096]{2,1,0:T(8,128)(2,1)S(1)}, bf16[1,128,4096]{2,1,0:T(8,128)(2,1)}, u32[]{:S(2)}) copy-start(bf16[1,128,4096]{2,1,0:T(8,128)(2,1)} %param.10) | copy-start | bytes 3145732
  38.6 18.3 %copy-start.6 = (f32[1,128,16]{1,2,0:T(8,128)S(1)}, f32[1,128,16]{1,2,0:T(8,128)}, u32[]{:S(2)}) copy-start(f32[1,128,16]{1,2,0:T(8,128)} %param.13) | copy-start | bytes 24580
  56.9 0.7 %copy-start.7 = (f32[1,256]{1,0:T(1,128)S(1)}, f32[1,256]{1,0:T(1,128)}, u32[]{:S(2)}) copy-start(f32[1,256]{1,0:T(1,128)} %steer_second.1) | copy-start | bytes 3076

commit v8 on v7

--- a/solution.py
+++ b/solution.py
@@ -167,61 +167,57 @@
             filtered[:, cols] = convolved(True, group_size, mid[:, cols], mid_halo[:, cols], taps, first // group_size)
 
 
-def grad_kernel(
-    group_size, role, gate, mid, inputs, mid_halo, inputs_halo, own, halo, outgoing, received, filtered,
-    tap_grad, steer_grad, left, right_own, right_halo,
-):
-    reverse = first_section(role)
-    width = own.shape[1]
+def tap_sums(reverse, group_size, left, own, halo):
     half = LANES // 2
     per_half = half // group_size
-
-    @pl.when(reverse)
-    def _():
-        grad = received[...]
-        weighted = times(gate[...], grad)
-        left[...] = weighted
-        right_own[...] = times(mid[...], inputs[...])
-        right_halo[...] = times(mid_halo[...], inputs_halo[...])
-        grad_in = grad.astype(F32) + weighted.astype(F32) * filtered[...]
-        steer_grad[...] = jnp.sum(grad_in, 0, keepdims=True)
-
-    @pl.when(jnp.logical_not(reverse))
-    def _():
-        left[...] = times(mid[...], inputs[...])
-        right_own[...] = own[...]
-        right_halo[...] = halo[...]
-        steer_grad[...] = jnp.sum(outgoing[...].astype(F32), 0, keepdims=True)
-
-    mask = near(role[0] & 1, (SUB, LANES))
+    mask = near(int(reverse), (SUB, LANES))
     lane_group = (lane_of((SUB, 2 * LANES)) % half) // group_size
     nothing = jnp.zeros((SUB, 2 * LANES), BF16)
-    for pair in range(width // LANES):
-        cols = pl.ds(pair * LANES, LANES)
-        ext = in_order(reverse, right_own[:, cols], right_halo[:, cols])
-        ext_turned = turned(ext)
-        rows = left[:, cols]
-        rows_turned = turned(rows)
-        blocks = []
-        for parity in range(2):
-            window = spread(ext, ext_turned, parity, own.shape[0] + SUB)
-            short = spread(rows, rows_turned, parity, SUB)
-            lhs = jnp.concatenate(
-                [jnp.where(lane_group == g, short, nothing) for g in range(per_half)], 0
-            )
-            product = lax.dot_general(lhs, window, (((1,), (1,)), ((), ())), preferred_element_type=F32)
-            for g in range(per_half):
-                block = product[g * SUB : (g + 1) * SUB]
-                late = jnp.concatenate([block[:, LANES:], jnp.zeros((SUB, LANES - SUB), F32)], 1)
-                blocks.append(jnp.where(mask, block[:, :LANES], late))
-        tap_grad[pl.ds(8 * pair, 8), :] = diagonal_sums(blocks)
-
-
-def pack_kernel(owners, *refs):
-    count = (len(refs) - 1) // 2
-    taps, steers, out = refs[:count], refs[count : 2 * count], refs[-1]
-    groups = sum(ref.shape[0] for ref in taps) // owners
-    channels = sum(ref.shape[1] for ref in steers) // owners
+    ext = jnp.concatenate([halo, own] if reverse else [own, halo], 0)
+    ext_turned, left_turned = turned(ext), turned(left)
+    blocks = []
+    for parity in range(2):
+        window = spread(ext, ext_turned, parity, own.shape[0] + SUB)
+        short = spread(left, left_turned, parity, SUB)
+        lhs = jnp.concatenate([jnp.where(lane_group == g, short, nothing) for g in range(per_half)], 0)
+        product = lax.dot_general(lhs, window, (((1,), (1,)), ((), ())), preferred_element_type=F32)
+        for g in range(per_half):
+            block = product[g * SUB : (g + 1) * SUB]
+            late = jnp.concatenate([block[:, LANES:], jnp.zeros((SUB, LANES - SUB), F32)], 1)
+            blocks.append(jnp.where(mask, block[:, :LANES], late))
+    return diagonal_sums(blocks)
+
+
+def upper_grad_kernel(group_size, role, mid, inputs, own, halo, outgoing, tap_grad, steer_grad):
+    @pl.when(role[0] == 0)
+    def _():
+        steer_grad[...] = jnp.sum(outgoing[...].astype(F32), 0, keepdims=True)
+        for pair in range(own.shape[1] // LANES):
+            cols = pl.ds(pair * LANES, LANES)
+            values = times(mid[:, cols], inputs[:, cols])
+            tap_grad[pl.ds(8 * pair, 8), :] = tap_sums(False, group_size, values, own[:, cols], halo[:, cols])
+
+
+def first_grad_kernel(
+    group_size, role, gate, mid, inputs, mid_halo, inputs_halo, received, filtered, tap_grad, steer_grad
+):
+    @pl.when(role[0] > 0)
+    def _():
+        for pair in range(gate.shape[1] // LANES):
+            cols = pl.ds(pair * LANES, LANES)
+            grad = received[:, cols]
+            weighted = times(gate[:, cols], grad)
+            grad_in = grad.astype(F32) + weighted.astype(F32) * filtered[:, cols]
+            steer_grad[:, cols] = jnp.sum(grad_in, 0, keepdims=True)
+            own, halo = times(mid[:, cols], inputs[:, cols]), times(mid_halo[:, cols], inputs_halo[:, cols])
+            tap_grad[pl.ds(8 * pair, 8), :] = tap_sums(True, group_size, weighted, own, halo)
+
+
+def pack_kernel(owners, role, steer_second, filter_second, *refs):
+    refs, (out, steer_out, filter_out) = refs[:-3], refs[-3:]
+    count = len(refs) // 4
+    steer_out[...] = steer_second[...]
+    filter_out[...] = filter_second[...]
 
     def part(parts, axis, at, size):
         for ref in parts:
@@ -229,15 +225,26 @@
                 return ref[at : at + size, :] if axis == 0 else ref[:, at : at + size]
             at -= ref.shape[axis]
 
-    for owner in range(owners):
-        lines = [part(taps, 0, owner * groups, groups)]
-        for at in range(0, channels, LANES):
-            size = min(LANES, channels - at)
-            steer = part(steers, 1, owner * channels + at, size)
-            if size < LANES:
-                steer = jnp.concatenate([steer, jnp.zeros((1, LANES - size), F32)], 1)
-            lines.append(steer)
-        out[owner] = jnp.concatenate(lines, 0).astype(BF16)
+    def pack(taps, steers):
+        groups = sum(ref.shape[0] for ref in taps) // owners
+        channels = sum(ref.shape[1] for ref in steers) // owners
+        for owner in range(owners):
+            lines = [part(taps, 0, owner * groups, groups)]
+            for at in range(0, channels, LANES):
+                size = min(LANES, channels - at)
+                steer = part(steers, 1, owner * channels + at, size)
+                if size < LANES:
+                    steer = jnp.concatenate([steer, jnp.zeros((1, LANES - size), F32)], 1)
+                lines.append(steer)
+            out[owner] = jnp.concatenate(lines, 0).astype(BF16)
+
+    @pl.when(first_section(role))
+    def _():
+        pack(refs[:count], refs[count : 2 * count])
+
+    @pl.when(jnp.logical_not(first_section(role)))
+    def _():
+        pack(refs[2 * count : 3 * count], refs[3 * count :])
 
 
 def step_kernel(role, parts, steer_second, filter_second, steer_out, filter_out):
@@ -337,7 +344,46 @@
     )(role, filters[0])
     group_spec = lambda first: pl.BlockSpec((block_groups, filt_len), lambda i: (i + first, 0))
 
+    grad_specs = [group_spec(0), pl.BlockSpec((1, block), lambda i: (0, i))]
+
+    def grad_shapes(k):
+        width = bounds[k][1] - bounds[k][0]
+        return [
+            jax.ShapeDtypeStruct((width // group_size, filt_len), F32),
+            jax.ShapeDtypeStruct((1, width), F32),
+        ]
+
+    def upper_grad(k, after):
+        first, last = bounds[k]
+        own, halo, at = sources[k]
+        here, there = spec(rows, block, first // block), spec(rows, block, at)
+        return call(
+            functools.partial(upper_grad_kernel, group_size),
+            ((last - first) // block,),
+            [SMEM, here, here, there, there, spec(rows, block)],
+            grad_specs,
+            grad_shapes(k),
+            name="upper_grads",
+            cycles=2000,
+            after=tuple(after),
+        )(role, mid_gate, layer_inputs, own, halo, outgoing[k], *after)
+
+    def turned_filter(k, after):
+        first, last = bounds[k]
+        here = spec(rows, block, first // block)
+        return call(
+            functools.partial(turned_filter_kernel, group_size),
+            ((last - first) // block,),
+            [SMEM, here, here, group_spec(first // block)],
+            spec(rows, block),
+            jax.ShapeDtypeStruct((rows, last - first), F32),
+            name="turned_filter",
+            cycles=1000,
+            after=tuple(after),
+        )(role, mid_gate, mid_halo, taps, *after)
+
     incoming = [(cotangent, 0)] * len(bounds)
+    early, uppers, filtered = [], [], []
     for hop in range(sections - 1):
         split = [channels * eighths // 8 for eighths in HALO_EDGES] if hop == 0 else edges
         starts, ends = split[:-1], split[1:]
@@ -362,10 +408,13 @@
         for k, (first, last) in enumerate(bounds):
             part = max(i for i, start in enumerate(starts) if start <= first)
             while part >= len(owns):
-                send_halo(tuple(received[:1]))
+                send_halo(tuple(received[:1]) + tuple(early))
             at = (first - starts[part]) // block
             array, offset = incoming[k]
             before = tuple(outgoing[-1:])
+            if hop == sections - 2 and k == 2:
+                uppers.append(upper_grad(1, owns[-1:]))
+                before += tuple(uppers[-1][:1])
             out = call(
                 functools.partial(filter_kernel, group_size),
                 ((last - first) // block,),
@@ -380,58 +429,53 @@
             sources.append((owns[part], halos[part], at))
             outgoing.append(out)
             received.append(lax.ppermute(out, "section", down))
+            if hop == sections - 2 and k == 1:
+                uppers = [upper_grad(0, (out,))]
+                filtered = [turned_filter(0, (out,))]
+                filtered.append(turned_filter(1, filtered[-1:]))
+                early = [uppers[0][0], filtered[-1]]
         top = my_section == sections - 1
         incoming = [
             (jnp.where(top, cotangent[:, first:last], arrived), first)
             for (first, last), arrived in zip(bounds, received)
         ]
 
-    filtered = []
-    for first, last in bounds:
-        after = tuple(outgoing[-1:]) + tuple(filtered[-1:])
-        filtered.append(call(
-            functools.partial(turned_filter_kernel, group_size),
+    latest = outgoing[-1:]
+    for k in range(len(filtered), len(bounds)):
+        filtered.append(turned_filter(k, latest))
+        latest = filtered[-1:]
+    for k in range(len(uppers), len(bounds)):
+        uppers.append(upper_grad(k, latest))
+        latest = uppers[-1][:1]
+    firsts = []
+    for k, (first, last) in enumerate(bounds):
+        here = spec(rows, block, first // block)
+        firsts.append(call(
+            functools.partial(first_grad_kernel, group_size),
             ((last - first) // block,),
-            [SMEM, spec(rows, block, first // block), spec(rows, block, first // block), group_spec(first // block)],
-            spec(rows, block),
-            jax.ShapeDtypeStruct((rows, last - first), F32),
-            name="turned_filter",
-            cycles=1000,
-            after=after,
-        )(role, mid_gate, mid_halo, taps, *after))
-
-    grads = []
-    for k, (first, last) in enumerate(bounds):
-        own, halo, at = sources[k]
-        width = last - first
-        here = spec(rows, block, first // block)
-        after = tuple(grads[-1][:1] if grads else ())
-        grads.append(call(
-            functools.partial(grad_kernel, group_size),
-            (width // block,),
-            [SMEM, here, here, here, here, here, spec(rows, block, at), spec(rows, block, at)]
-            + [spec(rows, block)] * 3,
-            [group_spec(0), pl.BlockSpec((1, block), lambda i: (0, i))],
-            [jax.ShapeDtypeStruct((width // group_size, filt_len), F32), jax.ShapeDtypeStruct((1, width), F32)],
-            scratch=[pltpu.VMEM((rows, block), BF16)] * 3,
-            name="grads",
+            [SMEM, here, here, here, here, here, spec(rows, block), spec(rows, block)],
+            grad_specs,
+            grad_shapes(k),
+            name="first_grads",
             cycles=2000,
-            after=after,
-        )(role, in_gate, mid_gate, layer_inputs, mid_halo, inputs_halo, own, halo, outgoing[k],
-          received[k], filtered[k], *after))
-    tap_grads, steer_grads = zip(*grads)
+            after=tuple(latest),
+        )(role, in_gate, mid_gate, layer_inputs, mid_halo, inputs_halo, received[k], filtered[k], *latest))
+        latest = firsts[-1][:1]
+    partial_sums = [grads[i] for both in (firsts, uppers) for i in range(2) for grads in both]
 
     own_channels = channels // seqs
     lines = groups // seqs + pl.cdiv(own_channels, LANES)
     vmem = pl.BlockSpec(memory_space=pltpu.VMEM)
-    packed = pl.pallas_call(
+    seconds = (steer_second, filter_second[0].T)
+    packed, *seconds = pl.pallas_call(
         functools.partial(pack_kernel, seqs),
-        in_specs=[vmem] * (2 * len(grads)),
-        out_specs=vmem,
-        out_shape=jax.ShapeDtypeStruct((seqs, lines, LANES), BF16),
+        in_specs=[SMEM] + [vmem] * (2 + len(partial_sums)),
+        out_specs=[vmem] * 3,
+        out_shape=[jax.ShapeDtypeStruct((seqs, lines, LANES), BF16)]
+        + [jax.ShapeDtypeStruct(second.shape, F32) for second in seconds],
         compiler_params=SMALL,
         name="pack",
-    )(*tap_grads, *steer_grads)
+    )(role, *seconds, *partial_sums)
     parts = lax.all_to_all(packed, "seq", 0, 0)
     steer_step, filter_step = pl.pallas_call(
         step_kernel,
@@ -442,7 +486,7 @@
         ],
         compiler_params=SMALL,
         name="step",
-    )(role, parts, steer_second, filter_second[0].T)
+    )(role, parts, *seconds)
     return steer_step, filter_step.T[None]
 
 

time: 58.8 us -> 59.4 us (1.010)
  the two profiles are of different devices: /device:TPU:2 before, /device:TPU:0 now
where the time goes in v8:
time: 59.4 us; the launch traced here: 58.9 us
  blocking collectives  18.1 us (30%)
  starting transfers between devices  14.3 us (24%)
  Pallas kernels  13 us (22%)
  waiting for transfers between devices  8.27 us (14%)
  local copies, waits for them, and re-layouts  4.33 us (7%)
  between operations  0.93 us (2%)
    all_to_all x1, blocking collectives, body(): parts = lax.all_to_all(packed, 'seq', 0, 0)  18.1 us
    ppermute x4, waiting for transfers between devices, body(): received.append(lax.ppermute(out, 'section', down))  8.26 us
    pallas_call x4, Pallas kernels, body(): call(functools.partial(first_grad_kernel, group_size), ((last - first) //...  6.42 us
    ppermute x4, starting transfers between devices, body(): received.append(lax.ppermute(out, 'section', down))  5.17 us
    ppermute x1, starting transfers between devices, body(): inputs_halo = lax.ppermute(inputs_sent, ('section', 'seq'), ahead)  4.54 us
    unnamed x18, local copies, waits for them, and re-layouts  4.33 us
    pallas_call x4, Pallas kernels, turned_filter(): call(functools.partial(turned_filter_kernel, group_size), ((last - first)...  4.09 us
    ppermute x1, starting transfers between devices, body(): mid_halo = lax.ppermute(mid_sent, ('section', 'seq'), ahead)  2.41 us
  transfers between devices with their start and end apart: 9, of which 2 were waited for; matrix products, arithmetic and copies ran while one was open for 0% of the time, Pallas kernels for 19%

profile of v8, /device:TPU:0, one launch (start us, length us, event | category | flops | bytes accessed | tf_op | source)
XLA Modules:
  0.0 58.9 jit_solution(7474353486953361908)
XLA Ops:
  0.6 0.0 copy-start
  0.6 0.0 copy-start.1
  0.7 0.1 first_weigh.1.refs_1_.refs_3_
  0.7 1.1 %copy-done = bf16[1,128,4096]{2,1,0:T(8,128)(2,1)S(1)} copy-done((bf16[1,128,4096]{2,1,0:T(8,128)(2,1)S(1)}, bf16[1,128,4096]{2,1,0:T(8,128)(2,1)}, u32[]{:S(2)}) %copy-start) | copy-done | bytes 1048600
  1.9 2.4 %collective-permute-start = (bf16[128,4096]{1,0:T(8,128)(2,1)S(1)}, bf16[128,4096]{1,0:T(8,128)(2,1)S(1)}, u32[]{:S(2)}, u32[]{:S(2)}) collective-permute-start(bf16[128,4096]{1,0:T(8,128)(2,1)S(1)} %bitcast.11), channel_id=1, source_target_pairs={{0,1},{1,2},{2,3},{3,4},{4,5},{5,6},{6,7},{7,8},{8,9},{9,10},{10,1... | collective-permute-start | bytes 3145736 | tf_op jit(solution)/shard_map/ppermute | solution.py:404
  4.3 0.7 %collective-permute-start.2 = (bf16[128,1536]{1,0:T(8,128)(2,1)S(1)}, bf16[128,1536]{1,0:T(8,128)(2,1)S(1)}, u32[]{:S(2)}, u32[]{:S(2)}) collective-permute-start(bf16[128,1536]{1,0:T(8,128)(2,1)S(1)} %first_weigh.1.refs_1_.refs_3_), channel_id=1, source_target_pairs={{17,16},{18,17},{19,18},{20,19},{21,20},{22,21},{23,22},{24,23},{2... | collective-permute-start | bytes 1179656 | tf_op jit(solution)/shard_map/ppermute | solution.py:399
  5.0 0.0 copy-done.1
  5.0 4.5 %collective-permute-start.1 = (bf16[128,4096]{1,0:T(8,128)(2,1)S(1)}, bf16[128,4096]{1,0:T(8,128)(2,1)S(1)}, u32[]{:S(2)}, u32[]{:S(2)}) collective-permute-start(bf16[128,4096]{1,0:T(8,128)(2,1)S(1)} %bitcast.28), channel_id=1, source_target_pairs={{0,1},{1,2},{2,3},{3,4},{4,5},{5,6},{6,7},{7,8},{8,9},{9,10},{10,1... | collective-permute-start | bytes 3145736 | tf_op jit(solution)/shard_map/ppermute | solution.py:405
  9.5 0.0 copy-start.2
  9.5 1.2 %copy-done.2 = bf16[128,4096]{1,0:T(8,128)(2,1)S(1)} copy-done((bf16[128,4096]{1,0:T(8,128)(2,1)S(1)}, bf16[128,4096]{1,0:T(8,128)(2,1)}, u32[]{:S(2)}) %copy-start.2) | copy-done | bytes 1048600
  10.8 0.0 copy-start.4
  10.8 1.2 %copy-done.4 = bf16[1,128,4096]{2,1,0:T(8,128)(2,1)S(1)} copy-done((bf16[1,128,4096]{2,1,0:T(8,128)(2,1)S(1)}, bf16[1,128,4096]{2,1,0:T(8,128)(2,1)}, u32[]{:S(2)}) %copy-start.4) | copy-done | bytes 1048600
  12.0 0.0 copy-start.6
  12.0 0.0 copy-start.3
  12.0 0.2 weigh.2.refs_1_.refs_3_
  12.2 0.8 %collective-permute-start.4 = (bf16[128,1536]{1,0:T(8,128)(2,1)S(1)}, bf16[128,1536]{1,0:T(8,128)(2,1)S(1)}, u32[]{:S(2)}, u32[]{:S(2)}) collective-permute-start(bf16[128,1536]{1,0:T(8,128)(2,1)S(1)} %weigh.2.refs_1_.refs_3_), channel_id=1, source_target_pairs={{17,16},{18,17},{19,18},{20,19},{21,20},{22,21},{23,22},{24,23},{2... | collective-permute-start | bytes 1179656 | tf_op jit(solution)/shard_map/ppermute | solution.py:399
  13.0 0.0 copy-done.6
  13.0 0.2 taps.1.refs_3_
  13.2 0.0 collective-permute-done.2.refs_2_.refs_4_
  13.2 0.0 copy-done.3
  13.2 0.2 filter.4.refs_6_.refs_5_
  13.5 1.3 %collective-permute-start.3 = (bf16[128,1536]{1,0:T(8,128)(2,1)S(1)}, bf16[128,1536]{1,0:T(8,128)(2,1)S(1)}, u32[]{:S(2)}, u32[]{:S(2)}) collective-permute-start(bf16[128,1536]{1,0:T(8,128)(2,1)S(1)} %filter.4.refs_6_.refs_5_), channel_id=1, source_target_pairs={{16,0},{17,1},{18,2},{19,3},{20,4},{21,5},{22,6},{23,7},{24,8},{25... | collective-permute-start | bytes 1179656 | tf_op jit(solution)/shard_map/ppermute | solution.py:431
  14.8 0.0 collective-permute-done.4.refs_2_.refs_4_
  14.8 0.3 filter.5.refs_4_.refs_6_.refs_5_
  15.1 0.0 collective-permute-done.refs_2_.refs_4_
  15.1 1.6 %turned_filter.4.refs_4_.refs_7_ = f32[128,1536]{1,0:T(8,128)S(1)} custom-call(s32[1]{0:T(128)} %bitcast.role.refs_0_, bf16[128,4096]{1,0:T(8,128)(2,1)S(1)} %bitcast.14, bf16[128,4096]{1,0:T(8,128)(2,1)S(1)} %collective-permute-done.refs_2_.refs_4_, f32[256,128]{1,0:T(8,128)S(1)} %taps.1.refs_3_, bf16[128,1536]{1,0:T(8,128)(2,1)S(1)} %filter.5.refs_4_.refs_6_.refs_5_), custom_call_target="tpu_custom_call" | custom-call | flops 1000 | tf_op jit(solution)/shard_map/turned_filter/pallas_call | solution.py:374
  16.7 1.3 %collective-permute-start.6 = (bf16[128,1536]{1,0:T(8,128)(2,1)S(1)}, bf16[128,1536]{1,0:T(8,128)(2,1)S(1)}, u32[]{:S(2)}, u32[]{:S(2)}) collective-permute-start(bf16[128,1536]{1,0:T(8,128)(2,1)S(1)} %filter.5.refs_4_.refs_6_.refs_5_), channel_id=1, source_target_pairs={{16,0},{17,1},{18,2},{19,3},{20,4},{21,5},{22,6},{23,7},{24,8},{25... | collective-permute-start | bytes 1179656 | tf_op jit(solution)/shard_map/ppermute | solution.py:431
  18.0 0.3 upper_grads.4
  18.2 0.0 copy-start.5
  18.3 1.6 %turned_filter.5.refs_5_.refs_7_ = f32[128,1536]{1,0:T(8,128)S(1)} custom-call(s32[1]{0:T(128)} %bitcast.role.refs_0_, bf16[128,4096]{1,0:T(8,128)(2,1)S(1)} %bitcast.16, bf16[128,4096]{1,0:T(8,128)(2,1)S(1)} %collective-permute-done.refs_2_.refs_4_, f32[256,128]{1,0:T(8,128)S(1)} %taps.1.refs_3_, f32[128,1536]{1,0:T(8,128)S(1)} %turned_filter.4.refs_4_.refs_7_), custom_call_target="tpu_custom_call" | custom-call | flops 1000 | tf_op jit(solution)/shard_map/turned_filter/pallas_call | solution.py:374
  19.8 7.5 %collective-permute-done.3.refs_3_.refs_6_ = bf16[128,1536]{1,0:T(8,128)(2,1)S(1)} collective-permute-done((bf16[128,1536]{1,0:T(8,128)(2,1)S(1)}, bf16[128,1536]{1,0:T(8,128)(2,1)S(1)}, u32[]{:S(2)}, u32[]{:S(2)}) %collective-permute-start.3) | collective-permute-done | bytes 393248 | tf_op jit(solution)/shard_map/ppermute | solution.py:431
  27.3 0.0 copy-done.5
  27.3 0.1 weigh.3.refs_6_.refs_1_.refs_3_
  27.4 0.7 %collective-permute-start.5 = (bf16[128,1024]{1,0:T(8,128)(2,1)S(1)}, bf16[128,1024]{1,0:T(8,128)(2,1)S(1)}, u32[]{:S(2)}, u32[]{:S(2)}) collective-permute-start(bf16[128,1024]{1,0:T(8,128)(2,1)S(1)} %weigh.3.refs_6_.refs_1_.refs_3_), channel_id=1, source_target_pairs={{17,16},{18,17},{19,18},{20,19},{21,20},{22,21},{23,22},{24,23},{2... | collective-permute-start | bytes 786440 | tf_op jit(solution)/shard_map/ppermute | solution.py:399
  28.1 0.3 upper_grads.5
  28.4 0.0 collective-permute-done.5.refs_2_.refs_4_
  28.5 1.3 %collective-permute-start.7 = (bf16[128,512]{1,0:T(8,128)(2,1)S(1)}, bf16[128,512]{1,0:T(8,128)(2,1)S(1)}, u32[]{:S(2)}, u32[]{:S(2)}) collective-permute-start(bf16[128,512]{1,0:T(8,128)(2,1)S(1)} %filter.6.refs_6_.refs_5_), channel_id=1, source_target_pairs={{16,0},{17,1},{18,2},{19,3},{20,4},{21,5},{22,6},{23,7},{24,8},{25... | collective-permute-start | bytes 393224 | tf_op jit(solution)/shard_map/ppermute | solution.py:431
  29.8 1.3 %collective-permute-start.8 = (bf16[128,512]{1,0:T(8,128)(2,1)S(1)}, bf16[128,512]{1,0:T(8,128)(2,1)S(1)}, u32[]{:S(2)}, u32[]{:S(2)}) collective-permute-start(bf16[128,512]{1,0:T(8,128)(2,1)S(1)} %filter.7.refs_4_.refs_5_), channel_id=1, source_target_pairs={{16,0},{17,1},{18,2},{19,3},{20,4},{21,5},{22,6},{23,7},{24,8},{25... | collective-permute-start | bytes 393224 | tf_op jit(solution)/shard_map/ppermute | solution.py:431
  31.1 0.5 turned_filter.6.refs_4_.refs_7_
  31.6 0.5 turned_filter.7.refs_6_.refs_7_
  32.2 0.0 collective-permute-done.1.refs_5_
  32.2 2.4 %first_grads.4 = (f32[96,128]{1,0:T(8,128)S(1)}, f32[1,1536]{1,0:T(1,128)S(1)}) custom-call(s32[1]{0:T(128)} %bitcast.role.refs_0_, bf16[128,4096]{1,0:T(8,128)(2,1)S(1)} %bitcast.40, bf16[128,4096]{1,0:T(8,128)(2,1)S(1)} %bitcast.24, bf16[128,4096]{1,0:T(8,128)(2,1)S(1)} %bitcast.33, bf16[128,4096]{1,0:T(8,128)(2,1)S(1)} %collective-permute-done.refs_2_.refs_4_, ...), custom_call_target="tpu_custom_call" | custom-call | flops 2000 | tf_op jit(solution)/shard_map/first_grads/pallas_call | solution.py:453
  34.6 0.8 %collective-permute-done.6.refs_6_ = bf16[128,1536]{1,0:T(8,128)(2,1)S(1)} collective-permute-done((bf16[128,1536]{1,0:T(8,128)(2,1)S(1)}, bf16[128,1536]{1,0:T(8,128)(2,1)S(1)}, u32[]{:S(2)}, u32[]{:S(2)}) %collective-permute-start.6) | collective-permute-done | bytes 393248 | tf_op jit(solution)/shard_map/ppermute | solution.py:431
  35.4 2.4 %first_grads.5 = (f32[96,128]{1,0:T(8,128)S(1)}, f32[1,1536]{1,0:T(1,128)S(1)}) custom-call(s32[1]{0:T(128)} %bitcast.role.refs_0_, bf16[128,4096]{1,0:T(8,128)(2,1)S(1)} %bitcast.41, bf16[128,4096]{1,0:T(8,128)(2,1)S(1)} %bitcast.25, bf16[128,4096]{1,0:T(8,128)(2,1)S(1)} %bitcast.34, bf16[128,4096]{1,0:T(8,128)(2,1)S(1)} %collective-permute-done.refs_2_.refs_4_, ...), custom_call_target="tpu_custom_call" | custom-call | flops 2000 | tf_op jit(solution)/shard_map/first_grads/pallas_call | solution.py:453
  37.8 0.0 collective-permute-done.7.refs_6_
  37.8 0.8 %first_grads.6 = (f32[32,128]{1,0:T(8,128)S(1)}, f32[1,512]{1,0:T(1,128)S(1)}) custom-call(s32[1]{0:T(128)} %bitcast.role.refs_0_, bf16[128,4096]{1,0:T(8,128)(2,1)S(1)} %bitcast.42, bf16[128,4096]{1,0:T(8,128)(2,1)S(1)} %bitcast.26, bf16[128,4096]{1,0:T(8,128)(2,1)S(1)} %bitcast.35, bf16[128,4096]{1,0:T(8,128)(2,1)S(1)} %collective-permute-done.refs_2_.refs_4_, ...), custom_call_target="tpu_custom_call" | custom-call | flops 2000 | tf_op jit(solution)/shard_map/first_grads/pallas_call | solution.py:453
  38.6 0.0 collective-permute-done.8.refs_6_
  38.6 0.8 %first_grads.7 = (f32[32,128]{1,0:T(8,128)S(1)}, f32[1,512]{1,0:T(1,128)S(1)}) custom-call(s32[1]{0:T(128)} %bitcast.role.refs_0_, bf16[128,4096]{1,0:T(8,128)(2,1)S(1)} %bitcast.43, bf16[128,4096]{1,0:T(8,128)(2,1)S(1)} %bitcast.27, bf16[128,4096]{1,0:T(8,128)(2,1)S(1)} %bitcast.36, bf16[128,4096]{1,0:T(8,128)(2,1)S(1)} %collective-permute-done.refs_2_.refs_4_, ...), custom_call_target="tpu_custom_call" | custom-call | flops 2000 | tf_op jit(solution)/shard_map/first_grads/pallas_call | solution.py:453
  39.4 0.0 copy-start.7
  39.4 0.0 copy-start.8
  39.4 0.7 %copy-done.7 = f32[1,128,16]{1,2,0:T(8,128)S(1)} copy-done((f32[1,128,16]{1,2,0:T(8,128)S(1)}, f32[1,128,16]{1,2,0:T(8,128)}, u32[]{:S(2)}) %copy-start.7) | copy-done | bytes 8216
  40.1 0.0 copy-done.8
  40.1 18.1 %all_to_all.5.parts = bf16[16,18,128]{2,1,0:T(8,128)(2,1)S(1)} all-to-all(bf16[16,18,128]{2,1,0:T(8,128)(2,1)S(1)} %get-tuple-element.43), channel_id=1, replica_groups=mesh['section'=2,'seq'=16] {'seq'}, dimensions={0} | all-to-all | bytes 147456 | tf_op jit(solution)/shard_map/all_to_all | solution.py:479
  58.2 0.7 %step.1 = (f32[1,256]{1,0:T(1,128)}, f32[16,128]{1,0:T(8,128)}) custom-call(s32[1]{0:T(128)} %bitcast.role.refs_0_, bf16[16,18,128]{2,1,0:T(8,128)(2,1)S(1)} %all_to_all.5.parts, f32[1,256]{1,0:T(1,128)S(1)} %get-tuple-element.44.steer_second, f32[16,128]{1,0:T(8,128)S(1)} %get-tuple-element.45.filter_second), custom_call_target="tpu_custom_call" | custom-call | tf_op jit(solution)/shard_map/step/pallas_call | solution.py:480
  (5 shorter events, 0.2 us)
Async XLA Ops:
  0.6 1.2 %copy-start = (bf16[1,128,4096]{2,1,0:T(8,128)(2,1)S(1)}, bf16[1,128,4096]{2,1,0:T(8,128)(2,1)}, u32[]{:S(2)}) copy-start(bf16[1,128,4096]{2,1,0:T(8,128)(2,1)} %param.9) | copy-start | bytes 3145732
  0.6 4.3 %copy-start.1 = (bf16[1,128,4096]{2,1,0:T(8,128)(2,1)S(1)}, bf16[1,128,4096]{2,1,0:T(8,128)(2,1)}, u32[]{:S(2)}) copy-start(bf16[1,128,4096]{2,1,0:T(8,128)(2,1)} %param.10) | copy-start | bytes 3145732
  1.9 13.2 %collective-permute-start = (bf16[128,4096]{1,0:T(8,128)(2,1)S(1)}, bf16[128,4096]{1,0:T(8,128)(2,1)S(1)}, u32[]{:S(2)}, u32[]{:S(2)}) collective-permute-start(bf16[128,4096]{1,0:T(8,128)(2,1)S(1)} %bitcast.11), channel_id=1, source_target_pairs={{0,1},{1,2},{2,3},{3,4},{4,5},{5,6},{6,7},{7,8},{8,9},{9,10},{10,1... | collective-permute-start | bytes 3145736 | tf_op jit(solution)/shard_map/ppermute | solution.py:404
  4.3 8.9 %collective-permute-start.2 = (bf16[128,1536]{1,0:T(8,128)(2,1)S(1)}, bf16[128,1536]{1,0:T(8,128)(2,1)S(1)}, u32[]{:S(2)}, u32[]{:S(2)}) collective-permute-start(bf16[128,1536]{1,0:T(8,128)(2,1)S(1)} %first_weigh.1.refs_1_.refs_3_), channel_id=1, source_target_pairs={{17,16},{18,17},{19,18},{20,19},{21,20},{22,21},{23,22},{24,23},{2... | collective-permute-start | bytes 1179656 | tf_op jit(solution)/shard_map/ppermute | solution.py:399
  5.0 27.2 %collective-permute-start.1 = (bf16[128,4096]{1,0:T(8,128)(2,1)S(1)}, bf16[128,4096]{1,0:T(8,128)(2,1)S(1)}, u32[]{:S(2)}, u32[]{:S(2)}) collective-permute-start(bf16[128,4096]{1,0:T(8,128)(2,1)S(1)} %bitcast.28), channel_id=1, source_target_pairs={{0,1},{1,2},{2,3},{3,4},{4,5},{5,6},{6,7},{7,8},{8,9},{9,10},{10,1... | collective-permute-start | bytes 3145736 | tf_op jit(solution)/shard_map/ppermute | solution.py:405
  9.5 1.2 %copy-start.2 = (bf16[128,4096]{1,0:T(8,128)(2,1)S(1)}, bf16[128,4096]{1,0:T(8,128)(2,1)}, u32[]{:S(2)}) copy-start(bf16[128,4096]{1,0:T(8,128)(2,1)} %refs_5_.7) | copy-start | bytes 3145732
  10.8 1.2 %copy-start.4 = (bf16[1,128,4096]{2,1,0:T(8,128)(2,1)S(1)}, bf16[1,128,4096]{2,1,0:T(8,128)(2,1)}, u32[]{:S(2)}) copy-start(bf16[1,128,4096]{2,1,0:T(8,128)(2,1)} %param.8) | copy-start | bytes 3145732
  12.0 1.0 %copy-start.6 = (bf16[1,128,256]{2,1,0:T(8,128)(2,1)S(1)}, bf16[1,128,256]{2,1,0:T(8,128)(2,1)}, u32[]{:S(2)}) copy-start(bf16[1,128,256]{2,1,0:T(8,128)(2,1)} %param.11) | copy-start | bytes 196612
  12.0 1.3 %copy-start.3 = (bf16[128,4096]{1,0:T(8,128)(2,1)S(1)}, bf16[128,4096]{1,0:T(8,128)(2,1)}, u32[]{:S(2)}) copy-start(bf16[128,4096]{1,0:T(8,128)(2,1)} %refs_5_.7) | copy-start | bytes 3145732
  12.2 2.6 %collective-permute-start.4 = (bf16[128,1536]{1,0:T(8,128)(2,1)S(1)}, bf16[128,1536]{1,0:T(8,128)(2,1)S(1)}, u32[]{:S(2)}, u32[]{:S(2)}) collective-permute-start(bf16[128,1536]{1,0:T(8,128)(2,1)S(1)} %weigh.2.refs_1_.refs_3_), channel_id=1, source_target_pairs={{17,16},{18,17},{19,18},{20,19},{21,20},{22,21},{23,22},{24,23},{2... | collective-permute-start | bytes 1179656 | tf_op jit(solution)/shard_map/ppermute | solution.py:399
  13.5 13.8 %collective-permute-start.3 = (bf16[128,1536]{1,0:T(8,128)(2,1)S(1)}, bf16[128,1536]{1,0:T(8,128)(2,1)S(1)}, u32[]{:S(2)}, u32[]{:S(2)}) collective-permute-start(bf16[128,1536]{1,0:T(8,128)(2,1)S(1)} %filter.4.refs_6_.refs_5_), channel_id=1, source_target_pairs={{16,0},{17,1},{18,2},{19,3},{20,4},{21,5},{22,6},{23,7},{24,8},{25... | collective-permute-start | bytes 1179656 | tf_op jit(solution)/shard_map/ppermute | solution.py:431
  16.7 18.7 %collective-permute-start.6 = (bf16[128,1536]{1,0:T(8,128)(2,1)S(1)}, bf16[128,1536]{1,0:T(8,128)(2,1)S(1)}, u32[]{:S(2)}, u32[]{:S(2)}) collective-permute-start(bf16[128,1536]{1,0:T(8,128)(2,1)S(1)} %filter.5.refs_4_.refs_6_.refs_5_), channel_id=1, source_target_pairs={{16,0},{17,1},{18,2},{19,3},{20,4},{21,5},{22,6},{23,7},{24,8},{25... | collective-permute-start | bytes 1179656 | tf_op jit(solution)/shard_map/ppermute | solution.py:431
  18.2 9.1 %copy-start.5 = (bf16[1,128,4096]{2,1,0:T(8,128)(2,1)S(1)}, bf16[1,128,4096]{2,1,0:T(8,128)(2,1)}, u32[]{:S(2)}) copy-start(bf16[1,128,4096]{2,1,0:T(8,128)(2,1)} %param.8) | copy-start | bytes 3145732
  27.4 1.0 %collective-permute-start.5 = (bf16[128,1024]{1,0:T(8,128)(2,1)S(1)}, bf16[128,1024]{1,0:T(8,128)(2,1)S(1)}, u32[]{:S(2)}, u32[]{:S(2)}) collective-permute-start(bf16[128,1024]{1,0:T(8,128)(2,1)S(1)} %weigh.3.refs_6_.refs_1_.refs_3_), channel_id=1, source_target_pairs={{17,16},{18,17},{19,18},{20,19},{21,20},{22,21},{23,22},{24,23},{2... | collective-permute-start | bytes 786440 | tf_op jit(solution)/shard_map/ppermute | solution.py:399
  28.5 9.4 %collective-permute-start.7 = (bf16[128,512]{1,0:T(8,128)(2,1)S(1)}, bf16[128,512]{1,0:T(8,128)(2,1)S(1)}, u32[]{:S(2)}, u32[]{:S(2)}) collective-permute-start(bf16[128,512]{1,0:T(8,128)(2,1)S(1)} %filter.6.refs_6_.refs_5_), channel_id=1, source_target_pairs={{16,0},{17,1},{18,2},{19,3},{20,4},{21,5},{22,6},{23,7},{24,8},{25... | collective-permute-start | bytes 393224 | tf_op jit(solution)/shard_map/ppermute | solution.py:431
  29.8 8.8 %collective-permute-start.8 = (bf16[128,512]{1,0:T(8,128)(2,1)S(1)}, bf16[128,512]{1,0:T(8,128)(2,1)S(1)}, u32[]{:S(2)}, u32[]{:S(2)}) collective-permute-start(bf16[128,512]{1,0:T(8,128)(2,1)S(1)} %filter.7.refs_4_.refs_5_), channel_id=1, source_target_pairs={{16,0},{17,1},{18,2},{19,3},{20,4},{21,5},{22,6},{23,7},{24,8},{25... | collective-permute-start | bytes 393224 | tf_op jit(solution)/shard_map/ppermute | solution.py:431
  39.4 0.7 %copy-start.7 = (f32[1,128,16]{1,2,0:T(8,128)S(1)}, f32[1,128,16]{1,2,0:T(8,128)}, u32[]{:S(2)}) copy-start(f32[1,128,16]{1,2,0:T(8,128)} %param.13) | copy-start | bytes 24580
  39.4 0.7 %copy-start.8 = (f32[1,256]{1,0:T(1,128)S(1)}, f32[1,256]{1,0:T(1,128)}, u32[]{:S(2)}) copy-start(f32[1,256]{1,0:T(1,128)} %steer_second.1) | copy-start | bytes 3076

commit v9 on v8

--- a/solution.py
+++ b/solution.py
@@ -116,7 +116,9 @@
             out[:, t] = times(gate_part[:, t], incoming_part[:, t])
 
 
-def taps_kernel(role, filters, taps_out):
+def taps_kernel(role, filters, steer_second, filter_second, taps_out, steer_out, filter_out):
+    steer_out[...] = steer_second[...]
+    filter_out[...] = filter_second[...]
     pick, _ = tap_matrix(first_section(role), filters[...])
     taps_out[...] = lax.dot_general(
         filters[...], pick.astype(BF16), (((0,), (0,)), ((), ())), preferred_element_type=F32
@@ -213,11 +215,9 @@
             tap_grad[pl.ds(8 * pair, 8), :] = tap_sums(True, group_size, weighted, own, halo)
 
 
-def pack_kernel(owners, role, steer_second, filter_second, *refs):
-    refs, (out, steer_out, filter_out) = refs[:-3], refs[-3:]
+def pack_kernel(owners, role, *refs):
+    refs, out = refs[:-1], refs[-1]
     count = len(refs) // 4
-    steer_out[...] = steer_second[...]
-    filter_out[...] = filter_second[...]
 
     def part(parts, axis, at, size):
         for ref in parts:
@@ -334,14 +334,17 @@
             name="first_weigh",
         )(role, *[pltpu.with_memory_space_constraint(a, pltpu.HBM) for a in (in_gate, cotangent)])
 
-    taps = call(
+    seconds = (steer_second, filter_second[0].T)
+    vmem = pl.BlockSpec(memory_space=pltpu.VMEM)
+    taps, *seconds = pl.pallas_call(
         taps_kernel,
-        (1,),
-        [SMEM, pl.BlockSpec((filt_len, groups), lambda i: (0, 0))],
-        pl.BlockSpec((groups, filt_len), lambda i: (0, 0)),
-        jax.ShapeDtypeStruct((groups, filt_len), F32),
+        in_specs=[SMEM] + [vmem] * 3,
+        out_specs=[vmem] * 3,
+        out_shape=[jax.ShapeDtypeStruct((groups, filt_len), F32)]
+        + [jax.ShapeDtypeStruct(second.shape, F32) for second in seconds],
+        compiler_params=SMALL,
         name="taps",
-    )(role, filters[0])
+    )(role, filters[0], *seconds)
     group_spec = lambda first: pl.BlockSpec((block_groups, filt_len), lambda i: (i + first, 0))
 
     grad_specs = [group_spec(0), pl.BlockSpec((1, block), lambda i: (0, i))]
@@ -414,7 +417,9 @@
             before = tuple(outgoing[-1:])
             if hop == sections - 2 and k == 2:
                 uppers.append(upper_grad(1, owns[-1:]))
-                before += tuple(uppers[-1][:1])
+                filtered.append(turned_filter(0, owns[-1:]))
+                filtered.append(turned_filter(1, filtered[-1:]))
+                before += (uppers[-1][0], filtered[-1])
             out = call(
                 functools.partial(filter_kernel, group_size),
                 ((last - first) // block,),
@@ -431,9 +436,7 @@
             received.append(lax.ppermute(out, "section", down))
             if hop == sections - 2 and k == 1:
                 uppers = [upper_grad(0, (out,))]
-                filtered = [turned_filter(0, (out,))]
-                filtered.append(turned_filter(1, filtered[-1:]))
-                early = [uppers[0][0], filtered[-1]]
+                early = [uppers[0][0]]
         top = my_section == sections - 1
         incoming = [
             (jnp.where(top, cotangent[:, first:last], arrived), first)
@@ -465,17 +468,14 @@
 
     own_channels = channels // seqs
     lines = groups // seqs + pl.cdiv(own_channels, LANES)
-    vmem = pl.BlockSpec(memory_space=pltpu.VMEM)
-    seconds = (steer_second, filter_second[0].T)
-    packed, *seconds = pl.pallas_call(
+    packed = pl.pallas_call(
         functools.partial(pack_kernel, seqs),
-        in_specs=[SMEM] + [vmem] * (2 + len(partial_sums)),
-        out_specs=[vmem] * 3,
-        out_shape=[jax.ShapeDtypeStruct((seqs, lines, LANES), BF16)]
-        + [jax.ShapeDtypeStruct(second.shape, F32) for second in seconds],
+        in_specs=[SMEM] + [vmem] * len(partial_sums),
+        out_specs=vmem,
+        out_shape=jax.ShapeDtypeStruct((seqs, lines, LANES), BF16),
         compiler_params=SMALL,
         name="pack",
-    )(role, *seconds, *partial_sums)
+    )(role, *partial_sums)
     parts = lax.all_to_all(packed, "seq", 0, 0)
     steer_step, filter_step = pl.pallas_call(
         step_kernel,

time: 59.4 us -> 57.3 us (0.965)
  blocking collectives: 18.1 us -> 12.9 us
  waiting for transfers between devices: 8.27 us -> 12 us
  local copies, waits for them, and re-layouts: 4.33 us -> 3.43 us
    all_to_all x1, blocking collectives: 18.1 us -> 12.9 us  [body(): parts = lax.all_to_all(packed, 'seq', 0, 0)]
    ppermute x4, waiting for transfers between devices: 8.26 us -> 11.9 us  [body(): received.append(lax.ppermute(out, 'section', down))]
    unnamed x18, local copies, waits for them, and re-layouts: 4.33 us -> 3.43 us
  transfers between devices with their start and end apart: 9 -> 9, of which waited for: 2 -> 2; matrix products, arithmetic and copies ran while one was open for 0% -> 0% of each run, Pallas kernels for 19% -> 20%
where the time goes in v9:
time: 57.3 us; the launch traced here: 56.8 us
  starting transfers between devices  14.6 us (25%)
  Pallas kernels  13 us (23%)
  blocking collectives  12.9 us (23%)
  waiting for transfers between devices  12 us (21%)
  local copies, waits for them, and re-layouts  3.43 us (6%)
  between operations  0.95 us (2%)
    all_to_all x1, blocking collectives, body(): parts = lax.all_to_all(packed, 'seq', 0, 0)  12.9 us
    ppermute x4, waiting for transfers between devices, body(): received.append(lax.ppermute(out, 'section', down))  11.9 us
    pallas_call x4, Pallas kernels, body(): call(functools.partial(first_grad_kernel, group_size), ((last - first) //...  6.41 us
    ppermute x4, starting transfers between devices, body(): received.append(lax.ppermute(out, 'section', down))  5.3 us
    ppermute x1, starting transfers between devices, body(): inputs_halo = lax.ppermute(inputs_sent, ('section', 'seq'), ahead)  4.54 us
    pallas_call x4, Pallas kernels, turned_filter(): call(functools.partial(turned_filter_kernel, group_size), ((last - first)...  4.08 us
    unnamed x18, local copies, waits for them, and re-layouts  3.43 us
    ppermute x1, starting transfers between devices, body(): mid_halo = lax.ppermute(mid_sent, ('section', 'seq'), ahead)  2.41 us
  transfers between devices with their start and end apart: 9, of which 2 were waited for; matrix products, arithmetic and copies ran while one was open for 0% of the time, Pallas kernels for 20%

profile of v9, /device:TPU:0, one launch (start us, length us, event | category | flops | bytes accessed | tf_op | source)
XLA Modules:
  0.0 56.8 jit_solution(18291584771177247861)
XLA Ops:
  0.6 0.0 copy-start
  0.6 0.0 copy-start.1
  0.7 0.1 first_weigh.1.refs_1_.refs_3_
  0.7 0.8 %collective-permute-start.2 = (bf16[128,1536]{1,0:T(8,128)(2,1)S(1)}, bf16[128,1536]{1,0:T(8,128)(2,1)S(1)}, u32[]{:S(2)}, u32[]{:S(2)}) collective-permute-start(bf16[128,1536]{1,0:T(8,128)(2,1)S(1)} %first_weigh.1.refs_1_.refs_3_), channel_id=1, source_target_pairs={{17,16},{18,17},{19,18},{20,19},{21,20},{22,21},{23,22},{24,23},{2... | collective-permute-start | bytes 1179656 | tf_op jit(solution)/shard_map/ppermute | solution.py:402
  1.6 0.3 copy-done
  1.9 2.4 %collective-permute-start = (bf16[128,4096]{1,0:T(8,128)(2,1)S(1)}, bf16[128,4096]{1,0:T(8,128)(2,1)S(1)}, u32[]{:S(2)}, u32[]{:S(2)}) collective-permute-start(bf16[128,4096]{1,0:T(8,128)(2,1)S(1)} %bitcast.11), channel_id=1, source_target_pairs={{0,1},{1,2},{2,3},{3,4},{4,5},{5,6},{6,7},{7,8},{8,9},{9,10},{10,1... | collective-permute-start | bytes 3145736 | tf_op jit(solution)/shard_map/ppermute | solution.py:407
  4.3 0.0 copy-done.1
  4.3 4.5 %collective-permute-start.1 = (bf16[128,4096]{1,0:T(8,128)(2,1)S(1)}, bf16[128,4096]{1,0:T(8,128)(2,1)S(1)}, u32[]{:S(2)}, u32[]{:S(2)}) collective-permute-start(bf16[128,4096]{1,0:T(8,128)(2,1)S(1)} %bitcast.28), channel_id=1, source_target_pairs={{0,1},{1,2},{2,3},{3,4},{4,5},{5,6},{6,7},{7,8},{8,9},{9,10},{10,1... | collective-permute-start | bytes 3145736 | tf_op jit(solution)/shard_map/ppermute | solution.py:408
  8.8 0.0 copy-start.2
  8.8 1.2 %copy-done.2 = bf16[1,128,4096]{2,1,0:T(8,128)(2,1)S(1)} copy-done((bf16[1,128,4096]{2,1,0:T(8,128)(2,1)S(1)}, bf16[1,128,4096]{2,1,0:T(8,128)(2,1)}, u32[]{:S(2)}) %copy-start.2) | copy-done | bytes 1048600
  10.1 0.0 copy-start.4
  10.1 1.2 %copy-done.4 = bf16[128,4096]{1,0:T(8,128)(2,1)S(1)} copy-done((bf16[128,4096]{1,0:T(8,128)(2,1)S(1)}, bf16[128,4096]{1,0:T(8,128)(2,1)}, u32[]{:S(2)}) %copy-start.4) | copy-done | bytes 1048600
  11.3 0.0 copy-start.6
  11.3 0.0 copy-start.7
  11.3 0.0 copy-start.5
  11.3 0.2 weigh.2.refs_1_.refs_3_
  11.5 0.8 %collective-permute-start.4 = (bf16[128,1536]{1,0:T(8,128)(2,1)S(1)}, bf16[128,1536]{1,0:T(8,128)(2,1)S(1)}, u32[]{:S(2)}, u32[]{:S(2)}) collective-permute-start(bf16[128,1536]{1,0:T(8,128)(2,1)S(1)} %weigh.2.refs_1_.refs_3_), channel_id=1, source_target_pairs={{17,16},{18,17},{19,18},{20,19},{21,20},{22,21},{23,22},{24,23},{2... | collective-permute-start | bytes 1179656 | tf_op jit(solution)/shard_map/ppermute | solution.py:402
  12.3 0.0 copy-start.8
  12.3 0.0 copy-done.6
  12.3 0.0 copy-done.7
  12.4 0.7 %copy-done.8 = f32[1,256]{1,0:T(1,128)S(1)} copy-done((f32[1,256]{1,0:T(1,128)S(1)}, f32[1,256]{1,0:T(1,128)}, u32[]{:S(2)}) %copy-start.8) | copy-done | bytes 1048
  13.0 0.2 taps.1
  13.2 0.0 collective-permute-done.2.refs_2_.refs_4_
  13.2 0.0 copy-done.5
  13.2 0.3 filter.4.refs_6_.refs_5_
  13.5 1.3 %collective-permute-start.3 = (bf16[128,1536]{1,0:T(8,128)(2,1)S(1)}, bf16[128,1536]{1,0:T(8,128)(2,1)S(1)}, u32[]{:S(2)}, u32[]{:S(2)}) collective-permute-start(bf16[128,1536]{1,0:T(8,128)(2,1)S(1)} %filter.4.refs_6_.refs_5_), channel_id=1, source_target_pairs={{16,0},{17,1},{18,2},{19,3},{20,4},{21,5},{22,6},{23,7},{24,8},{25... | collective-permute-start | bytes 1179656 | tf_op jit(solution)/shard_map/ppermute | solution.py:436
  14.8 0.0 collective-permute-done.4.refs_2_.refs_4_
  14.8 0.3 filter.5.refs_6_.refs_5_
  15.1 0.0 copy-start.3
  15.1 1.4 %collective-permute-start.6 = (bf16[128,1536]{1,0:T(8,128)(2,1)S(1)}, bf16[128,1536]{1,0:T(8,128)(2,1)S(1)}, u32[]{:S(2)}, u32[]{:S(2)}) collective-permute-start(bf16[128,1536]{1,0:T(8,128)(2,1)S(1)} %filter.5.refs_6_.refs_5_), channel_id=1, source_target_pairs={{16,0},{17,1},{18,2},{19,3},{20,4},{21,5},{22,6},{23,7},{24,8},{25... | collective-permute-start | bytes 1179656 | tf_op jit(solution)/shard_map/ppermute | solution.py:436
  16.5 0.3 upper_grads.4
  16.8 10.5 %collective-permute-done.3.refs_3_.refs_6_ = bf16[128,1536]{1,0:T(8,128)(2,1)S(1)} collective-permute-done((bf16[128,1536]{1,0:T(8,128)(2,1)S(1)}, bf16[128,1536]{1,0:T(8,128)(2,1)S(1)}, u32[]{:S(2)}, u32[]{:S(2)}) %collective-permute-start.3) | collective-permute-done | bytes 393248 | tf_op jit(solution)/shard_map/ppermute | solution.py:436
  27.3 0.0 copy-done.3
  27.3 0.1 weigh.3.refs_4_.refs_6_.refs_1_.refs_3_
  27.4 0.7 %collective-permute-start.5 = (bf16[128,1024]{1,0:T(8,128)(2,1)S(1)}, bf16[128,1024]{1,0:T(8,128)(2,1)S(1)}, u32[]{:S(2)}, u32[]{:S(2)}) collective-permute-start(bf16[128,1024]{1,0:T(8,128)(2,1)S(1)} %weigh.3.refs_4_.refs_6_.refs_1_.refs_3_), channel_id=1, source_target_pairs={{17,16},{18,17},{19,18},{20,19},{21,20},{22,21},{23,22},{24,23},{2... | collective-permute-start | bytes 786440 | tf_op jit(solution)/shard_map/ppermute | solution.py:402
  28.1 0.0 collective-permute-done.refs_2_.refs_4_
  28.1 1.6 %turned_filter.4.refs_4_.refs_7_ = f32[128,1536]{1,0:T(8,128)S(1)} custom-call(s32[1]{0:T(128)} %bitcast.role.refs_0_, bf16[128,4096]{1,0:T(8,128)(2,1)S(1)} %bitcast.15, bf16[128,4096]{1,0:T(8,128)(2,1)S(1)} %collective-permute-done.refs_2_.refs_4_, f32[256,128]{1,0:T(8,128)S(1)} %get-tuple-element.27.refs_3_, ...), custom_call_target="tpu_custom_call" | custom-call | flops 1000 | tf_op jit(solution)/shard_map/turned_filter/pallas_call | solution.py:377
  29.7 0.3 upper_grads.5
  30.0 1.6 %turned_filter.5.refs_8_.refs_7_ = f32[128,1536]{1,0:T(8,128)S(1)} custom-call(s32[1]{0:T(128)} %bitcast.role.refs_0_, bf16[128,4096]{1,0:T(8,128)(2,1)S(1)} %bitcast.17, bf16[128,4096]{1,0:T(8,128)(2,1)S(1)} %collective-permute-done.refs_2_.refs_4_, f32[256,128]{1,0:T(8,128)S(1)} %get-tuple-element.27.refs_3_, f32[128,1536]{1,0:T(8,128)S(1)} %turned_filter.4.refs_4_.refs_7_), custom_call_target="tpu_custom_call" | custom-call | flops 1000 | tf_op jit(solution)/shard_map/turned_filter/pallas_call | solution.py:377
  31.6 0.0 collective-permute-done.5.refs_2_.refs_4_
  31.6 1.3 %collective-permute-start.7 = (bf16[128,512]{1,0:T(8,128)(2,1)S(1)}, bf16[128,512]{1,0:T(8,128)(2,1)S(1)}, u32[]{:S(2)}, u32[]{:S(2)}) collective-permute-start(bf16[128,512]{1,0:T(8,128)(2,1)S(1)} %filter.6.refs_6_.refs_5_), channel_id=1, source_target_pairs={{16,0},{17,1},{18,2},{19,3},{20,4},{21,5},{22,6},{23,7},{24,8},{25... | collective-permute-start | bytes 393224 | tf_op jit(solution)/shard_map/ppermute | solution.py:436
  33.0 1.3 %collective-permute-start.8 = (bf16[128,512]{1,0:T(8,128)(2,1)S(1)}, bf16[128,512]{1,0:T(8,128)(2,1)S(1)}, u32[]{:S(2)}, u32[]{:S(2)}) collective-permute-start(bf16[128,512]{1,0:T(8,128)(2,1)S(1)} %filter.7.refs_4_.refs_5_), channel_id=1, source_target_pairs={{16,0},{17,1},{18,2},{19,3},{20,4},{21,5},{22,6},{23,7},{24,8},{25... | collective-permute-start | bytes 393224 | tf_op jit(solution)/shard_map/ppermute | solution.py:436
  34.3 0.5 turned_filter.6.refs_4_.refs_7_
  34.8 0.5 turned_filter.7.refs_6_.refs_7_
  35.3 0.0 collective-permute-done.1.refs_5_
  35.4 2.4 %first_grads.4 = (f32[96,128]{1,0:T(8,128)S(1)}, f32[1,1536]{1,0:T(1,128)S(1)}) custom-call(s32[1]{0:T(128)} %bitcast.role.refs_0_, bf16[128,4096]{1,0:T(8,128)(2,1)S(1)} %bitcast.40, bf16[128,4096]{1,0:T(8,128)(2,1)S(1)} %bitcast.24, bf16[128,4096]{1,0:T(8,128)(2,1)S(1)} %bitcast.33, bf16[128,4096]{1,0:T(8,128)(2,1)S(1)} %collective-permute-done.refs_2_.refs_4_, ...), custom_call_target="tpu_custom_call" | custom-call | flops 2000 | tf_op jit(solution)/shard_map/first_grads/pallas_call | solution.py:456
  37.8 0.0 collective-permute-done.6.refs_6_
  37.8 2.4 %first_grads.5 = (f32[96,128]{1,0:T(8,128)S(1)}, f32[1,1536]{1,0:T(1,128)S(1)}) custom-call(s32[1]{0:T(128)} %bitcast.role.refs_0_, bf16[128,4096]{1,0:T(8,128)(2,1)S(1)} %bitcast.41, bf16[128,4096]{1,0:T(8,128)(2,1)S(1)} %bitcast.25, bf16[128,4096]{1,0:T(8,128)(2,1)S(1)} %bitcast.34, bf16[128,4096]{1,0:T(8,128)(2,1)S(1)} %collective-permute-done.refs_2_.refs_4_, ...), custom_call_target="tpu_custom_call" | custom-call | flops 2000 | tf_op jit(solution)/shard_map/first_grads/pallas_call | solution.py:456
  40.2 0.0 collective-permute-done.7.refs_6_
  40.2 0.8 %first_grads.6 = (f32[32,128]{1,0:T(8,128)S(1)}, f32[1,512]{1,0:T(1,128)S(1)}) custom-call(s32[1]{0:T(128)} %bitcast.role.refs_0_, bf16[128,4096]{1,0:T(8,128)(2,1)S(1)} %bitcast.42, bf16[128,4096]{1,0:T(8,128)(2,1)S(1)} %bitcast.26, bf16[128,4096]{1,0:T(8,128)(2,1)S(1)} %bitcast.35, bf16[128,4096]{1,0:T(8,128)(2,1)S(1)} %collective-permute-done.refs_2_.refs_4_, ...), custom_call_target="tpu_custom_call" | custom-call | flops 2000 | tf_op jit(solution)/shard_map/first_grads/pallas_call | solution.py:456
  41.0 1.4 %collective-permute-done.8.refs_6_ = bf16[128,512]{1,0:T(8,128)(2,1)S(1)} collective-permute-done((bf16[128,512]{1,0:T(8,128)(2,1)S(1)}, bf16[128,512]{1,0:T(8,128)(2,1)S(1)}, u32[]{:S(2)}, u32[]{:S(2)}) %collective-permute-start.8) | collective-permute-done | bytes 131104 | tf_op jit(solution)/shard_map/ppermute | solution.py:436
  42.4 0.8 %first_grads.7 = (f32[32,128]{1,0:T(8,128)S(1)}, f32[1,512]{1,0:T(1,128)S(1)}) custom-call(s32[1]{0:T(128)} %bitcast.role.refs_0_, bf16[128,4096]{1,0:T(8,128)(2,1)S(1)} %bitcast.43, bf16[128,4096]{1,0:T(8,128)(2,1)S(1)} %bitcast.27, bf16[128,4096]{1,0:T(8,128)(2,1)S(1)} %bitcast.36, bf16[128,4096]{1,0:T(8,128)(2,1)S(1)} %collective-permute-done.refs_2_.refs_4_, ...), custom_call_target="tpu_custom_call" | custom-call | flops 2000 | tf_op jit(solution)/shard_map/first_grads/pallas_call | solution.py:456
  43.2 12.9 %all_to_all.5.parts = bf16[16,18,128]{2,1,0:T(8,128)(2,1)S(1)} all-to-all(bf16[16,18,128]{2,1,0:T(8,128)(2,1)S(1)} %pack.1), channel_id=1, replica_groups=mesh['section'=2,'seq'=16] {'seq'}, dimensions={0} | all-to-all | bytes 147456 | tf_op jit(solution)/shard_map/all_to_all | solution.py:479
  56.1 0.7 %step.1 = (f32[1,256]{1,0:T(1,128)}, f32[16,128]{1,0:T(8,128)}) custom-call(s32[1]{0:T(128)} %bitcast.role.refs_0_, bf16[16,18,128]{2,1,0:T(8,128)(2,1)S(1)} %all_to_all.5.parts, f32[1,256]{1,0:T(1,128)S(1)} %get-tuple-element.44.steer_second, f32[16,128]{1,0:T(8,128)S(1)} %get-tuple-element.45.filter_second), custom_call_target="tpu_custom_call" | custom-call | tf_op jit(solution)/shard_map/step/pallas_call | solution.py:480
  (5 shorter events, 0.2 us)
Async XLA Ops:
  0.6 1.2 %copy-start = (bf16[1,128,4096]{2,1,0:T(8,128)(2,1)S(1)}, bf16[1,128,4096]{2,1,0:T(8,128)(2,1)}, u32[]{:S(2)}) copy-start(bf16[1,128,4096]{2,1,0:T(8,128)(2,1)} %param.9) | copy-start | bytes 3145732
  0.6 3.6 %copy-start.1 = (bf16[1,128,4096]{2,1,0:T(8,128)(2,1)S(1)}, bf16[1,128,4096]{2,1,0:T(8,128)(2,1)}, u32[]{:S(2)}) copy-start(bf16[1,128,4096]{2,1,0:T(8,128)(2,1)} %param.10) | copy-start | bytes 3145732
  0.7 12.5 %collective-permute-start.2 = (bf16[128,1536]{1,0:T(8,128)(2,1)S(1)}, bf16[128,1536]{1,0:T(8,128)(2,1)S(1)}, u32[]{:S(2)}, u32[]{:S(2)}) collective-permute-start(bf16[128,1536]{1,0:T(8,128)(2,1)S(1)} %first_weigh.1.refs_1_.refs_3_), channel_id=1, source_target_pairs={{17,16},{18,17},{19,18},{20,19},{21,20},{22,21},{23,22},{24,23},{2... | collective-permute-start | bytes 1179656 | tf_op jit(solution)/shard_map/ppermute | solution.py:402
  1.9 26.3 %collective-permute-start = (bf16[128,4096]{1,0:T(8,128)(2,1)S(1)}, bf16[128,4096]{1,0:T(8,128)(2,1)S(1)}, u32[]{:S(2)}, u32[]{:S(2)}) collective-permute-start(bf16[128,4096]{1,0:T(8,128)(2,1)S(1)} %bitcast.11), channel_id=1, source_target_pairs={{0,1},{1,2},{2,3},{3,4},{4,5},{5,6},{6,7},{7,8},{8,9},{9,10},{10,1... | collective-permute-start | bytes 3145736 | tf_op jit(solution)/shard_map/ppermute | solution.py:407
  4.3 31.1 %collective-permute-start.1 = (bf16[128,4096]{1,0:T(8,128)(2,1)S(1)}, bf16[128,4096]{1,0:T(8,128)(2,1)S(1)}, u32[]{:S(2)}, u32[]{:S(2)}) collective-permute-start(bf16[128,4096]{1,0:T(8,128)(2,1)S(1)} %bitcast.28), channel_id=1, source_target_pairs={{0,1},{1,2},{2,3},{3,4},{4,5},{5,6},{6,7},{7,8},{8,9},{9,10},{10,1... | collective-permute-start | bytes 3145736 | tf_op jit(solution)/shard_map/ppermute | solution.py:408
  8.8 1.2 %copy-start.2 = (bf16[1,128,4096]{2,1,0:T(8,128)(2,1)S(1)}, bf16[1,128,4096]{2,1,0:T(8,128)(2,1)}, u32[]{:S(2)}) copy-start(bf16[1,128,4096]{2,1,0:T(8,128)(2,1)} %param.8) | copy-start | bytes 3145732
  10.1 1.2 %copy-start.4 = (bf16[128,4096]{1,0:T(8,128)(2,1)S(1)}, bf16[128,4096]{1,0:T(8,128)(2,1)}, u32[]{:S(2)}) copy-start(bf16[128,4096]{1,0:T(8,128)(2,1)} %refs_5_.7) | copy-start | bytes 3145732
  11.3 1.0 %copy-start.6 = (bf16[1,128,256]{2,1,0:T(8,128)(2,1)S(1)}, bf16[1,128,256]{2,1,0:T(8,128)(2,1)}, u32[]{:S(2)}) copy-start(bf16[1,128,256]{2,1,0:T(8,128)(2,1)} %param.11) | copy-start | bytes 196612
  11.3 1.1 %copy-start.7 = (f32[1,128,16]{1,2,0:T(8,128)S(1)}, f32[1,128,16]{1,2,0:T(8,128)}, u32[]{:S(2)}) copy-start(f32[1,128,16]{1,2,0:T(8,128)} %param.13) | copy-start | bytes 24580
  11.3 1.9 %copy-start.5 = (bf16[128,4096]{1,0:T(8,128)(2,1)S(1)}, bf16[128,4096]{1,0:T(8,128)(2,1)}, u32[]{:S(2)}) copy-start(bf16[128,4096]{1,0:T(8,128)(2,1)} %refs_5_.7) | copy-start | bytes 3145732
  11.5 3.3 %collective-permute-start.4 = (bf16[128,1536]{1,0:T(8,128)(2,1)S(1)}, bf16[128,1536]{1,0:T(8,128)(2,1)S(1)}, u32[]{:S(2)}, u32[]{:S(2)}) collective-permute-start(bf16[128,1536]{1,0:T(8,128)(2,1)S(1)} %weigh.2.refs_1_.refs_3_), channel_id=1, source_target_pairs={{17,16},{18,17},{19,18},{20,19},{21,20},{22,21},{23,22},{24,23},{2... | collective-permute-start | bytes 1179656 | tf_op jit(solution)/shard_map/ppermute | solution.py:402
  12.3 0.7 %copy-start.8 = (f32[1,256]{1,0:T(1,128)S(1)}, f32[1,256]{1,0:T(1,128)}, u32[]{:S(2)}) copy-start(f32[1,256]{1,0:T(1,128)} %steer_second.1) | copy-start | bytes 3076
  13.5 13.8 %collective-permute-start.3 = (bf16[128,1536]{1,0:T(8,128)(2,1)S(1)}, bf16[128,1536]{1,0:T(8,128)(2,1)S(1)}, u32[]{:S(2)}, u32[]{:S(2)}) collective-permute-start(bf16[128,1536]{1,0:T(8,128)(2,1)S(1)} %filter.4.refs_6_.refs_5_), channel_id=1, source_target_pairs={{16,0},{17,1},{18,2},{19,3},{20,4},{21,5},{22,6},{23,7},{24,8},{25... | collective-permute-start | bytes 1179656 | tf_op jit(solution)/shard_map/ppermute | solution.py:436
  15.1 12.2 %copy-start.3 = (bf16[1,128,4096]{2,1,0:T(8,128)(2,1)S(1)}, bf16[1,128,4096]{2,1,0:T(8,128)(2,1)}, u32[]{:S(2)}) copy-start(bf16[1,128,4096]{2,1,0:T(8,128)(2,1)} %param.8) | copy-start | bytes 3145732
  15.1 22.7 %collective-permute-start.6 = (bf16[128,1536]{1,0:T(8,128)(2,1)S(1)}, bf16[128,1536]{1,0:T(8,128)(2,1)S(1)}, u32[]{:S(2)}, u32[]{:S(2)}) collective-permute-start(bf16[128,1536]{1,0:T(8,128)(2,1)S(1)} %filter.5.refs_6_.refs_5_), channel_id=1, source_target_pairs={{16,0},{17,1},{18,2},{19,3},{20,4},{21,5},{22,6},{23,7},{24,8},{25... | collective-permute-start | bytes 1179656 | tf_op jit(solution)/shard_map/ppermute | solution.py:436
  27.4 4.1 %collective-permute-start.5 = (bf16[128,1024]{1,0:T(8,128)(2,1)S(1)}, bf16[128,1024]{1,0:T(8,128)(2,1)S(1)}, u32[]{:S(2)}, u32[]{:S(2)}) collective-permute-start(bf16[128,1024]{1,0:T(8,128)(2,1)S(1)} %weigh.3.refs_4_.refs_6_.refs_1_.refs_3_), channel_id=1, source_target_pairs={{17,16},{18,17},{19,18},{20,19},{21,20},{22,21},{23,22},{24,23},{2... | collective-permute-start | bytes 786440 | tf_op jit(solution)/shard_map/ppermute | solution.py:402
  31.6 8.6 %collective-permute-start.7 = (bf16[128,512]{1,0:T(8,128)(2,1)S(1)}, bf16[128,512]{1,0:T(8,128)(2,1)S(1)}, u32[]{:S(2)}, u32[]{:S(2)}) collective-permute-start(bf16[128,512]{1,0:T(8,128)(2,1)S(1)} %filter.6.refs_6_.refs_5_), channel_id=1, source_target_pairs={{16,0},{17,1},{18,2},{19,3},{20,4},{21,5},{22,6},{23,7},{24,8},{25... | collective-permute-start | bytes 393224 | tf_op jit(solution)/shard_map/ppermute | solution.py:436
  33.0 9.4 %collective-permute-start.8 = (bf16[128,512]{1,0:T(8,128)(2,1)S(1)}, bf16[128,512]{1,0:T(8,128)(2,1)S(1)}, u32[]{:S(2)}, u32[]{:S(2)}) collective-permute-start(bf16[128,512]{1,0:T(8,128)(2,1)S(1)} %filter.7.refs_4_.refs_5_), channel_id=1, source_target_pairs={{16,0},{17,1},{18,2},{19,3},{20,4},{21,5},{22,6},{23,7},{24,8},{25... | collective-permute-start | bytes 393224 | tf_op jit(solution)/shard_map/ppermute | solution.py:436

commit v10 on v9

--- a/solution.py
+++ b/solution.py
@@ -96,13 +96,13 @@
         out[...] = times(gate[...], incoming[...])
 
 
-def first_weigh_kernel(block, role, gate, incoming, out, gate_part, incoming_part, sems):
+def direct_weigh_kernel(first, block, role, gate, incoming, out, gate_part, incoming_part, sems):
     @pl.when(jnp.logical_not(first_section(role)))
     def _():
         tiles = [pl.ds(at, block) for at in range(0, out.shape[1], block)]
         copies = [
             [
-                pltpu.make_async_copy(source.at[:, t], part.at[:, t], sems.at[which, i])
+                pltpu.make_async_copy(source.at[:, pl.ds(first + i * block, block)], part.at[:, t], sems.at[which, i])
                 for which, (source, part) in enumerate(((gate, gate_part), (incoming, incoming_part)))
             ]
             for i, t in enumerate(tiles)
@@ -116,9 +116,13 @@
             out[:, t] = times(gate_part[:, t], incoming_part[:, t])
 
 
-def taps_kernel(role, filters, steer_second, filter_second, taps_out, steer_out, filter_out):
+def moments_kernel(role, steer_second, filter_second, *refs):
+    steer_out, filter_out = refs[-2:]
     steer_out[...] = steer_second[...]
     filter_out[...] = filter_second[...]
+
+
+def taps_kernel(role, filters, taps_out):
     pick, _ = tap_matrix(first_section(role), filters[...])
     taps_out[...] = lax.dot_general(
         filters[...], pick.astype(BF16), (((0,), (0,)), ((), ())), preferred_element_type=F32
@@ -322,29 +326,44 @@
             after=after,
         )(role, in_gate, incoming, *after)
 
-    def first_weigh(last):
-        part = pltpu.VMEM((rows, last), BF16)
+    def direct_weigh(first, last, after):
+        width = last - first
+        part = pltpu.VMEM((rows, width), BF16)
+
+        def kernel(*refs):
+            direct_weigh_kernel(first, block, *refs[:3], *refs[3 + len(after) :])
+
         return pl.pallas_call(
-            functools.partial(first_weigh_kernel, block),
-            in_specs=[SMEM] + [pl.BlockSpec(memory_space=pl.ANY)] * 2,
+            kernel,
+            in_specs=[SMEM] + [ANY] * (2 + len(after)),
             out_specs=pl.BlockSpec(memory_space=pltpu.VMEM),
-            out_shape=bf16(last),
-            scratch_shapes=[part, part, pltpu.SemaphoreType.DMA((2, last // block))],
+            out_shape=bf16(width),
+            scratch_shapes=[part, part, pltpu.SemaphoreType.DMA((2, width // block))],
             compiler_params=SMALL,
-            name="first_weigh",
-        )(role, *[pltpu.with_memory_space_constraint(a, pltpu.HBM) for a in (in_gate, cotangent)])
-
-    seconds = (steer_second, filter_second[0].T)
+            name="direct_weigh",
+        )(role, *[pltpu.with_memory_space_constraint(a, pltpu.HBM) for a in (in_gate, cotangent)], *after)
+
     vmem = pl.BlockSpec(memory_space=pltpu.VMEM)
-    taps, *seconds = pl.pallas_call(
+    taps = pl.pallas_call(
         taps_kernel,
-        in_specs=[SMEM] + [vmem] * 3,
-        out_specs=[vmem] * 3,
-        out_shape=[jax.ShapeDtypeStruct((groups, filt_len), F32)]
-        + [jax.ShapeDtypeStruct(second.shape, F32) for second in seconds],
+        in_specs=[SMEM, vmem],
+        out_specs=vmem,
+        out_shape=jax.ShapeDtypeStruct((groups, filt_len), F32),
         compiler_params=SMALL,
         name="taps",
-    )(role, filters[0], *seconds)
+    )(role, filters[0])
+
+    def moments(after):
+        seconds = (steer_second, filter_second[0].T)
+        return pl.pallas_call(
+            moments_kernel,
+            in_specs=[SMEM] + [vmem] * 2 + [ANY] * len(after),
+            out_specs=[vmem] * 2,
+            out_shape=[jax.ShapeDtypeStruct(second.shape, F32) for second in seconds],
+            compiler_params=SMALL,
+            name="moments",
+        )(role, *seconds, *after)
+
     group_spec = lambda first: pl.BlockSpec((block_groups, filt_len), lambda i: (i + first, 0))
 
     grad_specs = [group_spec(0), pl.BlockSpec((1, block), lambda i: (0, i))]
@@ -395,8 +414,8 @@
         def send_halo(after):
             first, last = starts[len(owns)], ends[len(owns)]
             array, offset = next(entry for entry, edge in zip(incoming, edges) if edge == first)
-            if hop == 0 and first == 0:
-                owns.append(first_weigh(last))
+            if hop == 0 and not early:
+                owns.append(direct_weigh(first, last, after))
             else:
                 owns.append(weigh(array, first, last, offset, after))
             halos.append(lax.ppermute(owns[-1], ("section", "seq"), behind))
@@ -436,7 +455,8 @@
             received.append(lax.ppermute(out, "section", down))
             if hop == sections - 2 and k == 1:
                 uppers = [upper_grad(0, (out,))]
-                early = [uppers[0][0]]
+                seconds = moments((out,))
+                early = [uppers[0][0], seconds[0]]
         top = my_section == sections - 1
         incoming = [
             (jnp.where(top, cotangent[:, first:last], arrived), first)

time: 57.3 us -> 55.8 us (0.974)
  blocking collectives: 12.9 us -> 18.2 us
  waiting for transfers between devices: 12 us -> 7.88 us
  local copies, waits for them, and re-layouts: 3.43 us -> 1.04 us
    all_to_all x1, blocking collectives: 12.9 us -> 18.2 us  [body(): parts = lax.all_to_all(packed, 'seq', 0, 0)]
    ppermute x4, waiting for transfers between devices: 11.9 us -> 7.86 us  [body(): received.append(lax.ppermute(out, 'section', down))]
    unnamed x18 -> x14, local copies, waits for them, and re-layouts: 3.43 us -> 1.04 us
  transfers between devices with their start and end apart: 9 -> 9, of which waited for: 2 -> 1; matrix products, arithmetic and copies ran while one was open for 0% -> 0% of each run, Pallas kernels for 20% -> 20%
where the time goes in v10:
time: 55.8 us; the launch traced here: 55.4 us
  blocking collectives  18.2 us (33%)
  starting transfers between devices  14.4 us (26%)
  Pallas kernels  12.9 us (23%)
  waiting for transfers between devices  7.88 us (14%)
  local copies, waits for them, and re-layouts  1.04 us (2%)
  between operations  0.95 us (2%)
    all_to_all x1, blocking collectives, body(): parts = lax.all_to_all(packed, 'seq', 0, 0)  18.2 us
    ppermute x4, waiting for transfers between devices, body(): received.append(lax.ppermute(out, 'section', down))  7.86 us
    pallas_call x4, Pallas kernels, body(): call(functools.partial(first_grad_kernel, group_size), ((last - first) //...  6.41 us
    ppermute x4, starting transfers between devices, body(): received.append(lax.ppermute(out, 'section', down))  5.17 us
    ppermute x1, starting transfers between devices, body(): inputs_halo = lax.ppermute(inputs_sent, ('section', 'seq'), ahead)  4.54 us
    pallas_call x4, Pallas kernels, turned_filter(): call(functools.partial(turned_filter_kernel, group_size), ((last - first)...  4.09 us
    ppermute x1, starting transfers between devices, body(): mid_halo = lax.ppermute(mid_sent, ('section', 'seq'), ahead)  2.54 us
    ppermute x3, starting transfers between devices, send_halo(): halos.append(lax.ppermute(owns[-1], ('section', 'seq'), behind))  2.18 us
  transfers between devices with their start and end apart: 9, of which 1 were waited for; matrix products, arithmetic and copies ran while one was open for 0% of the time, Pallas kernels for 20%

profile of v10, /device:TPU:0, one launch (start us, length us, event | category | flops | bytes accessed | tf_op | source)
XLA Modules:
  0.0 55.4 jit_solution(4289692945109596189)
XLA Ops:
  0.6 0.0 copy-start
  0.6 0.0 copy-start.1
  0.7 0.1 direct_weigh.2.refs_1_.refs_3_
  0.7 0.8 %collective-permute-start.2 = (bf16[128,1536]{1,0:T(8,128)(2,1)S(1)}, bf16[128,1536]{1,0:T(8,128)(2,1)S(1)}, u32[]{:S(2)}, u32[]{:S(2)}) collective-permute-start(bf16[128,1536]{1,0:T(8,128)(2,1)S(1)} %direct_weigh.2.refs_1_.refs_3_), channel_id=1, source_target_pairs={{17,16},{18,17},{19,18},{20,19},{21,20},{22,21},{23,22},{24,23},{2... | collective-permute-start | bytes 1179656 | tf_op jit(solution)/shard_map/ppermute | solution.py:421
  1.6 0.3 copy-done
  1.9 0.0 copy-start.4
  1.9 0.0 copy-start.3
  1.9 2.5 %collective-permute-start = (bf16[128,4096]{1,0:T(8,128)(2,1)S(1)}, bf16[128,4096]{1,0:T(8,128)(2,1)S(1)}, u32[]{:S(2)}, u32[]{:S(2)}) collective-permute-start(bf16[128,4096]{1,0:T(8,128)(2,1)S(1)} %bitcast.11), channel_id=1, source_target_pairs={{0,1},{1,2},{2,3},{3,4},{4,5},{5,6},{6,7},{7,8},{8,9},{9,10},{10,1... | collective-permute-start | bytes 3145736 | tf_op jit(solution)/shard_map/ppermute | solution.py:426
  4.4 0.0 copy-done.1
  4.4 4.5 %collective-permute-start.1 = (bf16[128,4096]{1,0:T(8,128)(2,1)S(1)}, bf16[128,4096]{1,0:T(8,128)(2,1)S(1)}, u32[]{:S(2)}, u32[]{:S(2)}) collective-permute-start(bf16[128,4096]{1,0:T(8,128)(2,1)S(1)} %bitcast.28), channel_id=1, source_target_pairs={{0,1},{1,2},{2,3},{3,4},{4,5},{5,6},{6,7},{7,8},{8,9},{9,10},{10,1... | collective-permute-start | bytes 3145736 | tf_op jit(solution)/shard_map/ppermute | solution.py:427
  9.0 0.1 direct_weigh.3.refs_1_.refs_3_
  9.0 0.7 %collective-permute-start.4 = (bf16[128,1536]{1,0:T(8,128)(2,1)S(1)}, bf16[128,1536]{1,0:T(8,128)(2,1)S(1)}, u32[]{:S(2)}, u32[]{:S(2)}) collective-permute-start(bf16[128,1536]{1,0:T(8,128)(2,1)S(1)} %direct_weigh.3.refs_1_.refs_3_), channel_id=1, source_target_pairs={{17,16},{18,17},{19,18},{20,19},{21,20},{22,21},{23,22},{24,23},{2... | collective-permute-start | bytes 1179656 | tf_op jit(solution)/shard_map/ppermute | solution.py:421
  9.7 0.0 copy-done.4
  9.7 0.2 taps.1.refs_3_
  9.9 0.0 collective-permute-done.2.refs_2_.refs_4_
  9.9 0.0 copy-done.3
  10.0 0.3 filter.4.refs_6_.refs_5_
  10.2 1.3 %collective-permute-start.3 = (bf16[128,1536]{1,0:T(8,128)(2,1)S(1)}, bf16[128,1536]{1,0:T(8,128)(2,1)S(1)}, u32[]{:S(2)}, u32[]{:S(2)}) collective-permute-start(bf16[128,1536]{1,0:T(8,128)(2,1)S(1)} %filter.4.refs_6_.refs_5_), channel_id=1, source_target_pairs={{16,0},{17,1},{18,2},{19,3},{20,4},{21,5},{22,6},{23,7},{24,8},{25... | collective-permute-start | bytes 1179656 | tf_op jit(solution)/shard_map/ppermute | solution.py:455
  11.5 0.0 collective-permute-done.4.refs_2_.refs_4_
  11.5 0.3 filter.5.refs_6_.refs_0_.refs_5_
  11.8 0.0 copy-start.5
  11.8 1.3 %collective-permute-start.6 = (bf16[128,1536]{1,0:T(8,128)(2,1)S(1)}, bf16[128,1536]{1,0:T(8,128)(2,1)S(1)}, u32[]{:S(2)}, u32[]{:S(2)}) collective-permute-start(bf16[128,1536]{1,0:T(8,128)(2,1)S(1)} %filter.5.refs_6_.refs_0_.refs_5_), channel_id=1, source_target_pairs={{16,0},{17,1},{18,2},{19,3},{20,4},{21,5},{22,6},{23,7},{24,8},{25... | collective-permute-start | bytes 1179656 | tf_op jit(solution)/shard_map/ppermute | solution.py:455
  13.1 0.0 copy-start.2
  13.1 0.3 upper_grads.4
  13.4 0.0 copy-start.6
  13.4 0.0 copy-done.5
  13.4 0.7 %copy-done.6 = f32[1,256]{1,0:T(1,128)S(1)} copy-done((f32[1,256]{1,0:T(1,128)S(1)}, f32[1,256]{1,0:T(1,128)}, u32[]{:S(2)}) %copy-start.6) | copy-done | bytes 1048
  14.1 7.9 %collective-permute-done.3.refs_3_.refs_6_ = bf16[128,1536]{1,0:T(8,128)(2,1)S(1)} collective-permute-done((bf16[128,1536]{1,0:T(8,128)(2,1)S(1)}, bf16[128,1536]{1,0:T(8,128)(2,1)S(1)}, u32[]{:S(2)}, u32[]{:S(2)}) %collective-permute-start.3) | collective-permute-done | bytes 393248 | tf_op jit(solution)/shard_map/ppermute | solution.py:455
  22.0 0.0 copy-done.2
  22.0 0.1 weigh.1.refs_4_.refs_6_.refs_1_.refs_3_
  22.1 0.7 %collective-permute-start.5 = (bf16[128,1024]{1,0:T(8,128)(2,1)S(1)}, bf16[128,1024]{1,0:T(8,128)(2,1)S(1)}, u32[]{:S(2)}, u32[]{:S(2)}) collective-permute-start(bf16[128,1024]{1,0:T(8,128)(2,1)S(1)} %weigh.1.refs_4_.refs_6_.refs_1_.refs_3_), channel_id=1, source_target_pairs={{17,16},{18,17},{19,18},{20,19},{21,20},{22,21},{23,22},{24,23},{2... | collective-permute-start | bytes 786440 | tf_op jit(solution)/shard_map/ppermute | solution.py:421
  22.8 0.0 collective-permute-done.refs_2_.refs_4_
  22.8 1.6 %turned_filter.4.refs_4_.refs_7_ = f32[128,1536]{1,0:T(8,128)S(1)} custom-call(s32[1]{0:T(128)} %bitcast.refs_0_.role, bf16[128,4096]{1,0:T(8,128)(2,1)S(1)} %bitcast.15, bf16[128,4096]{1,0:T(8,128)(2,1)S(1)} %collective-permute-done.refs_2_.refs_4_, f32[256,128]{1,0:T(8,128)S(1)} %taps.1.refs_3_, bf16[128,1024]{1,0:T(8,128)(2,1)S(1)} %weigh.1.refs_4_.refs_6_.refs_1_.refs_3_), custom_call_target="tpu_custom_call" | custom-call | flops 1000 | tf_op jit(solution)/shard_map/turned_filter/pallas_call | solution.py:396
  24.4 0.3 upper_grads.5
  24.7 1.6 %turned_filter.5.refs_8_.refs_7_ = f32[128,1536]{1,0:T(8,128)S(1)} custom-call(s32[1]{0:T(128)} %bitcast.refs_0_.role, bf16[128,4096]{1,0:T(8,128)(2,1)S(1)} %bitcast.17, bf16[128,4096]{1,0:T(8,128)(2,1)S(1)} %collective-permute-done.refs_2_.refs_4_, f32[256,128]{1,0:T(8,128)S(1)} %taps.1.refs_3_, f32[128,1536]{1,0:T(8,128)S(1)} %turned_filter.4.refs_4_.refs_7_), custom_call_target="tpu_custom_call" | custom-call | flops 1000 | tf_op jit(solution)/shard_map/turned_filter/pallas_call | solution.py:396
  26.3 0.0 collective-permute-done.5.refs_2_.refs_4_
  26.3 1.3 %collective-permute-start.7 = (bf16[128,512]{1,0:T(8,128)(2,1)S(1)}, bf16[128,512]{1,0:T(8,128)(2,1)S(1)}, u32[]{:S(2)}, u32[]{:S(2)}) collective-permute-start(bf16[128,512]{1,0:T(8,128)(2,1)S(1)} %filter.6.refs_6_.refs_5_), channel_id=1, source_target_pairs={{16,0},{17,1},{18,2},{19,3},{20,4},{21,5},{22,6},{23,7},{24,8},{25... | collective-permute-start | bytes 393224 | tf_op jit(solution)/shard_map/ppermute | solution.py:455
  27.7 1.3 %collective-permute-start.8 = (bf16[128,512]{1,0:T(8,128)(2,1)S(1)}, bf16[128,512]{1,0:T(8,128)(2,1)S(1)}, u32[]{:S(2)}, u32[]{:S(2)}) collective-permute-start(bf16[128,512]{1,0:T(8,128)(2,1)S(1)} %filter.7.refs_4_.refs_5_), channel_id=1, source_target_pairs={{16,0},{17,1},{18,2},{19,3},{20,4},{21,5},{22,6},{23,7},{24,8},{25... | collective-permute-start | bytes 393224 | tf_op jit(solution)/shard_map/ppermute | solution.py:455
  29.0 0.5 turned_filter.6.refs_4_.refs_7_
  29.5 0.5 turned_filter.7.refs_6_.refs_7_
  30.0 0.0 collective-permute-done.1.refs_5_
  30.0 2.4 %first_grads.4 = (f32[96,128]{1,0:T(8,128)S(1)}, f32[1,1536]{1,0:T(1,128)S(1)}) custom-call(s32[1]{0:T(128)} %bitcast.refs_0_.role, bf16[128,4096]{1,0:T(8,128)(2,1)S(1)} %bitcast.40, bf16[128,4096]{1,0:T(8,128)(2,1)S(1)} %bitcast.24, bf16[128,4096]{1,0:T(8,128)(2,1)S(1)} %bitcast.33, bf16[128,4096]{1,0:T(8,128)(2,1)S(1)} %collective-permute-done.refs_2_.refs_4_, ...), custom_call_target="tpu_custom_call" | custom-call | flops 2000 | tf_op jit(solution)/shard_map/first_grads/pallas_call | solution.py:476
  32.5 0.0 collective-permute-done.6.refs_6_
  32.5 2.4 %first_grads.5 = (f32[96,128]{1,0:T(8,128)S(1)}, f32[1,1536]{1,0:T(1,128)S(1)}) custom-call(s32[1]{0:T(128)} %bitcast.refs_0_.role, bf16[128,4096]{1,0:T(8,128)(2,1)S(1)} %bitcast.41, bf16[128,4096]{1,0:T(8,128)(2,1)S(1)} %bitcast.25, bf16[128,4096]{1,0:T(8,128)(2,1)S(1)} %bitcast.34, bf16[128,4096]{1,0:T(8,128)(2,1)S(1)} %collective-permute-done.refs_2_.refs_4_, ...), custom_call_target="tpu_custom_call" | custom-call | flops 2000 | tf_op jit(solution)/shard_map/first_grads/pallas_call | solution.py:476
  34.9 0.0 collective-permute-done.7.refs_6_
  34.9 0.8 %first_grads.6 = (f32[32,128]{1,0:T(8,128)S(1)}, f32[1,512]{1,0:T(1,128)S(1)}) custom-call(s32[1]{0:T(128)} %bitcast.refs_0_.role, bf16[128,4096]{1,0:T(8,128)(2,1)S(1)} %bitcast.42, bf16[128,4096]{1,0:T(8,128)(2,1)S(1)} %bitcast.26, bf16[128,4096]{1,0:T(8,128)(2,1)S(1)} %bitcast.35, bf16[128,4096]{1,0:T(8,128)(2,1)S(1)} %collective-permute-done.refs_2_.refs_4_, ...), custom_call_target="tpu_custom_call" | custom-call | flops 2000 | tf_op jit(solution)/shard_map/first_grads/pallas_call | solution.py:476
  35.7 0.0 collective-permute-done.8.refs_6_
  35.7 0.8 %first_grads.7 = (f32[32,128]{1,0:T(8,128)S(1)}, f32[1,512]{1,0:T(1,128)S(1)}) custom-call(s32[1]{0:T(128)} %bitcast.refs_0_.role, bf16[128,4096]{1,0:T(8,128)(2,1)S(1)} %bitcast.43, bf16[128,4096]{1,0:T(8,128)(2,1)S(1)} %bitcast.27, bf16[128,4096]{1,0:T(8,128)(2,1)S(1)} %bitcast.36, bf16[128,4096]{1,0:T(8,128)(2,1)S(1)} %collective-permute-done.refs_2_.refs_4_, ...), custom_call_target="tpu_custom_call" | custom-call | flops 2000 | tf_op jit(solution)/shard_map/first_grads/pallas_call | solution.py:476
  36.5 18.2 %all_to_all.5.parts = bf16[16,18,128]{2,1,0:T(8,128)(2,1)S(1)} all-to-all(bf16[16,18,128]{2,1,0:T(8,128)(2,1)S(1)} %pack.1), channel_id=1, replica_groups=mesh['section'=2,'seq'=16] {'seq'}, dimensions={0} | all-to-all | bytes 147456 | tf_op jit(solution)/shard_map/all_to_all | solution.py:499
  54.7 0.7 %step.1 = (f32[1,256]{1,0:T(1,128)}, f32[16,128]{1,0:T(8,128)}) custom-call(s32[1]{0:T(128)} %bitcast.refs_0_.role, bf16[16,18,128]{2,1,0:T(8,128)(2,1)S(1)} %all_to_all.5.parts, f32[1,256]{1,0:T(1,128)S(1)} %get-tuple-element.27.refs_5_.steer_second, f32[16,128]{1,0:T(8,128)S(1)} %get-tuple-element.43.filter_second), custom_call_target="tpu_custom_call" | custom-call | tf_op jit(solution)/shard_map/step/pallas_call | solution.py:500
  (6 shorter events, 0.2 us)
Async XLA Ops:
  0.6 1.2 %copy-start = (bf16[1,128,4096]{2,1,0:T(8,128)(2,1)S(1)}, bf16[1,128,4096]{2,1,0:T(8,128)(2,1)}, u32[]{:S(2)}) copy-start(bf16[1,128,4096]{2,1,0:T(8,128)(2,1)} %param.9) | copy-start | bytes 3145732
  0.6 3.8 %copy-start.1 = (bf16[1,128,4096]{2,1,0:T(8,128)(2,1)S(1)}, bf16[1,128,4096]{2,1,0:T(8,128)(2,1)}, u32[]{:S(2)}) copy-start(bf16[1,128,4096]{2,1,0:T(8,128)(2,1)} %param.10) | copy-start | bytes 3145732
  0.7 9.2 %collective-permute-start.2 = (bf16[128,1536]{1,0:T(8,128)(2,1)S(1)}, bf16[128,1536]{1,0:T(8,128)(2,1)S(1)}, u32[]{:S(2)}, u32[]{:S(2)}) collective-permute-start(bf16[128,1536]{1,0:T(8,128)(2,1)S(1)} %direct_weigh.2.refs_1_.refs_3_), channel_id=1, source_target_pairs={{17,16},{18,17},{19,18},{20,19},{21,20},{22,21},{23,22},{24,23},{2... | collective-permute-start | bytes 1179656 | tf_op jit(solution)/shard_map/ppermute | solution.py:421
  1.9 7.9 %copy-start.4 = (bf16[1,128,256]{2,1,0:T(8,128)(2,1)S(1)}, bf16[1,128,256]{2,1,0:T(8,128)(2,1)}, u32[]{:S(2)}) copy-start(bf16[1,128,256]{2,1,0:T(8,128)(2,1)} %param.11) | copy-start | bytes 196612
  1.9 8.1 %copy-start.3 = (bf16[128,4096]{1,0:T(8,128)(2,1)S(1)}, bf16[128,4096]{1,0:T(8,128)(2,1)}, u32[]{:S(2)}) copy-start(bf16[128,4096]{1,0:T(8,128)(2,1)} %refs_5_.7) | copy-start | bytes 3145732
  1.9 21.0 %collective-permute-start = (bf16[128,4096]{1,0:T(8,128)(2,1)S(1)}, bf16[128,4096]{1,0:T(8,128)(2,1)S(1)}, u32[]{:S(2)}, u32[]{:S(2)}) collective-permute-start(bf16[128,4096]{1,0:T(8,128)(2,1)S(1)} %bitcast.11), channel_id=1, source_target_pairs={{0,1},{1,2},{2,3},{3,4},{4,5},{5,6},{6,7},{7,8},{8,9},{9,10},{10,1... | collective-permute-start | bytes 3145736 | tf_op jit(solution)/shard_map/ppermute | solution.py:426
  4.4 25.6 %collective-permute-start.1 = (bf16[128,4096]{1,0:T(8,128)(2,1)S(1)}, bf16[128,4096]{1,0:T(8,128)(2,1)S(1)}, u32[]{:S(2)}, u32[]{:S(2)}) collective-permute-start(bf16[128,4096]{1,0:T(8,128)(2,1)S(1)} %bitcast.28), channel_id=1, source_target_pairs={{0,1},{1,2},{2,3},{3,4},{4,5},{5,6},{6,7},{7,8},{8,9},{9,10},{10,1... | collective-permute-start | bytes 3145736 | tf_op jit(solution)/shard_map/ppermute | solution.py:427
  9.0 2.5 %collective-permute-start.4 = (bf16[128,1536]{1,0:T(8,128)(2,1)S(1)}, bf16[128,1536]{1,0:T(8,128)(2,1)S(1)}, u32[]{:S(2)}, u32[]{:S(2)}) collective-permute-start(bf16[128,1536]{1,0:T(8,128)(2,1)S(1)} %direct_weigh.3.refs_1_.refs_3_), channel_id=1, source_target_pairs={{17,16},{18,17},{19,18},{20,19},{21,20},{22,21},{23,22},{24,23},{2... | collective-permute-start | bytes 1179656 | tf_op jit(solution)/shard_map/ppermute | solution.py:421
  10.2 11.8 %collective-permute-start.3 = (bf16[128,1536]{1,0:T(8,128)(2,1)S(1)}, bf16[128,1536]{1,0:T(8,128)(2,1)S(1)}, u32[]{:S(2)}, u32[]{:S(2)}) collective-permute-start(bf16[128,1536]{1,0:T(8,128)(2,1)S(1)} %filter.4.refs_6_.refs_5_), channel_id=1, source_target_pairs={{16,0},{17,1},{18,2},{19,3},{20,4},{21,5},{22,6},{23,7},{24,8},{25... | collective-permute-start | bytes 1179656 | tf_op jit(solution)/shard_map/ppermute | solution.py:455
  11.8 1.6 %copy-start.5 = (f32[1,128,16]{1,2,0:T(8,128)S(1)}, f32[1,128,16]{1,2,0:T(8,128)}, u32[]{:S(2)}) copy-start(f32[1,128,16]{1,2,0:T(8,128)} %param.13) | copy-start | bytes 24580
  11.8 20.7 %collective-permute-start.6 = (bf16[128,1536]{1,0:T(8,128)(2,1)S(1)}, bf16[128,1536]{1,0:T(8,128)(2,1)S(1)}, u32[]{:S(2)}, u32[]{:S(2)}) collective-permute-start(bf16[128,1536]{1,0:T(8,128)(2,1)S(1)} %filter.5.refs_6_.refs_0_.refs_5_), channel_id=1, source_target_pairs={{16,0},{17,1},{18,2},{19,3},{20,4},{21,5},{22,6},{23,7},{24,8},{25... | collective-permute-start | bytes 1179656 | tf_op jit(solution)/shard_map/ppermute | solution.py:455
  13.1 8.9 %copy-start.2 = (bf16[1,128,4096]{2,1,0:T(8,128)(2,1)S(1)}, bf16[1,128,4096]{2,1,0:T(8,128)(2,1)}, u32[]{:S(2)}) copy-start(bf16[1,128,4096]{2,1,0:T(8,128)(2,1)} %param.8) | copy-start | bytes 3145732
  13.4 0.7 %copy-start.6 = (f32[1,256]{1,0:T(1,128)S(1)}, f32[1,256]{1,0:T(1,128)}, u32[]{:S(2)}) copy-start(f32[1,256]{1,0:T(1,128)} %steer_second.1) | copy-start | bytes 3076
  22.1 4.1 %collective-permute-start.5 = (bf16[128,1024]{1,0:T(8,128)(2,1)S(1)}, bf16[128,1024]{1,0:T(8,128)(2,1)S(1)}, u32[]{:S(2)}, u32[]{:S(2)}) collective-permute-start(bf16[128,1024]{1,0:T(8,128)(2,1)S(1)} %weigh.1.refs_4_.refs_6_.refs_1_.refs_3_), channel_id=1, source_target_pairs={{17,16},{18,17},{19,18},{20,19},{21,20},{22,21},{23,22},{24,23},{2... | collective-permute-start | bytes 786440 | tf_op jit(solution)/shard_map/ppermute | solution.py:421
  26.3 8.6 %collective-permute-start.7 = (bf16[128,512]{1,0:T(8,128)(2,1)S(1)}, bf16[128,512]{1,0:T(8,128)(2,1)S(1)}, u32[]{:S(2)}, u32[]{:S(2)}) collective-permute-start(bf16[128,512]{1,0:T(8,128)(2,1)S(1)} %filter.6.refs_6_.refs_5_), channel_id=1, source_target_pairs={{16,0},{17,1},{18,2},{19,3},{20,4},{21,5},{22,6},{23,7},{24,8},{25... | collective-permute-start | bytes 393224 | tf_op jit(solution)/shard_map/ppermute | solution.py:455
  27.7 8.0 %collective-permute-start.8 = (bf16[128,512]{1,0:T(8,128)(2,1)S(1)}, bf16[128,512]{1,0:T(8,128)(2,1)S(1)}, u32[]{:S(2)}, u32[]{:S(2)}) collective-permute-start(bf16[128,512]{1,0:T(8,128)(2,1)S(1)} %filter.7.refs_4_.refs_5_), channel_id=1, source_target_pairs={{16,0},{17,1},{18,2},{19,3},{20,4},{21,5},{22,6},{23,7},{24,8},{25... | collective-permute-start | bytes 393224 | tf_op jit(solution)/shard_map/ppermute | solution.py:455

commit v11 on v10

--- a/solution.py
+++ b/solution.py
@@ -386,7 +386,7 @@
             grad_specs,
             grad_shapes(k),
             name="upper_grads",
-            cycles=2000,
+            cycles=6 * 10**9 if k == 0 else 2000,
             after=tuple(after),
         )(role, mid_gate, layer_inputs, own, halo, outgoing[k], *after)
 
@@ -430,13 +430,13 @@
         for k, (first, last) in enumerate(bounds):
             part = max(i for i, start in enumerate(starts) if start <= first)
             while part >= len(owns):
-                send_halo(tuple(received[:1]) + tuple(early))
+                send_halo(tuple(early))
             at = (first - starts[part]) // block
             array, offset = incoming[k]
             before = tuple(outgoing[-1:])
             if hop == sections - 2 and k == 2:
                 uppers.append(upper_grad(1, owns[-1:]))
-                filtered.append(turned_filter(0, owns[-1:]))
+                filtered.append(turned_filter(0, owns[-1:] + received[:1]))
                 filtered.append(turned_filter(1, filtered[-1:]))
                 before += (uppers[-1][0], filtered[-1])
             out = call(

time: 55.8 us -> 54.5 us (0.977)
  blocking collectives: 18.2 us -> 17.6 us
    all_to_all x1, blocking collectives: 18.2 us -> 17.6 us  [body(): parts = lax.all_to_all(packed, 'seq', 0, 0)]
  transfers between devices with their start and end apart: 9 -> 9, of which waited for: 1 -> 3; matrix products, arithmetic and copies ran while one was open for 0% -> 0% of each run, Pallas kernels for 20% -> 21%
where the time goes in v11:
time: 54.5 us; the launch traced here: 54.1 us
  blocking collectives  17.6 us (32%)
  starting transfers between devices  14.3 us (26%)
  Pallas kernels  12.9 us (24%)
  waiting for transfers between devices  7.41 us (14%)
  between operations  0.97 us (2%)
  local copies, waits for them, and re-layouts  0.96 us (2%)
    all_to_all x1, blocking collectives, body(): parts = lax.all_to_all(packed, 'seq', 0, 0)  17.6 us
    ppermute x4, waiting for transfers between devices, body(): received.append(lax.ppermute(out, 'section', down))  7.4 us
    pallas_call x4, Pallas kernels, body(): call(functools.partial(first_grad_kernel, group_size), ((last - first) //...  6.4 us
    ppermute x4, starting transfers between devices, body(): received.append(lax.ppermute(out, 'section', down))  5.17 us
    ppermute x1, starting transfers between devices, body(): inputs_halo = lax.ppermute(inputs_sent, ('section', 'seq'), ahead)  4.54 us
    pallas_call x4, Pallas kernels, turned_filter(): call(functools.partial(turned_filter_kernel, group_size), ((last - first)...  4.07 us
    ppermute x1, starting transfers between devices, body(): mid_halo = lax.ppermute(mid_sent, ('section', 'seq'), ahead)  2.42 us
    ppermute x3, starting transfers between devices, send_halo(): halos.append(lax.ppermute(owns[-1], ('section', 'seq'), behind))  2.18 us
  transfers between devices with their start and end apart: 9, of which 3 were waited for; matrix products, arithmetic and copies ran while one was open for 0% of the time, Pallas kernels for 21%

profile of v11, /device:TPU:0, one launch (start us, length us, event | category | flops | bytes accessed | tf_op | source)
XLA Modules:
  0.0 54.1 jit_solution(17152362803525765892)
XLA Ops:
  0.6 0.0 copy-start.3
  0.6 0.1 direct_weigh.2.refs_1_.refs_3_
  0.7 0.0 copy-start
  0.7 0.0 copy-start.4
  0.7 0.0 copy-start.1
  0.8 0.8 %collective-permute-start.2 = (bf16[128,1536]{1,0:T(8,128)(2,1)S(1)}, bf16[128,1536]{1,0:T(8,128)(2,1)S(1)}, u32[]{:S(2)}, u32[]{:S(2)}) collective-permute-start(bf16[128,1536]{1,0:T(8,128)(2,1)S(1)} %direct_weigh.2.refs_1_.refs_3_), channel_id=1, source_target_pairs={{17,16},{18,17},{19,18},{20,19},{21,20},{22,21},{23,22},{24,23},{2... | collective-permute-start | bytes 1179656 | tf_op jit(solution)/shard_map/ppermute | solution.py:421
  1.6 0.1 direct_weigh.3.refs_1_.refs_3_
  1.7 0.7 %collective-permute-start.4 = (bf16[128,1536]{1,0:T(8,128)(2,1)S(1)}, bf16[128,1536]{1,0:T(8,128)(2,1)S(1)}, u32[]{:S(2)}, u32[]{:S(2)}) collective-permute-start(bf16[128,1536]{1,0:T(8,128)(2,1)S(1)} %direct_weigh.3.refs_1_.refs_3_), channel_id=1, source_target_pairs={{17,16},{18,17},{19,18},{20,19},{21,20},{22,21},{23,22},{24,23},{2... | collective-permute-start | bytes 1179656 | tf_op jit(solution)/shard_map/ppermute | solution.py:421
  2.3 0.0 copy-done
  2.4 2.4 %collective-permute-start = (bf16[128,4096]{1,0:T(8,128)(2,1)S(1)}, bf16[128,4096]{1,0:T(8,128)(2,1)S(1)}, u32[]{:S(2)}, u32[]{:S(2)}) collective-permute-start(bf16[128,4096]{1,0:T(8,128)(2,1)S(1)} %bitcast.11), channel_id=1, source_target_pairs={{0,1},{1,2},{2,3},{3,4},{4,5},{5,6},{6,7},{7,8},{8,9},{9,10},{10,1... | collective-permute-start | bytes 3145736 | tf_op jit(solution)/shard_map/ppermute | solution.py:426
  4.8 0.0 copy-done.3
  4.8 4.5 %collective-permute-start.1 = (bf16[128,4096]{1,0:T(8,128)(2,1)S(1)}, bf16[128,4096]{1,0:T(8,128)(2,1)S(1)}, u32[]{:S(2)}, u32[]{:S(2)}) collective-permute-start(bf16[128,4096]{1,0:T(8,128)(2,1)S(1)} %bitcast.35), channel_id=1, source_target_pairs={{0,1},{1,2},{2,3},{3,4},{4,5},{5,6},{6,7},{7,8},{8,9},{9,10},{10,1... | collective-permute-start | bytes 3145736 | tf_op jit(solution)/shard_map/ppermute | solution.py:427
  9.3 0.0 copy-done.4
  9.4 0.2 taps.1.refs_3_
  9.5 0.0 collective-permute-done.2.refs_2_.refs_4_
  9.5 0.0 copy-done.1
  9.6 0.3 filter.4.refs_6_.refs_5_
  9.8 1.3 %collective-permute-start.3 = (bf16[128,1536]{1,0:T(8,128)(2,1)S(1)}, bf16[128,1536]{1,0:T(8,128)(2,1)S(1)}, u32[]{:S(2)}, u32[]{:S(2)}) collective-permute-start(bf16[128,1536]{1,0:T(8,128)(2,1)S(1)} %filter.4.refs_6_.refs_5_), channel_id=1, source_target_pairs={{16,0},{17,1},{18,2},{19,3},{20,4},{21,5},{22,6},{23,7},{24,8},{25... | collective-permute-start | bytes 1179656 | tf_op jit(solution)/shard_map/ppermute | solution.py:455
  11.1 0.0 collective-permute-done.4.refs_2_.refs_4_
  11.1 0.3 filter.5.refs_6_.refs_0_.refs_5_
  11.4 0.0 copy-start.5
  11.4 1.3 %collective-permute-start.6 = (bf16[128,1536]{1,0:T(8,128)(2,1)S(1)}, bf16[128,1536]{1,0:T(8,128)(2,1)S(1)}, u32[]{:S(2)}, u32[]{:S(2)}) collective-permute-start(bf16[128,1536]{1,0:T(8,128)(2,1)S(1)} %filter.5.refs_6_.refs_0_.refs_5_), channel_id=1, source_target_pairs={{16,0},{17,1},{18,2},{19,3},{20,4},{21,5},{22,6},{23,7},{24,8},{25... | collective-permute-start | bytes 1179656 | tf_op jit(solution)/shard_map/ppermute | solution.py:455
  12.7 0.0 copy-start.2
  12.7 0.3 upper_grads.4
  13.0 0.0 copy-start.6
  13.0 0.0 copy-done.5
  13.0 0.7 %copy-done.6 = f32[1,256]{1,0:T(1,128)S(1)} copy-done((f32[1,256]{1,0:T(1,128)S(1)}, f32[1,256]{1,0:T(1,128)}, u32[]{:S(2)}) %copy-start.6) | copy-done | bytes 1048
  13.7 0.2 copy-done.2
  14.0 0.1 weigh.1.refs_4_.refs_6_.refs_1_.refs_3_
  14.1 0.7 %collective-permute-start.5 = (bf16[128,1024]{1,0:T(8,128)(2,1)S(1)}, bf16[128,1024]{1,0:T(8,128)(2,1)S(1)}, u32[]{:S(2)}, u32[]{:S(2)}) collective-permute-start(bf16[128,1024]{1,0:T(8,128)(2,1)S(1)} %weigh.1.refs_4_.refs_6_.refs_1_.refs_3_), channel_id=1, source_target_pairs={{17,16},{18,17},{19,18},{20,19},{21,20},{22,21},{23,22},{24,23},{2... | collective-permute-start | bytes 786440 | tf_op jit(solution)/shard_map/ppermute | solution.py:421
  14.8 6.3 %collective-permute-done.3.refs_5_.refs_6_ = bf16[128,1536]{1,0:T(8,128)(2,1)S(1)} collective-permute-done((bf16[128,1536]{1,0:T(8,128)(2,1)S(1)}, bf16[128,1536]{1,0:T(8,128)(2,1)S(1)}, u32[]{:S(2)}, u32[]{:S(2)}) %collective-permute-start.3) | collective-permute-done | bytes 393248 | tf_op jit(solution)/shard_map/ppermute | solution.py:455
  21.1 0.0 collective-permute-done.refs_2_.refs_4_
  21.1 1.5 %turned_filter.4.refs_4_.refs_7_ = f32[128,1536]{1,0:T(8,128)S(1)} custom-call(s32[1]{0:T(128)} %bitcast.refs_0_.role, bf16[128,4096]{1,0:T(8,128)(2,1)S(1)} %bitcast.15, bf16[128,4096]{1,0:T(8,128)(2,1)S(1)} %collective-permute-done.refs_2_.refs_4_, f32[256,128]{1,0:T(8,128)S(1)} %taps.1.refs_3_, ...), custom_call_target="tpu_custom_call" | custom-call | flops 1000 | tf_op jit(solution)/shard_map/turned_filter/pallas_call | solution.py:396
  22.6 0.3 upper_grads.5
  22.9 1.6 %turned_filter.5.refs_8_.refs_7_ = f32[128,1536]{1,0:T(8,128)S(1)} custom-call(s32[1]{0:T(128)} %bitcast.refs_0_.role, bf16[128,4096]{1,0:T(8,128)(2,1)S(1)} %bitcast.17, bf16[128,4096]{1,0:T(8,128)(2,1)S(1)} %collective-permute-done.refs_2_.refs_4_, f32[256,128]{1,0:T(8,128)S(1)} %taps.1.refs_3_, f32[128,1536]{1,0:T(8,128)S(1)} %turned_filter.4.refs_4_.refs_7_), custom_call_target="tpu_custom_call" | custom-call | flops 1000 | tf_op jit(solution)/shard_map/turned_filter/pallas_call | solution.py:396
  24.5 0.0 collective-permute-done.5.refs_2_.refs_4_
  24.6 1.3 %collective-permute-start.7 = (bf16[128,512]{1,0:T(8,128)(2,1)S(1)}, bf16[128,512]{1,0:T(8,128)(2,1)S(1)}, u32[]{:S(2)}, u32[]{:S(2)}) collective-permute-start(bf16[128,512]{1,0:T(8,128)(2,1)S(1)} %filter.6.refs_6_.refs_5_), channel_id=1, source_target_pairs={{16,0},{17,1},{18,2},{19,3},{20,4},{21,5},{22,6},{23,7},{24,8},{25... | collective-permute-start | bytes 393224 | tf_op jit(solution)/shard_map/ppermute | solution.py:455
  25.9 1.3 %collective-permute-start.8 = (bf16[128,512]{1,0:T(8,128)(2,1)S(1)}, bf16[128,512]{1,0:T(8,128)(2,1)S(1)}, u32[]{:S(2)}, u32[]{:S(2)}) collective-permute-start(bf16[128,512]{1,0:T(8,128)(2,1)S(1)} %filter.7.refs_4_.refs_5_), channel_id=1, source_target_pairs={{16,0},{17,1},{18,2},{19,3},{20,4},{21,5},{22,6},{23,7},{24,8},{25... | collective-permute-start | bytes 393224 | tf_op jit(solution)/shard_map/ppermute | solution.py:455
  27.2 0.5 turned_filter.6.refs_4_.refs_7_
  27.7 0.5 turned_filter.7.refs_6_.refs_7_
  28.3 0.0 collective-permute-done.1.refs_5_
  28.3 2.4 %first_grads.4 = (f32[96,128]{1,0:T(8,128)S(1)}, f32[1,1536]{1,0:T(1,128)S(1)}) custom-call(s32[1]{0:T(128)} %bitcast.refs_0_.role, bf16[128,4096]{1,0:T(8,128)(2,1)S(1)} %bitcast.31, bf16[128,4096]{1,0:T(8,128)(2,1)S(1)} %bitcast.24, bf16[128,4096]{1,0:T(8,128)(2,1)S(1)} %bitcast.40, bf16[128,4096]{1,0:T(8,128)(2,1)S(1)} %collective-permute-done.refs_2_.refs_4_, ...), custom_call_target="tpu_custom_call" | custom-call | flops 2000 | tf_op jit(solution)/shard_map/first_grads/pallas_call | solution.py:476
  30.7 0.0 collective-permute-done.6.refs_6_
  30.7 2.4 %first_grads.5 = (f32[96,128]{1,0:T(8,128)S(1)}, f32[1,1536]{1,0:T(1,128)S(1)}) custom-call(s32[1]{0:T(128)} %bitcast.refs_0_.role, bf16[128,4096]{1,0:T(8,128)(2,1)S(1)} %bitcast.32, bf16[128,4096]{1,0:T(8,128)(2,1)S(1)} %bitcast.25, bf16[128,4096]{1,0:T(8,128)(2,1)S(1)} %bitcast.41, bf16[128,4096]{1,0:T(8,128)(2,1)S(1)} %collective-permute-done.refs_2_.refs_4_, ...), custom_call_target="tpu_custom_call" | custom-call | flops 2000 | tf_op jit(solution)/shard_map/first_grads/pallas_call | solution.py:476
  33.1 0.4 collective-permute-done.7.refs_6_
  33.5 0.8 %first_grads.6 = (f32[32,128]{1,0:T(8,128)S(1)}, f32[1,512]{1,0:T(1,128)S(1)}) custom-call(s32[1]{0:T(128)} %bitcast.refs_0_.role, bf16[128,4096]{1,0:T(8,128)(2,1)S(1)} %bitcast.33, bf16[128,4096]{1,0:T(8,128)(2,1)S(1)} %bitcast.26, bf16[128,4096]{1,0:T(8,128)(2,1)S(1)} %bitcast.42, bf16[128,4096]{1,0:T(8,128)(2,1)S(1)} %collective-permute-done.refs_2_.refs_4_, ...), custom_call_target="tpu_custom_call" | custom-call | flops 2000 | tf_op jit(solution)/shard_map/first_grads/pallas_call | solution.py:476
  34.3 0.7 %collective-permute-done.8.refs_6_ = bf16[128,512]{1,0:T(8,128)(2,1)S(1)} collective-permute-done((bf16[128,512]{1,0:T(8,128)(2,1)S(1)}, bf16[128,512]{1,0:T(8,128)(2,1)S(1)}, u32[]{:S(2)}, u32[]{:S(2)}) %collective-permute-start.8) | collective-permute-done | bytes 131104 | tf_op jit(solution)/shard_map/ppermute | solution.py:455
  35.0 0.8 %first_grads.7 = (f32[32,128]{1,0:T(8,128)S(1)}, f32[1,512]{1,0:T(1,128)S(1)}) custom-call(s32[1]{0:T(128)} %bitcast.refs_0_.role, bf16[128,4096]{1,0:T(8,128)(2,1)S(1)} %bitcast.34, bf16[128,4096]{1,0:T(8,128)(2,1)S(1)} %bitcast.27, bf16[128,4096]{1,0:T(8,128)(2,1)S(1)} %bitcast.43, bf16[128,4096]{1,0:T(8,128)(2,1)S(1)} %collective-permute-done.refs_2_.refs_4_, ...), custom_call_target="tpu_custom_call" | custom-call | flops 2000 | tf_op jit(solution)/shard_map/first_grads/pallas_call | solution.py:476
  35.8 17.6 %all_to_all.5.parts = bf16[16,18,128]{2,1,0:T(8,128)(2,1)S(1)} all-to-all(bf16[16,18,128]{2,1,0:T(8,128)(2,1)S(1)} %pack.1), channel_id=1, replica_groups=mesh['section'=2,'seq'=16] {'seq'}, dimensions={0} | all-to-all | bytes 147456 | tf_op jit(solution)/shard_map/all_to_all | solution.py:499
  53.4 0.7 %step.1 = (f32[1,256]{1,0:T(1,128)}, f32[16,128]{1,0:T(8,128)}) custom-call(s32[1]{0:T(128)} %bitcast.refs_0_.role, bf16[16,18,128]{2,1,0:T(8,128)(2,1)S(1)} %all_to_all.5.parts, f32[1,256]{1,0:T(1,128)S(1)} %get-tuple-element.27.refs_4_.steer_second, f32[16,128]{1,0:T(8,128)S(1)} %get-tuple-element.43.filter_second), custom_call_target="tpu_custom_call" | custom-call | tf_op jit(solution)/shard_map/step/pallas_call | solution.py:500
  (6 shorter events, 0.2 us)
Async XLA Ops:
  0.6 4.2 %copy-start.3 = (bf16[1,128,4096]{2,1,0:T(8,128)(2,1)S(1)}, bf16[1,128,4096]{2,1,0:T(8,128)(2,1)}, u32[]{:S(2)}) copy-start(bf16[1,128,4096]{2,1,0:T(8,128)(2,1)} %param.10) | copy-start | bytes 3145732
  0.7 1.6 %copy-start = (bf16[1,128,4096]{2,1,0:T(8,128)(2,1)S(1)}, bf16[1,128,4096]{2,1,0:T(8,128)(2,1)}, u32[]{:S(2)}) copy-start(bf16[1,128,4096]{2,1,0:T(8,128)(2,1)} %param.9) | copy-start | bytes 3145732
  0.7 8.6 %copy-start.4 = (bf16[1,128,256]{2,1,0:T(8,128)(2,1)S(1)}, bf16[1,128,256]{2,1,0:T(8,128)(2,1)}, u32[]{:S(2)}) copy-start(bf16[1,128,256]{2,1,0:T(8,128)(2,1)} %param.11) | copy-start | bytes 196612
  0.7 8.8 %copy-start.1 = (bf16[128,4096]{1,0:T(8,128)(2,1)S(1)}, bf16[128,4096]{1,0:T(8,128)(2,1)}, u32[]{:S(2)}) copy-start(bf16[128,4096]{1,0:T(8,128)(2,1)} %refs_5_.7) | copy-start | bytes 3145732
  0.8 8.8 %collective-permute-start.2 = (bf16[128,1536]{1,0:T(8,128)(2,1)S(1)}, bf16[128,1536]{1,0:T(8,128)(2,1)S(1)}, u32[]{:S(2)}, u32[]{:S(2)}) collective-permute-start(bf16[128,1536]{1,0:T(8,128)(2,1)S(1)} %direct_weigh.2.refs_1_.refs_3_), channel_id=1, source_target_pairs={{17,16},{18,17},{19,18},{20,19},{21,20},{22,21},{23,22},{24,23},{2... | collective-permute-start | bytes 1179656 | tf_op jit(solution)/shard_map/ppermute | solution.py:421
  1.7 9.5 %collective-permute-start.4 = (bf16[128,1536]{1,0:T(8,128)(2,1)S(1)}, bf16[128,1536]{1,0:T(8,128)(2,1)S(1)}, u32[]{:S(2)}, u32[]{:S(2)}) collective-permute-start(bf16[128,1536]{1,0:T(8,128)(2,1)S(1)} %direct_weigh.3.refs_1_.refs_3_), channel_id=1, source_target_pairs={{17,16},{18,17},{19,18},{20,19},{21,20},{22,21},{23,22},{24,23},{2... | collective-permute-start | bytes 1179656 | tf_op jit(solution)/shard_map/ppermute | solution.py:421
  2.4 18.7 %collective-permute-start = (bf16[128,4096]{1,0:T(8,128)(2,1)S(1)}, bf16[128,4096]{1,0:T(8,128)(2,1)S(1)}, u32[]{:S(2)}, u32[]{:S(2)}) collective-permute-start(bf16[128,4096]{1,0:T(8,128)(2,1)S(1)} %bitcast.11), channel_id=1, source_target_pairs={{0,1},{1,2},{2,3},{3,4},{4,5},{5,6},{6,7},{7,8},{8,9},{9,10},{10,1... | collective-permute-start | bytes 3145736 | tf_op jit(solution)/shard_map/ppermute | solution.py:426
  4.8 23.5 %collective-permute-start.1 = (bf16[128,4096]{1,0:T(8,128)(2,1)S(1)}, bf16[128,4096]{1,0:T(8,128)(2,1)S(1)}, u32[]{:S(2)}, u32[]{:S(2)}) collective-permute-start(bf16[128,4096]{1,0:T(8,128)(2,1)S(1)} %bitcast.35), channel_id=1, source_target_pairs={{0,1},{1,2},{2,3},{3,4},{4,5},{5,6},{6,7},{7,8},{8,9},{9,10},{10,1... | collective-permute-start | bytes 3145736 | tf_op jit(solution)/shard_map/ppermute | solution.py:427
  9.8 11.3 %collective-permute-start.3 = (bf16[128,1536]{1,0:T(8,128)(2,1)S(1)}, bf16[128,1536]{1,0:T(8,128)(2,1)S(1)}, u32[]{:S(2)}, u32[]{:S(2)}) collective-permute-start(bf16[128,1536]{1,0:T(8,128)(2,1)S(1)} %filter.4.refs_6_.refs_5_), channel_id=1, source_target_pairs={{16,0},{17,1},{18,2},{19,3},{20,4},{21,5},{22,6},{23,7},{24,8},{25... | collective-permute-start | bytes 1179656 | tf_op jit(solution)/shard_map/ppermute | solution.py:455
  11.4 1.6 %copy-start.5 = (f32[1,128,16]{1,2,0:T(8,128)S(1)}, f32[1,128,16]{1,2,0:T(8,128)}, u32[]{:S(2)}) copy-start(f32[1,128,16]{1,2,0:T(8,128)} %param.13) | copy-start | bytes 24580
  11.4 19.3 %collective-permute-start.6 = (bf16[128,1536]{1,0:T(8,128)(2,1)S(1)}, bf16[128,1536]{1,0:T(8,128)(2,1)S(1)}, u32[]{:S(2)}, u32[]{:S(2)}) collective-permute-start(bf16[128,1536]{1,0:T(8,128)(2,1)S(1)} %filter.5.refs_6_.refs_0_.refs_5_), channel_id=1, source_target_pairs={{16,0},{17,1},{18,2},{19,3},{20,4},{21,5},{22,6},{23,7},{24,8},{25... | collective-permute-start | bytes 1179656 | tf_op jit(solution)/shard_map/ppermute | solution.py:455
  12.7 1.2 %copy-start.2 = (bf16[1,128,4096]{2,1,0:T(8,128)(2,1)S(1)}, bf16[1,128,4096]{2,1,0:T(8,128)(2,1)}, u32[]{:S(2)}) copy-start(bf16[1,128,4096]{2,1,0:T(8,128)(2,1)} %param.8) | copy-start | bytes 3145732
  13.0 0.7 %copy-start.6 = (f32[1,256]{1,0:T(1,128)S(1)}, f32[1,256]{1,0:T(1,128)}, u32[]{:S(2)}) copy-start(f32[1,256]{1,0:T(1,128)} %steer_second.1) | copy-start | bytes 3076
  14.1 10.4 %collective-permute-start.5 = (bf16[128,1024]{1,0:T(8,128)(2,1)S(1)}, bf16[128,1024]{1,0:T(8,128)(2,1)S(1)}, u32[]{:S(2)}, u32[]{:S(2)}) collective-permute-start(bf16[128,1024]{1,0:T(8,128)(2,1)S(1)} %weigh.1.refs_4_.refs_6_.refs_1_.refs_3_), channel_id=1, source_target_pairs={{17,16},{18,17},{19,18},{20,19},{21,20},{22,21},{23,22},{24,23},{2... | collective-permute-start | bytes 786440 | tf_op jit(solution)/shard_map/ppermute | solution.py:421
  24.6 9.0 %collective-permute-start.7 = (bf16[128,512]{1,0:T(8,128)(2,1)S(1)}, bf16[128,512]{1,0:T(8,128)(2,1)S(1)}, u32[]{:S(2)}, u32[]{:S(2)}) collective-permute-start(bf16[128,512]{1,0:T(8,128)(2,1)S(1)} %filter.6.refs_6_.refs_5_), channel_id=1, source_target_pairs={{16,0},{17,1},{18,2},{19,3},{20,4},{21,5},{22,6},{23,7},{24,8},{25... | collective-permute-start | bytes 393224 | tf_op jit(solution)/shard_map/ppermute | solution.py:455
  25.9 9.1 %collective-permute-start.8 = (bf16[128,512]{1,0:T(8,128)(2,1)S(1)}, bf16[128,512]{1,0:T(8,128)(2,1)S(1)}, u32[]{:S(2)}, u32[]{:S(2)}) collective-permute-start(bf16[128,512]{1,0:T(8,128)(2,1)S(1)} %filter.7.refs_4_.refs_5_), channel_id=1, source_target_pairs={{16,0},{17,1},{18,2},{19,3},{20,4},{21,5},{22,6},{23,7},{24,8},{25... | collective-permute-start | bytes 393224 | tf_op jit(solution)/shard_map/ppermute | solution.py:455

commit v12 on v11

--- a/solution.py
+++ b/solution.py
@@ -11,7 +11,7 @@
 BF16 = jnp.bfloat16
 LANES = 128
 SUB = 32
-CHUNK_EDGES = (0, 3, 6, 7, 8)
+CHUNK_EDGES = (0, 2, 3, 6, 7, 8)
 HALO_EDGES = (0, 3, 6, 8)
 
 
@@ -406,6 +406,7 @@
 
     incoming = [(cotangent, 0)] * len(bounds)
     early, uppers, filtered = [], [], []
+    ready = CHUNK_EDGES.index(HALO_EDGES[-2])
     for hop in range(sections - 1):
         split = [channels * eighths // 8 for eighths in HALO_EDGES] if hop == 0 else edges
         starts, ends = split[:-1], split[1:]
@@ -434,10 +435,11 @@
             at = (first - starts[part]) // block
             array, offset = incoming[k]
             before = tuple(outgoing[-1:])
-            if hop == sections - 2 and k == 2:
-                uppers.append(upper_grad(1, owns[-1:]))
+            if hop == sections - 2 and k == ready:
+                uppers.append(upper_grad(k - 1, owns[-1:]))
                 filtered.append(turned_filter(0, owns[-1:] + received[:1]))
-                filtered.append(turned_filter(1, filtered[-1:]))
+                for early_chunk in range(1, k):
+                    filtered.append(turned_filter(early_chunk, filtered[-1:]))
                 before += (uppers[-1][0], filtered[-1])
             out = call(
                 functools.partial(filter_kernel, group_size),
@@ -453,10 +455,13 @@
             sources.append((owns[part], halos[part], at))
             outgoing.append(out)
             received.append(lax.ppermute(out, "section", down))
-            if hop == sections - 2 and k == 1:
-                uppers = [upper_grad(0, (out,))]
+            if hop == sections - 2 and k == ready - 1:
+                latest = (out,)
+                for early_chunk in range(k):
+                    uppers.append(upper_grad(early_chunk, latest))
+                    latest = uppers[-1][:1]
                 seconds = moments((out,))
-                early = [uppers[0][0], seconds[0]]
+                early = [uppers[-1][0], seconds[0]]
         top = my_section == sections - 1
         incoming = [
             (jnp.where(top, cotangent[:, first:last], arrived), first)

time: 54.5 us -> 54.5 us (level)
  waiting for transfers between devices: 7.41 us -> 5.84 us
  starting transfers between devices: 14.3 us -> 15.6 us
    ppermute x4 -> x5, waiting for transfers between devices: 7.4 us -> 5.82 us  [body(): received.append(lax.ppermute(out, 'section', down))]
    ppermute x4 -> x5, starting transfers between devices: 5.17 us -> 6.45 us  [body(): received.append(lax.ppermute(out, 'section', down))]
    pallas_call x4 -> x5, Pallas kernels: 6.4 us -> 6.38 us  [body(): call(functools.partial(first_grad_kernel, group_size), ((last - first) //...]
    pallas_call x4 -> x5, Pallas kernels: 4.07 us -> 4.06 us  [turned_filter(): call(functools.partial(turned_filter_kernel, group_size), ((last - first)...]
  transfers between devices with their start and end apart: 9 -> 10, of which waited for: 3 -> 4; matrix products, arithmetic and copies ran while one was open for 0% -> 0% of each run, Pallas kernels for 21% -> 21%
where the time goes in v12:
time: 54.5 us; the launch traced here: 54.1 us
  blocking collectives  17.7 us (32%)
  starting transfers between devices  15.6 us (29%)
  Pallas kernels  12.8 us (23%)
  waiting for transfers between devices  5.84 us (11%)
  local copies, waits for them, and re-layouts  1.21 us (2%)
  between operations  1 us (2%)
    all_to_all x1, blocking collectives, body(): parts = lax.all_to_all(packed, 'seq', 0, 0)  17.7 us
    ppermute x5, starting transfers between devices, body(): received.append(lax.ppermute(out, 'section', down))  6.45 us
    pallas_call x5, Pallas kernels, body(): call(functools.partial(first_grad_kernel, group_size), ((last - first) //...  6.38 us
    ppermute x5, waiting for transfers between devices, body(): received.append(lax.ppermute(out, 'section', down))  5.82 us
    ppermute x1, starting transfers between devices, body(): inputs_halo = lax.ppermute(inputs_sent, ('section', 'seq'), ahead)  4.54 us
    pallas_call x5, Pallas kernels, turned_filter(): call(functools.partial(turned_filter_kernel, group_size), ((last - first)...  4.06 us
    ppermute x1, starting transfers between devices, body(): mid_halo = lax.ppermute(mid_sent, ('section', 'seq'), ahead)  2.42 us
    ppermute x3, starting transfers between devices, send_halo(): halos.append(lax.ppermute(owns[-1], ('section', 'seq'), behind))  2.18 us
  transfers between devices with their start and end apart: 10, of which 4 were waited for; matrix products, arithmetic and copies ran while one was open for 0% of the time, Pallas kernels for 21%

profile of v12, /device:TPU:0, one launch (start us, length us, event | category | flops | bytes accessed | tf_op | source)
XLA Modules:
  0.0 54.1 jit_solution(3240326690567582367)
XLA Ops:
  0.6 0.0 copy-start.2
  0.6 0.1 direct_weigh.2.refs_1_.refs_3_
  0.7 0.0 copy-start
  0.7 0.0 copy-start.1
  0.7 0.0 copy-start.4
  0.8 0.8 %collective-permute-start.2 = (bf16[128,1536]{1,0:T(8,128)(2,1)S(1)}, bf16[128,1536]{1,0:T(8,128)(2,1)S(1)}, u32[]{:S(2)}, u32[]{:S(2)}) collective-permute-start(bf16[128,1536]{1,0:T(8,128)(2,1)S(1)} %direct_weigh.2.refs_1_.refs_3_), channel_id=1, source_target_pairs={{17,16},{18,17},{19,18},{20,19},{21,20},{22,21},{23,22},{24,23},{2... | collective-permute-start | bytes 1179656 | tf_op jit(solution)/shard_map/ppermute | solution.py:422
  1.6 0.1 direct_weigh.3.refs_1_.refs_3_
  1.7 0.7 %collective-permute-start.4 = (bf16[128,1536]{1,0:T(8,128)(2,1)S(1)}, bf16[128,1536]{1,0:T(8,128)(2,1)S(1)}, u32[]{:S(2)}, u32[]{:S(2)}) collective-permute-start(bf16[128,1536]{1,0:T(8,128)(2,1)S(1)} %direct_weigh.3.refs_1_.refs_3_), channel_id=1, source_target_pairs={{17,16},{18,17},{19,18},{20,19},{21,20},{22,21},{23,22},{24,23},{2... | collective-permute-start | bytes 1179656 | tf_op jit(solution)/shard_map/ppermute | solution.py:422
  2.3 0.0 copy-done
  2.4 2.4 %collective-permute-start = (bf16[128,4096]{1,0:T(8,128)(2,1)S(1)}, bf16[128,4096]{1,0:T(8,128)(2,1)S(1)}, u32[]{:S(2)}, u32[]{:S(2)}) collective-permute-start(bf16[128,4096]{1,0:T(8,128)(2,1)S(1)} %bitcast.11), channel_id=1, source_target_pairs={{0,1},{1,2},{2,3},{3,4},{4,5},{5,6},{6,7},{7,8},{8,9},{9,10},{10,1... | collective-permute-start | bytes 3145736 | tf_op jit(solution)/shard_map/ppermute | solution.py:427
  4.8 0.0 copy-done.1
  4.8 4.5 %collective-permute-start.1 = (bf16[128,4096]{1,0:T(8,128)(2,1)S(1)}, bf16[128,4096]{1,0:T(8,128)(2,1)S(1)}, u32[]{:S(2)}, u32[]{:S(2)}) collective-permute-start(bf16[128,4096]{1,0:T(8,128)(2,1)S(1)} %bitcast.32), channel_id=1, source_target_pairs={{0,1},{1,2},{2,3},{3,4},{4,5},{5,6},{6,7},{7,8},{8,9},{9,10},{10,1... | collective-permute-start | bytes 3145736 | tf_op jit(solution)/shard_map/ppermute | solution.py:428
  9.3 0.0 copy-done.4
  9.4 0.2 taps.1.refs_3_
  9.5 0.0 collective-permute-done.2.refs_2_.refs_4_
  9.6 0.0 copy-done.2
  9.6 0.2 filter.5.refs_6_.refs_5_
  9.8 1.3 %collective-permute-start.3 = (bf16[128,1024]{1,0:T(8,128)(2,1)S(1)}, bf16[128,1024]{1,0:T(8,128)(2,1)S(1)}, u32[]{:S(2)}, u32[]{:S(2)}) collective-permute-start(bf16[128,1024]{1,0:T(8,128)(2,1)S(1)} %filter.5.refs_6_.refs_5_), channel_id=1, source_target_pairs={{16,0},{17,1},{18,2},{19,3},{20,4},{21,5},{22,6},{23,7},{24,8},{25... | collective-permute-start | bytes 786440 | tf_op jit(solution)/shard_map/ppermute | solution.py:457
  11.1 0.0 collective-permute-done.4.refs_2_.refs_4_
  11.1 0.3 filter.7.refs_6_.refs_0_.refs_5_
  11.4 1.3 %collective-permute-start.7 = (bf16[128,1536]{1,0:T(8,128)(2,1)S(1)}, bf16[128,1536]{1,0:T(8,128)(2,1)S(1)}, u32[]{:S(2)}, u32[]{:S(2)}) collective-permute-start(bf16[128,1536]{1,0:T(8,128)(2,1)S(1)} %filter.7.refs_6_.refs_0_.refs_5_), channel_id=1, source_target_pairs={{16,0},{17,1},{18,2},{19,3},{20,4},{21,5},{22,6},{23,7},{24,8},{25... | collective-permute-start | bytes 1179656 | tf_op jit(solution)/shard_map/ppermute | solution.py:457
  12.7 0.2 upper_grads.5
  12.9 0.0 copy-start.5
  12.9 0.0 copy-start.3
  13.0 0.0 copy-start.6
  13.0 0.6 %copy-done.5 = f32[1,128,16]{1,2,0:T(8,128)S(1)} copy-done((f32[1,128,16]{1,2,0:T(8,128)S(1)}, f32[1,128,16]{1,2,0:T(8,128)}, u32[]{:S(2)}) %copy-start.5) | copy-done | bytes 8216
  13.6 0.1 copy-done.6
  13.7 0.4 copy-done.3
  14.2 0.1 weigh.1.refs_4_.refs_6_.refs_1_.refs_3_
  14.3 0.7 %collective-permute-start.5 = (bf16[128,1024]{1,0:T(8,128)(2,1)S(1)}, bf16[128,1024]{1,0:T(8,128)(2,1)S(1)}, u32[]{:S(2)}, u32[]{:S(2)}) collective-permute-start(bf16[128,1024]{1,0:T(8,128)(2,1)S(1)} %weigh.1.refs_4_.refs_6_.refs_1_.refs_3_), channel_id=1, source_target_pairs={{17,16},{18,17},{19,18},{20,19},{21,20},{22,21},{23,22},{24,23},{2... | collective-permute-start | bytes 786440 | tf_op jit(solution)/shard_map/ppermute | solution.py:422
  15.0 3.7 %collective-permute-done.3.refs_5_.refs_6_ = bf16[128,1024]{1,0:T(8,128)(2,1)S(1)} collective-permute-done((bf16[128,1024]{1,0:T(8,128)(2,1)S(1)}, bf16[128,1024]{1,0:T(8,128)(2,1)S(1)}, u32[]{:S(2)}, u32[]{:S(2)}) %collective-permute-start.3) | collective-permute-done | bytes 262176 | tf_op jit(solution)/shard_map/ppermute | solution.py:457
  18.6 1.3 %collective-permute-start.6 = (bf16[128,512]{1,0:T(8,128)(2,1)S(1)}, bf16[128,512]{1,0:T(8,128)(2,1)S(1)}, u32[]{:S(2)}, u32[]{:S(2)}) collective-permute-start(bf16[128,512]{1,0:T(8,128)(2,1)S(1)} %filter.6.refs_6_.refs_5_), channel_id=1, source_target_pairs={{16,0},{17,1},{18,2},{19,3},{20,4},{21,5},{22,6},{23,7},{24,8},{25... | collective-permute-start | bytes 393224 | tf_op jit(solution)/shard_map/ppermute | solution.py:457
  19.9 0.0 collective-permute-done.refs_2_.refs_4_
  19.9 1.1 %turned_filter.5.refs_4_.refs_7_ = f32[128,1024]{1,0:T(8,128)S(1)} custom-call(s32[1]{0:T(128)} %bitcast.refs_0_.role, bf16[128,4096]{1,0:T(8,128)(2,1)S(1)} %bitcast.17, bf16[128,4096]{1,0:T(8,128)(2,1)S(1)} %collective-permute-done.refs_2_.refs_4_, f32[256,128]{1,0:T(8,128)S(1)} %taps.1.refs_3_, ...), custom_call_target="tpu_custom_call" | custom-call | flops 1000 | tf_op jit(solution)/shard_map/turned_filter/pallas_call | solution.py:396
  21.0 0.5 turned_filter.6.refs_4_.refs_7_
  21.5 0.3 upper_grads.7
  21.8 1.6 %turned_filter.7.refs_8_.refs_7_ = f32[128,1536]{1,0:T(8,128)S(1)} custom-call(s32[1]{0:T(128)} %bitcast.refs_0_.role, bf16[128,4096]{1,0:T(8,128)(2,1)S(1)} %bitcast.20, bf16[128,4096]{1,0:T(8,128)(2,1)S(1)} %collective-permute-done.refs_2_.refs_4_, f32[256,128]{1,0:T(8,128)S(1)} %taps.1.refs_3_, f32[128,512]{1,0:T(8,128)S(1)} %turned_filter.6.refs_4_.refs_7_), custom_call_target="tpu_custom_call" | custom-call | flops 1000 | tf_op jit(solution)/shard_map/turned_filter/pallas_call | solution.py:396
  23.4 0.0 collective-permute-done.5.refs_2_.refs_4_
  23.4 1.3 %collective-permute-start.8 = (bf16[128,512]{1,0:T(8,128)(2,1)S(1)}, bf16[128,512]{1,0:T(8,128)(2,1)S(1)}, u32[]{:S(2)}, u32[]{:S(2)}) collective-permute-start(bf16[128,512]{1,0:T(8,128)(2,1)S(1)} %filter.8.refs_6_.refs_5_), channel_id=1, source_target_pairs={{16,0},{17,1},{18,2},{19,3},{20,4},{21,5},{22,6},{23,7},{24,8},{25... | collective-permute-start | bytes 393224 | tf_op jit(solution)/shard_map/ppermute | solution.py:457
  24.8 1.3 %collective-permute-start.9 = (bf16[128,512]{1,0:T(8,128)(2,1)S(1)}, bf16[128,512]{1,0:T(8,128)(2,1)S(1)}, u32[]{:S(2)}, u32[]{:S(2)}) collective-permute-start(bf16[128,512]{1,0:T(8,128)(2,1)S(1)} %filter.9.refs_4_.refs_5_), channel_id=1, source_target_pairs={{16,0},{17,1},{18,2},{19,3},{20,4},{21,5},{22,6},{23,7},{24,8},{25... | collective-permute-start | bytes 393224 | tf_op jit(solution)/shard_map/ppermute | solution.py:457
  26.1 0.5 turned_filter.8.refs_4_.refs_7_
  26.6 0.5 turned_filter.9.refs_6_.refs_7_
  27.1 0.0 collective-permute-done.1.refs_5_
  27.1 1.6 %first_grads.5 = (f32[64,128]{1,0:T(8,128)S(1)}, f32[1,1024]{1,0:T(1,128)S(1)}) custom-call(s32[1]{0:T(128)} %bitcast.refs_0_.role, bf16[128,4096]{1,0:T(8,128)(2,1)S(1)} %bitcast.46, bf16[128,4096]{1,0:T(8,128)(2,1)S(1)} %bitcast.27, bf16[128,4096]{1,0:T(8,128)(2,1)S(1)} %bitcast.38, bf16[128,4096]{1,0:T(8,128)(2,1)S(1)} %collective-permute-done.refs_2_.refs_4_, ...), custom_call_target="tpu_custom_call" | custom-call | flops 2000 | tf_op jit(solution)/shard_map/first_grads/pallas_call | solution.py:481
  28.8 1.1 %collective-permute-done.6.refs_6_ = bf16[128,512]{1,0:T(8,128)(2,1)S(1)} collective-permute-done((bf16[128,512]{1,0:T(8,128)(2,1)S(1)}, bf16[128,512]{1,0:T(8,128)(2,1)S(1)}, u32[]{:S(2)}, u32[]{:S(2)}) %collective-permute-start.6) | collective-permute-done | bytes 131104 | tf_op jit(solution)/shard_map/ppermute | solution.py:457
  29.9 0.8 %first_grads.6 = (f32[32,128]{1,0:T(8,128)S(1)}, f32[1,512]{1,0:T(1,128)S(1)}) custom-call(s32[1]{0:T(128)} %bitcast.refs_0_.role, bf16[128,4096]{1,0:T(8,128)(2,1)S(1)} %bitcast.47, bf16[128,4096]{1,0:T(8,128)(2,1)S(1)} %bitcast.28, bf16[128,4096]{1,0:T(8,128)(2,1)S(1)} %bitcast.39, bf16[128,4096]{1,0:T(8,128)(2,1)S(1)} %collective-permute-done.refs_2_.refs_4_, ...), custom_call_target="tpu_custom_call" | custom-call | flops 2000 | tf_op jit(solution)/shard_map/first_grads/pallas_call | solution.py:481
  30.7 0.0 collective-permute-done.7.refs_6_
  30.7 2.4 %first_grads.7 = (f32[96,128]{1,0:T(8,128)S(1)}, f32[1,1536]{1,0:T(1,128)S(1)}) custom-call(s32[1]{0:T(128)} %bitcast.refs_0_.role, bf16[128,4096]{1,0:T(8,128)(2,1)S(1)} %bitcast.48, bf16[128,4096]{1,0:T(8,128)(2,1)S(1)} %bitcast.29, bf16[128,4096]{1,0:T(8,128)(2,1)S(1)} %bitcast.40, bf16[128,4096]{1,0:T(8,128)(2,1)S(1)} %collective-permute-done.refs_2_.refs_4_, ...), custom_call_target="tpu_custom_call" | custom-call | flops 2000 | tf_op jit(solution)/shard_map/first_grads/pallas_call | solution.py:481
  33.1 0.3 collective-permute-done.8.refs_6_
  33.5 0.8 %first_grads.8 = (f32[32,128]{1,0:T(8,128)S(1)}, f32[1,512]{1,0:T(1,128)S(1)}) custom-call(s32[1]{0:T(128)} %bitcast.refs_0_.role, bf16[128,4096]{1,0:T(8,128)(2,1)S(1)} %bitcast.49, bf16[128,4096]{1,0:T(8,128)(2,1)S(1)} %bitcast.30, bf16[128,4096]{1,0:T(8,128)(2,1)S(1)} %bitcast.41, bf16[128,4096]{1,0:T(8,128)(2,1)S(1)} %collective-permute-done.refs_2_.refs_4_, ...), custom_call_target="tpu_custom_call" | custom-call | flops 2000 | tf_op jit(solution)/shard_map/first_grads/pallas_call | solution.py:481
  34.2 0.7 %collective-permute-done.9.refs_6_ = bf16[128,512]{1,0:T(8,128)(2,1)S(1)} collective-permute-done((bf16[128,512]{1,0:T(8,128)(2,1)S(1)}, bf16[128,512]{1,0:T(8,128)(2,1)S(1)}, u32[]{:S(2)}, u32[]{:S(2)}) %collective-permute-start.9) | collective-permute-done | bytes 131104 | tf_op jit(solution)/shard_map/ppermute | solution.py:457
  34.9 0.8 %first_grads.9 = (f32[32,128]{1,0:T(8,128)S(1)}, f32[1,512]{1,0:T(1,128)S(1)}) custom-call(s32[1]{0:T(128)} %bitcast.refs_0_.role, bf16[128,4096]{1,0:T(8,128)(2,1)S(1)} %bitcast.50, bf16[128,4096]{1,0:T(8,128)(2,1)S(1)} %bitcast.31, bf16[128,4096]{1,0:T(8,128)(2,1)S(1)} %bitcast.42, bf16[128,4096]{1,0:T(8,128)(2,1)S(1)} %collective-permute-done.refs_2_.refs_4_, ...), custom_call_target="tpu_custom_call" | custom-call | flops 2000 | tf_op jit(solution)/shard_map/first_grads/pallas_call | solution.py:481
  35.7 17.7 %all_to_all.5.parts = bf16[16,18,128]{2,1,0:T(8,128)(2,1)S(1)} all-to-all(bf16[16,18,128]{2,1,0:T(8,128)(2,1)S(1)} %pack.1), channel_id=1, replica_groups=mesh['section'=2,'seq'=16] {'seq'}, dimensions={0} | all-to-all | bytes 147456 | tf_op jit(solution)/shard_map/all_to_all | solution.py:504
  53.4 0.7 %step.1 = (f32[1,256]{1,0:T(1,128)}, f32[16,128]{1,0:T(8,128)}) custom-call(s32[1]{0:T(128)} %bitcast.refs_0_.role, bf16[16,18,128]{2,1,0:T(8,128)(2,1)S(1)} %all_to_all.5.parts, f32[1,256]{1,0:T(1,128)S(1)} %get-tuple-element.32.refs_4_.steer_second, f32[16,128]{1,0:T(8,128)S(1)} %get-tuple-element.51.filter_second), custom_call_target="tpu_custom_call" | custom-call | tf_op jit(solution)/shard_map/step/pallas_call | solution.py:505
  (8 shorter events, 0.3 us)
Async XLA Ops:
  0.6 8.9 %copy-start.2 = (bf16[128,4096]{1,0:T(8,128)(2,1)S(1)}, bf16[128,4096]{1,0:T(8,128)(2,1)}, u32[]{:S(2)}) copy-start(bf16[128,4096]{1,0:T(8,128)(2,1)} %refs_5_.9) | copy-start | bytes 3145732
  0.7 1.6 %copy-start = (bf16[1,128,4096]{2,1,0:T(8,128)(2,1)S(1)}, bf16[1,128,4096]{2,1,0:T(8,128)(2,1)}, u32[]{:S(2)}) copy-start(bf16[1,128,4096]{2,1,0:T(8,128)(2,1)} %param.9) | copy-start | bytes 3145732
  0.7 4.1 %copy-start.1 = (bf16[1,128,4096]{2,1,0:T(8,128)(2,1)S(1)}, bf16[1,128,4096]{2,1,0:T(8,128)(2,1)}, u32[]{:S(2)}) copy-start(bf16[1,128,4096]{2,1,0:T(8,128)(2,1)} %param.10) | copy-start | bytes 3145732
  0.7 8.6 %copy-start.4 = (bf16[1,128,256]{2,1,0:T(8,128)(2,1)S(1)}, bf16[1,128,256]{2,1,0:T(8,128)(2,1)}, u32[]{:S(2)}) copy-start(bf16[1,128,256]{2,1,0:T(8,128)(2,1)} %param.11) | copy-start | bytes 196612
  0.8 8.8 %collective-permute-start.2 = (bf16[128,1536]{1,0:T(8,128)(2,1)S(1)}, bf16[128,1536]{1,0:T(8,128)(2,1)S(1)}, u32[]{:S(2)}, u32[]{:S(2)}) collective-permute-start(bf16[128,1536]{1,0:T(8,128)(2,1)S(1)} %direct_weigh.2.refs_1_.refs_3_), channel_id=1, source_target_pairs={{17,16},{18,17},{19,18},{20,19},{21,20},{22,21},{23,22},{24,23},{2... | collective-permute-start | bytes 1179656 | tf_op jit(solution)/shard_map/ppermute | solution.py:422
  1.7 9.5 %collective-permute-start.4 = (bf16[128,1536]{1,0:T(8,128)(2,1)S(1)}, bf16[128,1536]{1,0:T(8,128)(2,1)S(1)}, u32[]{:S(2)}, u32[]{:S(2)}) collective-permute-start(bf16[128,1536]{1,0:T(8,128)(2,1)S(1)} %direct_weigh.3.refs_1_.refs_3_), channel_id=1, source_target_pairs={{17,16},{18,17},{19,18},{20,19},{21,20},{22,21},{23,22},{24,23},{2... | collective-permute-start | bytes 1179656 | tf_op jit(solution)/shard_map/ppermute | solution.py:422
  2.4 17.6 %collective-permute-start = (bf16[128,4096]{1,0:T(8,128)(2,1)S(1)}, bf16[128,4096]{1,0:T(8,128)(2,1)S(1)}, u32[]{:S(2)}, u32[]{:S(2)}) collective-permute-start(bf16[128,4096]{1,0:T(8,128)(2,1)S(1)} %bitcast.11), channel_id=1, source_target_pairs={{0,1},{1,2},{2,3},{3,4},{4,5},{5,6},{6,7},{7,8},{8,9},{9,10},{10,1... | collective-permute-start | bytes 3145736 | tf_op jit(solution)/shard_map/ppermute | solution.py:427
  4.8 22.3 %collective-permute-start.1 = (bf16[128,4096]{1,0:T(8,128)(2,1)S(1)}, bf16[128,4096]{1,0:T(8,128)(2,1)S(1)}, u32[]{:S(2)}, u32[]{:S(2)}) collective-permute-start(bf16[128,4096]{1,0:T(8,128)(2,1)S(1)} %bitcast.32), channel_id=1, source_target_pairs={{0,1},{1,2},{2,3},{3,4},{4,5},{5,6},{6,7},{7,8},{8,9},{9,10},{10,1... | collective-permute-start | bytes 3145736 | tf_op jit(solution)/shard_map/ppermute | solution.py:428
  9.8 8.9 %collective-permute-start.3 = (bf16[128,1024]{1,0:T(8,128)(2,1)S(1)}, bf16[128,1024]{1,0:T(8,128)(2,1)S(1)}, u32[]{:S(2)}, u32[]{:S(2)}) collective-permute-start(bf16[128,1024]{1,0:T(8,128)(2,1)S(1)} %filter.5.refs_6_.refs_5_), channel_id=1, source_target_pairs={{16,0},{17,1},{18,2},{19,3},{20,4},{21,5},{22,6},{23,7},{24,8},{25... | collective-permute-start | bytes 786440 | tf_op jit(solution)/shard_map/ppermute | solution.py:457
  11.4 19.3 %collective-permute-start.7 = (bf16[128,1536]{1,0:T(8,128)(2,1)S(1)}, bf16[128,1536]{1,0:T(8,128)(2,1)S(1)}, u32[]{:S(2)}, u32[]{:S(2)}) collective-permute-start(bf16[128,1536]{1,0:T(8,128)(2,1)S(1)} %filter.7.refs_6_.refs_0_.refs_5_), channel_id=1, source_target_pairs={{16,0},{17,1},{18,2},{19,3},{20,4},{21,5},{22,6},{23,7},{24,8},{25... | collective-permute-start | bytes 1179656 | tf_op jit(solution)/shard_map/ppermute | solution.py:457
  12.9 0.7 %copy-start.5 = (f32[1,128,16]{1,2,0:T(8,128)S(1)}, f32[1,128,16]{1,2,0:T(8,128)}, u32[]{:S(2)}) copy-start(f32[1,128,16]{1,2,0:T(8,128)} %param.13) | copy-start | bytes 24580
  12.9 1.2 %copy-start.3 = (bf16[1,128,4096]{2,1,0:T(8,128)(2,1)S(1)}, bf16[1,128,4096]{2,1,0:T(8,128)(2,1)}, u32[]{:S(2)}) copy-start(bf16[1,128,4096]{2,1,0:T(8,128)(2,1)} %param.8) | copy-start | bytes 3145732
  13.0 0.8 %copy-start.6 = (f32[1,256]{1,0:T(1,128)S(1)}, f32[1,256]{1,0:T(1,128)}, u32[]{:S(2)}) copy-start(f32[1,256]{1,0:T(1,128)} %steer_second.1) | copy-start | bytes 3076
  14.3 9.1 %collective-permute-start.5 = (bf16[128,1024]{1,0:T(8,128)(2,1)S(1)}, bf16[128,1024]{1,0:T(8,128)(2,1)S(1)}, u32[]{:S(2)}, u32[]{:S(2)}) collective-permute-start(bf16[128,1024]{1,0:T(8,128)(2,1)S(1)} %weigh.1.refs_4_.refs_6_.refs_1_.refs_3_), channel_id=1, source_target_pairs={{17,16},{18,17},{19,18},{20,19},{21,20},{22,21},{23,22},{24,23},{2... | collective-permute-start | bytes 786440 | tf_op jit(solution)/shard_map/ppermute | solution.py:422
  18.6 11.3 %collective-permute-start.6 = (bf16[128,512]{1,0:T(8,128)(2,1)S(1)}, bf16[128,512]{1,0:T(8,128)(2,1)S(1)}, u32[]{:S(2)}, u32[]{:S(2)}) collective-permute-start(bf16[128,512]{1,0:T(8,128)(2,1)S(1)} %filter.6.refs_6_.refs_5_), channel_id=1, source_target_pairs={{16,0},{17,1},{18,2},{19,3},{20,4},{21,5},{22,6},{23,7},{24,8},{25... | collective-permute-start | bytes 393224 | tf_op jit(solution)/shard_map/ppermute | solution.py:457
  23.4 10.0 %collective-permute-start.8 = (bf16[128,512]{1,0:T(8,128)(2,1)S(1)}, bf16[128,512]{1,0:T(8,128)(2,1)S(1)}, u32[]{:S(2)}, u32[]{:S(2)}) collective-permute-start(bf16[128,512]{1,0:T(8,128)(2,1)S(1)} %filter.8.refs_6_.refs_5_), channel_id=1, source_target_pairs={{16,0},{17,1},{18,2},{19,3},{20,4},{21,5},{22,6},{23,7},{24,8},{25... | collective-permute-start | bytes 393224 | tf_op jit(solution)/shard_map/ppermute | solution.py:457
  24.8 10.1 %collective-permute-start.9 = (bf16[128,512]{1,0:T(8,128)(2,1)S(1)}, bf16[128,512]{1,0:T(8,128)(2,1)S(1)}, u32[]{:S(2)}, u32[]{:S(2)}) collective-permute-start(bf16[128,512]{1,0:T(8,128)(2,1)S(1)} %filter.9.refs_4_.refs_5_), channel_id=1, source_target_pairs={{16,0},{17,1},{18,2},{19,3},{20,4},{21,5},{22,6},{23,7},{24,8},{25... | collective-permute-start | bytes 393224 | tf_op jit(solution)/shard_map/ppermute | solution.py:457

commit v13 on v11

--- a/solution.py
+++ b/solution.py
@@ -96,24 +96,25 @@
         out[...] = times(gate[...], incoming[...])
 
 
-def direct_weigh_kernel(first, block, role, gate, incoming, out, gate_part, incoming_part, sems):
-    @pl.when(jnp.logical_not(first_section(role)))
-    def _():
-        tiles = [pl.ds(at, block) for at in range(0, out.shape[1], block)]
+def direct_weigh_kernel(first, role, gate, incoming, out, gate_part, incoming_part, sems):
+    @pl.when(role[0] == 0)
+    def _():
+        cols = pl.ds(first, out.shape[1])
+        pieces = [pl.ds(at, SUB) for at in range(0, out.shape[0], SUB)]
         copies = [
             [
-                pltpu.make_async_copy(source.at[:, pl.ds(first + i * block, block)], part.at[:, t], sems.at[which, i])
+                pltpu.make_async_copy(source.at[piece, cols], part.at[piece, :], sems.at[which, i])
                 for which, (source, part) in enumerate(((gate, gate_part), (incoming, incoming_part)))
             ]
-            for i, t in enumerate(tiles)
+            for i, piece in enumerate(pieces)
         ]
         for pair in copies:
             for copy in pair:
                 copy.start()
-        for t, pair in zip(tiles, copies):
+        for piece, pair in zip(pieces, copies):
             for copy in pair:
                 copy.wait()
-            out[:, t] = times(gate_part[:, t], incoming_part[:, t])
+            out[piece, :] = times(gate_part[piece, :], incoming_part[piece, :])
 
 
 def moments_kernel(role, steer_second, filter_second, *refs):
@@ -331,14 +332,14 @@
         part = pltpu.VMEM((rows, width), BF16)
 
         def kernel(*refs):
-            direct_weigh_kernel(first, block, *refs[:3], *refs[3 + len(after) :])
+            direct_weigh_kernel(first, *refs[:3], *refs[3 + len(after) :])
 
         return pl.pallas_call(
             kernel,
             in_specs=[SMEM] + [ANY] * (2 + len(after)),
             out_specs=pl.BlockSpec(memory_space=pltpu.VMEM),
             out_shape=bf16(width),
-            scratch_shapes=[part, part, pltpu.SemaphoreType.DMA((2, width // block))],
+            scratch_shapes=[part, part, pltpu.SemaphoreType.DMA((2, rows // SUB))],
             compiler_params=SMALL,
             name="direct_weigh",
         )(role, *[pltpu.with_memory_space_constraint(a, pltpu.HBM) for a in (in_gate, cotangent)], *after)

time: 54.5 us -> 54.6 us (level)
  no operation moved by 1% of the time
where the time goes in v13:
time: 54.6 us; the launch traced here: 54.1 us
  blocking collectives  17.5 us (32%)
  starting transfers between devices  14.3 us (26%)
  Pallas kernels  12.9 us (24%)
  waiting for transfers between devices  7.44 us (14%)
  local copies, waits for them, and re-layouts  0.96 us (2%)
  between operations  0.96 us (2%)
    all_to_all x1, blocking collectives, body(): parts = lax.all_to_all(packed, 'seq', 0, 0)  17.5 us
    ppermute x4, waiting for transfers between devices, body(): received.append(lax.ppermute(out, 'section', down))  7.43 us
    pallas_call x4, Pallas kernels, body(): call(functools.partial(first_grad_kernel, group_size), ((last - first) //...  6.4 us
    ppermute x4, starting transfers between devices, body(): received.append(lax.ppermute(out, 'section', down))  5.17 us
    ppermute x1, starting transfers between devices, body(): inputs_halo = lax.ppermute(inputs_sent, ('section', 'seq'), ahead)  4.54 us
    pallas_call x4, Pallas kernels, turned_filter(): call(functools.partial(turned_filter_kernel, group_size), ((last - first)...  4.07 us
    ppermute x1, starting transfers between devices, body(): mid_halo = lax.ppermute(mid_sent, ('section', 'seq'), ahead)  2.42 us
    ppermute x3, starting transfers between devices, send_halo(): halos.append(lax.ppermute(owns[-1], ('section', 'seq'), behind))  2.18 us
  transfers between devices with their start and end apart: 9, of which 3 were waited for; matrix products, arithmetic and copies ran while one was open for 0% of the time, Pallas kernels for 21%

profile of v13, /device:TPU:0, one launch (start us, length us, event | category | flops | bytes accessed | tf_op | source)
XLA Modules:
  0.0 54.1 jit_solution(2934047464326103087)
XLA Ops:
  0.6 0.0 copy-start.3
  0.6 0.1 direct_weigh.2.refs_1_.refs_3_
  0.7 0.0 copy-start
  0.7 0.0 copy-start.4
  0.8 0.0 copy-start.1
  0.8 0.8 %collective-permute-start.2 = (bf16[128,1536]{1,0:T(8,128)(2,1)S(1)}, bf16[128,1536]{1,0:T(8,128)(2,1)S(1)}, u32[]{:S(2)}, u32[]{:S(2)}) collective-permute-start(bf16[128,1536]{1,0:T(8,128)(2,1)S(1)} %direct_weigh.2.refs_1_.refs_3_), channel_id=1, source_target_pairs={{17,16},{18,17},{19,18},{20,19},{21,20},{22,21},{23,22},{24,23},{2... | collective-permute-start | bytes 1179656 | tf_op jit(solution)/shard_map/ppermute | solution.py:422
  1.6 0.1 direct_weigh.3.refs_1_.refs_3_
  1.7 0.7 %collective-permute-start.4 = (bf16[128,1536]{1,0:T(8,128)(2,1)S(1)}, bf16[128,1536]{1,0:T(8,128)(2,1)S(1)}, u32[]{:S(2)}, u32[]{:S(2)}) collective-permute-start(bf16[128,1536]{1,0:T(8,128)(2,1)S(1)} %direct_weigh.3.refs_1_.refs_3_), channel_id=1, source_target_pairs={{17,16},{18,17},{19,18},{20,19},{21,20},{22,21},{23,22},{24,23},{2... | collective-permute-start | bytes 1179656 | tf_op jit(solution)/shard_map/ppermute | solution.py:422
  2.4 0.0 copy-done
  2.4 2.4 %collective-permute-start = (bf16[128,4096]{1,0:T(8,128)(2,1)S(1)}, bf16[128,4096]{1,0:T(8,128)(2,1)S(1)}, u32[]{:S(2)}, u32[]{:S(2)}) collective-permute-start(bf16[128,4096]{1,0:T(8,128)(2,1)S(1)} %bitcast.11), channel_id=1, source_target_pairs={{0,1},{1,2},{2,3},{3,4},{4,5},{5,6},{6,7},{7,8},{8,9},{9,10},{10,1... | collective-permute-start | bytes 3145736 | tf_op jit(solution)/shard_map/ppermute | solution.py:427
  4.8 0.0 copy-done.3
  4.8 4.5 %collective-permute-start.1 = (bf16[128,4096]{1,0:T(8,128)(2,1)S(1)}, bf16[128,4096]{1,0:T(8,128)(2,1)S(1)}, u32[]{:S(2)}, u32[]{:S(2)}) collective-permute-start(bf16[128,4096]{1,0:T(8,128)(2,1)S(1)} %bitcast.35), channel_id=1, source_target_pairs={{0,1},{1,2},{2,3},{3,4},{4,5},{5,6},{6,7},{7,8},{8,9},{9,10},{10,1... | collective-permute-start | bytes 3145736 | tf_op jit(solution)/shard_map/ppermute | solution.py:428
  9.4 0.0 copy-done.4
  9.4 0.2 taps.1.refs_3_
  9.6 0.0 collective-permute-done.2.refs_2_.refs_4_
  9.6 0.0 copy-done.1
  9.6 0.3 filter.4.refs_6_.refs_5_
  9.9 1.3 %collective-permute-start.3 = (bf16[128,1536]{1,0:T(8,128)(2,1)S(1)}, bf16[128,1536]{1,0:T(8,128)(2,1)S(1)}, u32[]{:S(2)}, u32[]{:S(2)}) collective-permute-start(bf16[128,1536]{1,0:T(8,128)(2,1)S(1)} %filter.4.refs_6_.refs_5_), channel_id=1, source_target_pairs={{16,0},{17,1},{18,2},{19,3},{20,4},{21,5},{22,6},{23,7},{24,8},{25... | collective-permute-start | bytes 1179656 | tf_op jit(solution)/shard_map/ppermute | solution.py:456
  11.2 0.0 collective-permute-done.4.refs_2_.refs_4_
  11.2 0.3 filter.5.refs_6_.refs_0_.refs_5_
  11.5 0.0 copy-start.5
  11.5 1.3 %collective-permute-start.6 = (bf16[128,1536]{1,0:T(8,128)(2,1)S(1)}, bf16[128,1536]{1,0:T(8,128)(2,1)S(1)}, u32[]{:S(2)}, u32[]{:S(2)}) collective-permute-start(bf16[128,1536]{1,0:T(8,128)(2,1)S(1)} %filter.5.refs_6_.refs_0_.refs_5_), channel_id=1, source_target_pairs={{16,0},{17,1},{18,2},{19,3},{20,4},{21,5},{22,6},{23,7},{24,8},{25... | collective-permute-start | bytes 1179656 | tf_op jit(solution)/shard_map/ppermute | solution.py:456
  12.8 0.0 copy-start.2
  12.8 0.3 upper_grads.4
  13.0 0.0 copy-start.6
  13.1 0.0 copy-done.5
  13.1 0.7 %copy-done.6 = f32[1,256]{1,0:T(1,128)S(1)} copy-done((f32[1,256]{1,0:T(1,128)S(1)}, f32[1,256]{1,0:T(1,128)}, u32[]{:S(2)}) %copy-start.6) | copy-done | bytes 1048
  13.8 0.2 copy-done.2
  14.0 0.1 weigh.1.refs_4_.refs_6_.refs_1_.refs_3_
  14.1 0.7 %collective-permute-start.5 = (bf16[128,1024]{1,0:T(8,128)(2,1)S(1)}, bf16[128,1024]{1,0:T(8,128)(2,1)S(1)}, u32[]{:S(2)}, u32[]{:S(2)}) collective-permute-start(bf16[128,1024]{1,0:T(8,128)(2,1)S(1)} %weigh.1.refs_4_.refs_6_.refs_1_.refs_3_), channel_id=1, source_target_pairs={{17,16},{18,17},{19,18},{20,19},{21,20},{22,21},{23,22},{24,23},{2... | collective-permute-start | bytes 786440 | tf_op jit(solution)/shard_map/ppermute | solution.py:422
  14.8 6.3 %collective-permute-done.3.refs_5_.refs_6_ = bf16[128,1536]{1,0:T(8,128)(2,1)S(1)} collective-permute-done((bf16[128,1536]{1,0:T(8,128)(2,1)S(1)}, bf16[128,1536]{1,0:T(8,128)(2,1)S(1)}, u32[]{:S(2)}, u32[]{:S(2)}) %collective-permute-start.3) | collective-permute-done | bytes 393248 | tf_op jit(solution)/shard_map/ppermute | solution.py:456
  21.1 0.0 collective-permute-done.refs_2_.refs_4_
  21.1 1.5 %turned_filter.4.refs_4_.refs_7_ = f32[128,1536]{1,0:T(8,128)S(1)} custom-call(s32[1]{0:T(128)} %bitcast.refs_0_.role, bf16[128,4096]{1,0:T(8,128)(2,1)S(1)} %bitcast.15, bf16[128,4096]{1,0:T(8,128)(2,1)S(1)} %collective-permute-done.refs_2_.refs_4_, f32[256,128]{1,0:T(8,128)S(1)} %taps.1.refs_3_, ...), custom_call_target="tpu_custom_call" | custom-call | flops 1000 | tf_op jit(solution)/shard_map/turned_filter/pallas_call | solution.py:397
  22.7 0.3 upper_grads.5
  23.0 1.6 %turned_filter.5.refs_8_.refs_7_ = f32[128,1536]{1,0:T(8,128)S(1)} custom-call(s32[1]{0:T(128)} %bitcast.refs_0_.role, bf16[128,4096]{1,0:T(8,128)(2,1)S(1)} %bitcast.17, bf16[128,4096]{1,0:T(8,128)(2,1)S(1)} %collective-permute-done.refs_2_.refs_4_, f32[256,128]{1,0:T(8,128)S(1)} %taps.1.refs_3_, f32[128,1536]{1,0:T(8,128)S(1)} %turned_filter.4.refs_4_.refs_7_), custom_call_target="tpu_custom_call" | custom-call | flops 1000 | tf_op jit(solution)/shard_map/turned_filter/pallas_call | solution.py:397
  24.6 0.0 collective-permute-done.5.refs_2_.refs_4_
  24.6 1.3 %collective-permute-start.7 = (bf16[128,512]{1,0:T(8,128)(2,1)S(1)}, bf16[128,512]{1,0:T(8,128)(2,1)S(1)}, u32[]{:S(2)}, u32[]{:S(2)}) collective-permute-start(bf16[128,512]{1,0:T(8,128)(2,1)S(1)} %filter.6.refs_6_.refs_5_), channel_id=1, source_target_pairs={{16,0},{17,1},{18,2},{19,3},{20,4},{21,5},{22,6},{23,7},{24,8},{25... | collective-permute-start | bytes 393224 | tf_op jit(solution)/shard_map/ppermute | solution.py:456
  26.0 1.3 %collective-permute-start.8 = (bf16[128,512]{1,0:T(8,128)(2,1)S(1)}, bf16[128,512]{1,0:T(8,128)(2,1)S(1)}, u32[]{:S(2)}, u32[]{:S(2)}) collective-permute-start(bf16[128,512]{1,0:T(8,128)(2,1)S(1)} %filter.7.refs_4_.refs_5_), channel_id=1, source_target_pairs={{16,0},{17,1},{18,2},{19,3},{20,4},{21,5},{22,6},{23,7},{24,8},{25... | collective-permute-start | bytes 393224 | tf_op jit(solution)/shard_map/ppermute | solution.py:456
  27.3 0.5 turned_filter.6.refs_4_.refs_7_
  27.7 0.5 turned_filter.7.refs_6_.refs_7_
  28.3 0.0 collective-permute-done.1.refs_5_
  28.3 2.4 %first_grads.4 = (f32[96,128]{1,0:T(8,128)S(1)}, f32[1,1536]{1,0:T(1,128)S(1)}) custom-call(s32[1]{0:T(128)} %bitcast.refs_0_.role, bf16[128,4096]{1,0:T(8,128)(2,1)S(1)} %bitcast.31, bf16[128,4096]{1,0:T(8,128)(2,1)S(1)} %bitcast.24, bf16[128,4096]{1,0:T(8,128)(2,1)S(1)} %bitcast.40, bf16[128,4096]{1,0:T(8,128)(2,1)S(1)} %collective-permute-done.refs_2_.refs_4_, ...), custom_call_target="tpu_custom_call" | custom-call | flops 2000 | tf_op jit(solution)/shard_map/first_grads/pallas_call | solution.py:477
  30.8 0.0 collective-permute-done.6.refs_6_
  30.8 2.4 %first_grads.5 = (f32[96,128]{1,0:T(8,128)S(1)}, f32[1,1536]{1,0:T(1,128)S(1)}) custom-call(s32[1]{0:T(128)} %bitcast.refs_0_.role, bf16[128,4096]{1,0:T(8,128)(2,1)S(1)} %bitcast.32, bf16[128,4096]{1,0:T(8,128)(2,1)S(1)} %bitcast.25, bf16[128,4096]{1,0:T(8,128)(2,1)S(1)} %bitcast.41, bf16[128,4096]{1,0:T(8,128)(2,1)S(1)} %collective-permute-done.refs_2_.refs_4_, ...), custom_call_target="tpu_custom_call" | custom-call | flops 2000 | tf_op jit(solution)/shard_map/first_grads/pallas_call | solution.py:477
  33.2 0.4 collective-permute-done.7.refs_6_
  33.6 0.8 %first_grads.6 = (f32[32,128]{1,0:T(8,128)S(1)}, f32[1,512]{1,0:T(1,128)S(1)}) custom-call(s32[1]{0:T(128)} %bitcast.refs_0_.role, bf16[128,4096]{1,0:T(8,128)(2,1)S(1)} %bitcast.33, bf16[128,4096]{1,0:T(8,128)(2,1)S(1)} %bitcast.26, bf16[128,4096]{1,0:T(8,128)(2,1)S(1)} %bitcast.42, bf16[128,4096]{1,0:T(8,128)(2,1)S(1)} %collective-permute-done.refs_2_.refs_4_, ...), custom_call_target="tpu_custom_call" | custom-call | flops 2000 | tf_op jit(solution)/shard_map/first_grads/pallas_call | solution.py:477
  34.4 0.7 %collective-permute-done.8.refs_6_ = bf16[128,512]{1,0:T(8,128)(2,1)S(1)} collective-permute-done((bf16[128,512]{1,0:T(8,128)(2,1)S(1)}, bf16[128,512]{1,0:T(8,128)(2,1)S(1)}, u32[]{:S(2)}, u32[]{:S(2)}) %collective-permute-start.8) | collective-permute-done | bytes 131104 | tf_op jit(solution)/shard_map/ppermute | solution.py:456
  35.1 0.8 %first_grads.7 = (f32[32,128]{1,0:T(8,128)S(1)}, f32[1,512]{1,0:T(1,128)S(1)}) custom-call(s32[1]{0:T(128)} %bitcast.refs_0_.role, bf16[128,4096]{1,0:T(8,128)(2,1)S(1)} %bitcast.34, bf16[128,4096]{1,0:T(8,128)(2,1)S(1)} %bitcast.27, bf16[128,4096]{1,0:T(8,128)(2,1)S(1)} %bitcast.43, bf16[128,4096]{1,0:T(8,128)(2,1)S(1)} %collective-permute-done.refs_2_.refs_4_, ...), custom_call_target="tpu_custom_call" | custom-call | flops 2000 | tf_op jit(solution)/shard_map/first_grads/pallas_call | solution.py:477
  35.9 17.5 %all_to_all.5.parts = bf16[16,18,128]{2,1,0:T(8,128)(2,1)S(1)} all-to-all(bf16[16,18,128]{2,1,0:T(8,128)(2,1)S(1)} %pack.1), channel_id=1, replica_groups=mesh['section'=2,'seq'=16] {'seq'}, dimensions={0} | all-to-all | bytes 147456 | tf_op jit(solution)/shard_map/all_to_all | solution.py:500
  53.4 0.7 %step.1 = (f32[1,256]{1,0:T(1,128)}, f32[16,128]{1,0:T(8,128)}) custom-call(s32[1]{0:T(128)} %bitcast.refs_0_.role, bf16[16,18,128]{2,1,0:T(8,128)(2,1)S(1)} %all_to_all.5.parts, f32[1,256]{1,0:T(1,128)S(1)} %get-tuple-element.27.refs_4_.steer_second, f32[16,128]{1,0:T(8,128)S(1)} %get-tuple-element.43.filter_second), custom_call_target="tpu_custom_call" | custom-call | tf_op jit(solution)/shard_map/step/pallas_call | solution.py:501
  (6 shorter events, 0.2 us)
Async XLA Ops:
  0.6 4.2 %copy-start.3 = (bf16[1,128,4096]{2,1,0:T(8,128)(2,1)S(1)}, bf16[1,128,4096]{2,1,0:T(8,128)(2,1)}, u32[]{:S(2)}) copy-start(bf16[1,128,4096]{2,1,0:T(8,128)(2,1)} %param.10) | copy-start | bytes 3145732
  0.7 1.6 %copy-start = (bf16[1,128,4096]{2,1,0:T(8,128)(2,1)S(1)}, bf16[1,128,4096]{2,1,0:T(8,128)(2,1)}, u32[]{:S(2)}) copy-start(bf16[1,128,4096]{2,1,0:T(8,128)(2,1)} %param.9) | copy-start | bytes 3145732
  0.7 8.6 %copy-start.4 = (bf16[1,128,256]{2,1,0:T(8,128)(2,1)S(1)}, bf16[1,128,256]{2,1,0:T(8,128)(2,1)}, u32[]{:S(2)}) copy-start(bf16[1,128,256]{2,1,0:T(8,128)(2,1)} %param.11) | copy-start | bytes 196612
  0.8 8.8 %copy-start.1 = (bf16[128,4096]{1,0:T(8,128)(2,1)S(1)}, bf16[128,4096]{1,0:T(8,128)(2,1)}, u32[]{:S(2)}) copy-start(bf16[128,4096]{1,0:T(8,128)(2,1)} %refs_5_.7) | copy-start | bytes 3145732
  0.8 8.8 %collective-permute-start.2 = (bf16[128,1536]{1,0:T(8,128)(2,1)S(1)}, bf16[128,1536]{1,0:T(8,128)(2,1)S(1)}, u32[]{:S(2)}, u32[]{:S(2)}) collective-permute-start(bf16[128,1536]{1,0:T(8,128)(2,1)S(1)} %direct_weigh.2.refs_1_.refs_3_), channel_id=1, source_target_pairs={{17,16},{18,17},{19,18},{20,19},{21,20},{22,21},{23,22},{24,23},{2... | collective-permute-start | bytes 1179656 | tf_op jit(solution)/shard_map/ppermute | solution.py:422
  1.7 9.5 %collective-permute-start.4 = (bf16[128,1536]{1,0:T(8,128)(2,1)S(1)}, bf16[128,1536]{1,0:T(8,128)(2,1)S(1)}, u32[]{:S(2)}, u32[]{:S(2)}) collective-permute-start(bf16[128,1536]{1,0:T(8,128)(2,1)S(1)} %direct_weigh.3.refs_1_.refs_3_), channel_id=1, source_target_pairs={{17,16},{18,17},{19,18},{20,19},{21,20},{22,21},{23,22},{24,23},{2... | collective-permute-start | bytes 1179656 | tf_op jit(solution)/shard_map/ppermute | solution.py:422
  2.4 18.7 %collective-permute-start = (bf16[128,4096]{1,0:T(8,128)(2,1)S(1)}, bf16[128,4096]{1,0:T(8,128)(2,1)S(1)}, u32[]{:S(2)}, u32[]{:S(2)}) collective-permute-start(bf16[128,4096]{1,0:T(8,128)(2,1)S(1)} %bitcast.11), channel_id=1, source_target_pairs={{0,1},{1,2},{2,3},{3,4},{4,5},{5,6},{6,7},{7,8},{8,9},{9,10},{10,1... | collective-permute-start | bytes 3145736 | tf_op jit(solution)/shard_map/ppermute | solution.py:427
  4.8 23.5 %collective-permute-start.1 = (bf16[128,4096]{1,0:T(8,128)(2,1)S(1)}, bf16[128,4096]{1,0:T(8,128)(2,1)S(1)}, u32[]{:S(2)}, u32[]{:S(2)}) collective-permute-start(bf16[128,4096]{1,0:T(8,128)(2,1)S(1)} %bitcast.35), channel_id=1, source_target_pairs={{0,1},{1,2},{2,3},{3,4},{4,5},{5,6},{6,7},{7,8},{8,9},{9,10},{10,1... | collective-permute-start | bytes 3145736 | tf_op jit(solution)/shard_map/ppermute | solution.py:428
  9.9 11.3 %collective-permute-start.3 = (bf16[128,1536]{1,0:T(8,128)(2,1)S(1)}, bf16[128,1536]{1,0:T(8,128)(2,1)S(1)}, u32[]{:S(2)}, u32[]{:S(2)}) collective-permute-start(bf16[128,1536]{1,0:T(8,128)(2,1)S(1)} %filter.4.refs_6_.refs_5_), channel_id=1, source_target_pairs={{16,0},{17,1},{18,2},{19,3},{20,4},{21,5},{22,6},{23,7},{24,8},{25... | collective-permute-start | bytes 1179656 | tf_op jit(solution)/shard_map/ppermute | solution.py:456
  11.5 1.6 %copy-start.5 = (f32[1,128,16]{1,2,0:T(8,128)S(1)}, f32[1,128,16]{1,2,0:T(8,128)}, u32[]{:S(2)}) copy-start(f32[1,128,16]{1,2,0:T(8,128)} %param.13) | copy-start | bytes 24580
  11.5 19.3 %collective-permute-start.6 = (bf16[128,1536]{1,0:T(8,128)(2,1)S(1)}, bf16[128,1536]{1,0:T(8,128)(2,1)S(1)}, u32[]{:S(2)}, u32[]{:S(2)}) collective-permute-start(bf16[128,1536]{1,0:T(8,128)(2,1)S(1)} %filter.5.refs_6_.refs_0_.refs_5_), channel_id=1, source_target_pairs={{16,0},{17,1},{18,2},{19,3},{20,4},{21,5},{22,6},{23,7},{24,8},{25... | collective-permute-start | bytes 1179656 | tf_op jit(solution)/shard_map/ppermute | solution.py:456
  12.8 1.2 %copy-start.2 = (bf16[1,128,4096]{2,1,0:T(8,128)(2,1)S(1)}, bf16[1,128,4096]{2,1,0:T(8,128)(2,1)}, u32[]{:S(2)}) copy-start(bf16[1,128,4096]{2,1,0:T(8,128)(2,1)} %param.8) | copy-start | bytes 3145732
  13.0 0.7 %copy-start.6 = (f32[1,256]{1,0:T(1,128)S(1)}, f32[1,256]{1,0:T(1,128)}, u32[]{:S(2)}) copy-start(f32[1,256]{1,0:T(1,128)} %steer_second.1) | copy-start | bytes 3076
  14.1 10.4 %collective-permute-start.5 = (bf16[128,1024]{1,0:T(8,128)(2,1)S(1)}, bf16[128,1024]{1,0:T(8,128)(2,1)S(1)}, u32[]{:S(2)}, u32[]{:S(2)}) collective-permute-start(bf16[128,1024]{1,0:T(8,128)(2,1)S(1)} %weigh.1.refs_4_.refs_6_.refs_1_.refs_3_), channel_id=1, source_target_pairs={{17,16},{18,17},{19,18},{20,19},{21,20},{22,21},{23,22},{24,23},{2... | collective-permute-start | bytes 786440 | tf_op jit(solution)/shard_map/ppermute | solution.py:422
  24.6 9.0 %collective-permute-start.7 = (bf16[128,512]{1,0:T(8,128)(2,1)S(1)}, bf16[128,512]{1,0:T(8,128)(2,1)S(1)}, u32[]{:S(2)}, u32[]{:S(2)}) collective-permute-start(bf16[128,512]{1,0:T(8,128)(2,1)S(1)} %filter.6.refs_6_.refs_5_), channel_id=1, source_target_pairs={{16,0},{17,1},{18,2},{19,3},{20,4},{21,5},{22,6},{23,7},{24,8},{25... | collective-permute-start | bytes 393224 | tf_op jit(solution)/shard_map/ppermute | solution.py:456
  26.0 9.1 %collective-permute-start.8 = (bf16[128,512]{1,0:T(8,128)(2,1)S(1)}, bf16[128,512]{1,0:T(8,128)(2,1)S(1)}, u32[]{:S(2)}, u32[]{:S(2)}) collective-permute-start(bf16[128,512]{1,0:T(8,128)(2,1)S(1)} %filter.7.refs_4_.refs_5_), channel_id=1, source_target_pairs={{16,0},{17,1},{18,2},{19,3},{20,4},{21,5},{22,6},{23,7},{24,8},{25... | collective-permute-start | bytes 393224 | tf_op jit(solution)/shard_map/ppermute | solution.py:456

commit v14 on v11

--- a/solution.py
+++ b/solution.py
@@ -438,7 +438,8 @@
                 uppers.append(upper_grad(1, owns[-1:]))
                 filtered.append(turned_filter(0, owns[-1:] + received[:1]))
                 filtered.append(turned_filter(1, filtered[-1:]))
-                before += (uppers[-1][0], filtered[-1])
+                seconds = moments(owns[-1:])
+                before += (uppers[-1][0], filtered[-1], seconds[0])
             out = call(
                 functools.partial(filter_kernel, group_size),
                 ((last - first) // block,),
@@ -455,8 +456,7 @@
             received.append(lax.ppermute(out, "section", down))
             if hop == sections - 2 and k == 1:
                 uppers = [upper_grad(0, (out,))]
-                seconds = moments((out,))
-                early = [uppers[0][0], seconds[0]]
+                early = [uppers[0][0]]
         top = my_section == sections - 1
         incoming = [
             (jnp.where(top, cotangent[:, first:last], arrived), first)

time: 54.5 us -> 55.4 us (1.017)
  local copies, waits for them, and re-layouts: 0.96 us -> 1.65 us
    unnamed x14, local copies, waits for them, and re-layouts: 0.96 us -> 1.65 us
  transfers between devices with their start and end apart: 9 -> 9, of which waited for: 3 -> 2; matrix products, arithmetic and copies ran while one was open for 0% -> 0% of each run, Pallas kernels for 21% -> 21%
where the time goes in v14:
time: 55.4 us; the launch traced here: 55 us
  blocking collectives  17.4 us (31%)
  starting transfers between devices  14.3 us (26%)
  Pallas kernels  12.9 us (23%)
  waiting for transfers between devices  7.8 us (14%)
  local copies, waits for them, and re-layouts  1.65 us (3%)
  between operations  0.97 us (2%)
    all_to_all x1, blocking collectives, body(): parts = lax.all_to_all(packed, 'seq', 0, 0)  17.4 us
    ppermute x4, waiting for transfers between devices, body(): received.append(lax.ppermute(out, 'section', down))  7.79 us
    pallas_call x4, Pallas kernels, body(): call(functools.partial(first_grad_kernel, group_size), ((last - first) //...  6.41 us
    ppermute x4, starting transfers between devices, body(): received.append(lax.ppermute(out, 'section', down))  5.17 us
    ppermute x1, starting transfers between devices, body(): inputs_halo = lax.ppermute(inputs_sent, ('section', 'seq'), ahead)  4.54 us
    pallas_call x4, Pallas kernels, turned_filter(): call(functools.partial(turned_filter_kernel, group_size), ((last - first)...  4.03 us
    ppermute x1, starting transfers between devices, body(): mid_halo = lax.ppermute(mid_sent, ('section', 'seq'), ahead)  2.42 us
    ppermute x3, starting transfers between devices, send_halo(): halos.append(lax.ppermute(owns[-1], ('section', 'seq'), behind))  2.18 us
  transfers between devices with their start and end apart: 9, of which 2 were waited for; matrix products, arithmetic and copies ran while one was open for 0% of the time, Pallas kernels for 21%

profile of v14, /device:TPU:0, one launch (start us, length us, event | category | flops | bytes accessed | tf_op | source)
XLA Modules:
  0.0 55.0 jit_solution(3972203545604256468)
XLA Ops:
  0.6 0.0 copy-start.3
  0.6 0.1 direct_weigh.2.refs_1_.refs_3_
  0.7 0.0 copy-start
  0.7 0.0 copy-start.4
  0.7 0.0 copy-start.1
  0.8 0.8 %collective-permute-start.2 = (bf16[128,1536]{1,0:T(8,128)(2,1)S(1)}, bf16[128,1536]{1,0:T(8,128)(2,1)S(1)}, u32[]{:S(2)}, u32[]{:S(2)}) collective-permute-start(bf16[128,1536]{1,0:T(8,128)(2,1)S(1)} %direct_weigh.2.refs_1_.refs_3_), channel_id=1, source_target_pairs={{17,16},{18,17},{19,18},{20,19},{21,20},{22,21},{23,22},{24,23},{2... | collective-permute-start | bytes 1179656 | tf_op jit(solution)/shard_map/ppermute | solution.py:421
  1.6 0.1 direct_weigh.3.refs_1_.refs_3_
  1.7 0.7 %collective-permute-start.4 = (bf16[128,1536]{1,0:T(8,128)(2,1)S(1)}, bf16[128,1536]{1,0:T(8,128)(2,1)S(1)}, u32[]{:S(2)}, u32[]{:S(2)}) collective-permute-start(bf16[128,1536]{1,0:T(8,128)(2,1)S(1)} %direct_weigh.3.refs_1_.refs_3_), channel_id=1, source_target_pairs={{17,16},{18,17},{19,18},{20,19},{21,20},{22,21},{23,22},{24,23},{2... | collective-permute-start | bytes 1179656 | tf_op jit(solution)/shard_map/ppermute | solution.py:421
  2.3 0.0 copy-done
  2.4 2.4 %collective-permute-start = (bf16[128,4096]{1,0:T(8,128)(2,1)S(1)}, bf16[128,4096]{1,0:T(8,128)(2,1)S(1)}, u32[]{:S(2)}, u32[]{:S(2)}) collective-permute-start(bf16[128,4096]{1,0:T(8,128)(2,1)S(1)} %bitcast.11), channel_id=1, source_target_pairs={{0,1},{1,2},{2,3},{3,4},{4,5},{5,6},{6,7},{7,8},{8,9},{9,10},{10,1... | collective-permute-start | bytes 3145736 | tf_op jit(solution)/shard_map/ppermute | solution.py:426
  4.8 0.0 copy-done.3
  4.8 4.5 %collective-permute-start.1 = (bf16[128,4096]{1,0:T(8,128)(2,1)S(1)}, bf16[128,4096]{1,0:T(8,128)(2,1)S(1)}, u32[]{:S(2)}, u32[]{:S(2)}) collective-permute-start(bf16[128,4096]{1,0:T(8,128)(2,1)S(1)} %bitcast.35), channel_id=1, source_target_pairs={{0,1},{1,2},{2,3},{3,4},{4,5},{5,6},{6,7},{7,8},{8,9},{9,10},{10,1... | collective-permute-start | bytes 3145736 | tf_op jit(solution)/shard_map/ppermute | solution.py:427
  9.3 0.0 copy-done.4
  9.4 0.2 taps.1.refs_3_
  9.5 0.0 collective-permute-done.2.refs_2_.refs_4_
  9.5 0.0 copy-done.1
  9.6 0.3 filter.4.refs_6_.refs_5_
  9.8 1.3 %collective-permute-start.3 = (bf16[128,1536]{1,0:T(8,128)(2,1)S(1)}, bf16[128,1536]{1,0:T(8,128)(2,1)S(1)}, u32[]{:S(2)}, u32[]{:S(2)}) collective-permute-start(bf16[128,1536]{1,0:T(8,128)(2,1)S(1)} %filter.4.refs_6_.refs_5_), channel_id=1, source_target_pairs={{16,0},{17,1},{18,2},{19,3},{20,4},{21,5},{22,6},{23,7},{24,8},{25... | collective-permute-start | bytes 1179656 | tf_op jit(solution)/shard_map/ppermute | solution.py:456
  11.1 0.0 collective-permute-done.4.refs_2_.refs_4_
  11.1 0.3 filter.5.refs_6_.refs_5_
  11.4 0.0 copy-start.2
  11.4 0.3 upper_grads.4
  11.7 1.0 %copy-done.2 = bf16[1,128,4096]{2,1,0:T(8,128)(2,1)S(1)} copy-done((bf16[1,128,4096]{2,1,0:T(8,128)(2,1)S(1)}, bf16[1,128,4096]{2,1,0:T(8,128)(2,1)}, u32[]{:S(2)}) %copy-start.2) | copy-done | bytes 1048600
  12.7 0.1 weigh.1.refs_4_.refs_6_.refs_0_.refs_1_.refs_3_
  12.8 0.7 %collective-permute-start.5 = (bf16[128,1024]{1,0:T(8,128)(2,1)S(1)}, bf16[128,1024]{1,0:T(8,128)(2,1)S(1)}, u32[]{:S(2)}, u32[]{:S(2)}) collective-permute-start(bf16[128,1024]{1,0:T(8,128)(2,1)S(1)} %weigh.1.refs_4_.refs_6_.refs_0_.refs_1_.refs_3_), channel_id=1, source_target_pairs={{17,16},{18,17},{19,18},{20,19},{21,20},{22,21},{23,22},{24,23},{2... | collective-permute-start | bytes 786440 | tf_op jit(solution)/shard_map/ppermute | solution.py:421
  13.5 1.3 %collective-permute-start.6 = (bf16[128,1536]{1,0:T(8,128)(2,1)S(1)}, bf16[128,1536]{1,0:T(8,128)(2,1)S(1)}, u32[]{:S(2)}, u32[]{:S(2)}) collective-permute-start(bf16[128,1536]{1,0:T(8,128)(2,1)S(1)} %filter.5.refs_6_.refs_5_), channel_id=1, source_target_pairs={{16,0},{17,1},{18,2},{19,3},{20,4},{21,5},{22,6},{23,7},{24,8},{25... | collective-permute-start | bytes 1179656 | tf_op jit(solution)/shard_map/ppermute | solution.py:456
  14.8 0.3 upper_grads.5
  15.1 0.0 copy-start.5
  15.1 6.0 %collective-permute-done.3.refs_5_.refs_6_ = bf16[128,1536]{1,0:T(8,128)(2,1)S(1)} collective-permute-done((bf16[128,1536]{1,0:T(8,128)(2,1)S(1)}, bf16[128,1536]{1,0:T(8,128)(2,1)S(1)}, u32[]{:S(2)}, u32[]{:S(2)}) %collective-permute-start.3) | collective-permute-done | bytes 393248 | tf_op jit(solution)/shard_map/ppermute | solution.py:456
  21.1 0.0 collective-permute-done.refs_2_.refs_4_
  21.1 1.5 %turned_filter.4.refs_4_.refs_7_ = f32[128,1536]{1,0:T(8,128)S(1)} custom-call(s32[1]{0:T(128)} %bitcast.refs_0_.role, bf16[128,4096]{1,0:T(8,128)(2,1)S(1)} %bitcast.16, bf16[128,4096]{1,0:T(8,128)(2,1)S(1)} %collective-permute-done.refs_2_.refs_4_, f32[256,128]{1,0:T(8,128)S(1)} %taps.1.refs_3_, ...), custom_call_target="tpu_custom_call" | custom-call | flops 1000 | tf_op jit(solution)/shard_map/turned_filter/pallas_call | solution.py:396
  22.6 0.0 copy-start.6
  22.6 0.0 copy-done.5
  22.7 0.7 %copy-done.6 = f32[1,256]{1,0:T(1,128)S(1)} copy-done((f32[1,256]{1,0:T(1,128)S(1)}, f32[1,256]{1,0:T(1,128)}, u32[]{:S(2)}) %copy-start.6) | copy-done | bytes 1048
  23.3 1.5 %turned_filter.5.refs_8_.refs_7_ = f32[128,1536]{1,0:T(8,128)S(1)} custom-call(s32[1]{0:T(128)} %bitcast.refs_0_.role, bf16[128,4096]{1,0:T(8,128)(2,1)S(1)} %bitcast.17, bf16[128,4096]{1,0:T(8,128)(2,1)S(1)} %collective-permute-done.refs_2_.refs_4_, f32[256,128]{1,0:T(8,128)S(1)} %taps.1.refs_3_, f32[128,1536]{1,0:T(8,128)S(1)} %turned_filter.4.refs_4_.refs_7_), custom_call_target="tpu_custom_call" | custom-call | flops 1000 | tf_op jit(solution)/shard_map/turned_filter/pallas_call | solution.py:396
  24.9 0.0 collective-permute-done.5.refs_2_.refs_4_
  24.9 1.3 %collective-permute-start.7 = (bf16[128,512]{1,0:T(8,128)(2,1)S(1)}, bf16[128,512]{1,0:T(8,128)(2,1)S(1)}, u32[]{:S(2)}, u32[]{:S(2)}) collective-permute-start(bf16[128,512]{1,0:T(8,128)(2,1)S(1)} %filter.6.refs_6_.refs_5_), channel_id=1, source_target_pairs={{16,0},{17,1},{18,2},{19,3},{20,4},{21,5},{22,6},{23,7},{24,8},{25... | collective-permute-start | bytes 393224 | tf_op jit(solution)/shard_map/ppermute | solution.py:456
  26.3 1.3 %collective-permute-start.8 = (bf16[128,512]{1,0:T(8,128)(2,1)S(1)}, bf16[128,512]{1,0:T(8,128)(2,1)S(1)}, u32[]{:S(2)}, u32[]{:S(2)}) collective-permute-start(bf16[128,512]{1,0:T(8,128)(2,1)S(1)} %filter.7.refs_4_.refs_5_), channel_id=1, source_target_pairs={{16,0},{17,1},{18,2},{19,3},{20,4},{21,5},{22,6},{23,7},{24,8},{25... | collective-permute-start | bytes 393224 | tf_op jit(solution)/shard_map/ppermute | solution.py:456
  27.6 0.5 turned_filter.6.refs_4_.refs_7_
  28.1 0.5 turned_filter.7.refs_6_.refs_7_
  28.6 0.0 collective-permute-done.1.refs_5_
  28.6 2.4 %first_grads.4 = (f32[96,128]{1,0:T(8,128)S(1)}, f32[1,1536]{1,0:T(1,128)S(1)}) custom-call(s32[1]{0:T(128)} %bitcast.refs_0_.role, bf16[128,4096]{1,0:T(8,128)(2,1)S(1)} %bitcast.31, bf16[128,4096]{1,0:T(8,128)(2,1)S(1)} %bitcast.24, bf16[128,4096]{1,0:T(8,128)(2,1)S(1)} %bitcast.40, bf16[128,4096]{1,0:T(8,128)(2,1)S(1)} %collective-permute-done.refs_2_.refs_4_, ...), custom_call_target="tpu_custom_call" | custom-call | flops 2000 | tf_op jit(solution)/shard_map/first_grads/pallas_call | solution.py:476
  31.1 0.0 collective-permute-done.6.refs_6_
  31.1 2.4 %first_grads.5 = (f32[96,128]{1,0:T(8,128)S(1)}, f32[1,1536]{1,0:T(1,128)S(1)}) custom-call(s32[1]{0:T(128)} %bitcast.refs_0_.role, bf16[128,4096]{1,0:T(8,128)(2,1)S(1)} %bitcast.32, bf16[128,4096]{1,0:T(8,128)(2,1)S(1)} %bitcast.25, bf16[128,4096]{1,0:T(8,128)(2,1)S(1)} %bitcast.41, bf16[128,4096]{1,0:T(8,128)(2,1)S(1)} %collective-permute-done.refs_2_.refs_4_, ...), custom_call_target="tpu_custom_call" | custom-call | flops 2000 | tf_op jit(solution)/shard_map/first_grads/pallas_call | solution.py:476
  33.5 0.0 collective-permute-done.7.refs_6_
  33.5 0.8 %first_grads.6 = (f32[32,128]{1,0:T(8,128)S(1)}, f32[1,512]{1,0:T(1,128)S(1)}) custom-call(s32[1]{0:T(128)} %bitcast.refs_0_.role, bf16[128,4096]{1,0:T(8,128)(2,1)S(1)} %bitcast.33, bf16[128,4096]{1,0:T(8,128)(2,1)S(1)} %bitcast.26, bf16[128,4096]{1,0:T(8,128)(2,1)S(1)} %bitcast.42, bf16[128,4096]{1,0:T(8,128)(2,1)S(1)} %collective-permute-done.refs_2_.refs_4_, ...), custom_call_target="tpu_custom_call" | custom-call | flops 2000 | tf_op jit(solution)/shard_map/first_grads/pallas_call | solution.py:476
  34.3 1.8 %collective-permute-done.8.refs_6_ = bf16[128,512]{1,0:T(8,128)(2,1)S(1)} collective-permute-done((bf16[128,512]{1,0:T(8,128)(2,1)S(1)}, bf16[128,512]{1,0:T(8,128)(2,1)S(1)}, u32[]{:S(2)}, u32[]{:S(2)}) %collective-permute-start.8) | collective-permute-done | bytes 131104 | tf_op jit(solution)/shard_map/ppermute | solution.py:456
  36.1 0.8 %first_grads.7 = (f32[32,128]{1,0:T(8,128)S(1)}, f32[1,512]{1,0:T(1,128)S(1)}) custom-call(s32[1]{0:T(128)} %bitcast.refs_0_.role, bf16[128,4096]{1,0:T(8,128)(2,1)S(1)} %bitcast.34, bf16[128,4096]{1,0:T(8,128)(2,1)S(1)} %bitcast.27, bf16[128,4096]{1,0:T(8,128)(2,1)S(1)} %bitcast.43, bf16[128,4096]{1,0:T(8,128)(2,1)S(1)} %collective-permute-done.refs_2_.refs_4_, ...), custom_call_target="tpu_custom_call" | custom-call | flops 2000 | tf_op jit(solution)/shard_map/first_grads/pallas_call | solution.py:476
  36.9 17.4 %all_to_all.5.parts = bf16[16,18,128]{2,1,0:T(8,128)(2,1)S(1)} all-to-all(bf16[16,18,128]{2,1,0:T(8,128)(2,1)S(1)} %pack.1), channel_id=1, replica_groups=mesh['section'=2,'seq'=16] {'seq'}, dimensions={0} | all-to-all | bytes 147456 | tf_op jit(solution)/shard_map/all_to_all | solution.py:499
  54.3 0.7 %step.1 = (f32[1,256]{1,0:T(1,128)}, f32[16,128]{1,0:T(8,128)}) custom-call(s32[1]{0:T(128)} %bitcast.refs_0_.role, bf16[16,18,128]{2,1,0:T(8,128)(2,1)S(1)} %all_to_all.5.parts, f32[1,256]{1,0:T(1,128)S(1)} %get-tuple-element.28.refs_9_.steer_second, f32[16,128]{1,0:T(8,128)S(1)} %get-tuple-element.43.filter_second), custom_call_target="tpu_custom_call" | custom-call | tf_op jit(solution)/shard_map/step/pallas_call | solution.py:500
  (6 shorter events, 0.2 us)
Async XLA Ops:
  0.6 4.2 %copy-start.3 = (bf16[1,128,4096]{2,1,0:T(8,128)(2,1)S(1)}, bf16[1,128,4096]{2,1,0:T(8,128)(2,1)}, u32[]{:S(2)}) copy-start(bf16[1,128,4096]{2,1,0:T(8,128)(2,1)} %param.10) | copy-start | bytes 3145732
  0.7 1.6 %copy-start = (bf16[1,128,4096]{2,1,0:T(8,128)(2,1)S(1)}, bf16[1,128,4096]{2,1,0:T(8,128)(2,1)}, u32[]{:S(2)}) copy-start(bf16[1,128,4096]{2,1,0:T(8,128)(2,1)} %param.9) | copy-start | bytes 3145732
  0.7 8.6 %copy-start.4 = (bf16[1,128,256]{2,1,0:T(8,128)(2,1)S(1)}, bf16[1,128,256]{2,1,0:T(8,128)(2,1)}, u32[]{:S(2)}) copy-start(bf16[1,128,256]{2,1,0:T(8,128)(2,1)} %param.11) | copy-start | bytes 196612
  0.7 8.8 %copy-start.1 = (bf16[128,4096]{1,0:T(8,128)(2,1)S(1)}, bf16[128,4096]{1,0:T(8,128)(2,1)}, u32[]{:S(2)}) copy-start(bf16[128,4096]{1,0:T(8,128)(2,1)} %refs_5_.7) | copy-start | bytes 3145732
  0.8 8.8 %collective-permute-start.2 = (bf16[128,1536]{1,0:T(8,128)(2,1)S(1)}, bf16[128,1536]{1,0:T(8,128)(2,1)S(1)}, u32[]{:S(2)}, u32[]{:S(2)}) collective-permute-start(bf16[128,1536]{1,0:T(8,128)(2,1)S(1)} %direct_weigh.2.refs_1_.refs_3_), channel_id=1, source_target_pairs={{17,16},{18,17},{19,18},{20,19},{21,20},{22,21},{23,22},{24,23},{2... | collective-permute-start | bytes 1179656 | tf_op jit(solution)/shard_map/ppermute | solution.py:421
  1.7 9.5 %collective-permute-start.4 = (bf16[128,1536]{1,0:T(8,128)(2,1)S(1)}, bf16[128,1536]{1,0:T(8,128)(2,1)S(1)}, u32[]{:S(2)}, u32[]{:S(2)}) collective-permute-start(bf16[128,1536]{1,0:T(8,128)(2,1)S(1)} %direct_weigh.3.refs_1_.refs_3_), channel_id=1, source_target_pairs={{17,16},{18,17},{19,18},{20,19},{21,20},{22,21},{23,22},{24,23},{2... | collective-permute-start | bytes 1179656 | tf_op jit(solution)/shard_map/ppermute | solution.py:421
  2.4 18.7 %collective-permute-start = (bf16[128,4096]{1,0:T(8,128)(2,1)S(1)}, bf16[128,4096]{1,0:T(8,128)(2,1)S(1)}, u32[]{:S(2)}, u32[]{:S(2)}) collective-permute-start(bf16[128,4096]{1,0:T(8,128)(2,1)S(1)} %bitcast.11), channel_id=1, source_target_pairs={{0,1},{1,2},{2,3},{3,4},{4,5},{5,6},{6,7},{7,8},{8,9},{9,10},{10,1... | collective-permute-start | bytes 3145736 | tf_op jit(solution)/shard_map/ppermute | solution.py:426
  4.8 23.8 %collective-permute-start.1 = (bf16[128,4096]{1,0:T(8,128)(2,1)S(1)}, bf16[128,4096]{1,0:T(8,128)(2,1)S(1)}, u32[]{:S(2)}, u32[]{:S(2)}) collective-permute-start(bf16[128,4096]{1,0:T(8,128)(2,1)S(1)} %bitcast.35), channel_id=1, source_target_pairs={{0,1},{1,2},{2,3},{3,4},{4,5},{5,6},{6,7},{7,8},{8,9},{9,10},{10,1... | collective-permute-start | bytes 3145736 | tf_op jit(solution)/shard_map/ppermute | solution.py:427
  9.8 11.3 %collective-permute-start.3 = (bf16[128,1536]{1,0:T(8,128)(2,1)S(1)}, bf16[128,1536]{1,0:T(8,128)(2,1)S(1)}, u32[]{:S(2)}, u32[]{:S(2)}) collective-permute-start(bf16[128,1536]{1,0:T(8,128)(2,1)S(1)} %filter.4.refs_6_.refs_5_), channel_id=1, source_target_pairs={{16,0},{17,1},{18,2},{19,3},{20,4},{21,5},{22,6},{23,7},{24,8},{25... | collective-permute-start | bytes 1179656 | tf_op jit(solution)/shard_map/ppermute | solution.py:456
  11.4 1.2 %copy-start.2 = (bf16[1,128,4096]{2,1,0:T(8,128)(2,1)S(1)}, bf16[1,128,4096]{2,1,0:T(8,128)(2,1)}, u32[]{:S(2)}) copy-start(bf16[1,128,4096]{2,1,0:T(8,128)(2,1)} %param.8) | copy-start | bytes 3145732
  12.8 12.1 %collective-permute-start.5 = (bf16[128,1024]{1,0:T(8,128)(2,1)S(1)}, bf16[128,1024]{1,0:T(8,128)(2,1)S(1)}, u32[]{:S(2)}, u32[]{:S(2)}) collective-permute-start(bf16[128,1024]{1,0:T(8,128)(2,1)S(1)} %weigh.1.refs_4_.refs_6_.refs_0_.refs_1_.refs_3_), channel_id=1, source_target_pairs={{17,16},{18,17},{19,18},{20,19},{21,20},{22,21},{23,22},{24,23},{2... | collective-permute-start | bytes 786440 | tf_op jit(solution)/shard_map/ppermute | solution.py:421
  13.5 17.6 %collective-permute-start.6 = (bf16[128,1536]{1,0:T(8,128)(2,1)S(1)}, bf16[128,1536]{1,0:T(8,128)(2,1)S(1)}, u32[]{:S(2)}, u32[]{:S(2)}) collective-permute-start(bf16[128,1536]{1,0:T(8,128)(2,1)S(1)} %filter.5.refs_6_.refs_5_), channel_id=1, source_target_pairs={{16,0},{17,1},{18,2},{19,3},{20,4},{21,5},{22,6},{23,7},{24,8},{25... | collective-permute-start | bytes 1179656 | tf_op jit(solution)/shard_map/ppermute | solution.py:456
  15.1 7.6 %copy-start.5 = (f32[1,128,16]{1,2,0:T(8,128)S(1)}, f32[1,128,16]{1,2,0:T(8,128)}, u32[]{:S(2)}) copy-start(f32[1,128,16]{1,2,0:T(8,128)} %param.13) | copy-start | bytes 24580
  22.6 0.7 %copy-start.6 = (f32[1,256]{1,0:T(1,128)S(1)}, f32[1,256]{1,0:T(1,128)}, u32[]{:S(2)}) copy-start(f32[1,256]{1,0:T(1,128)} %steer_second.1) | copy-start | bytes 3076
  24.9 8.6 %collective-permute-start.7 = (bf16[128,512]{1,0:T(8,128)(2,1)S(1)}, bf16[128,512]{1,0:T(8,128)(2,1)S(1)}, u32[]{:S(2)}, u32[]{:S(2)}) collective-permute-start(bf16[128,512]{1,0:T(8,128)(2,1)S(1)} %filter.6.refs_6_.refs_5_), channel_id=1, source_target_pairs={{16,0},{17,1},{18,2},{19,3},{20,4},{21,5},{22,6},{23,7},{24,8},{25... | collective-permute-start | bytes 393224 | tf_op jit(solution)/shard_map/ppermute | solution.py:456
  26.3 9.8 %collective-permute-start.8 = (bf16[128,512]{1,0:T(8,128)(2,1)S(1)}, bf16[128,512]{1,0:T(8,128)(2,1)S(1)}, u32[]{:S(2)}, u32[]{:S(2)}) collective-permute-start(bf16[128,512]{1,0:T(8,128)(2,1)S(1)} %filter.7.refs_4_.refs_5_), channel_id=1, source_target_pairs={{16,0},{17,1},{18,2},{19,3},{20,4},{21,5},{22,6},{23,7},{24,8},{25... | collective-permute-start | bytes 393224 | tf_op jit(solution)/shard_map/ppermute | solution.py:456

commit v15 on v11

--- a/solution.py
+++ b/solution.py
@@ -11,7 +11,7 @@
 BF16 = jnp.bfloat16
 LANES = 128
 SUB = 32
-CHUNK_EDGES = (0, 3, 6, 7, 8)
+CHUNK_EDGES = (0, 3, 6, 8)
 HALO_EDGES = (0, 3, 6, 8)
 
 

time: 54.5 us -> 56.9 us (1.044)
  waiting for transfers between devices: 7.41 us -> 9.88 us
  starting transfers between devices: 14.3 us -> 13 us
  blocking collectives: 17.6 us -> 18.4 us
    ppermute x4 -> x3, waiting for transfers between devices: 7.4 us -> 9.87 us  [body(): received.append(lax.ppermute(out, 'section', down))]
    ppermute x4 -> x3, starting transfers between devices: 5.17 us -> 3.88 us  [body(): received.append(lax.ppermute(out, 'section', down))]
    all_to_all x1, blocking collectives: 17.6 us -> 18.4 us  [body(): parts = lax.all_to_all(packed, 'seq', 0, 0)]
    pallas_call x4 -> x3, Pallas kernels: 4.07 us -> 4.19 us  [turned_filter(): call(functools.partial(turned_filter_kernel, group_size), ((last - first)...]
    pallas_call x4 -> x3, Pallas kernels: 6.4 us -> 6.47 us  [body(): call(functools.partial(first_grad_kernel, group_size), ((last - first) //...]
  transfers between devices with their start and end apart: 9 -> 8, of which waited for: 3 -> 2; matrix products, arithmetic and copies ran while one was open for 0% -> 0% of each run, Pallas kernels for 21% -> 19%
where the time goes in v15:
time: 56.9 us; the launch traced here: 56.5 us
  blocking collectives  18.4 us (32%)
  Pallas kernels  13.3 us (23%)
  starting transfers between devices  13 us (23%)
  waiting for transfers between devices  9.88 us (17%)
  local copies, waits for them, and re-layouts  0.98 us (2%)
  between operations  0.93 us (2%)
    all_to_all x1, blocking collectives, body(): parts = lax.all_to_all(packed, 'seq', 0, 0)  18.4 us
    ppermute x3, waiting for transfers between devices, body(): received.append(lax.ppermute(out, 'section', down))  9.87 us
    pallas_call x3, Pallas kernels, body(): call(functools.partial(first_grad_kernel, group_size), ((last - first) //...  6.47 us
    ppermute x1, starting transfers between devices, body(): inputs_halo = lax.ppermute(inputs_sent, ('section', 'seq'), ahead)  4.54 us
    pallas_call x3, Pallas kernels, turned_filter(): call(functools.partial(turned_filter_kernel, group_size), ((last - first)...  4.19 us
    ppermute x3, starting transfers between devices, body(): received.append(lax.ppermute(out, 'section', down))  3.88 us
    ppermute x1, starting transfers between devices, body(): mid_halo = lax.ppermute(mid_sent, ('section', 'seq'), ahead)  2.42 us
    ppermute x3, starting transfers between devices, send_halo(): halos.append(lax.ppermute(owns[-1], ('section', 'seq'), behind))  2.18 us
  transfers between devices with their start and end apart: 8, of which 2 were waited for; matrix products, arithmetic and copies ran while one was open for 0% of the time, Pallas kernels for 19%

profile of v15, /device:TPU:0, one launch (start us, length us, event | category | flops | bytes accessed | tf_op | source)
XLA Modules:
  0.0 56.5 jit_solution(14369121083634889363)
XLA Ops:
  0.6 0.0 copy-start.3
  0.6 0.1 direct_weigh.2.refs_1_.refs_3_
  0.7 0.0 copy-start
  0.7 0.0 copy-start.4
  0.7 0.0 copy-start.2
  0.8 0.8 %collective-permute-start.2 = (bf16[128,1536]{1,0:T(8,128)(2,1)S(1)}, bf16[128,1536]{1,0:T(8,128)(2,1)S(1)}, u32[]{:S(2)}, u32[]{:S(2)}) collective-permute-start(bf16[128,1536]{1,0:T(8,128)(2,1)S(1)} %direct_weigh.2.refs_1_.refs_3_), channel_id=1, source_target_pairs={{17,16},{18,17},{19,18},{20,19},{21,20},{22,21},{23,22},{24,23},{2... | collective-permute-start | bytes 1179656 | tf_op jit(solution)/shard_map/ppermute | solution.py:421
  1.6 0.1 direct_weigh.3.refs_1_.refs_3_
  1.7 0.7 %collective-permute-start.4 = (bf16[128,1536]{1,0:T(8,128)(2,1)S(1)}, bf16[128,1536]{1,0:T(8,128)(2,1)S(1)}, u32[]{:S(2)}, u32[]{:S(2)}) collective-permute-start(bf16[128,1536]{1,0:T(8,128)(2,1)S(1)} %direct_weigh.3.refs_1_.refs_3_), channel_id=1, source_target_pairs={{17,16},{18,17},{19,18},{20,19},{21,20},{22,21},{23,22},{24,23},{2... | collective-permute-start | bytes 1179656 | tf_op jit(solution)/shard_map/ppermute | solution.py:421
  2.3 0.0 copy-done
  2.4 2.4 %collective-permute-start = (bf16[128,4096]{1,0:T(8,128)(2,1)S(1)}, bf16[128,4096]{1,0:T(8,128)(2,1)S(1)}, u32[]{:S(2)}, u32[]{:S(2)}) collective-permute-start(bf16[128,4096]{1,0:T(8,128)(2,1)S(1)} %bitcast.11), channel_id=1, source_target_pairs={{0,1},{1,2},{2,3},{3,4},{4,5},{5,6},{6,7},{7,8},{8,9},{9,10},{10,1... | collective-permute-start | bytes 3145736 | tf_op jit(solution)/shard_map/ppermute | solution.py:426
  4.8 0.0 copy-done.3
  4.8 4.5 %collective-permute-start.1 = (bf16[128,4096]{1,0:T(8,128)(2,1)S(1)}, bf16[128,4096]{1,0:T(8,128)(2,1)S(1)}, u32[]{:S(2)}, u32[]{:S(2)}) collective-permute-start(bf16[128,4096]{1,0:T(8,128)(2,1)S(1)} %bitcast.30), channel_id=1, source_target_pairs={{0,1},{1,2},{2,3},{3,4},{4,5},{5,6},{6,7},{7,8},{8,9},{9,10},{10,1... | collective-permute-start | bytes 3145736 | tf_op jit(solution)/shard_map/ppermute | solution.py:427
  9.3 0.0 copy-done.4
  9.4 0.2 taps.1.refs_3_
  9.5 0.0 collective-permute-done.2.refs_2_.refs_4_
  9.5 0.0 copy-done.2
  9.6 0.3 filter.3.refs_6_.refs_5_
  9.8 1.3 %collective-permute-start.3 = (bf16[128,1536]{1,0:T(8,128)(2,1)S(1)}, bf16[128,1536]{1,0:T(8,128)(2,1)S(1)}, u32[]{:S(2)}, u32[]{:S(2)}) collective-permute-start(bf16[128,1536]{1,0:T(8,128)(2,1)S(1)} %filter.3.refs_6_.refs_5_), channel_id=1, source_target_pairs={{16,0},{17,1},{18,2},{19,3},{20,4},{21,5},{22,6},{23,7},{24,8},{25... | collective-permute-start | bytes 1179656 | tf_op jit(solution)/shard_map/ppermute | solution.py:455
  11.1 0.0 collective-permute-done.4.refs_2_.refs_4_
  11.1 0.3 filter.4.refs_6_.refs_0_.refs_5_
  11.4 0.0 copy-start.5
  11.4 0.0 copy-start.1
  11.4 0.3 upper_grads.3
  11.7 0.0 copy-start.6
  11.7 0.4 copy-done.5
  12.1 0.3 copy-done.6
  12.4 0.2 copy-done.1
  12.7 0.1 weigh.1.refs_4_.refs_6_.refs_1_.refs_3_
  12.8 0.7 %collective-permute-start.5 = (bf16[128,1024]{1,0:T(8,128)(2,1)S(1)}, bf16[128,1024]{1,0:T(8,128)(2,1)S(1)}, u32[]{:S(2)}, u32[]{:S(2)}) collective-permute-start(bf16[128,1024]{1,0:T(8,128)(2,1)S(1)} %weigh.1.refs_4_.refs_6_.refs_1_.refs_3_), channel_id=1, source_target_pairs={{17,16},{18,17},{19,18},{20,19},{21,20},{22,21},{23,22},{24,23},{2... | collective-permute-start | bytes 786440 | tf_op jit(solution)/shard_map/ppermute | solution.py:421
  13.5 1.3 %collective-permute-start.6 = (bf16[128,1536]{1,0:T(8,128)(2,1)S(1)}, bf16[128,1536]{1,0:T(8,128)(2,1)S(1)}, u32[]{:S(2)}, u32[]{:S(2)}) collective-permute-start(bf16[128,1536]{1,0:T(8,128)(2,1)S(1)} %filter.4.refs_6_.refs_0_.refs_5_), channel_id=1, source_target_pairs={{16,0},{17,1},{18,2},{19,3},{20,4},{21,5},{22,6},{23,7},{24,8},{25... | collective-permute-start | bytes 1179656 | tf_op jit(solution)/shard_map/ppermute | solution.py:455
  14.8 6.3 %collective-permute-done.3.refs_5_.refs_6_ = bf16[128,1536]{1,0:T(8,128)(2,1)S(1)} collective-permute-done((bf16[128,1536]{1,0:T(8,128)(2,1)S(1)}, bf16[128,1536]{1,0:T(8,128)(2,1)S(1)}, u32[]{:S(2)}, u32[]{:S(2)}) %collective-permute-start.3) | collective-permute-done | bytes 393248 | tf_op jit(solution)/shard_map/ppermute | solution.py:455
  21.1 0.0 collective-permute-done.refs_2_.refs_4_
  21.1 1.5 %turned_filter.3.refs_4_.refs_7_ = f32[128,1536]{1,0:T(8,128)S(1)} custom-call(s32[1]{0:T(128)} %bitcast.refs_0_.role, bf16[128,4096]{1,0:T(8,128)(2,1)S(1)} %bitcast.15, bf16[128,4096]{1,0:T(8,128)(2,1)S(1)} %collective-permute-done.refs_2_.refs_4_, f32[256,128]{1,0:T(8,128)S(1)} %taps.1.refs_3_, ...), custom_call_target="tpu_custom_call" | custom-call | flops 1000 | tf_op jit(solution)/shard_map/turned_filter/pallas_call | solution.py:396
  22.6 0.3 upper_grads.4
  22.9 1.6 %turned_filter.4.refs_8_.refs_7_ = f32[128,1536]{1,0:T(8,128)S(1)} custom-call(s32[1]{0:T(128)} %bitcast.refs_0_.role, bf16[128,4096]{1,0:T(8,128)(2,1)S(1)} %bitcast.17, bf16[128,4096]{1,0:T(8,128)(2,1)S(1)} %collective-permute-done.refs_2_.refs_4_, f32[256,128]{1,0:T(8,128)S(1)} %taps.1.refs_3_, f32[128,1536]{1,0:T(8,128)S(1)} %turned_filter.3.refs_4_.refs_7_), custom_call_target="tpu_custom_call" | custom-call | flops 1000 | tf_op jit(solution)/shard_map/turned_filter/pallas_call | solution.py:396
  24.5 0.0 collective-permute-done.5.refs_2_.refs_4_
  24.5 0.2 filter.5.refs_4_.refs_5_
  24.7 1.3 %collective-permute-start.7 = (bf16[128,1024]{1,0:T(8,128)(2,1)S(1)}, bf16[128,1024]{1,0:T(8,128)(2,1)S(1)}, u32[]{:S(2)}, u32[]{:S(2)}) collective-permute-start(bf16[128,1024]{1,0:T(8,128)(2,1)S(1)} %filter.5.refs_4_.refs_5_), channel_id=1, source_target_pairs={{16,0},{17,1},{18,2},{19,3},{20,4},{21,5},{22,6},{23,7},{24,8},{25... | collective-permute-start | bytes 786440 | tf_op jit(solution)/shard_map/ppermute | solution.py:455
  26.0 1.1 %turned_filter.5.refs_6_.refs_7_ = f32[128,1024]{1,0:T(8,128)S(1)} custom-call(s32[1]{0:T(128)} %bitcast.refs_0_.role, bf16[128,4096]{1,0:T(8,128)(2,1)S(1)} %bitcast.19, bf16[128,4096]{1,0:T(8,128)(2,1)S(1)} %collective-permute-done.refs_2_.refs_4_, f32[256,128]{1,0:T(8,128)S(1)} %taps.1.refs_3_, bf16[128,1024]{1,0:T(8,128)(2,1)S(1)} %filter.5.refs_4_.refs_5_), custom_call_target="tpu_custom_call" | custom-call | flops 1000 | tf_op jit(solution)/shard_map/turned_filter/pallas_call | solution.py:396
  27.1 0.2 upper_grads.5
  27.3 0.0 collective-permute-done.1.refs_5_
  27.3 2.4 %first_grads.3 = (f32[96,128]{1,0:T(8,128)S(1)}, f32[1,1536]{1,0:T(1,128)S(1)}) custom-call(s32[1]{0:T(128)} %bitcast.refs_0_.role, bf16[128,4096]{1,0:T(8,128)(2,1)S(1)} %bitcast.27, bf16[128,4096]{1,0:T(8,128)(2,1)S(1)} %bitcast.21, bf16[128,4096]{1,0:T(8,128)(2,1)S(1)} %bitcast.34, bf16[128,4096]{1,0:T(8,128)(2,1)S(1)} %collective-permute-done.refs_2_.refs_4_, ...), custom_call_target="tpu_custom_call" | custom-call | flops 2000 | tf_op jit(solution)/shard_map/first_grads/pallas_call | solution.py:476
  29.8 0.0 collective-permute-done.6.refs_6_
  29.8 2.4 %first_grads.4 = (f32[96,128]{1,0:T(8,128)S(1)}, f32[1,1536]{1,0:T(1,128)S(1)}) custom-call(s32[1]{0:T(128)} %bitcast.refs_0_.role, bf16[128,4096]{1,0:T(8,128)(2,1)S(1)} %bitcast.28, bf16[128,4096]{1,0:T(8,128)(2,1)S(1)} %bitcast.22, bf16[128,4096]{1,0:T(8,128)(2,1)S(1)} %bitcast.35, bf16[128,4096]{1,0:T(8,128)(2,1)S(1)} %collective-permute-done.refs_2_.refs_4_, ...), custom_call_target="tpu_custom_call" | custom-call | flops 2000 | tf_op jit(solution)/shard_map/first_grads/pallas_call | solution.py:476
  32.2 3.6 %collective-permute-done.7.refs_6_ = bf16[128,1024]{1,0:T(8,128)(2,1)S(1)} collective-permute-done((bf16[128,1024]{1,0:T(8,128)(2,1)S(1)}, bf16[128,1024]{1,0:T(8,128)(2,1)S(1)}, u32[]{:S(2)}, u32[]{:S(2)}) %collective-permute-start.7) | collective-permute-done | bytes 262176 | tf_op jit(solution)/shard_map/ppermute | solution.py:455
  35.8 1.6 %first_grads.5 = (f32[64,128]{1,0:T(8,128)S(1)}, f32[1,1024]{1,0:T(1,128)S(1)}) custom-call(s32[1]{0:T(128)} %bitcast.refs_0_.role, bf16[128,4096]{1,0:T(8,128)(2,1)S(1)} %bitcast.29, bf16[128,4096]{1,0:T(8,128)(2,1)S(1)} %bitcast.23, bf16[128,4096]{1,0:T(8,128)(2,1)S(1)} %bitcast.36, bf16[128,4096]{1,0:T(8,128)(2,1)S(1)} %collective-permute-done.refs_2_.refs_4_, ...), custom_call_target="tpu_custom_call" | custom-call | flops 2000 | tf_op jit(solution)/shard_map/first_grads/pallas_call | solution.py:476
  37.4 18.4 %all_to_all.5.parts = bf16[16,18,128]{2,1,0:T(8,128)(2,1)S(1)} all-to-all(bf16[16,18,128]{2,1,0:T(8,128)(2,1)S(1)} %pack.1), channel_id=1, replica_groups=mesh['section'=2,'seq'=16] {'seq'}, dimensions={0} | all-to-all | bytes 147456 | tf_op jit(solution)/shard_map/all_to_all | solution.py:499
  55.8 0.7 %step.1 = (f32[1,256]{1,0:T(1,128)}, f32[16,128]{1,0:T(8,128)}) custom-call(s32[1]{0:T(128)} %bitcast.refs_0_.role, bf16[16,18,128]{2,1,0:T(8,128)(2,1)S(1)} %all_to_all.5.parts, f32[1,256]{1,0:T(1,128)S(1)} %get-tuple-element.23.refs_4_.steer_second, f32[16,128]{1,0:T(8,128)S(1)} %get-tuple-element.35.filter_second), custom_call_target="tpu_custom_call" | custom-call | tf_op jit(solution)/shard_map/step/pallas_call | solution.py:500
  (2 shorter events, 0.0 us)
Async XLA Ops:
  0.6 4.2 %copy-start.3 = (bf16[1,128,4096]{2,1,0:T(8,128)(2,1)S(1)}, bf16[1,128,4096]{2,1,0:T(8,128)(2,1)}, u32[]{:S(2)}) copy-start(bf16[1,128,4096]{2,1,0:T(8,128)(2,1)} %param.10) | copy-start | bytes 3145732
  0.7 1.6 %copy-start = (bf16[1,128,4096]{2,1,0:T(8,128)(2,1)S(1)}, bf16[1,128,4096]{2,1,0:T(8,128)(2,1)}, u32[]{:S(2)}) copy-start(bf16[1,128,4096]{2,1,0:T(8,128)(2,1)} %param.9) | copy-start | bytes 3145732
  0.7 8.6 %copy-start.4 = (bf16[1,128,256]{2,1,0:T(8,128)(2,1)S(1)}, bf16[1,128,256]{2,1,0:T(8,128)(2,1)}, u32[]{:S(2)}) copy-start(bf16[1,128,256]{2,1,0:T(8,128)(2,1)} %param.11) | copy-start | bytes 196612
  0.7 8.8 %copy-start.2 = (bf16[128,4096]{1,0:T(8,128)(2,1)S(1)}, bf16[128,4096]{1,0:T(8,128)(2,1)}, u32[]{:S(2)}) copy-start(bf16[128,4096]{1,0:T(8,128)(2,1)} %refs_5_.5) | copy-start | bytes 3145732
  0.8 8.8 %collective-permute-start.2 = (bf16[128,1536]{1,0:T(8,128)(2,1)S(1)}, bf16[128,1536]{1,0:T(8,128)(2,1)S(1)}, u32[]{:S(2)}, u32[]{:S(2)}) collective-permute-start(bf16[128,1536]{1,0:T(8,128)(2,1)S(1)} %direct_weigh.2.refs_1_.refs_3_), channel_id=1, source_target_pairs={{17,16},{18,17},{19,18},{20,19},{21,20},{22,21},{23,22},{24,23},{2... | collective-permute-start | bytes 1179656 | tf_op jit(solution)/shard_map/ppermute | solution.py:421
  1.7 9.5 %collective-permute-start.4 = (bf16[128,1536]{1,0:T(8,128)(2,1)S(1)}, bf16[128,1536]{1,0:T(8,128)(2,1)S(1)}, u32[]{:S(2)}, u32[]{:S(2)}) collective-permute-start(bf16[128,1536]{1,0:T(8,128)(2,1)S(1)} %direct_weigh.3.refs_1_.refs_3_), channel_id=1, source_target_pairs={{17,16},{18,17},{19,18},{20,19},{21,20},{22,21},{23,22},{24,23},{2... | collective-permute-start | bytes 1179656 | tf_op jit(solution)/shard_map/ppermute | solution.py:421
  2.4 18.7 %collective-permute-start = (bf16[128,4096]{1,0:T(8,128)(2,1)S(1)}, bf16[128,4096]{1,0:T(8,128)(2,1)S(1)}, u32[]{:S(2)}, u32[]{:S(2)}) collective-permute-start(bf16[128,4096]{1,0:T(8,128)(2,1)S(1)} %bitcast.11), channel_id=1, source_target_pairs={{0,1},{1,2},{2,3},{3,4},{4,5},{5,6},{6,7},{7,8},{8,9},{9,10},{10,1... | collective-permute-start | bytes 3145736 | tf_op jit(solution)/shard_map/ppermute | solution.py:426
  4.8 22.5 %collective-permute-start.1 = (bf16[128,4096]{1,0:T(8,128)(2,1)S(1)}, bf16[128,4096]{1,0:T(8,128)(2,1)S(1)}, u32[]{:S(2)}, u32[]{:S(2)}) collective-permute-start(bf16[128,4096]{1,0:T(8,128)(2,1)S(1)} %bitcast.30), channel_id=1, source_target_pairs={{0,1},{1,2},{2,3},{3,4},{4,5},{5,6},{6,7},{7,8},{8,9},{9,10},{10,1... | collective-permute-start | bytes 3145736 | tf_op jit(solution)/shard_map/ppermute | solution.py:427
  9.8 11.3 %collective-permute-start.3 = (bf16[128,1536]{1,0:T(8,128)(2,1)S(1)}, bf16[128,1536]{1,0:T(8,128)(2,1)S(1)}, u32[]{:S(2)}, u32[]{:S(2)}) collective-permute-start(bf16[128,1536]{1,0:T(8,128)(2,1)S(1)} %filter.3.refs_6_.refs_5_), channel_id=1, source_target_pairs={{16,0},{17,1},{18,2},{19,3},{20,4},{21,5},{22,6},{23,7},{24,8},{25... | collective-permute-start | bytes 1179656 | tf_op jit(solution)/shard_map/ppermute | solution.py:455
  11.4 0.7 %copy-start.5 = (f32[1,128,16]{1,2,0:T(8,128)S(1)}, f32[1,128,16]{1,2,0:T(8,128)}, u32[]{:S(2)}) copy-start(f32[1,128,16]{1,2,0:T(8,128)} %param.13) | copy-start | bytes 24580
  11.4 1.2 %copy-start.1 = (bf16[1,128,4096]{2,1,0:T(8,128)(2,1)S(1)}, bf16[1,128,4096]{2,1,0:T(8,128)(2,1)}, u32[]{:S(2)}) copy-start(bf16[1,128,4096]{2,1,0:T(8,128)(2,1)} %param.8) | copy-start | bytes 3145732
  11.7 0.7 %copy-start.6 = (f32[1,256]{1,0:T(1,128)S(1)}, f32[1,256]{1,0:T(1,128)}, u32[]{:S(2)}) copy-start(f32[1,256]{1,0:T(1,128)} %steer_second.1) | copy-start | bytes 3076
  12.8 11.7 %collective-permute-start.5 = (bf16[128,1024]{1,0:T(8,128)(2,1)S(1)}, bf16[128,1024]{1,0:T(8,128)(2,1)S(1)}, u32[]{:S(2)}, u32[]{:S(2)}) collective-permute-start(bf16[128,1024]{1,0:T(8,128)(2,1)S(1)} %weigh.1.refs_4_.refs_6_.refs_1_.refs_3_), channel_id=1, source_target_pairs={{17,16},{18,17},{19,18},{20,19},{21,20},{22,21},{23,22},{24,23},{2... | collective-permute-start | bytes 786440 | tf_op jit(solution)/shard_map/ppermute | solution.py:421
  13.5 16.3 %collective-permute-start.6 = (bf16[128,1536]{1,0:T(8,128)(2,1)S(1)}, bf16[128,1536]{1,0:T(8,128)(2,1)S(1)}, u32[]{:S(2)}, u32[]{:S(2)}) collective-permute-start(bf16[128,1536]{1,0:T(8,128)(2,1)S(1)} %filter.4.refs_6_.refs_0_.refs_5_), channel_id=1, source_target_pairs={{16,0},{17,1},{18,2},{19,3},{20,4},{21,5},{22,6},{23,7},{24,8},{25... | collective-permute-start | bytes 1179656 | tf_op jit(solution)/shard_map/ppermute | solution.py:455
  24.7 11.0 %collective-permute-start.7 = (bf16[128,1024]{1,0:T(8,128)(2,1)S(1)}, bf16[128,1024]{1,0:T(8,128)(2,1)S(1)}, u32[]{:S(2)}, u32[]{:S(2)}) collective-permute-start(bf16[128,1024]{1,0:T(8,128)(2,1)S(1)} %filter.5.refs_4_.refs_5_), channel_id=1, source_target_pairs={{16,0},{17,1},{18,2},{19,3},{20,4},{21,5},{22,6},{23,7},{24,8},{25... | collective-permute-start | bytes 786440 | tf_op jit(solution)/shard_map/ppermute | solution.py:455
